TPU v7x, 256 devices: a whole 4x4x8 slice. The times are simulated.
256 devices in a mesh: dp: 2 (over core), row: 8 (over z_lo, x), col: 16 (over z_hi, y).
Axes of the slice: x: 4, y: 4, z: 8 (z_hi: 4, z_lo: 2; z = z_hi * 2 + z_lo), core: 2. Of those that a mesh axis runs over, the one named last changes fastest.
Arguments:
- stream: bfloat16 [2048, 8192], P(('dp', 'row'), 'col'), may hold values from -96 to 96
- hidden: bfloat16 [2048, 29568], P(('dp', 'col'), 'row'), may hold values from -4 to 4
- w_down: bfloat16 [29568, 8192], P('row', 'col'), may hold values from -0.03125 to 0.03125
- norm_gain: float32 [8192], P('col'), may hold values from 0.5 to 1.5
- value_head: float32 [8192], P('col'), may hold values from -0.00048828125 to 0.00048828125
- value_bias: float32 [1], replicated, may hold values from -1 to 1
- rewards: float32 [2, 1024], P('dp', 'row'), may hold values from -16 to 16
- segments: int32 [2, 1024], P('dp', 'row'), may hold values from 0 to 5, never falling along the last dimension, each value on 1 to 512 neighbouring positions
Outputs:
- weight_grad: bfloat16 [29568, 8192], P('row', 'col')
- hidden_grad: bfloat16 [2048, 29568], P(('dp', 'col'), 'row')
- stream_grad: bfloat16 [2048, 8192], P(('dp', 'row'), 'col')
All inputs are finite; a program needn't handle non-finite values.
Results may differ from a plain program's by a relative error of at most 0.02.
Values may be sent and summed in bfloat16 or wider, within the bound.
No kernel may reach another device: no remote copies, remote signals or barrier semaphores. Data moves between devices by JAX's collectives and lax.ppermute only.
A program may use at most 128 MiB of HBM per device.

v0:
```python
import jax
import jax.numpy as jnp
from jax import lax
from jax.sharding import PartitionSpec as P

loss_scale = 2097152.0


def carried_in(part, axis, combine, identity):
    count = lax.axis_size(axis)
    place = lax.axis_index(axis)
    ahead = count - 1 - place
    gathered = jax.tree.map(lambda a: lax.all_gather(a, axis), part)
    state = jax.tree.map(lambda a, e: jnp.zeros_like(a) + jnp.asarray(e, a.dtype), part, identity)

    def one(step, state):
        source = count - 1 - step
        return combine(
            state, jax.tree.map(lambda a: lax.dynamic_index_in_dim(a, source, 0, False), gathered)
        )

    return lax.fori_loop(0, ahead, one, state)


def join_ranges(earlier, later):
    owed_high, whole_high, first_high, last_high = earlier
    owed_low, whole_low, first_low, last_low = later
    joined = (last_low == first_high).astype(jnp.float32)
    owed = owed_low + whole_low * joined * owed_high
    whole = whole_low * joined * whole_high
    high_empty = first_high < 0
    low_empty = first_low < 0
    owed = jnp.where(high_empty, owed_low, jnp.where(low_empty, owed_high, owed))
    whole = jnp.where(high_empty, whole_low, jnp.where(low_empty, whole_high, whole))
    first = jnp.where(low_empty, first_high, first_low)
    last = jnp.where(high_empty, last_low, last_high)
    return (owed, whole, first, last)


def per_device(stream, hidden, w_down, norm_gain, value_head, value_bias, rewards, segments):
    y = stream.astype(jnp.float32)
    gw = norm_gain * value_head
    sq, lin = lax.psum((jnp.sum(y * y, axis=1), jnp.sum(y * gw[None, :], axis=1)), "col")
    width_full = stream.shape[1] * lax.axis_size("col")
    rms = jnp.sqrt(sq / width_full + 1e-05)
    value = lin / rms + value_bias[0]
    segment_row = segments[0]
    reward_row = rewards[0]
    tok_here = segment_row.shape[0]
    place = jnp.arange(tok_here, dtype=jnp.int32)
    owed_mask = (segment_row[None, :] == segment_row[:, None]) & (place[None, :] >= place[:, None])
    local_owed = jnp.dot(owed_mask.astype(jnp.float32), reward_row, precision=lax.Precision.HIGHEST)
    tail_link = (segment_row == segment_row[-1]).astype(jnp.float32)
    element = (local_owed[0:1], tail_link[0:1], segment_row[0:1], segment_row[-1:])
    identity = (
        jnp.zeros((1,), jnp.float32),
        jnp.zeros((1,), jnp.float32),
        jnp.full((1,), -1, jnp.int32),
        jnp.full((1,), -1, jnp.int32),
    )
    owed_rest, whole_rest, first_rest, last_rest = carried_in(element, "row", join_ranges, identity)
    carried = (segment_row[-1:] == first_rest).astype(jnp.float32) * owed_rest
    returns = local_owed + tail_link * carried
    count = lax.axis_size("dp") * lax.axis_size("row") * tok_here
    mean = lax.psum(jnp.sum(returns), ("dp", "row")) / count
    spread = lax.psum(jnp.sum((returns - mean) ** 2), ("dp", "row")) / count
    target = (returns - mean) / jnp.sqrt(spread + 1e-05)
    dvalue = loss_scale * (value - target) / count
    grad_full = (dvalue / rms)[:, None] * (
        gw[None, :] - y / rms[:, None] * ((value - value_bias[0]) / width_full)[:, None]
    )
    stream_grad = grad_full.astype(jnp.bfloat16)
    replica_grad = lax.all_gather(stream_grad, "row", axis=0, tiled=True)
    rows = replica_grad
    partial_grad = lax.dot_general(
        lax.all_gather(hidden, "col", axis=0, tiled=True),
        rows,
        (((0,), (0,)), ((), ())),
        preferred_element_type=jnp.float32,
    )
    weight_sum = lax.psum(partial_grad.astype(jnp.bfloat16), "dp")
    rows = replica_grad
    hidden_sum = lax.psum_scatter(
        lax.dot_general(
            rows, w_down, (((1,), (1,)), ((), ())), preferred_element_type=jnp.float32
        ).astype(jnp.bfloat16),
        "col",
        scatter_dimension=0,
        tiled=True,
    )
    return (weight_sum, hidden_sum, stream_grad)


def solution(mesh):
    in_specs = (
        P(("dp", "row"), "col"),
        P(("dp", "col"), "row"),
        P("row", "col"),
        P("col"),
        P("col"),
        P(),
        P("dp", "row"),
        P("dp", "row"),
    )
    out_specs = (P("row", "col"), P(("dp", "col"), "row"), P(("dp", "row"), "col"))
    return jax.shard_map(
        per_device, mesh=mesh, in_specs=in_specs, out_specs=out_specs, check_vma=False
    )
```

profile of v0, /device:TPU:6, one launch (start us, length us, event | category | flops | bytes accessed | tf_op | source)
XLA Modules:
  0.0 505.6 jit_solution(985065910665134869)
XLA Ops:
  7.2 0.0 copy-start
  7.2 0.0 all-gather.5.cloned.1.call-start
  7.2 1.3 fusion.15
  8.5 1.3 broadcast_compare_fusion
  9.8 1.3 dynamic-slice
  11.1 0.0 copy-done
  11.1 0.9 convolution_bitcast_fusion
  12.0 1.3 bitcast_dynamic-update-slice_fusion.1
  13.3 0.7 slice_dynamic-update-slice_fusion
  14.0 1.2 bitcast_dynamic-update-slice_fusion
  15.3 0.7 fusion.12
  15.9 10.8 %all-reduce.4 = (s32[8]{0:T(128)S(1)}, s32[8]{0:T(128)S(1)}) all-reduce(s32[8]{0:T(128)S(1)} %bitcast_dynamic-update-slice_fusion, s32[8]{0:T(128)S(1)} %bitcast_dynamic-update-slice_fusion.1), channel_id=1, replica_groups=mesh['dp'=2,'row'=8,'col'=16] {'row'}, use_global_device_ids=true, to_apply=%add.1 | all-reduce | flops 16 | bytes 128
  26.7 15.7 %all-reduce.6 = (f32[8]{0:T(128)S(1)}, f32[8]{0:T(128)S(1)}) all-reduce(f32[8]{0:T(128)S(1)} %slice_dynamic-update-slice_fusion, f32[8]{0:T(128)S(1)} %fusion.12), channel_id=2, replica_groups=mesh['dp'=2,'row'=8,'col'=16] {'row'}, use_global_device_ids=true, to_apply=%add | all-reduce | flops 16 | bytes 128
  42.4 19.1 %while.17 = (s32[]{:T(128)}, f32[1]{0:T(128)}, s32[1]{0:T(128)}, s32[]{:T(128)}, f32[8,1]{0,1:T(1,128)S(1)}, /*index=5*/s32[8,1]{0,1:T(1,128)S(1)}, s32[8,1]{0,1...) while((s32[]{:T(128)}, f32[1]{0:T(128)}, s32[1]{0:T(128)}, ...), condition=%wide.region_5.6_spmd, body=%wide.region_4.5_spmd.sunk | while | flops 15 | bytes 330 | solution.py:22
  42.4 0.6 constant_dynamic-slice_fusion.6
  43.0 0.6 constant_dynamic-slice_fusion.7
  47.1 0.6 constant_dynamic-slice_fusion.6
  47.8 0.6 constant_dynamic-slice_fusion.7
  51.9 0.6 constant_dynamic-slice_fusion.6
  52.5 0.6 constant_dynamic-slice_fusion.7
  56.7 0.6 constant_dynamic-slice_fusion.6
  57.3 0.6 constant_dynamic-slice_fusion.7
  62.1 1.9 fusion.14
  64.0 44.1 %psum.37 = f32[]{:T(128)} all-reduce(f32[]{:T(128)} %get-tuple-element.162), channel_id=1, replica_groups=mesh['dp'=2,'row'=8,'col'=16] {'dp','row'}, use_global_device_ids=true, to_apply=%region_7.8 | all-reduce | flops 1 | bytes 8 | tf_op jit(solution)/shard_map/psum | solution.py:65
  108.7 0.6 multiply_reduce_fusion
  110.0 31.2 %psum.38 = f32[]{:T(128)} all-reduce(f32[]{:T(128)} %multiply_reduce_fusion), channel_id=1, replica_groups=mesh['dp'=2,'row'=8,'col'=16] {'dp','row'}, use_global_device_ids=true, to_apply=%region_9.10 | all-reduce | flops 1 | bytes 8 | tf_op jit(solution)/shard_map/psum | solution.py:66
  141.8 0.7 mul.58
  142.5 1.0 fusion.2
  143.6 47.5 %all-reduce.5 = (f32[128]{0:T(128)S(1)}, f32[128]{0:T(128)S(1)}) all-reduce(f32[128]{0:T(128)S(1)} %get-tuple-element.137, f32[128]{0:T(128)S(1)} %get-tuple-element.136), channel_id=1, replica_groups=mesh['dp'=2,'row'=8,'col'=16] {'col'}, use_global_device_ids=true, to_apply=%region_1.0 | all-reduce | flops 256 | bytes 2048 | tf_op jit(solution)/shard_map/psum | solution.py:43
  191.1 1.7 fusion.6
  192.8 0.0 all-gather.5.cloned.1.call-update
  192.8 0.0 all-gather.7.cloned.1.call-start
  192.9 0.7 all-gather.7.cloned.1.call-update
  193.6 0.0 reduce-scatter.2.cloned.1.call-start
  193.6 33.6 %all-gather.5.cloned.1.call-done = bf16[1024,512]{1,0:T(8,128)(2,1)} async-done(((bf16[128,512]{1,0:T(8,128)(2,1)}), bf16[1024,512]{1,0:T(8,128)(2,1)}) %all-gather.5.cloned.1.call-update) | async-done | bytes 1048592 | tf_op jit(solution)/shard_map/all_gather | solution.py:73
  227.2 9.7 %convolution_convert_fusion = bf16[1024,3696]{1,0:T(8,128)(2,1)} fusion(bf16[1024,512]{1,0:T(8,128)(2,1)} %all-gather.5.cloned.1.call-done, bf16[3696,512]{1,0:T(8,128)(2,1)} %param.12), kind=kOutput, calls=%fused_computation.4 | convolution fusion | flops 3879321600 | bytes 12402688 | tf_op jit(solution)/shard_map/dot_general | solution.py:84
  236.9 0.0 copy-start.1
  236.9 0.0 reduce-scatter.2.cloned.1.call-update
  236.9 0.0 all-reduce.9.cloned.1.call-start
  237.0 95.4 %all-gather.7.cloned.1.call-done = bf16[1024,3696]{1,0:T(8,128)(2,1)} async-done(((bf16[64,3696]{1,0:T(8,128)(2,1)}), bf16[1024,3696]{1,0:T(8,128)(2,1)}) %all-gather.7.cloned.1.call-update) | async-done | bytes 7569424 | tf_op jit(solution)/shard_map/all_gather | solution.py:76
  332.3 0.0 copy-done.1
  332.3 10.7 %fusion = bf16[3696,512]{1,0:T(8,128)(2,1)} fusion(bf16[1024,512]{1,0:T(8,128)(2,1)S(1)} %copy-done.1, bf16[1024,3696]{1,0:T(8,128)(2,1)} %all-gather.7.cloned.1.call-done), kind=kOutput, calls=%fused_computation.6 | convolution fusion | flops 3877429248 | bytes 12402688 | tf_op jit(solution)/shard_map/dot_general | solution.py:75
  343.0 0.0 all-reduce.9.cloned.1.call-update
  343.0 114.9 %reduce-scatter.2.cloned.1.call-done = bf16[64,3696]{1,0:T(8,128)(2,1)} async-done(((bf16[1024,3696]{1,0:T(8,128)(2,1)}), bf16[64,3696]{1,0:T(8,128)(2,1)}) %reduce-scatter.2.cloned.1.call-update) | async-done | bytes 473104 | tf_op jit(solution)/shard_map/reduce_scatter | solution.py:83
  457.9 36.9 %all-reduce.9.cloned.1.call-done = bf16[3696,512]{1,0:T(8,128)(2,1)} async-done(((bf16[3696,512]{1,0:T(8,128)(2,1)}), bf16[3696,512]{1,0:T(8,128)(2,1)}) %all-reduce.9.cloned.1.call-update) | async-done | bytes 3784720 | tf_op jit(solution)/shard_map/psum | solution.py:81
  494.8 4.2 copy.30
  (6 shorter events, 0.0 us)
Async XLA Ops:
  7.2 3.9 copy-start
  7.2 220.0 %all-gather.5.cloned.1.call-start = ((), (), s32[]{:S(2)}) async-start(), calls=%async_computation.1 | async-start | bytes 1179648 | tf_op jit(solution)/shard_map/all_gather | solution.py:73
  192.8 139.5 %all-gather.7.cloned.1.call-start = ((), (), s32[]{:S(2)}) async-start(), calls=%async_computation.2 | async-start | bytes 8077312 | tf_op jit(solution)/shard_map/all_gather | solution.py:76
  193.6 264.3 %reduce-scatter.2.cloned.1.call-start = ((), (), s32[]{:S(2)}) async-start(), calls=%async_computation.4 | async-start | bytes 8077312 | tf_op jit(solution)/shard_map/reduce_scatter | solution.py:83
  236.9 95.4 %copy-start.1 = (bf16[1024,512]{1,0:T(8,128)(2,1)S(1)}, bf16[1024,512]{1,0:T(8,128)(2,1)}, u32[]{:S(2)}) copy-start(bf16[1024,512]{1,0:T(8,128)(2,1)} %all-gather.5.cloned.1.call-done) | copy-start | bytes 3145732
  236.9 257.9 %all-reduce.9.cloned.1.call-start = ((), (), s32[]{:S(2)}) async-start(), calls=%async_computation.3 | async-start | bytes 7569408 | tf_op jit(solution)/shard_map/psum | solution.py:81
Sparse Core Ops, SparseCore 0:
  193.0 34.2 all-gather.4
  229.7 102.6 all-gather.6
  336.7 121.1 reduce-scatter.1
  461.2 33.6 all-reduce.8
where the time goes:
time: 508 us; the launch traced here: 506 us
  waiting for transfers between devices  281 us (55%)
  blocking collectives  149 us (29%)
  matrix products  21.3 us (4%)
  between operations  16.5 us (3%)
  local copies, waits for them, and re-layouts  14.8 us (3%)
  loops' own time  14.2 us (3%)
  other arithmetic  7.91 us (2%)
    reduce_scatter x1, waiting for transfers between devices, per_device(): lax.psum_scatter(lax.dot_general(rows, w_down, (((1,), (1,)), ((), ())),...  115 us
    all_gather x1, waiting for transfers between devices, per_device(): lax.all_gather(hidden, 'col', axis=0, tiled=True)  95.4 us
    psum x1, blocking collectives, per_device(): lax.psum((jnp.sum(y * y, axis=1), jnp.sum(y * gw[None, :], axis=1)), 'col')  47.5 us
    psum x1, blocking collectives, per_device(): mean = lax.psum(jnp.sum(returns), ('dp', 'row')) / count  44.1 us
    psum x1, waiting for transfers between devices, per_device(): weight_sum = lax.psum(partial_grad.astype(jnp.bfloat16), 'dp')  36.9 us
    all_gather x1, waiting for transfers between devices, per_device(): replica_grad = lax.all_gather(stream_grad, 'row', axis=0, tiled=True)  33.6 us
    psum x1, blocking collectives, per_device(): spread = lax.psum(jnp.sum((returns - mean) ** 2), ('dp', 'row')) / count  31.2 us
    unnamed x2, blocking collectives  26.4 us
  transfers between devices with their start and end apart: 4, of which 4 were waited for; matrix products, arithmetic and copies ran while one was open for 4% of the time, Pallas kernels for 0%

commit v1 on v0

v1 whole, which is shorter than its diff:
```python
import functools

import jax
import jax.numpy as jnp
from jax import lax
from jax.experimental import pallas as pl
from jax.experimental.pallas import tpu as pltpu
from jax.sharding import PartitionSpec as P

loss_scale = 2097152.0
bf16, f32 = jnp.bfloat16, jnp.float32
WIDTH, COUNT = 8192.0, 2048.0

PAIR = [(c, c ^ 1) for c in range(16)]
MATE = [(c, c ^ 3) for c in range(16)]
ZUP = [(c, (c + 4) % 16) for c in range(16)]
ZDOWN = [(c, (c + 12) % 16) for c in range(16)]
ZONE = [(c, c ^ 4) for c in range(16)]
ZTHREE = [(c, c ^ 12) for c in range(16)]
ZLO = [(r, r ^ 4) for r in range(8)]
CORE = [(0, 1), (1, 0)]
XONE = [(r, r ^ 1) for r in range(8)]
XTHREE = [(r, r ^ 3) for r in range(8)]
VMEM_LIMIT = 48 * 1024 * 1024


def send(a, axis, perm, name):
    with jax.named_scope(name):
        return lax.ppermute(a, axis, perm)


def col(a, perm, name):
    return send(a, "col", perm, name)


def row(a, perm, name):
    return send(a, "row", perm, name)


def core(a, name):
    return send(a, "dp", CORE, name)


def after(a, *others):
    return lax.optimization_barrier((a, *others))[0]


def sds(shape, dtype):
    return jax.ShapeDtypeStruct(shape, dtype)


def call(body, out_shape, args, in_specs=None, scratch=(), flops=0, moved=0, name=None):
    extra = {} if in_specs is None else {"in_specs": in_specs}
    with jax.named_scope(name or getattr(body, "__name__", "fold")):
      return pl.pallas_call(
        body,
        out_shape=out_shape,
        scratch_shapes=list(scratch),
        compiler_params=pltpu.CompilerParams(vmem_limit_bytes=VMEM_LIMIT),
        cost_estimate=pl.CostEstimate(flops=flops, bytes_accessed=moved, transcendentals=0),
        **extra,
    )(*args)


def place():
    r, c = lax.axis_index("row"), lax.axis_index("col")
    return r % 4, r // 4, c % 4, c // 4


def prep_body(stream, gain, head, reward, segment, out, s_v, g_v, h_v, r_v, i_v, sems):
    moves = [
        pltpu.make_async_copy(src, dst, sems.at[i])
        for i, (src, dst) in enumerate(
            ((stream, s_v), (gain, g_v), (head, h_v), (reward, r_v), (segment, i_v))
        )
    ]
    for m in moves:
        m.start()
    for m in moves:
        m.wait()

    def parts(v):
        high = v.astype(bf16).astype(f32)
        mid = (v - high).astype(bf16).astype(f32)
        return high, mid, v - high - mid

    out[0:128] = s_v[...]
    rows = parts(g_v[...] * h_v[...])
    rows += (jnp.concatenate([*parts(r_v[...]), i_v[...].astype(f32)], 1),)
    line = lax.broadcasted_iota(jnp.int32, (16, 512), 0)
    extra = jnp.zeros((16, 512), f32)
    for i, a in enumerate(rows):
        extra = jnp.where(line == i, jnp.broadcast_to(a, (16, 512)), extra)
    out[128:144] = extra.astype(bf16)


def pick_body(own, other, out):
    x, _, y, _ = place()

    @pl.when(lax.rem(x, 2) == y // 2)
    def _():
        out[0:128] = own[0:128]

    @pl.when(lax.rem(x, 2) != y // 2)
    def _():
        out[0:128] = other[0:128]

    mine, theirs = own[128:144].astype(f32), other[128:144].astype(f32)
    even = lax.rem(x, 2) == 0
    line = lax.broadcasted_iota(jnp.int32, mine.shape, 0)
    first = jnp.where(even, mine, theirs)
    second = jnp.where(even, theirs, mine)
    second = jnp.broadcast_to(second[3:4], mine.shape)
    out[128:144] = jnp.where(line == 4, second, jnp.where(line == 3, first, mine)).astype(bf16)


def gains_of(block):
    extra = block[128:144].astype(f32)
    return extra[0:1] + extra[1:2] + extra[2:3]


def sums_body(near, away, sums, owed):
    x, _, _, _ = place()
    gw = gains_of(near)
    sums[...] = jnp.zeros(sums.shape, f32)

    def total(a):
        a = sum(a[:, 128 * i : 128 * i + 128] for i in range(8))
        return jnp.sum(a.T, axis=0, keepdims=True)

    for i, block in enumerate((near, away)):
        v = block[0:128].astype(f32)
        sums[2 * i : 2 * i + 1] = total(v * v)
        sums[2 * i + 1 : 2 * i + 2] = total(v * gw)
        extra = block[128:144].astype(f32)
        side = jnp.where(i == 0, x // 2, 1 - x // 2)
        for j in range(2):
            line = extra[3 + j : 4 + j]
            owed[pl.ds(2 * side + j, 1)] = line[:, 0:128] + line[:, 128:256] + line[:, 256:384]
            owed[pl.ds(4 + 2 * side + j, 1)] = line[:, 384:512]


def coefs_body(here, there, bias, out, target):
    x, zlo, y, _ = place()

    def rows(at):
        mine, theirs = here[at : at + 4], there[at : at + 4]
        return jnp.where(zlo == 0, mine, theirs), jnp.where(zlo == 0, theirs, mine)

    value = jnp.concatenate([*rows(8), *rows(16)], 0)
    segment = jnp.concatenate([*rows(12), *rows(20)], 0)
    shape = value.shape
    line = lax.broadcasted_iota(jnp.int32, shape, 0) % 8
    lane = lax.broadcasted_iota(jnp.int32, shape, 1)

    def ahead(a, step):
        if step >= 128:
            return pltpu.roll(a, shape[0] - step // 128, 0)
        here = pltpu.roll(a, 128 - step, 1)
        below = pltpu.roll(here, shape[0] - 1, 0)
        return jnp.where(lane + step < 128, here, below)

    step = 1
    while step < 1024:
        inside = line * 128 + lane + step < 1024
        same = inside & (ahead(segment, step) == segment)
        value = value + jnp.where(same, ahead(value, step), 0.0)
        step *= 2
    mean = jnp.sum(value) / COUNT
    off = value - mean
    spread = jnp.sum(off * off) / COUNT
    target[...] = (off / jnp.sqrt(jnp.broadcast_to(spread, shape) + 1e-05))[:8]
    wanted, sq, lin = [], [], []
    for i in range(4):
        zl = zlo if i < 2 else 1 - zlo
        b = x // 2 if i % 2 == 0 else 1 - x // 2
        wanted.append(target[pl.ds(4 * zl + 2 * b + y // 2, 1)])
        src = (here, there)[i // 2]
        at = 2 * (i % 2)
        sq.append(src[at : at + 1])
        lin.append(src[at + 1 : at + 2])
    wanted, sq, lin = (jnp.concatenate(a, 0) for a in (wanted, sq, lin))
    rms = jnp.sqrt(sq / WIDTH + 1e-05)
    head = lin / rms
    dvalue = loss_scale * (head + bias[0] - wanted) / COUNT
    out[0:4] = dvalue / rms
    out[4:8] = head / WIDTH / rms


def columns(coefs):
    padded = jnp.concatenate([coefs, jnp.zeros((120, 128), f32)], 0).T
    lane = lax.broadcasted_iota(jnp.int32, (128, 128), 1)

    def column(at):
        return jnp.sum(jnp.where(lane == at, padded, 0.0), axis=1, keepdims=True)

    return column


def formed(block, s, l, gains):
    return (s * (gains - block.astype(f32) * l)).astype(bf16)


def own_grad_body(stream, block, coefs, coefs_mate, grad):
    x, _, y, _ = place()
    column = columns(jnp.where(lax.rem(x, 2) == y // 2, coefs[...], coefs_mate[...]))
    grad[...] = formed(stream[...], column(0), column(4), gains_of(block)[:, :512])


def grad_body(coefs, here, there, g_own, g_other):
    x, zlo, y, zhi = place()
    odd = lax.rem(y, 2)
    column = columns(coefs[...])
    gains = gains_of(here)
    spots = {2: (0, 32), 1: (128, 64), 3: (96, 160), 0: (192, 224)}
    for k in range(4):
        z = lax.rem(zhi + k, 4)
        zl, b = z // 2, lax.rem(z, 2)
        at = jnp.where(zl == zlo, 0, 2) + jnp.where(b == x // 2, 0, 1)
        s_all, l_all = column(at), column(4 + at)
        s_all = jnp.where(odd == 0, s_all, jnp.concatenate([s_all[64:], s_all[:64]], 0))
        l_all = jnp.where(odd == 0, l_all, jnp.concatenate([l_all[64:], l_all[:64]], 0))
        start = jnp.where(b == x // 2, 0, 144)
        for same, src in ((True, here), (False, there)):

            @pl.when((zl == zlo) == same)
            def _(src=src, s_all=s_all, l_all=l_all, start=start, k=k):
                for who, out in ((0, g_own), (1, g_other)):
                    parity = odd if who == 0 else 1 - odd
                    for i in range(2):
                        first = pl.multiple_of(start + 64 * parity + 32 * i, 16)
                        rows = slice(64 * who + 32 * i, 64 * who + 32 * i + 32)
                        out[spots[k][i] : spots[k][i] + 32] = formed(
                            src[pl.ds(first, 32)], s_all[rows], l_all[rows], gains
                        )


LO = 1856
CHUNKS = ((0, 1024), (1024, 2048), (2048, 3072), (3072, 3696))
GOT = LO // 2
HIGH = 3696 - LO
SPANS = ((0, GOT), (GOT, LO), (LO, HIGH + GOT), (HIGH + GOT, 3696))
def inner_body(*refs):
    g_own, g_other, w, got0, got1, other0, other1 = refs[:7]
    sent, own, (w_v, m_v, sems) = refs[7:11], refs[11:15], refs[15:]
    p = lax.axis_index("dp")
    for i, (a, b) in enumerate(CHUNKS):
        pltpu.make_async_copy(w.at[a:b], w_v.at[a:b], sems.at[i]).start()

    def mate_copy(j, low, high):
        a, b = SPANS[j]
        src = (*low, *high)[j]
        off = (0, GOT, HIGH, HIGH + GOT)[j]
        return pltpu.make_async_copy(src.at[a - off : b - off], m_v.at[a:b], sems.at[4 + j])

    got, other = (got0, got1), (other0, other1)

    @pl.when(p == 0)
    def _():
        for j in range(4):
            mate_copy(j, got, other).start()

    @pl.when(p == 1)
    def _():
        for j in range(4):
            mate_copy(j, other, got).start()

    left = jnp.concatenate([g_other[:, :512], g_own[:, :512]], 0)
    right = jnp.concatenate([g_other[:, 512:], g_own[:, 512:]], 0)
    nt = (((1,), (1,)), ((), ()))
    waits = ((0, 1), (2,), (3,), ())
    for i, (a, b) in enumerate(CHUNKS):
        pltpu.make_async_copy(w.at[a:b], w_v.at[a:b], sems.at[i]).wait()
        for j in waits[i]:
            mate_copy(j, other, other).wait()
        for f in range(a, b, 512):
            e = min(f + 512, b)
            out = lax.dot_general(left, w_v[f:e], nt, preferred_element_type=f32)
            out = out + lax.dot_general(right, m_v[f:e], nt, preferred_element_type=f32)
            for n in range(4):
                sent[n][:, f:e] = out[64 * n : 64 * n + 64].astype(bf16)
                own[n][:, f:e] = out[256 + 64 * n : 256 + 64 * n + 64]


def outer_body(*refs, first):
    pieces, (g_own, g_other), (give, keep, h_v, g_v) = refs[:8], refs[8:10], refs[10:]
    p = lax.axis_index("dp")
    for n, piece in enumerate(pieces):
        h_v[64 * n : 64 * n + 64] = piece[...]
    for n, side in enumerate((1 - p, p)):
        start = pl.multiple_of(first + 256 * side, 256)
        g_v[:256, 256 * n : 256 * n + 256] = g_own[:, pl.ds(start, 256)]
        g_v[256:, 256 * n : 256 * n + 256] = g_other[:, pl.ds(start, 256)]
    for f in range(0, 3696, 512):
        e = min(f + 512, 3696)
        out = lax.dot_general(
            h_v[:, f:e], g_v[...], (((0,), (0,)), ((), ())), preferred_element_type=f32
        )
        give[f:e] = out[:, :256].astype(bf16)
        keep[f:e] = out[:, 256:]


def outer(pieces, g_own, g_other, first, name):
    return call(
        functools.partial(outer_body, first=first),
        [sds((3696, 256), bf16), sds((3696, 256), f32)],
        (*pieces, g_own, g_other),
        scratch=[pltpu.VMEM((512, 3696), bf16), pltpu.VMEM((512, 512), bf16)],
        flops=512 * 1024 * 3696,
        moved=8 << 20,
        name=name,
    )


def fold_body(*refs, extra, split):
    own, other = refs[:2]
    for i in range(2):
        rows = slice(32 * i, 32 * i + 32)
        total = own[rows] + other[rows].astype(f32)
        for m in refs[2 + i * extra : 2 + i * extra + extra]:
            total = total + m[...].astype(f32)
        if split:
            refs[2 + 2 * extra + i][...] = total.astype(bf16)
        else:
            refs[2 + 2 * extra][rows] = total.astype(bf16)


def fold(own, other, first=(), second=(), split=True):
    extra = len(first)
    wide = own.shape[1]
    out = [sds((32, wide), bf16)] * 2 if split else sds((64, wide), bf16)
    return call(
        functools.partial(fold_body, extra=extra, split=split),
        out,
        (own, other, *first, *second),
        moved=64 * wide * 10,
    )


def join_body(mine, other, out):
    p = lax.axis_index("dp")
    out[:, pl.ds(pl.multiple_of(256 * p, 256), 256)] = mine[...]
    out[:, pl.ds(pl.multiple_of(256 * (1 - p), 256), 256)] = other[...]


def join(mine, other):
    rows = mine.shape[0]
    tile = 1232
    return pl.pallas_call(
        join_body,
        grid=(rows // tile,),
        in_specs=[pl.BlockSpec((tile, 256), lambda i: (i, 0))] * 2,
        out_specs=pl.BlockSpec((tile, 512), lambda i: (i, 0)),
        out_shape=sds((rows, 512), bf16),
        compiler_params=pltpu.CompilerParams(vmem_limit_bytes=VMEM_LIMIT),
        cost_estimate=pl.CostEstimate(flops=0, bytes_accessed=rows * 2048, transcendentals=0),
    )(mine, other)


def per_device(stream, hidden, w_down, norm_gain, value_head, value_bias, rewards, segments):
    p = lax.axis_index("dp")
    smem = pl.BlockSpec(memory_space=pltpu.SMEM)
    vmem = pl.BlockSpec(memory_space=pltpu.VMEM)
    hbm = pl.BlockSpec(memory_space=pl.ANY)

    payload = call(
        prep_body,
        sds((144, 512), bf16),
        (stream, norm_gain[None], value_head[None], rewards, segments),
        in_specs=[hbm] * 5,
        scratch=[
            pltpu.VMEM((128, 512), bf16),
            pltpu.VMEM((1, 512), f32),
            pltpu.VMEM((1, 512), f32),
            pltpu.VMEM((1, 128), f32),
            pltpu.VMEM((1, 128), jnp.int32),
            pltpu.SemaphoreType.DMA((5,)),
        ],
    )
    payload_mate = col(payload, MATE, "payload_mate")
    ready = after(hidden, payload)
    y3 = col(ready, PAIR, "y3")
    ha, hb = ready[:32], ready[32:]
    down_a = col(ha, ZUP, "down_a")
    up_b = col(hb, ZDOWN, "up_b")

    w_half = lax.dynamic_slice_in_dim(w_down, p * HIGH, LO, 0)
    got0 = col(after(w_half[:GOT], payload_mate), MATE, "got0")
    got1 = col(after(w_half[GOT:], got0), MATE, "got1")

    block = jnp.concatenate([payload, payload_mate], 1)
    near = call(
        pick_body, sds((144, 1024), bf16), (block, row(block, XONE, "block_x1"))
    )
    near = after(near, y3, down_a, up_b)
    away = row(near, XTHREE, "block_x3")
    here = jnp.concatenate([near, away], 0)
    there = row(here, ZLO, "block_zlo")

    h1 = jnp.concatenate([up_b, down_a], 0)
    y1 = col(h1, PAIR, "y1")
    far_a = col(down_a, ZUP, "far_a")
    far_b = col(up_b, ZDOWN, "far_b")
    far_a, far_b = lax.optimization_barrier((far_a, far_b, away))[:2]
    up_a = col(after(ha, far_b), ZDOWN, "up_a")
    down_b = col(after(hb, far_a), ZUP, "down_b")
    h0 = jnp.concatenate([far_a, far_b], 0)
    h2 = jnp.concatenate([up_a, down_b], 0)
    y0 = col(after(h0, y1), PAIR, "y0")

    sums, owed = call(sums_body, (sds((8, 128), f32), sds((8, 128), f32)), (near, away))
    owed_other = core(owed, "owed_other")
    gates = ((y1, far_a, far_b), (got0,), (up_a, down_b))
    for i, perm in enumerate((PAIR, ZONE, ZTHREE)):
        sums = after(sums, *gates[i])
        sums = sums + col(sums, perm, f"sums{i}")
    y2 = col(after(h2, y0, sums), PAIR, "y2")
    got_other0 = core(got0, "got_other0")
    tiny = jnp.concatenate([sums, owed, owed_other], 0)
    coefs = call(
        coefs_body,
        sds((8, 128), f32),
        (tiny, row(tiny, ZLO, "sums_zlo"), value_bias),
        in_specs=[vmem, vmem, smem],
        scratch=[pltpu.VMEM((8, 128), f32)],
    )
    g_own, g_other = call(
        grad_body,
        (sds((256, 1024), bf16), sds((256, 1024), bf16)),
        (after(coefs, there, got1), here, there),
        moved=4 << 20,
    )
    got_other1 = core(got1, "got_other1")

    pieces = (h0, h1, h2, hidden, y0, y1, y2, y3)
    mate_give, mate_keep = outer(pieces, g_own, g_other, 512, "outer_mate")
    mate_got = core(mate_give, "mate_got")
    outs = call(
        inner_body,
        [sds((64, 3696), bf16)] * 4 + [sds((64, 3696), f32)] * 4,
        (after(g_own, mate_keep), g_other, w_down, got0, got1, got_other0, got_other1),
        in_specs=[vmem] * 2 + [hbm] * 5,
        scratch=[
            pltpu.VMEM((3696, 512), bf16),
            pltpu.VMEM((3696, 512), bf16),
            pltpu.SemaphoreType.DMA((8,)),
        ],
        flops=2 * 512 * 1024 * 3696,
        moved=13 << 20,
    )
    sent, own = outs[:4], outs[4:]
    w_send = (mate_keep + mate_got.astype(f32)).astype(bf16)
    w_recv = col(w_send, MATE, "w_recv")
    t = [col(a, PAIR, f"t{i}") for i, a in enumerate(sent)]

    give, keep = outer(pieces, after(g_own, w_send, own[0]), g_other, 0, "outer_own")
    own_got = core(give, "own_got")
    q0a, q0b = fold(own[0], after(t[0], keep))
    from_down = col(q0a, ZUP, "from_down")
    from_up = col(q0b, ZDOWN, "from_up")
    q1b, q1a = fold(own[1], t[1])
    from_down, from_up, q1a, q1b = lax.optimization_barrier((from_down, from_up, q1a, q1b))
    pure_b = col(q1b, ZUP, "pure_b")
    pure_a = col(q1a, ZDOWN, "pure_a")
    q2a, q2b = fold(own[2], after(t[2], pure_a, pure_b), (from_down,), (from_up,))
    mixed_a = col(q2a, ZUP, "mixed_a")
    mixed_b = col(q2b, ZDOWN, "mixed_b")
    hidden_grad = fold(own[3], t[3], (pure_a, mixed_a), (pure_b, mixed_b), split=False)

    coefs_mate = col(after(coefs, q0a), MATE, "coefs_mate")
    stream_grad = call(
        own_grad_body, sds((128, 512), bf16), (stream, near, coefs, coefs_mate)
    )

    keep = after(keep, hidden_grad)
    w_sum = (keep + own_got.astype(f32) + w_recv.astype(f32)).astype(bf16)
    weight_grad = join(w_sum, core(w_sum, "w_sum"))
    return weight_grad, hidden_grad, stream_grad


def solution(mesh):
    in_specs = (
        P(("dp", "row"), "col"),
        P(("dp", "col"), "row"),
        P("row", "col"),
        P("col"),
        P("col"),
        P(),
        P("dp", "row"),
        P("dp", "row"),
    )
    out_specs = (P("row", "col"), P(("dp", "col"), "row"), P(("dp", "row"), "col"))
    return jax.shard_map(
        per_device, mesh=mesh, in_specs=in_specs, out_specs=out_specs, check_vma=False
    )
```

time: 508 us -> 191 us (0.38)
  waiting for transfers between devices: 281 us -> 92.9 us
  blocking collectives: 149 us -> 0 us
  starting transfers between devices: 0.16 us -> 59.3 us
  Pallas kernels: 0 us -> 25.6 us
  matrix products: 21.3 us -> 0 us
  between operations: 16.5 us -> 1.55 us
  loops' own time: 14.2 us -> 0 us
  local copies, waits for them, and re-layouts: 14.8 us -> 7.43 us
    all_gather x2 -> x0, waiting for transfers between devices: 129 us -> none  [the longest x1 95.4 us: per_device(): lax.all_gather(hidden, 'col', axis=0, tiled=True)]
    psum x3 -> x0, blocking collectives: 123 us -> none  [the longest x1 47.5 us: per_device(): lax.psum((jnp.sum(y * y, axis=1), jnp.sum(y * gw[None, :], axis=1)), 'col')]
    reduce_scatter x1 -> x0, waiting for transfers between devices: 115 us -> none  [per_device(): lax.psum_scatter(lax.dot_general(rows, w_down, (((1,), (1,)), ((), ())),...]
    ppermute x0 -> x38, waiting for transfers between devices: none -> 92.9 us  [send(): return lax.ppermute(a, axis, perm)]
    ppermute x0 -> x38, starting transfers between devices: none -> 59.3 us  [send(): return lax.ppermute(a, axis, perm)]
    psum x1 -> x0, waiting for transfers between devices: 36.9 us -> none  [per_device(): weight_sum = lax.psum(partial_grad.astype(jnp.bfloat16), 'dp')]
    unnamed x2 -> x0, blocking collectives: 26.4 us -> none
    pallas_call x0 -> x14, Pallas kernels: none -> 25.6 us  [the longest x13 23.2 us: call(): pl.pallas_call(body, out_shape=out_shape, scratch_shapes=list(scratch), c...]
  transfers between devices with their start and end apart: 4 -> 38, of which waited for: 4 -> 17; matrix products, arithmetic and copies ran while one was open for 4% -> 2% of each run, Pallas kernels for 0% -> 10%
where the time goes in v1:
time: 191 us
  waiting for transfers between devices  92.9 us (49%)
  starting transfers between devices  59.3 us (31%)
  Pallas kernels  25.6 us (13%)
  local copies, waits for them, and re-layouts  7.43 us (4%)
  other arithmetic  4.09 us (2%)
    ppermute x38, waiting for transfers between devices, send(): return lax.ppermute(a, axis, perm)  92.9 us
    ppermute x38, starting transfers between devices, send(): return lax.ppermute(a, axis, perm)  59.3 us
    pallas_call x13, Pallas kernels, call(): pl.pallas_call(body, out_shape=out_shape, scratch_shapes=list(scratch), c...  23.2 us
    unnamed x30, local copies, waits for them, and re-layouts  4.65 us
  transfers between devices with their start and end apart: 38, of which 17 were waited for; matrix products, arithmetic and copies ran while one was open for 2% of the time, Pallas kernels for 10%

profile of v1, /device:TPU:6, one launch (start us, length us, event | category | flops | bytes accessed | tf_op | source)
XLA Modules:
  0.0 190.9 jit_solution(7466221805331987646)
XLA Ops:
  0.6 0.9 copy-done.1
  1.5 0.7 copy-done.4
  2.2 0.7 copy-done.5
  2.9 0.7 copy-done.6
  3.6 0.7 copy-done.7
  4.4 3.1 %collective-permute-start.4 = (bf16[144,512]{1,0:T(8,128)(2,1)S(1)}, bf16[144,512]{1,0:T(8,128)(2,1)S(1)}, u32[]{:S(2)}, u32[]{:S(2)}) collective-permute-start(bf16[144,512]{1,0:T(8,128)(2,1)S(1)} %prep_body.1), channel_id=1, source_target_pairs={{0,3},{1,2},{2,1},{3,0},{4,7},{5,6},{6,5},{7,4},{8,11},{9,10},{10,... | collective-permute-start | bytes 442376 | tf_op jit(solution)/shard_map/payload_mate/ppermute | solution.py:29
  7.7 1.1 fusion
  8.8 3.3 %collective-permute-start = (bf16[32,3696]{1,0:T(8,128)(2,1)S(1)}, bf16[32,3696]{1,0:T(8,128)(2,1)S(1)}, u32[]{:S(2)}, u32[]{:S(2)}) collective-permute-start(bf16[32,3696]{1,0:T(8,128)(2,1)S(1)} %get-tuple-element.53), channel_id=1, source_target_pairs={{0,4},{1,5},{2,6},{3,7},{4,8},{5,9},{6,10},{7,11},{8,12},{9,13},{1... | collective-permute-start | bytes 709640 | tf_op jit(solution)/shard_map/down_a/ppermute | solution.py:29
  12.1 3.1 %collective-permute-start.2 = (bf16[32,3696]{1,0:T(8,128)(2,1)S(1)}, bf16[32,3696]{1,0:T(8,128)(2,1)S(1)}, u32[]{:S(2)}, u32[]{:S(2)}) collective-permute-start(bf16[32,3696]{1,0:T(8,128)(2,1)S(1)} %get-tuple-element.54), channel_id=1, source_target_pairs={{0,12},{1,13},{2,14},{3,15},{4,0},{5,1},{6,2},{7,3},{8,4},{9,5},{1... | collective-permute-start | bytes 709640 | tf_op jit(solution)/shard_map/up_b/ppermute | solution.py:29
  15.2 1.6 constant_dynamic-slice_fusion.1
  16.9 0.9 collective-permute-start.5
  17.8 1.1 collective-permute-start.13
  18.9 3.2 %collective-permute-done = bf16[32,3696]{1,0:T(8,128)(2,1)S(1)} collective-permute-done((bf16[32,3696]{1,0:T(8,128)(2,1)S(1)}, bf16[32,3696]{1,0:T(8,128)(2,1)S(1)}, u32[]{:S(2)}, u32[]{:S(2)}) %collective-permute-start) | collective-permute-done | bytes 236576 | tf_op jit(solution)/shard_map/down_a/ppermute | solution.py:29
  22.1 4.1 %collective-permute-start.1 = (bf16[32,3696]{1,0:T(8,128)(2,1)S(1)}, bf16[32,3696]{1,0:T(8,128)(2,1)S(1)}, u32[]{:S(2)}, u32[]{:S(2)}) collective-permute-start(bf16[32,3696]{1,0:T(8,128)(2,1)S(1)} %collective-permute-done), channel_id=1, source_target_pairs={{0,4},{1,5},{2,6},{3,7},{4,8},{5,9},{6,10},{7,11},{8,12},{9,13},{1... | collective-permute-start | bytes 709640 | tf_op jit(solution)/shard_map/far_a/ppermute | solution.py:29
  26.2 0.6 collective-permute-done.2
  26.8 2.8 %collective-permute-start.3 = (bf16[32,3696]{1,0:T(8,128)(2,1)S(1)}, bf16[32,3696]{1,0:T(8,128)(2,1)S(1)}, u32[]{:S(2)}, u32[]{:S(2)}) collective-permute-start(bf16[32,3696]{1,0:T(8,128)(2,1)S(1)} %collective-permute-done.2), channel_id=1, source_target_pairs={{0,12},{1,13},{2,14},{3,15},{4,0},{5,1},{6,2},{7,3},{8,4},{9,5},{1... | collective-permute-start | bytes 709640 | tf_op jit(solution)/shard_map/far_b/ppermute | solution.py:29
  29.7 0.6 collective-permute-start.7
  30.2 1.8 collective-permute-start.10
  32.1 3.7 %collective-permute-done.1 = bf16[32,3696]{1,0:T(8,128)(2,1)S(1)} collective-permute-done((bf16[32,3696]{1,0:T(8,128)(2,1)S(1)}, bf16[32,3696]{1,0:T(8,128)(2,1)S(1)}, u32[]{:S(2)}, u32[]{:S(2)}) %collective-permute-start.1) | collective-permute-done | bytes 236576 | tf_op jit(solution)/shard_map/far_a/ppermute | solution.py:29
  35.8 4.4 %collective-permute-done.3 = bf16[32,3696]{1,0:T(8,128)(2,1)S(1)} collective-permute-done((bf16[32,3696]{1,0:T(8,128)(2,1)S(1)}, bf16[32,3696]{1,0:T(8,128)(2,1)S(1)}, u32[]{:S(2)}, u32[]{:S(2)}) %collective-permute-start.3) | collective-permute-done | bytes 236576 | tf_op jit(solution)/shard_map/far_b/ppermute | solution.py:29
  40.2 2.9 %collective-permute-start.8 = (bf16[32,3696]{1,0:T(8,128)(2,1)S(1)}, bf16[32,3696]{1,0:T(8,128)(2,1)S(1)}, u32[]{:S(2)}, u32[]{:S(2)}) collective-permute-start(bf16[32,3696]{1,0:T(8,128)(2,1)S(1)} %get-tuple-element.53), channel_id=1, source_target_pairs={{0,12},{1,13},{2,14},{3,15},{4,0},{5,1},{6,2},{7,3},{8,4},{9,5},{1... | collective-permute-start | bytes 709640 | tf_op jit(solution)/shard_map/up_a/ppermute | solution.py:29
  43.1 1.0 collective-permute-start.9
  44.1 1.7 collective-permute-start.11
  46.1 0.4 collective-permute-start.12
  46.5 9.2 %collective-permute-done.12 = f32[8,128]{1,0:T(8,128)S(1)} collective-permute-done((f32[8,128]{1,0:T(8,128)S(1)}, f32[8,128]{1,0:T(8,128)S(1)}, u32[]{:S(2)}, u32[]{:S(2)}) %collective-permute-start.12) | collective-permute-done | bytes 4128 | tf_op jit(solution)/shard_map/sums0/ppermute | solution.py:29
  55.6 3.9 %collective-permute-start.14 = (f32[8,128]{1,0:T(8,128)S(1)}, f32[8,128]{1,0:T(8,128)S(1)}, u32[]{:S(2)}, u32[]{:S(2)}) collective-permute-start(f32[8,128]{1,0:T(8,128)S(1)} %add.21), channel_id=1, source_target_pairs={{0,4},{1,5},{2,6},{3,7},{4,0},{5,1},{6,2},{7,3},{8,12},{9,13},{10,... | collective-permute-start | bytes 12296 | tf_op jit(solution)/shard_map/sums1/ppermute | solution.py:29
  59.6 0.9 collective-permute-start.20
  60.5 7.1 %collective-permute-done.14 = f32[8,128]{1,0:T(8,128)S(1)} collective-permute-done((f32[8,128]{1,0:T(8,128)S(1)}, f32[8,128]{1,0:T(8,128)S(1)}, u32[]{:S(2)}, u32[]{:S(2)}) %collective-permute-start.14) | collective-permute-done | bytes 4128 | tf_op jit(solution)/shard_map/sums1/ppermute | solution.py:29
  67.6 3.6 %collective-permute-start.15 = (f32[8,128]{1,0:T(8,128)S(1)}, f32[8,128]{1,0:T(8,128)S(1)}, u32[]{:S(2)}, u32[]{:S(2)}) collective-permute-start(f32[8,128]{1,0:T(8,128)S(1)} %add.23), channel_id=1, source_target_pairs={{0,12},{1,13},{2,14},{3,15},{4,8},{5,9},{6,10},{7,11},{8,4},{9,5},... | collective-permute-start | bytes 12296 | tf_op jit(solution)/shard_map/sums2/ppermute | solution.py:29
  71.2 2.1 %collective-permute-done.15 = f32[8,128]{1,0:T(8,128)S(1)} collective-permute-done((f32[8,128]{1,0:T(8,128)S(1)}, f32[8,128]{1,0:T(8,128)S(1)}, u32[]{:S(2)}, u32[]{:S(2)}) %collective-permute-start.15) | collective-permute-done | bytes 4128 | tf_op jit(solution)/shard_map/sums2/ppermute | solution.py:29
  73.3 1.8 collective-permute-start.16
  75.1 1.2 collective-permute-done.17
  76.3 4.6 %collective-permute-start.18 = (f32[24,128]{1,0:T(8,128)S(1)}, f32[24,128]{1,0:T(8,128)S(1)}, u32[]{:S(2)}, u32[]{:S(2)}) collective-permute-start(f32[24,128]{1,0:T(8,128)S(1)} %pad_maximum_fusion.1.here), channel_id=1, source_target_pairs={{0,64},{16,80},{32,96},{48,112},{64,0},{80,16},{96,32},{112,48},{1... | collective-permute-start | bytes 36872 | tf_op jit(solution)/shard_map/sums_zlo/ppermute | solution.py:29
  81.5 1.0 collective-permute-done.18.there
  82.6 0.8 coefs_body.1.coefs
  83.4 1.2 grad_body.1
  84.6 4.7 %outer_mate.1 = (bf16[3696,256]{1,0:T(8,128)(2,1)}, f32[3696,256]{1,0:T(8,128)}) custom-call(bf16[64,3696]{1,0:T(8,128)(2,1)S(1)} %constant_dynamic-update-slice_fusion.refs_0_, bf16[64,3696]{1,0:T(8,128)(2,1)S(1)} %constant_dynamic-update-slice_fusion.2.refs_1_, bf16[64,3696]{1,0:T(8,128)(2,1)S(1)} %constant_dynamic-update-slice_fusion.4.refs_2_, ...), custom_call_target="tpu_custom_call" | custom-call | flops 1937768448 | bytes 8388608 | tf_op jit(solution)/shard_map/outer_mate/pallas_call | solution.py:55
  89.3 0.5 collective-permute-start.22
  89.9 5.6 %collective-permute-done.22.refs_5_ = bf16[928,512]{1,0:T(8,128)(2,1)S(1)} collective-permute-done((bf16[928,512]{1,0:T(8,128)(2,1)S(1)}, bf16[928,512]{1,0:T(8,128)(2,1)S(1)}, u32[]{:S(2)}, u32[]{:S(2)}) %collective-permute-start.22) | collective-permute-done | bytes 950304 | tf_op jit(solution)/shard_map/got_other0/ppermute | solution.py:29
  95.5 1.0 copy-done.12
  96.5 9.1 %inner_body.1 = (bf16[64,3696]{1,0:T(8,128)(2,1)S(1)}, bf16[64,3696]{1,0:T(8,128)(2,1)S(1)}, bf16[64,3696]{1,0:T(8,128)(2,1)S(1)}, bf16[64,3696]{1,0:T(8,128)(2,...) custom-call(bf16[256,1024]{1,0:T(8,128)(2,1)S(1)} %get-tuple-element.71.r, ...), custom_call_target="tpu_custom_call" | custom-call | flops 3875536896 | bytes 13631488 | tf_op jit(solution)/shard_map/inner_body/pallas_call | solution.py:55
  105.6 3.3 %add_convert_fusion.1 = bf16[3696,256]{1,0:T(8,128)(2,1)} fusion(f32[3696,256]{1,0:T(8,128)S(1)} %copy-done.9, bf16[3696,256]{1,0:T(8,128)(2,1)} %collective-permute-done.21), kind=kLoop, calls=%fused_computation.1 | loop fusion | flops 2838528 | bytes 7569408 | tf_op jit(solution)/shard_map/convert_element_type | solution.py:452
  108.9 0.3 collective-permute-start.35
  109.2 4.7 %outer_own.1 = (bf16[3696,256]{1,0:T(8,128)(2,1)}, f32[3696,256]{1,0:T(8,128)}) custom-call(bf16[64,3696]{1,0:T(8,128)(2,1)S(1)} %constant_dynamic-update-slice_fusion.refs_0_, bf16[64,3696]{1,0:T(8,128)(2,1)S(1)} %constant_dynamic-update-slice_fusion.2.refs_1_, bf16[64,3696]{1,0:T(8,128)(2,1)S(1)} %constant_dynamic-update-slice_fusion.4.refs_2_, ...), custom_call_target="tpu_custom_call" | custom-call | flops 1937768448 | bytes 8388608 | tf_op jit(solution)/shard_map/outer_own/pallas_call | solution.py:55
  114.0 0.3 collective-permute-start.25
  114.4 1.7 collective-permute-start.28
  116.0 0.3 collective-permute-start.30
  116.4 11.3 %collective-permute-done.25.refs_1_ = bf16[64,3696]{1,0:T(8,128)(2,1)S(1)} collective-permute-done((bf16[64,3696]{1,0:T(8,128)(2,1)S(1)}, bf16[64,3696]{1,0:T(8,128)(2,1)S(1)}, u32[]{:S(2)}, u32[]{:S(2)}) %collective-permute-start.25) | collective-permute-done | bytes 473120 | tf_op jit(solution)/shard_map/t0/ppermute | solution.py:29
  127.8 2.7 %collective-permute-start.26 = (bf16[32,3696]{1,0:T(8,128)(2,1)S(1)}, bf16[32,3696]{1,0:T(8,128)(2,1)S(1)}, u32[]{:S(2)}, u32[]{:S(2)}) collective-permute-start(bf16[32,3696]{1,0:T(8,128)(2,1)S(1)} %get-tuple-element.77), channel_id=1, source_target_pairs={{0,4},{1,5},{2,6},{3,7},{4,8},{5,9},{6,10},{7,11},{8,12},{9,13},{1... | collective-permute-start | bytes 709640 | tf_op jit(solution)/shard_map/from_down/ppermute | solution.py:29
  130.4 7.4 %collective-permute-done.28.refs_1_ = bf16[64,3696]{1,0:T(8,128)(2,1)S(1)} collective-permute-done((bf16[64,3696]{1,0:T(8,128)(2,1)S(1)}, bf16[64,3696]{1,0:T(8,128)(2,1)S(1)}, u32[]{:S(2)}, u32[]{:S(2)}) %collective-permute-start.28) | collective-permute-done | bytes 473120 | tf_op jit(solution)/shard_map/t1/ppermute | solution.py:29
  137.9 1.6 collective-permute-start.27
  139.6 10.7 %collective-permute-done.27.refs_3_ = bf16[32,3696]{1,0:T(8,128)(2,1)S(1)} collective-permute-done((bf16[32,3696]{1,0:T(8,128)(2,1)S(1)}, bf16[32,3696]{1,0:T(8,128)(2,1)S(1)}, u32[]{:S(2)}, u32[]{:S(2)}) %collective-permute-start.27) | collective-permute-done | bytes 236576 | tf_op jit(solution)/shard_map/from_up/ppermute | solution.py:29
  150.3 0.6 collective-permute-start.29
  150.9 3.7 %collective-permute-start.31 = (bf16[32,3696]{1,0:T(8,128)(2,1)S(1)}, bf16[32,3696]{1,0:T(8,128)(2,1)S(1)}, u32[]{:S(2)}, u32[]{:S(2)}) collective-permute-start(bf16[32,3696]{1,0:T(8,128)(2,1)S(1)} %get-tuple-element.86), channel_id=1, source_target_pairs={{0,4},{1,5},{2,6},{3,7},{4,8},{5,9},{6,10},{7,11},{8,12},{9,13},{1... | collective-permute-start | bytes 709640 | tf_op jit(solution)/shard_map/pure_b/ppermute | solution.py:29
  154.7 9.6 %collective-permute-done.29.refs_2_ = bf16[32,3696]{1,0:T(8,128)(2,1)S(1)} collective-permute-done((bf16[32,3696]{1,0:T(8,128)(2,1)S(1)}, bf16[32,3696]{1,0:T(8,128)(2,1)S(1)}, u32[]{:S(2)}, u32[]{:S(2)}) %collective-permute-start.29) | collective-permute-done | bytes 236576 | tf_op jit(solution)/shard_map/pure_a/ppermute | solution.py:29
  164.5 4.5 %collective-permute-start.32 = (bf16[32,3696]{1,0:T(8,128)(2,1)S(1)}, bf16[32,3696]{1,0:T(8,128)(2,1)S(1)}, u32[]{:S(2)}, u32[]{:S(2)}) collective-permute-start(bf16[32,3696]{1,0:T(8,128)(2,1)S(1)} %get-tuple-element.90), channel_id=1, source_target_pairs={{0,4},{1,5},{2,6},{3,7},{4,8},{5,9},{6,10},{7,11},{8,12},{9,13},{1... | collective-permute-start | bytes 709640 | tf_op jit(solution)/shard_map/mixed_a/ppermute | solution.py:29
  169.2 10.2 %collective-permute-done.32.refs_3_ = bf16[32,3696]{1,0:T(8,128)(2,1)S(1)} collective-permute-done((bf16[32,3696]{1,0:T(8,128)(2,1)S(1)}, bf16[32,3696]{1,0:T(8,128)(2,1)S(1)}, u32[]{:S(2)}, u32[]{:S(2)}) %collective-permute-start.32) | collective-permute-done | bytes 236576 | tf_op jit(solution)/shard_map/mixed_a/ppermute | solution.py:29
  179.4 1.4 collective-permute-done.33.refs_5_
  180.8 1.0 fold.7
  181.8 0.8 add_convert_fusion.mine
  182.7 0.6 collective-permute-start.37
  183.3 4.3 %collective-permute-done.37.coefs_mate = f32[8,128]{1,0:T(8,128)S(1)} collective-permute-done((f32[8,128]{1,0:T(8,128)S(1)}, f32[8,128]{1,0:T(8,128)S(1)}, u32[]{:S(2)}, u32[]{:S(2)}) %collective-permute-start.37) | collective-permute-done | bytes 4128 | tf_op jit(solution)/shard_map/coefs_mate/ppermute | solution.py:29
  187.6 0.9 own_grad_body.1
  188.5 2.4 %shard_map.103 = bf16[3696,512]{1,0:T(8,128)(2,1)} custom-call(bf16[3696,256]{1,0:T(8,128)(2,1)S(1)} %add_convert_fusion.mine, bf16[3696,256]{1,0:T(8,128)(2,1)S(1)} %collective-permute-done.36.other), custom_call_target="tpu_custom_call" | custom-call | bytes 7569408 | tf_op jit(solution)/shard_map/pallas_call | solution.py:349
  (69 shorter events, 1.9 us)
Async XLA Ops:
  0.6 0.9 copy-start.1
  1.5 0.7 copy-start.4
  2.2 0.7 copy-start.5
  2.9 0.7 copy-start.6
  3.6 0.7 copy-start.7
  4.4 12.4 %collective-permute-start.4 = (bf16[144,512]{1,0:T(8,128)(2,1)S(1)}, bf16[144,512]{1,0:T(8,128)(2,1)S(1)}, u32[]{:S(2)}, u32[]{:S(2)}) collective-permute-start(bf16[144,512]{1,0:T(8,128)(2,1)S(1)} %prep_body.1), channel_id=1, source_target_pairs={{0,3},{1,2},{2,1},{3,0},{4,7},{5,6},{6,5},{7,4},{8,11},{9,10},{10,... | collective-permute-start | bytes 442376 | tf_op jit(solution)/shard_map/payload_mate/ppermute | solution.py:29
  7.5 22.1 %collective-permute-start.6 = (bf16[64,3696]{1,0:T(8,128)(2,1)}, bf16[64,3696]{1,0:T(8,128)(2,1)S(1)}, u32[]{:S(2)}, u32[]{:S(2)}) collective-permute-start(bf16[64,3696]{1,0:T(8,128)(2,1)} %refs_3_.3), channel_id=1, source_target_pairs={{0,1},{1,0},{2,3},{3,2},{4,5},{5,4},{6,7},{7,6},{8,9},{9,8},{10,11... | collective-permute-start | bytes 1419272 | tf_op jit(solution)/shard_map/y3/ppermute | solution.py:29
  8.8 13.3 %collective-permute-start = (bf16[32,3696]{1,0:T(8,128)(2,1)S(1)}, bf16[32,3696]{1,0:T(8,128)(2,1)S(1)}, u32[]{:S(2)}, u32[]{:S(2)}) collective-permute-start(bf16[32,3696]{1,0:T(8,128)(2,1)S(1)} %get-tuple-element.53), channel_id=1, source_target_pairs={{0,4},{1,5},{2,6},{3,7},{4,8},{5,9},{6,10},{7,11},{8,12},{9,13},{1... | collective-permute-start | bytes 709640 | tf_op jit(solution)/shard_map/down_a/ppermute | solution.py:29
  12.1 14.7 %collective-permute-start.2 = (bf16[32,3696]{1,0:T(8,128)(2,1)S(1)}, bf16[32,3696]{1,0:T(8,128)(2,1)S(1)}, u32[]{:S(2)}, u32[]{:S(2)}) collective-permute-start(bf16[32,3696]{1,0:T(8,128)(2,1)S(1)} %get-tuple-element.54), channel_id=1, source_target_pairs={{0,12},{1,13},{2,14},{3,15},{4,0},{5,1},{6,2},{7,3},{8,4},{9,5},{1... | collective-permute-start | bytes 709640 | tf_op jit(solution)/shard_map/up_b/ppermute | solution.py:29
  16.9 67.7 %copy-start.3 = (bf16[64,3696]{1,0:T(8,128)(2,1)S(1)}, bf16[64,3696]{1,0:T(8,128)(2,1)}, u32[]{:S(2)}) copy-start(bf16[64,3696]{1,0:T(8,128)(2,1)} %refs_3_.3) | copy-start | bytes 1419268
  16.9 12.7 %collective-permute-start.5 = (bf16[144,1024]{1,0:T(8,128)(2,1)S(1)}, bf16[144,1024]{1,0:T(8,128)(2,1)S(1)}, u32[]{:S(2)}, u32[]{:S(2)}) collective-permute-start(bf16[144,1024]{1,0:T(8,128)(2,1)S(1)} %pad_maximum_fusion.own), channel_id=1, source_target_pairs={{0,16},{16,0},{32,48},{48,32},{64,80},{80,64},{96,112},{112,96},{1... | collective-permute-start | bytes 884744 | tf_op jit(solution)/shard_map/block_x1/ppermute | solution.py:29
  17.8 37.8 %collective-permute-start.13 = (bf16[928,512]{1,0:T(8,128)(2,1)S(1)}, bf16[928,512]{1,0:T(8,128)(2,1)S(1)}, u32[]{:S(2)}, u32[]{:S(2)}) collective-permute-start(bf16[928,512]{1,0:T(8,128)(2,1)S(1)} %get-tuple-element.58), channel_id=1, source_target_pairs={{0,3},{1,2},{2,1},{3,0},{4,7},{5,6},{6,5},{7,4},{8,11},{9,10},{10,... | collective-permute-start | bytes 2850824 | tf_op jit(solution)/shard_map/got0/ppermute | solution.py:29
  22.1 13.7 %collective-permute-start.1 = (bf16[32,3696]{1,0:T(8,128)(2,1)S(1)}, bf16[32,3696]{1,0:T(8,128)(2,1)S(1)}, u32[]{:S(2)}, u32[]{:S(2)}) collective-permute-start(bf16[32,3696]{1,0:T(8,128)(2,1)S(1)} %collective-permute-done), channel_id=1, source_target_pairs={{0,4},{1,5},{2,6},{3,7},{4,8},{5,9},{6,10},{7,11},{8,12},{9,13},{1... | collective-permute-start | bytes 709640 | tf_op jit(solution)/shard_map/far_a/ppermute | solution.py:29
  26.8 13.4 %collective-permute-start.3 = (bf16[32,3696]{1,0:T(8,128)(2,1)S(1)}, bf16[32,3696]{1,0:T(8,128)(2,1)S(1)}, u32[]{:S(2)}, u32[]{:S(2)}) collective-permute-start(bf16[32,3696]{1,0:T(8,128)(2,1)S(1)} %collective-permute-done.2), channel_id=1, source_target_pairs={{0,12},{1,13},{2,14},{3,15},{4,0},{5,1},{6,2},{7,3},{8,4},{9,5},{1... | collective-permute-start | bytes 709640 | tf_op jit(solution)/shard_map/far_b/ppermute | solution.py:29
  29.7 10.5 %collective-permute-start.7 = (bf16[144,1024]{1,0:T(8,128)(2,1)S(1)}, bf16[144,1024]{1,0:T(8,128)(2,1)S(1)}, u32[]{:S(2)}, u32[]{:S(2)}) collective-permute-start(bf16[144,1024]{1,0:T(8,128)(2,1)S(1)} %pick_body.1.near.block), channel_id=1, source_target_pairs={{0,48},{16,32},{32,16},{48,0},{64,112},{80,96},{96,80},{112,64},{1... | collective-permute-start | bytes 884744 | tf_op jit(solution)/shard_map/block_x3/ppermute | solution.py:29
  30.2 13.8 %collective-permute-start.10 = (bf16[64,3696]{1,0:T(8,128)(2,1)S(1)}, bf16[64,3696]{1,0:T(8,128)(2,1)S(1)}, u32[]{:S(2)}, u32[]{:S(2)}) collective-permute-start(bf16[64,3696]{1,0:T(8,128)(2,1)S(1)} %constant_dynamic-update-slice_fusion.2.refs_1_), channel_id=1, source_target_pairs={{0,1},{1,0},{2,3},{3,2},{4,5},{5,4},{6,7},{7,6},{8,9},{9,8},{10,11... | collective-permute-start | bytes 1419272 | tf_op jit(solution)/shard_map/y1/ppermute | solution.py:29
  40.2 19.4 %collective-permute-start.8 = (bf16[32,3696]{1,0:T(8,128)(2,1)S(1)}, bf16[32,3696]{1,0:T(8,128)(2,1)S(1)}, u32[]{:S(2)}, u32[]{:S(2)}) collective-permute-start(bf16[32,3696]{1,0:T(8,128)(2,1)S(1)} %get-tuple-element.53), channel_id=1, source_target_pairs={{0,12},{1,13},{2,14},{3,15},{4,0},{5,1},{6,2},{7,3},{8,4},{9,5},{1... | collective-permute-start | bytes 709640 | tf_op jit(solution)/shard_map/up_a/ppermute | solution.py:29
  43.1 24.5 %collective-permute-start.9 = (bf16[32,3696]{1,0:T(8,128)(2,1)S(1)}, bf16[32,3696]{1,0:T(8,128)(2,1)S(1)}, u32[]{:S(2)}, u32[]{:S(2)}) collective-permute-start(bf16[32,3696]{1,0:T(8,128)(2,1)S(1)} %get-tuple-element.54), channel_id=1, source_target_pairs={{0,4},{1,5},{2,6},{3,7},{4,8},{5,9},{6,10},{7,11},{8,12},{9,13},{1... | collective-permute-start | bytes 709640 | tf_op jit(solution)/shard_map/down_b/ppermute | solution.py:29
  44.1 29.2 %collective-permute-start.11 = (bf16[64,3696]{1,0:T(8,128)(2,1)S(1)}, bf16[64,3696]{1,0:T(8,128)(2,1)S(1)}, u32[]{:S(2)}, u32[]{:S(2)}) collective-permute-start(bf16[64,3696]{1,0:T(8,128)(2,1)S(1)} %constant_dynamic-update-slice_fusion.refs_0_), channel_id=1, source_target_pairs={{0,1},{1,0},{2,3},{3,2},{4,5},{5,4},{6,7},{7,6},{8,9},{9,8},{10,11... | collective-permute-start | bytes 1419272 | tf_op jit(solution)/shard_map/y0/ppermute | solution.py:29
  46.1 9.6 %collective-permute-start.12 = (f32[8,128]{1,0:T(8,128)S(1)}, f32[8,128]{1,0:T(8,128)S(1)}, u32[]{:S(2)}, u32[]{:S(2)}) collective-permute-start(f32[8,128]{1,0:T(8,128)S(1)} %get-tuple-element.57), channel_id=1, source_target_pairs={{0,1},{1,0},{2,3},{3,2},{4,5},{5,4},{6,7},{7,6},{8,9},{9,8},{10,11... | collective-permute-start | bytes 12296 | tf_op jit(solution)/shard_map/sums0/ppermute | solution.py:29
  55.6 27.7 %collective-permute-start.19 = (bf16[288,1024]{1,0:T(8,128)(2,1)S(1)}, bf16[288,1024]{1,0:T(8,128)(2,1)S(1)}, u32[]{:S(2)}, u32[]{:S(2)}) collective-permute-start(bf16[288,1024]{1,0:T(8,128)(2,1)S(1)} %constant_dynamic-update-slice_fusion.6.here), channel_id=1, source_target_pairs={{0,64},{16,80},{32,96},{48,112},{64,0},{80,16},{96,32},{112,48},{1... | collective-permute-start | bytes 1769480 | tf_op jit(solution)/shard_map/block_zlo/ppermute | solution.py:29
  55.6 33.7 %copy-start.10 = (bf16[928,512]{1,0:T(8,128)(2,1)}, bf16[928,512]{1,0:T(8,128)(2,1)S(1)}, u32[]{:S(2)}) copy-start(bf16[928,512]{1,0:T(8,128)(2,1)S(1)} %collective-permute-done.13.refs_3_) | copy-start | bytes 2850820
  55.6 11.9 %collective-permute-start.14 = (f32[8,128]{1,0:T(8,128)S(1)}, f32[8,128]{1,0:T(8,128)S(1)}, u32[]{:S(2)}, u32[]{:S(2)}) collective-permute-start(f32[8,128]{1,0:T(8,128)S(1)} %add.21), channel_id=1, source_target_pairs={{0,4},{1,5},{2,6},{3,7},{4,0},{5,1},{6,2},{7,3},{8,12},{9,13},{10,... | collective-permute-start | bytes 12296 | tf_op jit(solution)/shard_map/sums1/ppermute | solution.py:29
  59.6 23.8 %collective-permute-start.20 = (bf16[928,512]{1,0:T(8,128)(2,1)S(1)}, bf16[928,512]{1,0:T(8,128)(2,1)S(1)}, u32[]{:S(2)}, u32[]{:S(2)}) collective-permute-start(bf16[928,512]{1,0:T(8,128)(2,1)S(1)} %get-tuple-element.63), channel_id=1, source_target_pairs={{0,3},{1,2},{2,1},{3,0},{4,7},{5,6},{6,5},{7,4},{8,11},{9,10},{10,... | collective-permute-start | bytes 2850824 | tf_op jit(solution)/shard_map/got1/ppermute | solution.py:29
  67.6 5.7 %collective-permute-start.15 = (f32[8,128]{1,0:T(8,128)S(1)}, f32[8,128]{1,0:T(8,128)S(1)}, u32[]{:S(2)}, u32[]{:S(2)}) collective-permute-start(f32[8,128]{1,0:T(8,128)S(1)} %add.23), channel_id=1, source_target_pairs={{0,12},{1,13},{2,14},{3,15},{4,8},{5,9},{6,10},{7,11},{8,4},{9,5},... | collective-permute-start | bytes 12296 | tf_op jit(solution)/shard_map/sums2/ppermute | solution.py:29
  73.3 11.3 %collective-permute-start.16 = (bf16[64,3696]{1,0:T(8,128)(2,1)S(1)}, bf16[64,3696]{1,0:T(8,128)(2,1)S(1)}, u32[]{:S(2)}, u32[]{:S(2)}) collective-permute-start(bf16[64,3696]{1,0:T(8,128)(2,1)S(1)} %constant_dynamic-update-slice_fusion.4.refs_2_), channel_id=1, source_target_pairs={{0,1},{1,0},{2,3},{3,2},{4,5},{5,4},{6,7},{7,6},{8,9},{9,8},{10,11... | collective-permute-start | bytes 1419272 | tf_op jit(solution)/shard_map/y2/ppermute | solution.py:29
  75.1 1.2 collective-permute-start.17
  76.3 6.3 %collective-permute-start.18 = (f32[24,128]{1,0:T(8,128)S(1)}, f32[24,128]{1,0:T(8,128)S(1)}, u32[]{:S(2)}, u32[]{:S(2)}) collective-permute-start(f32[24,128]{1,0:T(8,128)S(1)} %pad_maximum_fusion.1.here), channel_id=1, source_target_pairs={{0,64},{16,80},{32,96},{48,112},{64,0},{80,16},{96,32},{112,48},{1... | collective-permute-start | bytes 36872 | tf_op jit(solution)/shard_map/sums_zlo/ppermute | solution.py:29
  83.4 6.4 %copy-start.11 = (bf16[928,512]{1,0:T(8,128)(2,1)}, bf16[928,512]{1,0:T(8,128)(2,1)S(1)}, u32[]{:S(2)}) copy-start(bf16[928,512]{1,0:T(8,128)(2,1)S(1)} %collective-permute-done.20.refs_4_) | copy-start | bytes 2850820
  89.3 16.3 %collective-permute-start.21 = (bf16[3696,256]{1,0:T(8,128)(2,1)}, bf16[3696,256]{1,0:T(8,128)(2,1)}, u32[]{:S(2)}, u32[]{:S(2)}) collective-permute-start(bf16[3696,256]{1,0:T(8,128)(2,1)} %get-tuple-element.68), channel_id=1, source_target_pairs={{0,128},{128,0},{1,129},{129,1},{2,130},{130,2},{3,131},{131,3},{4... | collective-permute-start | bytes 5677064 | tf_op jit(solution)/shard_map/mate_got/ppermute | solution.py:29
  89.3 6.2 %collective-permute-start.22 = (bf16[928,512]{1,0:T(8,128)(2,1)S(1)}, bf16[928,512]{1,0:T(8,128)(2,1)S(1)}, u32[]{:S(2)}, u32[]{:S(2)}) collective-permute-start(bf16[928,512]{1,0:T(8,128)(2,1)S(1)} %collective-permute-done.13.refs_3_), channel_id=1, source_target_pairs={{0,128},{128,0},{1,129},{129,1},{2,130},{130,2},{3,131},{131,3},{4... | collective-permute-start | bytes 2850824 | tf_op jit(solution)/shard_map/got_other0/ppermute | solution.py:29
  89.8 6.7 %collective-permute-start.23 = (bf16[928,512]{1,0:T(8,128)(2,1)S(1)}, bf16[928,512]{1,0:T(8,128)(2,1)}, u32[]{:S(2)}, u32[]{:S(2)}) collective-permute-start(bf16[928,512]{1,0:T(8,128)(2,1)S(1)} %collective-permute-done.20.refs_4_), channel_id=1, source_target_pairs={{0,128},{128,0},{1,129},{129,1},{2,130},{130,2},{3,131},{131,3},{4... | collective-permute-start | bytes 2850824 | tf_op jit(solution)/shard_map/got_other1/ppermute | solution.py:29
  89.9 15.7 %copy-start.9 = (f32[3696,256]{1,0:T(8,128)S(1)}, f32[3696,256]{1,0:T(8,128)}, u32[]{:S(2)}) copy-start(f32[3696,256]{1,0:T(8,128)} %get-tuple-element.67) | copy-start | bytes 11354116
  95.5 1.0 copy-start.12
  108.9 73.0 %collective-permute-start.35 = (bf16[3696,256]{1,0:T(8,128)(2,1)}, bf16[3696,256]{1,0:T(8,128)(2,1)S(1)}, u32[]{:S(2)}, u32[]{:S(2)}) collective-permute-start(bf16[3696,256]{1,0:T(8,128)(2,1)} %add_convert_fusion.1), channel_id=1, source_target_pairs={{0,3},{1,2},{2,1},{3,0},{4,7},{5,6},{6,5},{7,4},{8,11},{9,10},{10,... | collective-permute-start | bytes 5677064 | tf_op jit(solution)/shard_map/w_recv/ppermute | solution.py:29
  113.9 66.9 %copy-start = (f32[64,3696]{1,0:T(8,128)S(1)}, f32[64,3696]{1,0:T(8,128)}, u32[]{:S(2)}) copy-start(f32[64,3696]{1,0:T(8,128)} %get-tuple-element.73.refs_0_) | copy-start | bytes 2838532
  113.9 67.9 %collective-permute-start.34 = (bf16[3696,256]{1,0:T(8,128)(2,1)}, bf16[3696,256]{1,0:T(8,128)(2,1)S(1)}, u32[]{:S(2)}, u32[]{:S(2)}) collective-permute-start(bf16[3696,256]{1,0:T(8,128)(2,1)} %get-tuple-element.93), channel_id=1, source_target_pairs={{0,128},{128,0},{1,129},{129,1},{2,130},{130,2},{3,131},{131,3},{4... | collective-permute-start | bytes 5677064 | tf_op jit(solution)/shard_map/own_got/ppermute | solution.py:29
  114.0 13.7 %collective-permute-start.25 = (bf16[64,3696]{1,0:T(8,128)(2,1)S(1)}, bf16[64,3696]{1,0:T(8,128)(2,1)S(1)}, u32[]{:S(2)}, u32[]{:S(2)}) collective-permute-start(bf16[64,3696]{1,0:T(8,128)(2,1)S(1)} %get-tuple-element.75), channel_id=1, source_target_pairs={{0,1},{1,0},{2,3},{3,2},{4,5},{5,4},{6,7},{7,6},{8,9},{9,8},{10,11... | collective-permute-start | bytes 1419272 | tf_op jit(solution)/shard_map/t0/ppermute | solution.py:29
  114.4 23.5 %collective-permute-start.28 = (bf16[64,3696]{1,0:T(8,128)(2,1)S(1)}, bf16[64,3696]{1,0:T(8,128)(2,1)S(1)}, u32[]{:S(2)}, u32[]{:S(2)}) collective-permute-start(bf16[64,3696]{1,0:T(8,128)(2,1)S(1)} %get-tuple-element.80), channel_id=1, source_target_pairs={{0,1},{1,0},{2,3},{3,2},{4,5},{5,4},{6,7},{7,6},{8,9},{9,8},{10,11... | collective-permute-start | bytes 1419272 | tf_op jit(solution)/shard_map/t1/ppermute | solution.py:29
  116.0 38.5 %collective-permute-start.30 = (bf16[64,3696]{1,0:T(8,128)(2,1)S(1)}, bf16[64,3696]{1,0:T(8,128)(2,1)S(1)}, u32[]{:S(2)}, u32[]{:S(2)}) collective-permute-start(bf16[64,3696]{1,0:T(8,128)(2,1)S(1)} %get-tuple-element.85), channel_id=1, source_target_pairs={{0,1},{1,0},{2,3},{3,2},{4,5},{5,4},{6,7},{7,6},{8,9},{9,8},{10,11... | collective-permute-start | bytes 1419272 | tf_op jit(solution)/shard_map/t2/ppermute | solution.py:29
  127.7 54.1 %copy-start.8 = (f32[3696,256]{1,0:T(8,128)S(1)}, f32[3696,256]{1,0:T(8,128)}, u32[]{:S(2)}) copy-start(f32[3696,256]{1,0:T(8,128)} %get-tuple-element.92) | copy-start | bytes 11354116
  127.8 11.8 %collective-permute-start.26 = (bf16[32,3696]{1,0:T(8,128)(2,1)S(1)}, bf16[32,3696]{1,0:T(8,128)(2,1)S(1)}, u32[]{:S(2)}, u32[]{:S(2)}) collective-permute-start(bf16[32,3696]{1,0:T(8,128)(2,1)S(1)} %get-tuple-element.77), channel_id=1, source_target_pairs={{0,4},{1,5},{2,6},{3,7},{4,8},{5,9},{6,10},{7,11},{8,12},{9,13},{1... | collective-permute-start | bytes 709640 | tf_op jit(solution)/shard_map/from_down/ppermute | solution.py:29
  137.9 12.4 %collective-permute-start.27 = (bf16[32,3696]{1,0:T(8,128)(2,1)S(1)}, bf16[32,3696]{1,0:T(8,128)(2,1)S(1)}, u32[]{:S(2)}, u32[]{:S(2)}) collective-permute-start(bf16[32,3696]{1,0:T(8,128)(2,1)S(1)} %get-tuple-element.78), channel_id=1, source_target_pairs={{0,12},{1,13},{2,14},{3,15},{4,0},{5,1},{6,2},{7,3},{8,4},{9,5},{1... | collective-permute-start | bytes 709640 | tf_op jit(solution)/shard_map/from_up/ppermute | solution.py:29
  150.3 14.0 %collective-permute-start.29 = (bf16[32,3696]{1,0:T(8,128)(2,1)S(1)}, bf16[32,3696]{1,0:T(8,128)(2,1)S(1)}, u32[]{:S(2)}, u32[]{:S(2)}) collective-permute-start(bf16[32,3696]{1,0:T(8,128)(2,1)S(1)} %get-tuple-element.83), channel_id=1, source_target_pairs={{0,12},{1,13},{2,14},{3,15},{4,0},{5,1},{6,2},{7,3},{8,4},{9,5},{1... | collective-permute-start | bytes 709640 | tf_op jit(solution)/shard_map/pure_a/ppermute | solution.py:29
  150.9 13.4 %collective-permute-start.31 = (bf16[32,3696]{1,0:T(8,128)(2,1)S(1)}, bf16[32,3696]{1,0:T(8,128)(2,1)S(1)}, u32[]{:S(2)}, u32[]{:S(2)}) collective-permute-start(bf16[32,3696]{1,0:T(8,128)(2,1)S(1)} %get-tuple-element.86), channel_id=1, source_target_pairs={{0,4},{1,5},{2,6},{3,7},{4,8},{5,9},{6,10},{7,11},{8,12},{9,13},{1... | collective-permute-start | bytes 709640 | tf_op jit(solution)/shard_map/pure_b/ppermute | solution.py:29
  154.6 14.6 %collective-permute-start.24 = (bf16[64,3696]{1,0:T(8,128)(2,1)S(1)}, bf16[64,3696]{1,0:T(8,128)(2,1)S(1)}, u32[]{:S(2)}, u32[]{:S(2)}) collective-permute-start(bf16[64,3696]{1,0:T(8,128)(2,1)S(1)} %get-tuple-element.74), channel_id=1, source_target_pairs={{0,1},{1,0},{2,3},{3,2},{4,5},{5,4},{6,7},{7,6},{8,9},{9,8},{10,11... | collective-permute-start | bytes 1419272 | tf_op jit(solution)/shard_map/t3/ppermute | solution.py:29
  164.5 14.9 %collective-permute-start.32 = (bf16[32,3696]{1,0:T(8,128)(2,1)S(1)}, bf16[32,3696]{1,0:T(8,128)(2,1)S(1)}, u32[]{:S(2)}, u32[]{:S(2)}) collective-permute-start(bf16[32,3696]{1,0:T(8,128)(2,1)S(1)} %get-tuple-element.90), channel_id=1, source_target_pairs={{0,4},{1,5},{2,6},{3,7},{4,8},{5,9},{6,10},{7,11},{8,12},{9,13},{1... | collective-permute-start | bytes 709640 | tf_op jit(solution)/shard_map/mixed_a/ppermute | solution.py:29
  169.0 11.8 %collective-permute-start.33 = (bf16[32,3696]{1,0:T(8,128)(2,1)S(1)}, bf16[32,3696]{1,0:T(8,128)(2,1)S(1)}, u32[]{:S(2)}, u32[]{:S(2)}) collective-permute-start(bf16[32,3696]{1,0:T(8,128)(2,1)S(1)} %get-tuple-element.91), channel_id=1, source_target_pairs={{0,12},{1,13},{2,14},{3,15},{4,0},{5,1},{6,2},{7,3},{8,4},{9,5},{1... | collective-permute-start | bytes 709640 | tf_op jit(solution)/shard_map/mixed_b/ppermute | solution.py:29
  181.8 5.8 %copy-start.2 = (bf16[128,512]{1,0:T(8,128)(2,1)S(1)}, bf16[128,512]{1,0:T(8,128)(2,1)}, u32[]{:S(2)}) copy-start(bf16[128,512]{1,0:T(8,128)(2,1)} %stream.3) | copy-start | bytes 393220
  182.6 5.9 %collective-permute-start.36 = (bf16[3696,256]{1,0:T(8,128)(2,1)S(1)}, bf16[3696,256]{1,0:T(8,128)(2,1)S(1)}, u32[]{:S(2)}, u32[]{:S(2)}) collective-permute-start(bf16[3696,256]{1,0:T(8,128)(2,1)S(1)} %add_convert_fusion.mine), channel_id=1, source_target_pairs={{0,128},{128,0},{1,129},{129,1},{2,130},{130,2},{3,131},{131,3},{4... | collective-permute-start | bytes 5677064 | tf_op jit(solution)/shard_map/w_sum/ppermute | solution.py:29
  182.7 4.9 %collective-permute-start.37 = (f32[8,128]{1,0:T(8,128)S(1)}, f32[8,128]{1,0:T(8,128)S(1)}, u32[]{:S(2)}, u32[]{:S(2)}) collective-permute-start(f32[8,128]{1,0:T(8,128)S(1)} %coefs_body.1.coefs), channel_id=1, source_target_pairs={{0,3},{1,2},{2,1},{3,0},{4,7},{5,6},{6,5},{7,4},{8,11},{9,10},{10,... | collective-permute-start | bytes 12296 | tf_op jit(solution)/shard_map/coefs_mate/ppermute | solution.py:29

commit v2 on v1

v2 whole, which is shorter than its diff:
```python
import functools

import jax
import jax.numpy as jnp
from jax import lax
from jax.experimental import pallas as pl
from jax.experimental.pallas import tpu as pltpu
from jax.sharding import PartitionSpec as P

loss_scale = 2097152.0
bf16, f32 = jnp.bfloat16, jnp.float32
WIDTH, COUNT = 8192.0, 2048.0

PAIR = [(c, c ^ 1) for c in range(16)]
MATE = [(c, c ^ 3) for c in range(16)]
ZUP = [(c, (c + 4) % 16) for c in range(16)]
ZDOWN = [(c, (c + 12) % 16) for c in range(16)]
ZONE = [(c, c ^ 4) for c in range(16)]
ZTHREE = [(c, c ^ 12) for c in range(16)]
ZLO = [(r, r ^ 4) for r in range(8)]
CORE = [(0, 1), (1, 0)]
XONE = [(r, r ^ 1) for r in range(8)]
XTHREE = [(r, r ^ 3) for r in range(8)]
VMEM_LIMIT = 56 * 1024 * 1024


def send(a, axis, perm, name):
    with jax.named_scope(name):
        return lax.ppermute(a, axis, perm)


def col(a, perm, name):
    return send(a, "col", perm, name)


def row(a, perm, name):
    return send(a, "row", perm, name)


def core(a, name):
    return send(a, "dp", CORE, name)


def after(a, *others):
    return lax.optimization_barrier((a, *others))[0]


def sds(shape, dtype):
    return jax.ShapeDtypeStruct(shape, dtype)


def call(body, out_shape, args, in_specs=None, scratch=(), flops=0, moved=0, name=None):
    extra = {} if in_specs is None else {"in_specs": in_specs}
    with jax.named_scope(name or getattr(body, "__name__", "mid")):
      return pl.pallas_call(
        body,
        out_shape=out_shape,
        scratch_shapes=list(scratch),
        compiler_params=pltpu.CompilerParams(vmem_limit_bytes=VMEM_LIMIT),
        cost_estimate=pl.CostEstimate(flops=flops, bytes_accessed=moved, transcendentals=0),
        **extra,
    )(*args)


def place():
    r, c = lax.axis_index("row"), lax.axis_index("col")
    return r % 4, r // 4, c % 4, c // 4


def prep_body(stream, gain, head, reward, segment, out, s_v, g_v, h_v, r_v, i_v, sems):
    moves = [
        pltpu.make_async_copy(src, dst, sems.at[i])
        for i, (src, dst) in enumerate(
            ((stream, s_v), (gain, g_v), (head, h_v), (reward, r_v), (segment, i_v))
        )
    ]
    for m in moves:
        m.start()
    for m in moves:
        m.wait()

    def parts(v):
        high = v.astype(bf16).astype(f32)
        mid = (v - high).astype(bf16).astype(f32)
        return high, mid, v - high - mid

    out[0:128] = s_v[...]
    rows = parts(g_v[...] * h_v[...])
    rows += (jnp.concatenate([*parts(r_v[...]), i_v[...].astype(f32)], 1),)
    line = lax.broadcasted_iota(jnp.int32, (16, 512), 0)
    extra = jnp.zeros((16, 512), f32)
    for i, a in enumerate(rows):
        extra = jnp.where(line == i, jnp.broadcast_to(a, (16, 512)), extra)
    out[128:144] = extra.astype(bf16)


def pick_body(own, other, out, sums, owed):
    x, _, y, _ = place()

    @pl.when(lax.rem(x, 2) == y // 2)
    def _():
        out[0:128] = own[0:128]

    @pl.when(lax.rem(x, 2) != y // 2)
    def _():
        out[0:128] = other[0:128]

    mine, theirs = own[128:144].astype(f32), other[128:144].astype(f32)
    even = lax.rem(x, 2) == 0
    first = jnp.where(even, mine, theirs)
    second = jnp.where(even, theirs, mine)
    for i, a in enumerate((first[3:4], second[3:4])):
        owed[i : i + 1] = a[:, 0:128] + a[:, 128:256] + a[:, 256:384]
        owed[2 + i : 3 + i] = a[:, 384:512]
    owed[4:8] = jnp.zeros((4, 128), f32)
    out[128:144] = mine.astype(bf16)
    gw = gains_of(own)

    def total(a):
        a = sum(a[:, 128 * i : 128 * i + 128] for i in range(8))
        return jnp.sum(a.T, axis=0, keepdims=True)

    v = out[0:128].astype(f32)
    sums[0:1] = total(v * v)
    sums[1:2] = total(v * gw)
    sums[2:8] = jnp.zeros((6, 128), f32)


def gains_of(block):
    extra = block[128:144].astype(f32)
    return extra[0:1] + extra[1:2] + extra[2:3]


def coefs_body(here, there, bias, out, target):
    x, zlo, y, _ = place()

    def side(src, at):
        near, away = src[at : at + 2], src[24 + at : 26 + at]
        low, high = jnp.where(x // 2 == 0, near, away), jnp.where(x // 2 == 0, away, near)
        return jnp.concatenate([low, high], 0)

    def rows(at):
        mine, theirs = side(here, at), side(there, at)
        return jnp.where(zlo == 0, mine, theirs), jnp.where(zlo == 0, theirs, mine)

    value = jnp.concatenate([*rows(8), *rows(16)], 0)
    segment = jnp.concatenate([*rows(10), *rows(18)], 0)
    shape = value.shape
    line = lax.broadcasted_iota(jnp.int32, shape, 0) % 8
    lane = lax.broadcasted_iota(jnp.int32, shape, 1)

    def ahead(a, step):
        if step >= 128:
            return pltpu.roll(a, shape[0] - step // 128, 0)
        here = pltpu.roll(a, 128 - step, 1)
        below = pltpu.roll(here, shape[0] - 1, 0)
        return jnp.where(lane + step < 128, here, below)

    step = 1
    while step < 1024:
        inside = line * 128 + lane + step < 1024
        same = inside & (ahead(segment, step) == segment)
        value = value + jnp.where(same, ahead(value, step), 0.0)
        step *= 2
    mean = jnp.sum(value) / COUNT
    off = value - mean
    spread = jnp.sum(off * off) / COUNT
    target[...] = (off / jnp.sqrt(jnp.broadcast_to(spread, shape) + 1e-05))[:8]
    wanted, sq, lin = [], [], []
    for i in range(4):
        zl = zlo if i < 2 else 1 - zlo
        b = x // 2 if i % 2 == 0 else 1 - x // 2
        wanted.append(target[pl.ds(4 * zl + 2 * b + y // 2, 1)])
        src = (here, there)[i // 2]
        at = 24 * (i % 2)
        sq.append(src[at : at + 1])
        lin.append(src[at + 1 : at + 2])
    wanted, sq, lin = (jnp.concatenate(a, 0) for a in (wanted, sq, lin))
    rms = jnp.sqrt(sq / WIDTH + 1e-05)
    head = lin / rms
    dvalue = loss_scale * (head + bias[0] - wanted) / COUNT
    out[0:4] = dvalue / rms
    out[4:8] = head / WIDTH / rms


def columns(coefs):
    padded = jnp.concatenate([coefs, jnp.zeros((120, 128), f32)], 0).T
    lane = lax.broadcasted_iota(jnp.int32, (128, 128), 1)

    def column(at):
        return jnp.sum(jnp.where(lane == at, padded, 0.0), axis=1, keepdims=True)

    return column


def formed(block, s, l, gains):
    return (s * (gains - block.astype(f32) * l)).astype(bf16)


def own_grad_body(stream, block, coefs, coefs_mate, grad):
    x, _, y, _ = place()
    column = columns(jnp.where(lax.rem(x, 2) == y // 2, coefs[...], coefs_mate[...]))
    grad[...] = formed(stream[...], column(0), column(4), gains_of(block)[:, :512])


def grad_body(coefs, here, there, g_own, g_other):
    x, zlo, y, zhi = place()
    odd = lax.rem(y, 2)
    column = columns(coefs[...])
    gains = gains_of(here)
    for spot, k in enumerate((2, 1, 3, 0)):
        z = lax.rem(zhi + k, 4)
        zl, b = z // 2, lax.rem(z, 2)
        at = jnp.where(zl == zlo, 0, 2) + jnp.where(b == x // 2, 0, 1)
        s_all, l_all = column(at), column(4 + at)
        s_all = jnp.where(odd == 0, s_all, jnp.concatenate([s_all[64:], s_all[:64]], 0))
        l_all = jnp.where(odd == 0, l_all, jnp.concatenate([l_all[64:], l_all[:64]], 0))
        start = jnp.where(b == x // 2, 0, 144)
        for same, src in ((True, here), (False, there)):

            @pl.when((zl == zlo) == same)
            def _(src=src, s_all=s_all, l_all=l_all, start=start, spot=spot):
                for who, out in ((0, g_own), (1, g_other)):
                    parity = odd if who == 0 else 1 - odd
                    first = pl.multiple_of(start + 64 * parity, 16)
                    rows = slice(64 * who, 64 * who + 64)
                    out[64 * spot : 64 * spot + 64] = formed(
                        src[pl.ds(first, 64)], s_all[rows], l_all[rows], gains
                    )


LO = 1856
CHUNKS = ((0, 1024), (1024, 2048), (2048, 3072), (3072, 3696))
HIGH = 3696 - LO
SPANS = ((0, LO), (LO, 3696))
PARTS = ((0, 64), (64, 128), (128, 192), (192, 256))
def inner_body(*refs):
    g_own, g_other, w, got, other = refs[:5]
    sent, own, (w_v, m_v, sems) = refs[5:9], refs[9:13], refs[13:]
    p = lax.axis_index("dp")
    for i, (a, b) in enumerate(CHUNKS):
        pltpu.make_async_copy(w.at[a:b], w_v.at[a:b], sems.at[i]).start()

    def mate_copy(j, low, high):
        a, b = SPANS[j]
        src, off = (low, high)[j], (0, HIGH)[j]
        return pltpu.make_async_copy(src.at[a - off : b - off], m_v.at[a:b], sems.at[4 + j])

    @pl.when(p == 0)
    def _():
        for j in range(2):
            mate_copy(j, got, other).start()

    @pl.when(p == 1)
    def _():
        for j in range(2):
            mate_copy(j, other, got).start()

    left = jnp.concatenate([g_other[:, :512], g_own[:, :512]], 0)
    right = jnp.concatenate([g_other[:, 512:], g_own[:, 512:]], 0)
    nt = (((1,), (1,)), ((), ()))
    waits = ((0,), (1,), (), ())
    for i, (a, b) in enumerate(CHUNKS):
        pltpu.make_async_copy(w.at[a:b], w_v.at[a:b], sems.at[i]).wait()
        for j in waits[i]:
            mate_copy(j, other, other).wait()
        for f in range(a, b, 512):
            e = min(f + 512, b)
            out = lax.dot_general(left, w_v[f:e], nt, preferred_element_type=f32)
            out = out + lax.dot_general(right, m_v[f:e], nt, preferred_element_type=f32)
            for n, (low, high) in enumerate(PARTS):
                sent[n][:, f:e] = out[low:high].astype(bf16)
                own[n][:, f:e] = out[256 + low : 256 + high]


def outer_body(*refs):
    pieces, (g_own, g_other) = refs[:8], refs[8:10]
    give, mate_keep, keep, h_v, g_v = refs[10:]
    p = lax.axis_index("dp")
    at = 0
    for piece in pieces:
        h_v[at : at + piece.shape[0]] = piece[...]
        at += piece.shape[0]
    for n, side in enumerate((1 - p, 3 - p, 2 + p, p)):
        start = pl.multiple_of(256 * side, 256)
        g_v[:256, 256 * n : 256 * n + 256] = g_own[:, pl.ds(start, 256)]
        g_v[256:, 256 * n : 256 * n + 256] = g_other[:, pl.ds(start, 256)]
    for f in range(0, 3696, 512):
        e = min(f + 512, 3696)
        out = lax.dot_general(
            h_v[:, f:e], g_v[...], (((0,), (0,)), ((), ())), preferred_element_type=f32
        )
        give[f:e] = out[:, :512].astype(bf16)
        mate_keep[f:e] = out[:, 512:768]
        keep[f:e] = out[:, 768:]


def outer(pieces, g_own, g_other):
    return call(
        outer_body,
        [sds((3696, 512), bf16), sds((3696, 256), f32), sds((3696, 256), f32)],
        (*pieces, g_own, g_other),
        scratch=[pltpu.VMEM((512, 3696), bf16), pltpu.VMEM((512, 1024), bf16)],
        flops=2 * 512 * 1024 * 3696,
        moved=16 << 20,
    )


def far_body(own, other, first, second):
    total = own[...] + other[...].astype(f32)
    first[...] = total[:32].astype(bf16)
    second[...] = total[32:].astype(bf16)


def mid_body(own, other, more, out, *, first):
    total = own[...] + other[...].astype(f32)
    for at in (0, 32):
        part = total[at : at + 32]
        if at == first:
            part = part + more[...].astype(f32)
        out[at : at + 32] = part.astype(bf16)


def here_body(own, other, below, above, out):
    total = own[...] + other[...].astype(f32)
    out[...] = (total + below[...].astype(f32) + above[...].astype(f32)).astype(bf16)


def join_body(mine, other, out):
    p = lax.axis_index("dp")
    out[:, pl.ds(pl.multiple_of(256 * p, 256), 256)] = mine[...]
    out[:, pl.ds(pl.multiple_of(256 * (1 - p), 256), 256)] = other[...]


def join(mine, other):
    rows = mine.shape[0]
    tile = 1232
    return pl.pallas_call(
        join_body,
        grid=(rows // tile,),
        in_specs=[pl.BlockSpec((tile, 256), lambda i: (i, 0))] * 2,
        out_specs=pl.BlockSpec((tile, 512), lambda i: (i, 0)),
        out_shape=sds((rows, 512), bf16),
        compiler_params=pltpu.CompilerParams(vmem_limit_bytes=VMEM_LIMIT),
        cost_estimate=pl.CostEstimate(flops=0, bytes_accessed=rows * 2048, transcendentals=0),
    )(mine, other)


def per_device(stream, hidden, w_down, norm_gain, value_head, value_bias, rewards, segments):
    p = lax.axis_index("dp")
    smem = pl.BlockSpec(memory_space=pltpu.SMEM)
    vmem = pl.BlockSpec(memory_space=pltpu.VMEM)
    hbm = pl.BlockSpec(memory_space=pl.ANY)

    payload = call(
        prep_body,
        sds((144, 512), bf16),
        (stream, norm_gain[None], value_head[None], rewards, segments),
        in_specs=[hbm] * 5,
        scratch=[
            pltpu.VMEM((128, 512), bf16),
            pltpu.VMEM((1, 512), f32),
            pltpu.VMEM((1, 512), f32),
            pltpu.VMEM((1, 128), f32),
            pltpu.VMEM((1, 128), jnp.int32),
            pltpu.SemaphoreType.DMA((5,)),
        ],
    )
    payload_mate = col(payload, MATE, "payload_mate")
    y3 = col(hidden, PAIR, "y3")
    down = col(hidden, ZUP, "down")
    up = col(hidden, ZDOWN, "up")

    w_half = lax.dynamic_slice_in_dim(w_down, p * HIGH, LO, 0)
    got = col(after(w_half, payload_mate), MATE, "got")

    block = jnp.concatenate([payload, payload_mate], 1)
    near, sums, owed = call(
        pick_body,
        (sds((144, 1024), bf16), sds((8, 128), f32), sds((8, 128), f32)),
        (block, row(block, XONE, "block_x1")),
    )
    away = row(near, XTHREE, "block_x3")
    here = jnp.concatenate([near, away], 0)
    there = row(here, ZLO, "block_zlo")
    owed_other = core(owed, "owed_other")

    gates = ((y3,), (down, up), (away,))
    for i, perm in enumerate((PAIR, ZONE, ZTHREE)):
        sums = after(sums, *gates[i])
        sums = sums + col(sums, perm, f"sums{i}")
        if i == 0:
            down, up = lax.optimization_barrier((down, up, sums))[:2]
            far_a = col(down[:32], ZUP, "far_a")
            far_b = col(up[32:], ZDOWN, "far_b")
            y12 = col(jnp.concatenate([up, down], 0), PAIR, "y12")
    y0 = col(after(jnp.concatenate([far_a, far_b], 0), sums), PAIR, "y0")
    tiny = jnp.concatenate([sums, owed, owed_other], 0)
    tiny = after(tiny, far_a, far_b)
    tiny = jnp.concatenate([tiny, row(tiny, XTHREE, "tiny_x3")], 0)
    tiny_zlo = row(tiny, ZLO, "tiny_zlo")
    coefs = call(
        coefs_body,
        sds((8, 128), f32),
        (after(tiny, got), tiny_zlo, value_bias),
        in_specs=[vmem, vmem, smem],
        scratch=[pltpu.VMEM((8, 128), f32)],
    )
    got_other = core(after(got, tiny_zlo), "got_other")
    coefs_mate = col(coefs, MATE, "coefs_mate")
    g_own, g_other = call(
        grad_body,
        (sds((256, 1024), bf16), sds((256, 1024), bf16)),
        (coefs, here, there),
        moved=4 << 20,
    )

    pieces = (far_a, far_b, up, down, hidden, y0, y12, y3)
    give, mate_keep, keep = outer(pieces, after(g_own, coefs_mate), g_other)
    both_got = core(give, "both_got")
    outs = call(
        inner_body,
        [sds((b - a, 3696), d) for d in (bf16, f32) for a, b in PARTS],
        (after(g_own, mate_keep), g_other, w_down, got, got_other),
        in_specs=[vmem] * 2 + [hbm] * 3,
        scratch=[
            pltpu.VMEM((3696, 512), bf16),
            pltpu.VMEM((3696, 512), bf16),
            pltpu.SemaphoreType.DMA((6,)),
        ],
        flops=2 * 512 * 1024 * 3696,
        moved=13 << 20,
    )
    sent, own = outs[:4], outs[4:]
    t = [col(a, PAIR, f"t{i}") for i, a in enumerate(sent)]

    w_send = (after(mate_keep, own[0]) + both_got[:, 256:].astype(f32)).astype(bf16)
    w_recv = col(w_send, MATE, "w_recv")

    half_rows = [sds((32, 3696), bf16)] * 2
    q_a, q_b = call(far_body, half_rows, (own[0], after(t[0], w_send)))
    from_down = col(q_a, ZUP, "from_down")
    from_up = col(q_b, ZDOWN, "from_up")
    q_up = call(
        functools.partial(mid_body, first=0), sds((64, 3696), bf16), (own[1], t[1], from_down)
    )
    below = col(q_up, ZUP, "below")
    q_down = call(
        functools.partial(mid_body, first=32), sds((64, 3696), bf16), (own[2], t[2], from_up)
    )
    above = col(q_down, ZDOWN, "above")

    stream_grad = call(
        own_grad_body, sds((128, 512), bf16), (stream, near, coefs, coefs_mate)
    )
    hidden_grad = call(here_body, sds((64, 3696), bf16), (own[3], t[3], below, above))
    keep = after(keep, hidden_grad, stream_grad)
    w_sum = (keep + both_got[:, :256].astype(f32) + w_recv.astype(f32)).astype(bf16)
    w_sum_other = core(w_sum, "w_sum")
    weight_grad = join(w_sum, w_sum_other)
    return weight_grad, hidden_grad, stream_grad


def solution(mesh):
    in_specs = (
        P(("dp", "row"), "col"),
        P(("dp", "col"), "row"),
        P("row", "col"),
        P("col"),
        P("col"),
        P(),
        P("dp", "row"),
        P("dp", "row"),
    )
    out_specs = (P("row", "col"), P(("dp", "col"), "row"), P(("dp", "row"), "col"))
    return jax.shard_map(
        per_device, mesh=mesh, in_specs=in_specs, out_specs=out_specs, check_vma=False
    )
```

time: 191 us -> 190 us (level)
  starting transfers between devices: 59.3 us -> 31.5 us
  Pallas kernels: 25.6 us -> 47.7 us
  waiting for transfers between devices: 92.9 us -> 83.6 us
  local copies, waits for them, and re-layouts: 7.43 us -> 14.7 us
  other arithmetic: 4.09 us -> 9.17 us
    ppermute x38 -> x31, starting transfers between devices: 59.3 us -> 31.5 us  [send(): return lax.ppermute(a, axis, perm)]
    pallas_call x13 -> x11, Pallas kernels: 23.2 us -> 42.8 us  [call(): pl.pallas_call(body, out_shape=out_shape, scratch_shapes=list(scratch), c...]
    ppermute x38 -> x31, waiting for transfers between devices: 92.9 us -> 83.6 us  [send(): return lax.ppermute(a, axis, perm)]
    concatenate x0 -> x2, other arithmetic: none -> 3.12 us  [the longest x1 1.89 us: per_device(): y0 = col(after(jnp.concatenate([far_a, far_b], 0), sums), PAIR, 'y0')]
    unnamed x30 -> x50, local copies, waits for them, and re-layouts: 4.65 us -> 7.41 us
    pallas_call x1, Pallas kernels: 2.44 us -> 4.89 us  [join(): pl.pallas_call(join_body, grid=(rows // tile,), in_specs=[pl.BlockSpec((t...]
  transfers between devices with their start and end apart: 38 -> 31, of which waited for: 17 -> 19; matrix products, arithmetic and copies ran while one was open for 2% -> 7% of each run, Pallas kernels for 10% -> 16%
where the time goes in v2:
time: 190 us; the launch traced here: 188 us
  waiting for transfers between devices  83.6 us (44%)
  Pallas kernels  47.7 us (25%)
  starting transfers between devices  31.5 us (17%)
  local copies, waits for them, and re-layouts  14.7 us (8%)
  other arithmetic  9.17 us (5%)
    ppermute x31, waiting for transfers between devices, send(): return lax.ppermute(a, axis, perm)  83.6 us
    pallas_call x11, Pallas kernels, call(): pl.pallas_call(body, out_shape=out_shape, scratch_shapes=list(scratch), c...  42.8 us
    ppermute x31, starting transfers between devices, send(): return lax.ppermute(a, axis, perm)  31.5 us
    unnamed x50, local copies, waits for them, and re-layouts  7.41 us
    pallas_call x1, Pallas kernels, join(): pl.pallas_call(join_body, grid=(rows // tile,), in_specs=[pl.BlockSpec((t...  4.89 us
  transfers between devices with their start and end apart: 31, of which 19 were waited for; matrix products, arithmetic and copies ran while one was open for 7% of the time, Pallas kernels for 16%

profile of v2, /device:TPU:6, one launch (start us, length us, event | category | flops | bytes accessed | tf_op | source)
XLA Modules:
  0.0 188.2 jit_solution(5504853961213944942)
XLA Ops:
  0.6 1.6 prep_body.1
  2.3 3.1 %collective-permute-start.2 = (bf16[144,512]{1,0:T(8,128)(2,1)}, bf16[144,512]{1,0:T(8,128)(2,1)S(1)}, u32[]{:S(2)}, u32[]{:S(2)}) collective-permute-start(bf16[144,512]{1,0:T(8,128)(2,1)} %prep_body.1), channel_id=1, source_target_pairs={{0,3},{1,2},{2,1},{3,0},{4,7},{5,6},{6,5},{7,4},{8,11},{9,10},{10,... | collective-permute-start | bytes 442376 | tf_op jit(solution)/shard_map/payload_mate/ppermute | solution.py:29
  5.4 6.3 %collective-permute-start.1 = (bf16[64,3696]{1,0:T(8,128)(2,1)}, bf16[64,3696]{1,0:T(8,128)(2,1)S(1)}, u32[]{:S(2)}, u32[]{:S(2)}) collective-permute-start(bf16[64,3696]{1,0:T(8,128)(2,1)} %refs_4_.1), channel_id=1, source_target_pairs={{0,12},{1,13},{2,14},{3,15},{4,0},{5,1},{6,2},{7,3},{8,4},{9,5},{1... | collective-permute-start | bytes 1419272 | tf_op jit(solution)/shard_map/up/ppermute | solution.py:29
  11.8 0.9 pad_maximum_fusion.2.own
  12.8 0.9 collective-permute-start.3
  13.7 1.6 constant_dynamic-slice_fusion
  15.4 1.1 collective-permute-start.15
  16.5 4.4 %collective-permute-done.3.other = bf16[144,1024]{1,0:T(8,128)(2,1)S(1)} collective-permute-done((bf16[144,1024]{1,0:T(8,128)(2,1)S(1)}, bf16[144,1024]{1,0:T(8,128)(2,1)S(1)}, u32[]{:S(2)}, u32[]{:S(2)}) %collective-permute-start.3) | collective-permute-done | bytes 294944 | tf_op jit(solution)/shard_map/block_x1/ppermute | solution.py:29
  20.9 0.7 copy-done.15
  21.6 1.9 pick_body.1
  24.1 1.7 collective-permute-start.5
  25.7 1.0 constant_dynamic-update-slice_fusion.3
  26.7 1.2 collective-permute-done.5
  28.6 3.5 %collective-permute-done.1.refs_2_ = bf16[64,3696]{1,0:T(8,128)(2,1)S(1)} collective-permute-done((bf16[64,3696]{1,0:T(8,128)(2,1)}, bf16[64,3696]{1,0:T(8,128)(2,1)S(1)}, u32[]{:S(2)}, u32[]{:S(2)}) %collective-permute-start.1) | collective-permute-done | bytes 473120 | tf_op jit(solution)/shard_map/up/ppermute | solution.py:29
  32.1 3.7 %collective-permute-done.refs_3_ = bf16[64,3696]{1,0:T(8,128)(2,1)S(1)} collective-permute-done((bf16[64,3696]{1,0:T(8,128)(2,1)}, bf16[64,3696]{1,0:T(8,128)(2,1)S(1)}, u32[]{:S(2)}, u32[]{:S(2)}) %collective-permute-start) | collective-permute-done | bytes 473120 | tf_op jit(solution)/shard_map/down/ppermute | solution.py:29
  35.8 0.8 slice.12
  36.6 0.7 slice.13
  37.3 1.0 collective-permute-start.7
  38.3 2.0 %collective-permute-start.6 = (bf16[32,3696]{1,0:T(8,128)(2,1)}, bf16[32,3696]{1,0:T(8,128)(2,1)}, u32[]{:S(2)}, u32[]{:S(2)}) collective-permute-start(bf16[32,3696]{1,0:T(8,128)(2,1)} %slice.12), channel_id=1, source_target_pairs={{0,4},{1,5},{2,6},{3,7},{4,8},{5,9},{6,10},{7,11},{8,12},{9,13},{1... | collective-permute-start | bytes 709640 | tf_op jit(solution)/shard_map/far_a/ppermute | solution.py:29
  40.3 1.2 pad_maximum_fusion
  41.5 1.3 copy.11
  43.0 2.2 %collective-permute-start.10 = (f32[8,128]{1,0:T(8,128)S(1)}, f32[8,128]{1,0:T(8,128)S(1)}, u32[]{:S(2)}, u32[]{:S(2)}) collective-permute-start(f32[8,128]{1,0:T(8,128)S(1)} %add.22), channel_id=1, source_target_pairs={{0,12},{1,13},{2,14},{3,15},{4,8},{5,9},{6,10},{7,11},{8,4},{9,5},... | collective-permute-start | bytes 12296 | tf_op jit(solution)/shard_map/sums2/ppermute | solution.py:29
  45.2 1.0 constant_dynamic-update-slice_fusion.2.here
  46.2 3.6 %collective-permute-done.7.refs_1_ = bf16[32,3696]{1,0:T(8,128)(2,1)} collective-permute-done((bf16[32,3696]{1,0:T(8,128)(2,1)}, bf16[32,3696]{1,0:T(8,128)(2,1)}, u32[]{:S(2)}, u32[]{:S(2)}) %collective-permute-start.7) | collective-permute-done | bytes 236576 | tf_op jit(solution)/shard_map/far_b/ppermute | solution.py:29
  49.8 3.8 %collective-permute-done.6.refs_0_ = bf16[32,3696]{1,0:T(8,128)(2,1)} collective-permute-done((bf16[32,3696]{1,0:T(8,128)(2,1)}, bf16[32,3696]{1,0:T(8,128)(2,1)}, u32[]{:S(2)}, u32[]{:S(2)}) %collective-permute-start.6) | collective-permute-done | bytes 236576 | tf_op jit(solution)/shard_map/far_a/ppermute | solution.py:29
  53.6 1.9 %pad_maximum_fusion.1 = bf16[64,3696]{1,0:T(8,128)(2,1)} fusion(bf16[32,3696]{1,0:T(8,128)(2,1)} %collective-permute-done.7.refs_1_, bf16[32,3696]{1,0:T(8,128)(2,1)} %collective-permute-done.6.refs_0_), kind=kLoop, calls=%fused_computation.3 | loop fusion | flops 946176 | bytes 946176 | tf_op jit(solution)/shard_map/concatenate | solution.py:397
  55.6 1.2 collective-permute-done.13
  57.2 4.4 %collective-permute-done.14 = f32[24,128]{1,0:T(8,128)S(1)} collective-permute-done((f32[24,128]{1,0:T(8,128)S(1)}, f32[24,128]{1,0:T(8,128)S(1)}, u32[]{:S(2)}, u32[]{:S(2)}) %collective-permute-start.14) | collective-permute-done | bytes 12320 | tf_op jit(solution)/shard_map/tiny_x3/ppermute | solution.py:29
  62.3 3.2 %collective-permute-done.16.there = f32[48,128]{1,0:T(8,128)S(1)} collective-permute-done((f32[48,128]{1,0:T(8,128)S(1)}, f32[48,128]{1,0:T(8,128)S(1)}, u32[]{:S(2)}, u32[]{:S(2)}) %collective-permute-start.16) | collective-permute-done | bytes 24608 | tf_op jit(solution)/shard_map/tiny_zlo/ppermute | solution.py:29
  66.1 2.1 %coefs_body.1.coefs = f32[8,128]{1,0:T(8,128)} custom-call(f32[48,128]{1,0:T(8,128)} %copy-done.18, f32[48,128]{1,0:T(8,128)} %copy-done.19, f32[1]{0:T(128)S(6)} %copy.15.bias), custom_call_target="tpu_custom_call" | custom-call | tf_op jit(solution)/shard_map/coefs_body/pallas_call | solution.py:55
  68.2 1.1 collective-permute-start.18
  69.3 1.9 copy.12.refs_6_
  71.2 3.4 %grad_body.1 = (bf16[256,1024]{1,0:T(8,128)(2,1)}, bf16[256,1024]{1,0:T(8,128)(2,1)}) custom-call(f32[8,128]{1,0:T(8,128)} %coefs_body.1.coefs, bf16[288,1024]{1,0:T(8,128)(2,1)} %copy-done.5, bf16[288,1024]{1,0:T(8,128)(2,1)} %collective-permute-done.17.there), custom_call_target="tpu_custom_call" | custom-call | bytes 4194304 | tf_op jit(solution)/shard_map/grad_body/pallas_call | solution.py:55
  74.5 10.8 %outer_body.1 = (bf16[3696,512]{1,0:T(8,128)(2,1)}, f32[3696,256]{1,0:T(8,128)}, f32[3696,256]{1,0:T(8,128)}) custom-call(bf16[32,3696]{1,0:T(8,128)(2,1)} %collective-permute-done.6.refs_0_, bf16[32,3696]{1,0:T(8,128)(2,1)} %collective-permute-done.7.refs_1_, bf16[64,3696]{1,0:T(8,128)(2,1)} %copy-done.7, bf16[64,3696]{1,0:T(8,128)(2,1)} %copy-done.8, ...), custom_call_target="tpu_custom_call" | custom-call | flops 3875536896 | bytes 16777216 | tf_op jit(solution)/shard_map/outer_body/pallas_call | solution.py:55
  85.9 8.8 %collective-permute-done.19.refs_4_ = bf16[1856,512]{1,0:T(8,128)(2,1)} collective-permute-done((bf16[1856,512]{1,0:T(8,128)(2,1)}, bf16[1856,512]{1,0:T(8,128)(2,1)}, u32[]{:S(2)}, u32[]{:S(2)}) %collective-permute-start.19) | collective-permute-done | bytes 1900576 | tf_op jit(solution)/shard_map/got_other/ppermute | solution.py:29
  94.6 11.7 %inner_body.1 = (bf16[64,3696]{1,0:T(8,128)(2,1)}, bf16[64,3696]{1,0:T(8,128)(2,1)}, bf16[64,3696]{1,0:T(8,128)(2,1)}, bf16[64,3696]{1,0:T(8,128)(2,1)}, f32[64,...) custom-call(bf16[256,1024]{1,0:T(8,128)(2,1)} %get-tuple-element.53.refs_8_.refs_0_, ...), custom_call_target="tpu_custom_call" | custom-call | flops 3875536896 | bytes 13631488 | tf_op jit(solution)/shard_map/inner_body/pallas_call | solution.py:55
  106.4 1.8 add_convert_fusion.1
  108.2 0.7 copy-done.3
  108.9 2.2 %collective-permute-start.29 = (bf16[3696,256]{1,0:T(8,128)(2,1)}, bf16[3696,256]{1,0:T(8,128)(2,1)}, u32[]{:S(2)}, u32[]{:S(2)}) collective-permute-start(bf16[3696,256]{1,0:T(8,128)(2,1)} %add_convert_fusion.1), channel_id=1, source_target_pairs={{0,3},{1,2},{2,1},{3,0},{4,7},{5,6},{6,5},{7,4},{8,11},{9,10},{10,... | collective-permute-start | bytes 5677064 | tf_op jit(solution)/shard_map/w_recv/ppermute | solution.py:29
  111.1 0.7 collective-permute-start.22
  111.8 1.3 collective-permute-start.26
  113.2 0.7 collective-permute-start.21
  113.9 11.0 %collective-permute-done.22.other = bf16[64,3696]{1,0:T(8,128)(2,1)S(1)} collective-permute-done((bf16[64,3696]{1,0:T(8,128)(2,1)S(1)}, bf16[64,3696]{1,0:T(8,128)(2,1)S(1)}, u32[]{:S(2)}, u32[]{:S(2)}) %collective-permute-start.22) | collective-permute-done | bytes 473120 | tf_op jit(solution)/shard_map/t0/ppermute | solution.py:29
  124.9 0.8 copy-done.9
  125.6 2.1 %far_body.1 = (bf16[32,3696]{1,0:T(8,128)(2,1)}, bf16[32,3696]{1,0:T(8,128)(2,1)}) custom-call(f32[64,3696]{1,0:T(8,128)} %get-tuple-element.59.own, bf16[64,3696]{1,0:T(8,128)(2,1)} %copy-done.9), custom_call_target="tpu_custom_call" | custom-call | tf_op jit(solution)/shard_map/far_body/pallas_call | solution.py:55
  128.3 2.3 %collective-permute-start.24 = (bf16[32,3696]{1,0:T(8,128)(2,1)}, bf16[32,3696]{1,0:T(8,128)(2,1)S(1)}, u32[]{:S(2)}, u32[]{:S(2)}) collective-permute-start(bf16[32,3696]{1,0:T(8,128)(2,1)} %get-tuple-element.64), channel_id=1, source_target_pairs={{0,4},{1,5},{2,6},{3,7},{4,8},{5,9},{6,10},{7,11},{8,12},{9,13},{1... | collective-permute-start | bytes 709640 | tf_op jit(solution)/shard_map/from_down/ppermute | solution.py:29
  130.7 4.4 %collective-permute-done.26.other = bf16[64,3696]{1,0:T(8,128)(2,1)S(1)} collective-permute-done((bf16[64,3696]{1,0:T(8,128)(2,1)}, bf16[64,3696]{1,0:T(8,128)(2,1)S(1)}, u32[]{:S(2)}, u32[]{:S(2)}) %collective-permute-start.26) | collective-permute-done | bytes 473120 | tf_op jit(solution)/shard_map/t2/ppermute | solution.py:29
  135.0 0.7 collective-permute-start.20
  135.7 2.5 %collective-permute-done.27.more = bf16[32,3696]{1,0:T(8,128)(2,1)S(1)} collective-permute-done((bf16[32,3696]{1,0:T(8,128)(2,1)}, bf16[32,3696]{1,0:T(8,128)(2,1)S(1)}, u32[]{:S(2)}, u32[]{:S(2)}) %collective-permute-start.27) | collective-permute-done | bytes 236576 | tf_op jit(solution)/shard_map/from_up/ppermute | solution.py:29
  139.0 2.4 %mid.3 = bf16[64,3696]{1,0:T(8,128)(2,1)} custom-call(f32[64,3696]{1,0:T(8,128)} %get-tuple-element.65.own, bf16[64,3696]{1,0:T(8,128)(2,1)} %copy-done.12, bf16[32,3696]{1,0:T(8,128)(2,1)} %copy-done.17), custom_call_target="tpu_custom_call" | custom-call | tf_op jit(solution)/shard_map/mid/pallas_call | solution.py:55
  141.7 3.5 %collective-permute-done.21.other = bf16[64,3696]{1,0:T(8,128)(2,1)S(1)} collective-permute-done((bf16[64,3696]{1,0:T(8,128)(2,1)}, bf16[64,3696]{1,0:T(8,128)(2,1)S(1)}, u32[]{:S(2)}, u32[]{:S(2)}) %collective-permute-start.21) | collective-permute-done | bytes 473120 | tf_op jit(solution)/shard_map/t1/ppermute | solution.py:29
  145.2 0.8 copy-done.10
  146.1 2.2 %mid.2 = bf16[64,3696]{1,0:T(8,128)(2,1)} custom-call(f32[64,3696]{1,0:T(8,128)} %get-tuple-element.57.own, bf16[64,3696]{1,0:T(8,128)(2,1)} %copy-done.10, bf16[32,3696]{1,0:T(8,128)(2,1)} %copy-done.16), custom_call_target="tpu_custom_call" | custom-call | tf_op jit(solution)/shard_map/mid/pallas_call | solution.py:55
  148.3 1.4 collective-permute-start.25
  149.7 1.9 own_grad_body.1
  151.6 2.9 %collective-permute-done.20.other = bf16[64,3696]{1,0:T(8,128)(2,1)S(1)} collective-permute-done((bf16[64,3696]{1,0:T(8,128)(2,1)S(1)}, bf16[64,3696]{1,0:T(8,128)(2,1)S(1)}, u32[]{:S(2)}, u32[]{:S(2)}) %collective-permute-start.20) | collective-permute-done | bytes 473120 | tf_op jit(solution)/shard_map/t3/ppermute | solution.py:29
  154.5 8.5 %collective-permute-done.28.above = bf16[64,3696]{1,0:T(8,128)(2,1)S(1)} collective-permute-done((bf16[64,3696]{1,0:T(8,128)(2,1)}, bf16[64,3696]{1,0:T(8,128)(2,1)S(1)}, u32[]{:S(2)}, u32[]{:S(2)}) %collective-permute-start.28) | collective-permute-done | bytes 473120 | tf_op jit(solution)/shard_map/above/ppermute | solution.py:29
  163.1 9.0 %collective-permute-done.25.below = bf16[64,3696]{1,0:T(8,128)(2,1)S(1)} collective-permute-done((bf16[64,3696]{1,0:T(8,128)(2,1)}, bf16[64,3696]{1,0:T(8,128)(2,1)S(1)}, u32[]{:S(2)}, u32[]{:S(2)}) %collective-permute-start.25) | collective-permute-done | bytes 473120 | tf_op jit(solution)/shard_map/below/ppermute | solution.py:29
  172.1 0.8 copy-done.14
  172.8 2.6 %here_body.1 = bf16[64,3696]{1,0:T(8,128)(2,1)} custom-call(f32[64,3696]{1,0:T(8,128)} %get-tuple-element.55.own, bf16[64,3696]{1,0:T(8,128)(2,1)} %copy-done.11, bf16[64,3696]{1,0:T(8,128)(2,1)} %copy-done.14, bf16[64,3696]{1,0:T(8,128)(2,1)} %copy-done.13), custom_call_target="tpu_custom_call" | custom-call | tf_op jit(solution)/shard_map/here_body/pallas_call | solution.py:55
  175.4 2.6 %add_convert_fusion.mine = bf16[3696,256]{1,0:T(8,128)(2,1)S(1)} fusion(bf16[3696,256]{1,0:T(8,128)(2,1)} %collective-permute-done.29, f32[3696,256]{1,0:T(8,128)S(1)} %copy-done.1, bf16[3696,512]{1,0:T(8,128)(2,1)} %copy-done.3), kind=kLoop, calls=%fused_computation | loop fusion | flops 4730880 | bytes 9461760 | tf_op jit(solution)/shard_map/convert_element_type | solution.py:458
  178.2 3.9 %collective-permute-done.30.other = bf16[3696,256]{1,0:T(8,128)(2,1)S(1)} collective-permute-done((bf16[3696,256]{1,0:T(8,128)(2,1)S(1)}, bf16[3696,256]{1,0:T(8,128)(2,1)S(1)}, u32[]{:S(2)}, u32[]{:S(2)}) %collective-permute-start.30) | collective-permute-done | bytes 1892384 | tf_op jit(solution)/shard_map/w_sum/ppermute | solution.py:29
  182.0 1.3 copy-done.4
  183.3 4.9 %shard_map.103 = bf16[3696,512]{1,0:T(8,128)(2,1)} custom-call(bf16[3696,256]{1,0:T(8,128)(2,1)} %copy-done, bf16[3696,256]{1,0:T(8,128)(2,1)} %copy-done.4), custom_call_target="tpu_custom_call" | custom-call | bytes 7569408 | tf_op jit(solution)/shard_map/pallas_call | solution.py:338
  (76 shorter events, 5.0 us)
Async XLA Ops:
  2.3 9.5 %collective-permute-start.2 = (bf16[144,512]{1,0:T(8,128)(2,1)}, bf16[144,512]{1,0:T(8,128)(2,1)S(1)}, u32[]{:S(2)}, u32[]{:S(2)}) collective-permute-start(bf16[144,512]{1,0:T(8,128)(2,1)} %prep_body.1), channel_id=1, source_target_pairs={{0,3},{1,2},{2,1},{3,0},{4,7},{5,6},{6,5},{7,4},{8,11},{9,10},{10,... | collective-permute-start | bytes 442376 | tf_op jit(solution)/shard_map/payload_mate/ppermute | solution.py:29
  5.4 26.7 %collective-permute-start.1 = (bf16[64,3696]{1,0:T(8,128)(2,1)}, bf16[64,3696]{1,0:T(8,128)(2,1)S(1)}, u32[]{:S(2)}, u32[]{:S(2)}) collective-permute-start(bf16[64,3696]{1,0:T(8,128)(2,1)} %refs_4_.1), channel_id=1, source_target_pairs={{0,12},{1,13},{2,14},{3,15},{4,0},{5,1},{6,2},{7,3},{8,4},{9,5},{1... | collective-permute-start | bytes 1419272 | tf_op jit(solution)/shard_map/up/ppermute | solution.py:29
  11.7 24.1 %collective-permute-start = (bf16[64,3696]{1,0:T(8,128)(2,1)}, bf16[64,3696]{1,0:T(8,128)(2,1)S(1)}, u32[]{:S(2)}, u32[]{:S(2)}) collective-permute-start(bf16[64,3696]{1,0:T(8,128)(2,1)} %refs_4_.1), channel_id=1, source_target_pairs={{0,4},{1,5},{2,6},{3,7},{4,8},{5,9},{6,10},{7,11},{8,12},{9,13},{1... | collective-permute-start | bytes 1419272 | tf_op jit(solution)/shard_map/down/ppermute | solution.py:29
  11.7 12.4 %collective-permute-start.4 = (bf16[64,3696]{1,0:T(8,128)(2,1)}, bf16[64,3696]{1,0:T(8,128)(2,1)}, u32[]{:S(2)}, u32[]{:S(2)}) collective-permute-start(bf16[64,3696]{1,0:T(8,128)(2,1)} %refs_4_.1), channel_id=1, source_target_pairs={{0,1},{1,0},{2,3},{3,2},{4,5},{5,4},{6,7},{7,6},{8,9},{9,8},{10,11... | collective-permute-start | bytes 1419272 | tf_op jit(solution)/shard_map/y3/ppermute | solution.py:29
  12.8 8.2 %copy-start.6 = (bf16[144,1024]{1,0:T(8,128)(2,1)}, bf16[144,1024]{1,0:T(8,128)(2,1)S(1)}, u32[]{:S(2)}) copy-start(bf16[144,1024]{1,0:T(8,128)(2,1)S(1)} %pad_maximum_fusion.2.own) | copy-start | bytes 884740
  12.8 8.1 %collective-permute-start.3 = (bf16[144,1024]{1,0:T(8,128)(2,1)S(1)}, bf16[144,1024]{1,0:T(8,128)(2,1)S(1)}, u32[]{:S(2)}, u32[]{:S(2)}) collective-permute-start(bf16[144,1024]{1,0:T(8,128)(2,1)S(1)} %pad_maximum_fusion.2.own), channel_id=1, source_target_pairs={{0,16},{16,0},{32,48},{48,32},{64,80},{80,64},{96,112},{112,96},{1... | collective-permute-start | bytes 884744 | tf_op jit(solution)/shard_map/block_x1/ppermute | solution.py:29
  15.4 47.0 %collective-permute-start.15 = (bf16[1856,512]{1,0:T(8,128)(2,1)S(1)}, bf16[1856,512]{1,0:T(8,128)(2,1)}, u32[]{:S(2)}, u32[]{:S(2)}) collective-permute-start(bf16[1856,512]{1,0:T(8,128)(2,1)S(1)} %constant_dynamic-slice_fusion), channel_id=1, source_target_pairs={{0,3},{1,2},{2,1},{3,0},{4,7},{5,6},{6,5},{7,4},{8,11},{9,10},{10,... | collective-permute-start | bytes 5701640 | tf_op jit(solution)/shard_map/got/ppermute | solution.py:29
  20.9 0.7 copy-start.15
  23.5 32.1 %copy-start.21 = (f32[8,128]{1,0:T(8,128)S(1)}, f32[8,128]{1,0:T(8,128)}, u32[]{:S(2)}) copy-start(f32[8,128]{1,0:T(8,128)} %get-tuple-element.44) | copy-start | bytes 12292
  23.5 19.5 %collective-permute-start.9 = (bf16[144,1024]{1,0:T(8,128)(2,1)}, bf16[144,1024]{1,0:T(8,128)(2,1)}, u32[]{:S(2)}, u32[]{:S(2)}) collective-permute-start(bf16[144,1024]{1,0:T(8,128)(2,1)} %get-tuple-element.41.block), channel_id=1, source_target_pairs={{0,48},{16,32},{32,16},{48,0},{64,112},{80,96},{96,80},{112,64},{1... | collective-permute-start | bytes 884744 | tf_op jit(solution)/shard_map/block_x3/ppermute | solution.py:29
  24.1 3.8 %collective-permute-start.5 = (f32[8,128]{1,0:T(8,128)}, f32[8,128]{1,0:T(8,128)S(1)}, u32[]{:S(2)}, u32[]{:S(2)}) collective-permute-start(f32[8,128]{1,0:T(8,128)} %get-tuple-element.37), channel_id=1, source_target_pairs={{0,1},{1,0},{2,3},{3,2},{4,5},{5,4},{6,7},{7,6},{8,9},{9,8},{10,11... | collective-permute-start | bytes 12296 | tf_op jit(solution)/shard_map/sums0/ppermute | solution.py:29
  32.1 6.2 %copy-start.7 = (bf16[64,3696]{1,0:T(8,128)(2,1)}, bf16[64,3696]{1,0:T(8,128)(2,1)S(1)}, u32[]{:S(2)}) copy-start(bf16[64,3696]{1,0:T(8,128)(2,1)S(1)} %collective-permute-done.1.refs_2_) | copy-start | bytes 1419268
  35.8 2.5 %copy-start.8 = (bf16[64,3696]{1,0:T(8,128)(2,1)}, bf16[64,3696]{1,0:T(8,128)(2,1)S(1)}, u32[]{:S(2)}) copy-start(bf16[64,3696]{1,0:T(8,128)(2,1)S(1)} %collective-permute-done.refs_3_) | copy-start | bytes 1419268
  35.8 7.0 %collective-permute-start.8 = (f32[8,128]{1,0:T(8,128)S(1)}, f32[8,128]{1,0:T(8,128)S(1)}, u32[]{:S(2)}, u32[]{:S(2)}) collective-permute-start(f32[8,128]{1,0:T(8,128)S(1)} %add.21), channel_id=1, source_target_pairs={{0,4},{1,5},{2,6},{3,7},{4,0},{5,1},{6,2},{7,3},{8,12},{9,13},{10,... | collective-permute-start | bytes 12296 | tf_op jit(solution)/shard_map/sums1/ppermute | solution.py:29
  37.3 12.5 %collective-permute-start.7 = (bf16[32,3696]{1,0:T(8,128)(2,1)}, bf16[32,3696]{1,0:T(8,128)(2,1)}, u32[]{:S(2)}, u32[]{:S(2)}) collective-permute-start(bf16[32,3696]{1,0:T(8,128)(2,1)} %slice.13), channel_id=1, source_target_pairs={{0,12},{1,13},{2,14},{3,15},{4,0},{5,1},{6,2},{7,3},{8,4},{9,5},{1... | collective-permute-start | bytes 709640 | tf_op jit(solution)/shard_map/far_b/ppermute | solution.py:29
  38.3 15.3 %collective-permute-start.6 = (bf16[32,3696]{1,0:T(8,128)(2,1)}, bf16[32,3696]{1,0:T(8,128)(2,1)}, u32[]{:S(2)}, u32[]{:S(2)}) collective-permute-start(bf16[32,3696]{1,0:T(8,128)(2,1)} %slice.12), channel_id=1, source_target_pairs={{0,4},{1,5},{2,6},{3,7},{4,8},{5,9},{6,10},{7,11},{8,12},{9,13},{1... | collective-permute-start | bytes 709640 | tf_op jit(solution)/shard_map/far_a/ppermute | solution.py:29
  42.8 26.5 %collective-permute-start.12 = (bf16[128,3696]{0,1:T(8,128)(2,1)}, bf16[128,3696]{0,1:T(8,128)(2,1)S(1)}, u32[]{:S(2)}, u32[]{:S(2)}) collective-permute-start(bf16[128,3696]{0,1:T(8,128)(2,1)} %copy.11), channel_id=1, source_target_pairs={{0,1},{1,0},{2,3},{3,2},{4,5},{5,4},{6,7},{7,6},{8,9},{9,8},{10,11... | collective-permute-start | bytes 2838536 | tf_op jit(solution)/shard_map/y12/ppermute | solution.py:29
  43.0 12.5 %collective-permute-start.10 = (f32[8,128]{1,0:T(8,128)S(1)}, f32[8,128]{1,0:T(8,128)S(1)}, u32[]{:S(2)}, u32[]{:S(2)}) collective-permute-start(f32[8,128]{1,0:T(8,128)S(1)} %add.22), channel_id=1, source_target_pairs={{0,12},{1,13},{2,14},{3,15},{4,8},{5,9},{6,10},{7,11},{8,4},{9,5},... | collective-permute-start | bytes 12296 | tf_op jit(solution)/shard_map/sums2/ppermute | solution.py:29
  46.2 25.0 %copy-start.5 = (bf16[288,1024]{1,0:T(8,128)(2,1)}, bf16[288,1024]{1,0:T(8,128)(2,1)S(1)}, u32[]{:S(2)}) copy-start(bf16[288,1024]{1,0:T(8,128)(2,1)S(1)} %constant_dynamic-update-slice_fusion.2.here) | copy-start | bytes 1769476
  49.8 21.4 %collective-permute-start.17 = (bf16[288,1024]{1,0:T(8,128)(2,1)S(1)}, bf16[288,1024]{1,0:T(8,128)(2,1)}, u32[]{:S(2)}, u32[]{:S(2)}) collective-permute-start(bf16[288,1024]{1,0:T(8,128)(2,1)S(1)} %constant_dynamic-update-slice_fusion.2.here), channel_id=1, source_target_pairs={{0,64},{16,80},{32,96},{48,112},{64,0},{80,16},{96,32},{112,48},{1... | collective-permute-start | bytes 1769480 | tf_op jit(solution)/shard_map/block_zlo/ppermute | solution.py:29
  55.5 19.0 %collective-permute-start.11 = (bf16[64,3696]{1,0:T(8,128)(2,1)}, bf16[64,3696]{1,0:T(8,128)(2,1)}, u32[]{:S(2)}, u32[]{:S(2)}) collective-permute-start(bf16[64,3696]{1,0:T(8,128)(2,1)} %pad_maximum_fusion.1), channel_id=1, source_target_pairs={{0,1},{1,0},{2,3},{3,2},{4,5},{5,4},{6,7},{7,6},{8,9},{9,8},{10,11... | collective-permute-start | bytes 1419272 | tf_op jit(solution)/shard_map/y0/ppermute | solution.py:29
  55.6 1.2 collective-permute-start.13
  56.8 4.9 %collective-permute-start.14 = (f32[24,128]{1,0:T(8,128)S(1)}, f32[24,128]{1,0:T(8,128)S(1)}, u32[]{:S(2)}, u32[]{:S(2)}) collective-permute-start(f32[24,128]{1,0:T(8,128)S(1)} %pad_maximum_fusion.3), channel_id=1, source_target_pairs={{0,48},{16,32},{32,16},{48,0},{64,112},{80,96},{96,80},{112,64},{1... | collective-permute-start | bytes 36872 | tf_op jit(solution)/shard_map/tiny_x3/ppermute | solution.py:29
  61.7 3.8 %copy-start.18 = (f32[48,128]{1,0:T(8,128)}, f32[48,128]{1,0:T(8,128)S(1)}, u32[]{:S(2)}) copy-start(f32[48,128]{1,0:T(8,128)S(1)} %constant_dynamic-update-slice_fusion.here) | copy-start | bytes 73732
  61.7 3.8 %collective-permute-start.16 = (f32[48,128]{1,0:T(8,128)S(1)}, f32[48,128]{1,0:T(8,128)S(1)}, u32[]{:S(2)}, u32[]{:S(2)}) collective-permute-start(f32[48,128]{1,0:T(8,128)S(1)} %constant_dynamic-update-slice_fusion.here), channel_id=1, source_target_pairs={{0,64},{16,80},{32,96},{48,112},{64,0},{80,16},{96,32},{112,48},{1... | collective-permute-start | bytes 73736 | tf_op jit(solution)/shard_map/tiny_zlo/ppermute | solution.py:29
  65.5 0.6 copy-start.19
  68.2 6.3 %collective-permute-start.18 = (f32[8,128]{1,0:T(8,128)}, f32[8,128]{1,0:T(8,128)S(1)}, u32[]{:S(2)}, u32[]{:S(2)}) collective-permute-start(f32[8,128]{1,0:T(8,128)} %coefs_body.1.coefs), channel_id=1, source_target_pairs={{0,3},{1,2},{2,1},{3,0},{4,7},{5,6},{6,5},{7,4},{8,11},{9,10},{10,... | collective-permute-start | bytes 12296 | tf_op jit(solution)/shard_map/coefs_mate/ppermute | solution.py:29
  74.5 10.8 %copy-start.20 = (f32[8,128]{1,0:T(8,128)}, f32[8,128]{1,0:T(8,128)S(1)}, u32[]{:S(2)}) copy-start(f32[8,128]{1,0:T(8,128)S(1)} %collective-permute-done.18.coefs_mate) | copy-start | bytes 12292
  85.4 21.0 %collective-permute-start.23 = (bf16[3696,512]{1,0:T(8,128)(2,1)}, bf16[3696,512]{1,0:T(8,128)(2,1)S(1)}, u32[]{:S(2)}, u32[]{:S(2)}) collective-permute-start(bf16[3696,512]{1,0:T(8,128)(2,1)} %get-tuple-element.62), channel_id=1, source_target_pairs={{0,128},{128,0},{1,129},{129,1},{2,130},{130,2},{3,131},{131,3},{4... | collective-permute-start | bytes 11354120 | tf_op jit(solution)/shard_map/both_got/ppermute | solution.py:29
  85.4 9.3 %collective-permute-start.19 = (bf16[1856,512]{1,0:T(8,128)(2,1)}, bf16[1856,512]{1,0:T(8,128)(2,1)}, u32[]{:S(2)}, u32[]{:S(2)}) collective-permute-start(bf16[1856,512]{1,0:T(8,128)(2,1)} %collective-permute-done.15.refs_3_), channel_id=1, source_target_pairs={{0,128},{128,0},{1,129},{129,1},{2,130},{130,2},{3,131},{131,3},{4... | collective-permute-start | bytes 5701640 | tf_op jit(solution)/shard_map/got_other/ppermute | solution.py:29
  85.9 20.5 %copy-start.2 = (f32[3696,256]{1,0:T(8,128)S(1)}, f32[3696,256]{1,0:T(8,128)}, u32[]{:S(2)}) copy-start(f32[3696,256]{1,0:T(8,128)} %get-tuple-element.61) | copy-start | bytes 11354116
  106.4 4.7 %copy-start.23 = (bf16[64,3696]{1,0:T(8,128)(2,1)S(1)}, bf16[64,3696]{1,0:T(8,128)(2,1)}, u32[]{:S(2)}) copy-start(bf16[64,3696]{1,0:T(8,128)(2,1)} %get-tuple-element.60) | copy-start | bytes 1419268
  106.4 28.6 %copy-start.22 = (bf16[64,3696]{1,0:T(8,128)(2,1)S(1)}, bf16[64,3696]{1,0:T(8,128)(2,1)}, u32[]{:S(2)}) copy-start(bf16[64,3696]{1,0:T(8,128)(2,1)} %get-tuple-element.56) | copy-start | bytes 1419268
  106.4 2.5 %copy-start.3 = (bf16[3696,512]{1,0:T(8,128)(2,1)}, bf16[3696,512]{1,0:T(8,128)(2,1)S(1)}, u32[]{:S(2)}) copy-start(bf16[3696,512]{1,0:T(8,128)(2,1)S(1)} %collective-permute-done.23) | copy-start | bytes 11354116
  108.9 66.5 %collective-permute-start.29 = (bf16[3696,256]{1,0:T(8,128)(2,1)}, bf16[3696,256]{1,0:T(8,128)(2,1)}, u32[]{:S(2)}, u32[]{:S(2)}) collective-permute-start(bf16[3696,256]{1,0:T(8,128)(2,1)} %add_convert_fusion.1), channel_id=1, source_target_pairs={{0,3},{1,2},{2,1},{3,0},{4,7},{5,6},{6,5},{7,4},{8,11},{9,10},{10,... | collective-permute-start | bytes 5677064 | tf_op jit(solution)/shard_map/w_recv/ppermute | solution.py:29
  111.1 13.7 %collective-permute-start.22 = (bf16[64,3696]{1,0:T(8,128)(2,1)S(1)}, bf16[64,3696]{1,0:T(8,128)(2,1)S(1)}, u32[]{:S(2)}, u32[]{:S(2)}) collective-permute-start(bf16[64,3696]{1,0:T(8,128)(2,1)S(1)} %copy-done.23), channel_id=1, source_target_pairs={{0,1},{1,0},{2,3},{3,2},{4,5},{5,4},{6,7},{7,6},{8,9},{9,8},{10,11... | collective-permute-start | bytes 1419272 | tf_op jit(solution)/shard_map/t0/ppermute | solution.py:29
  111.8 23.2 %collective-permute-start.26 = (bf16[64,3696]{1,0:T(8,128)(2,1)}, bf16[64,3696]{1,0:T(8,128)(2,1)S(1)}, u32[]{:S(2)}, u32[]{:S(2)}) collective-permute-start(bf16[64,3696]{1,0:T(8,128)(2,1)} %get-tuple-element.66), channel_id=1, source_target_pairs={{0,1},{1,0},{2,3},{3,2},{4,5},{5,4},{6,7},{7,6},{8,9},{9,8},{10,11... | collective-permute-start | bytes 1419272 | tf_op jit(solution)/shard_map/t2/ppermute | solution.py:29
  113.2 32.1 %collective-permute-start.21 = (bf16[64,3696]{1,0:T(8,128)(2,1)}, bf16[64,3696]{1,0:T(8,128)(2,1)S(1)}, u32[]{:S(2)}, u32[]{:S(2)}) collective-permute-start(bf16[64,3696]{1,0:T(8,128)(2,1)} %get-tuple-element.58), channel_id=1, source_target_pairs={{0,1},{1,0},{2,3},{3,2},{4,5},{5,4},{6,7},{7,6},{8,9},{9,8},{10,11... | collective-permute-start | bytes 1419272 | tf_op jit(solution)/shard_map/t1/ppermute | solution.py:29
  124.8 0.8 copy-start.9
  127.7 10.5 %collective-permute-start.27 = (bf16[32,3696]{1,0:T(8,128)(2,1)}, bf16[32,3696]{1,0:T(8,128)(2,1)S(1)}, u32[]{:S(2)}, u32[]{:S(2)}) collective-permute-start(bf16[32,3696]{1,0:T(8,128)(2,1)} %get-tuple-element.67), channel_id=1, source_target_pairs={{0,12},{1,13},{2,14},{3,15},{4,0},{5,1},{6,2},{7,3},{8,4},{9,5},{1... | collective-permute-start | bytes 709640 | tf_op jit(solution)/shard_map/from_up/ppermute | solution.py:29
  128.3 16.9 %collective-permute-start.24 = (bf16[32,3696]{1,0:T(8,128)(2,1)}, bf16[32,3696]{1,0:T(8,128)(2,1)S(1)}, u32[]{:S(2)}, u32[]{:S(2)}) collective-permute-start(bf16[32,3696]{1,0:T(8,128)(2,1)} %get-tuple-element.64), channel_id=1, source_target_pairs={{0,4},{1,5},{2,6},{3,7},{4,8},{5,9},{6,10},{7,11},{8,12},{9,13},{1... | collective-permute-start | bytes 709640 | tf_op jit(solution)/shard_map/from_down/ppermute | solution.py:29
  135.0 3.2 %copy-start.12 = (bf16[64,3696]{1,0:T(8,128)(2,1)}, bf16[64,3696]{1,0:T(8,128)(2,1)S(1)}, u32[]{:S(2)}) copy-start(bf16[64,3696]{1,0:T(8,128)(2,1)S(1)} %collective-permute-done.26.other) | copy-start | bytes 1419268
  135.0 19.5 %collective-permute-start.20 = (bf16[64,3696]{1,0:T(8,128)(2,1)S(1)}, bf16[64,3696]{1,0:T(8,128)(2,1)S(1)}, u32[]{:S(2)}, u32[]{:S(2)}) collective-permute-start(bf16[64,3696]{1,0:T(8,128)(2,1)S(1)} %copy-done.22), channel_id=1, source_target_pairs={{0,1},{1,0},{2,3},{3,2},{4,5},{5,4},{6,7},{7,6},{8,9},{9,8},{10,11... | collective-permute-start | bytes 1419272 | tf_op jit(solution)/shard_map/t3/ppermute | solution.py:29
  138.3 0.7 copy-start.17
  139.0 36.4 %copy-start.1 = (f32[3696,256]{1,0:T(8,128)S(1)}, f32[3696,256]{1,0:T(8,128)}, u32[]{:S(2)}) copy-start(f32[3696,256]{1,0:T(8,128)} %get-tuple-element.68) | copy-start | bytes 11354116
  141.4 21.7 %collective-permute-start.28 = (bf16[64,3696]{1,0:T(8,128)(2,1)}, bf16[64,3696]{1,0:T(8,128)(2,1)S(1)}, u32[]{:S(2)}, u32[]{:S(2)}) collective-permute-start(bf16[64,3696]{1,0:T(8,128)(2,1)} %mid.3), channel_id=1, source_target_pairs={{0,12},{1,13},{2,14},{3,15},{4,0},{5,1},{6,2},{7,3},{8,4},{9,5},{1... | collective-permute-start | bytes 1419272 | tf_op jit(solution)/shard_map/above/ppermute | solution.py:29
  145.2 0.8 copy-start.10
  145.2 0.8 copy-start.16
  148.3 23.8 %collective-permute-start.25 = (bf16[64,3696]{1,0:T(8,128)(2,1)}, bf16[64,3696]{1,0:T(8,128)(2,1)S(1)}, u32[]{:S(2)}, u32[]{:S(2)}) collective-permute-start(bf16[64,3696]{1,0:T(8,128)(2,1)} %mid.2), channel_id=1, source_target_pairs={{0,4},{1,5},{2,6},{3,7},{4,8},{5,9},{6,10},{7,11},{8,12},{9,13},{1... | collective-permute-start | bytes 1419272 | tf_op jit(solution)/shard_map/below/ppermute | solution.py:29
  154.5 17.5 %copy-start.11 = (bf16[64,3696]{1,0:T(8,128)(2,1)}, bf16[64,3696]{1,0:T(8,128)(2,1)S(1)}, u32[]{:S(2)}) copy-start(bf16[64,3696]{1,0:T(8,128)(2,1)S(1)} %collective-permute-done.20.other) | copy-start | bytes 1419268
  163.1 9.0 %copy-start.13 = (bf16[64,3696]{1,0:T(8,128)(2,1)}, bf16[64,3696]{1,0:T(8,128)(2,1)S(1)}, u32[]{:S(2)}) copy-start(bf16[64,3696]{1,0:T(8,128)(2,1)S(1)} %collective-permute-done.28.above) | copy-start | bytes 1419268
  172.1 0.8 copy-start.14
  178.1 4.0 %copy-start = (bf16[3696,256]{1,0:T(8,128)(2,1)}, bf16[3696,256]{1,0:T(8,128)(2,1)S(1)}, u32[]{:S(2)}) copy-start(bf16[3696,256]{1,0:T(8,128)(2,1)S(1)} %add_convert_fusion.mine) | copy-start | bytes 5677060
  178.1 4.0 %collective-permute-start.30 = (bf16[3696,256]{1,0:T(8,128)(2,1)S(1)}, bf16[3696,256]{1,0:T(8,128)(2,1)S(1)}, u32[]{:S(2)}, u32[]{:S(2)}) collective-permute-start(bf16[3696,256]{1,0:T(8,128)(2,1)S(1)} %add_convert_fusion.mine), channel_id=1, source_target_pairs={{0,128},{128,0},{1,129},{129,1},{2,130},{130,2},{3,131},{131,3},{4... | collective-permute-start | bytes 5677064 | tf_op jit(solution)/shard_map/w_sum/ppermute | solution.py:29
  182.0 1.3 copy-start.4

commit v3 on v2

--- a/solution.py
+++ b/solution.py
@@ -21,7 +21,7 @@
 CORE = [(0, 1), (1, 0)]
 XONE = [(r, r ^ 1) for r in range(8)]
 XTHREE = [(r, r ^ 3) for r in range(8)]
-VMEM_LIMIT = 56 * 1024 * 1024
+MIB = 1024 * 1024
 
 
 def send(a, axis, perm, name):
@@ -49,14 +49,14 @@
     return jax.ShapeDtypeStruct(shape, dtype)
 
 
-def call(body, out_shape, args, in_specs=None, scratch=(), flops=0, moved=0, name=None):
+def call(body, out_shape, args, in_specs=None, scratch=(), flops=0, moved=0, name=None, grant=16):
     extra = {} if in_specs is None else {"in_specs": in_specs}
     with jax.named_scope(name or getattr(body, "__name__", "mid")):
       return pl.pallas_call(
         body,
         out_shape=out_shape,
         scratch_shapes=list(scratch),
-        compiler_params=pltpu.CompilerParams(vmem_limit_bytes=VMEM_LIMIT),
+        compiler_params=pltpu.CompilerParams(vmem_limit_bytes=grant * MIB),
         cost_estimate=pl.CostEstimate(flops=flops, bytes_accessed=moved, transcendentals=0),
         **extra,
     )(*args)
@@ -208,7 +208,7 @@
     odd = lax.rem(y, 2)
     column = columns(coefs[...])
     gains = gains_of(here)
-    for spot, k in enumerate((2, 1, 3, 0)):
+    for k, spots in enumerate(((192, 224), (128, 64), (0, 32), (96, 160))):
         z = lax.rem(zhi + k, 4)
         zl, b = z // 2, lax.rem(z, 2)
         at = jnp.where(zl == zlo, 0, 2) + jnp.where(b == x // 2, 0, 1)
@@ -219,14 +219,14 @@
         for same, src in ((True, here), (False, there)):
 
             @pl.when((zl == zlo) == same)
-            def _(src=src, s_all=s_all, l_all=l_all, start=start, spot=spot):
+            def _(src=src, s_all=s_all, l_all=l_all, start=start, spots=spots):
                 for who, out in ((0, g_own), (1, g_other)):
                     parity = odd if who == 0 else 1 - odd
                     first = pl.multiple_of(start + 64 * parity, 16)
                     rows = slice(64 * who, 64 * who + 64)
-                    out[64 * spot : 64 * spot + 64] = formed(
-                        src[pl.ds(first, 64)], s_all[rows], l_all[rows], gains
-                    )
+                    made = formed(src[pl.ds(first, 64)], s_all[rows], l_all[rows], gains)
+                    for i, spot in enumerate(spots):
+                        out[spot : spot + 32] = made[32 * i : 32 * i + 32]
 
 
 LO = 1856
@@ -273,16 +273,27 @@
                 own[n][:, f:e] = out[256 + low : 256 + high]
 
 
-def outer_body(*refs):
-    pieces, (g_own, g_other) = refs[:8], refs[8:10]
-    give, mate_keep, keep, h_v, g_v = refs[10:]
+def outer_body(*refs, first):
+    pieces, (g_own, g_other), (give, keep, h_v, g_v) = refs[:8], refs[8:10], refs[10:]
     p = lax.axis_index("dp")
-    at = 0
-    for piece in pieces:
-        h_v[at : at + piece.shape[0]] = piece[...]
-        at += piece.shape[0]
-    for n, side in enumerate((1 - p, 3 - p, 2 + p, p)):
-        start = pl.multiple_of(256 * side, 256)
+    far_a, far_b, up, down, here, y0, y12, y3 = pieces
+    for at, src in (
+        (0, far_a[...]),
+        (32, far_b[...]),
+        (64, up[32:64]),
+        (96, down[0:32]),
+        (128, up[0:32]),
+        (160, down[32:64]),
+        (192, here[...]),
+        (256, y0[...]),
+        (320, y12[32:96]),
+        (384, y12[0:32]),
+        (416, y12[96:128]),
+        (448, y3[...]),
+    ):
+        h_v[at : at + src.shape[0]] = src
+    for n, side in enumerate((1 - p, p)):
+        start = pl.multiple_of(first + 256 * side, 256)
         g_v[:256, 256 * n : 256 * n + 256] = g_own[:, pl.ds(start, 256)]
         g_v[256:, 256 * n : 256 * n + 256] = g_other[:, pl.ds(start, 256)]
     for f in range(0, 3696, 512):
@@ -290,60 +301,58 @@
         out = lax.dot_general(
             h_v[:, f:e], g_v[...], (((0,), (0,)), ((), ())), preferred_element_type=f32
         )
-        give[f:e] = out[:, :512].astype(bf16)
-        mate_keep[f:e] = out[:, 512:768]
-        keep[f:e] = out[:, 768:]
-
-
-def outer(pieces, g_own, g_other):
+        give[f:e] = out[:, :256].astype(bf16)
+        keep[f:e] = out[:, 256:]
+
+
+def outer(pieces, g_own, g_other, first, name):
     return call(
-        outer_body,
-        [sds((3696, 512), bf16), sds((3696, 256), f32), sds((3696, 256), f32)],
+        functools.partial(outer_body, first=first),
+        [sds((3696, 256), bf16), sds((3696, 256), f32)],
         (*pieces, g_own, g_other),
-        scratch=[pltpu.VMEM((512, 3696), bf16), pltpu.VMEM((512, 1024), bf16)],
-        flops=2 * 512 * 1024 * 3696,
-        moved=16 << 20,
-    )
-
-
-def far_body(own, other, first, second):
+        scratch=[pltpu.VMEM((512, 3696), bf16), pltpu.VMEM((512, 512), bf16)],
+        flops=512 * 1024 * 3696,
+        moved=8 << 20,
+        name=name,
+        grant=28,
+    )
+
+
+def fold_body(own, other, *refs):
+    *more, first, second = refs
     total = own[...] + other[...].astype(f32)
-    first[...] = total[:32].astype(bf16)
-    second[...] = total[32:].astype(bf16)
-
-
-def mid_body(own, other, more, out, *, first):
+    for i, out in enumerate((first, second)):
+        part = total[32 * i : 32 * i + 32]
+        if more:
+            part = part + more[i][...].astype(f32)
+        out[...] = part.astype(bf16)
+
+
+def fold(own, other, *more):
+    return call(fold_body, [sds((32, own.shape[1]), bf16)] * 2, (own, other, *more))
+
+
+def here_body(own, other, pure_a, pure_b, mixed_a, mixed_b, out):
     total = own[...] + other[...].astype(f32)
-    for at in (0, 32):
-        part = total[at : at + 32]
-        if at == first:
-            part = part + more[...].astype(f32)
+    for at, (one, two) in ((0, (pure_a, mixed_a)), (32, (pure_b, mixed_b))):
+        part = total[at : at + 32] + one[...].astype(f32) + two[...].astype(f32)
         out[at : at + 32] = part.astype(bf16)
 
 
-def here_body(own, other, below, above, out):
-    total = own[...] + other[...].astype(f32)
-    out[...] = (total + below[...].astype(f32) + above[...].astype(f32)).astype(bf16)
-
-
-def join_body(mine, other, out):
+SHARES = ((0, 3696),)
+
+
+def join_body(*refs):
     p = lax.axis_index("dp")
-    out[:, pl.ds(pl.multiple_of(256 * p, 256), 256)] = mine[...]
-    out[:, pl.ds(pl.multiple_of(256 * (1 - p), 256), 256)] = other[...]
+    out = refs[-1]
+    n = len(SHARES)
+    for (a, b), mine, other in zip(SHARES, refs[:n], refs[n : 2 * n]):
+        out[a:b, pl.ds(pl.multiple_of(256 * p, 256), 256)] = mine[...]
+        out[a:b, pl.ds(pl.multiple_of(256 * (1 - p), 256), 256)] = other[...]
 
 
 def join(mine, other):
-    rows = mine.shape[0]
-    tile = 1232
-    return pl.pallas_call(
-        join_body,
-        grid=(rows // tile,),
-        in_specs=[pl.BlockSpec((tile, 256), lambda i: (i, 0))] * 2,
-        out_specs=pl.BlockSpec((tile, 512), lambda i: (i, 0)),
-        out_shape=sds((rows, 512), bf16),
-        compiler_params=pltpu.CompilerParams(vmem_limit_bytes=VMEM_LIMIT),
-        cost_estimate=pl.CostEstimate(flops=0, bytes_accessed=rows * 2048, transcendentals=0),
-    )(mine, other)
+    return call(join_body, sds((3696, 512), bf16), (*mine, *other))
 
 
 def per_device(stream, hidden, w_down, norm_gain, value_head, value_bias, rewards, segments):
@@ -365,6 +374,7 @@
             pltpu.VMEM((1, 128), jnp.int32),
             pltpu.SemaphoreType.DMA((5,)),
         ],
+        grant=56,
     )
     payload_mate = col(payload, MATE, "payload_mate")
     y3 = col(hidden, PAIR, "y3")
@@ -416,12 +426,15 @@
     )
 
     pieces = (far_a, far_b, up, down, hidden, y0, y12, y3)
-    give, mate_keep, keep = outer(pieces, after(g_own, coefs_mate), g_other)
-    both_got = core(give, "both_got")
+    mate_give, mate_keep = outer(pieces, after(g_own, coefs_mate), g_other, 512, "outer_mate")
+    mate_got = core(mate_give, "mate_got")
+    w_send = [(mate_keep[a:b] + mate_got[a:b].astype(f32)).astype(bf16) for a, b in SHARES]
+    w_recv = col(w_send[0], MATE, "w_recv")
+
     outs = call(
         inner_body,
         [sds((b - a, 3696), d) for d in (bf16, f32) for a, b in PARTS],
-        (after(g_own, mate_keep), g_other, w_down, got, got_other),
+        (after(g_own, w_send[0]), g_other, w_down, got, got_other),
         in_specs=[vmem] * 2 + [hbm] * 3,
         scratch=[
             pltpu.VMEM((3696, 512), bf16),
@@ -430,33 +443,37 @@
         ],
         flops=2 * 512 * 1024 * 3696,
         moved=13 << 20,
+        grant=28,
     )
     sent, own = outs[:4], outs[4:]
-    t = [col(a, PAIR, f"t{i}") for i, a in enumerate(sent)]
-
-    w_send = (after(mate_keep, own[0]) + both_got[:, 256:].astype(f32)).astype(bf16)
-    w_recv = col(w_send, MATE, "w_recv")
-
-    half_rows = [sds((32, 3696), bf16)] * 2
-    q_a, q_b = call(far_body, half_rows, (own[0], after(t[0], w_send)))
-    from_down = col(q_a, ZUP, "from_down")
-    from_up = col(q_b, ZDOWN, "from_up")
-    q_up = call(
-        functools.partial(mid_body, first=0), sds((64, 3696), bf16), (own[1], t[1], from_down)
-    )
-    below = col(q_up, ZUP, "below")
-    q_down = call(
-        functools.partial(mid_body, first=32), sds((64, 3696), bf16), (own[2], t[2], from_up)
-    )
-    above = col(q_down, ZDOWN, "above")
+    t = [col(sent[0], PAIR, "t0")]
+    t += [col(after(sent[i], mate_got), PAIR, f"t{i}") for i in (1, 2)]
 
     stream_grad = call(
-        own_grad_body, sds((128, 512), bf16), (stream, near, coefs, coefs_mate)
-    )
-    hidden_grad = call(here_body, sds((64, 3696), bf16), (own[3], t[3], below, above))
-    keep = after(keep, hidden_grad, stream_grad)
-    w_sum = (keep + both_got[:, :256].astype(f32) + w_recv.astype(f32)).astype(bf16)
-    w_sum_other = core(w_sum, "w_sum")
+        own_grad_body, sds((128, 512), bf16), (after(stream, own[0]), near, coefs, coefs_mate)
+    )
+    q0a, q0b = fold(own[0], after(t[0], w_send[0]))
+    from_down = col(q0a, ZUP, "from_down")
+    from_up = col(q0b, ZDOWN, "from_up")
+    q1b, q1a = fold(own[1], after(t[1], from_down, from_up))
+    t.append(col(after(sent[3], q1a), PAIR, "t3"))
+    give, keep = outer(pieces, g_own, g_other, 0, "outer_own")
+    own_got = core(give, "own_got")
+    pure_b = col(q1b, ZUP, "pure_b")
+    pure_a = col(q1a, ZDOWN, "pure_a")
+    q2a, q2b = fold(own[2], after(t[2], w_recv, pure_a, pure_b, stream_grad), from_down, from_up)
+    mixed_a = col(q2a, ZUP, "mixed_a")
+    mixed_b = col(q2b, ZDOWN, "mixed_b")
+    hidden_grad = call(
+        here_body, sds((64, 3696), bf16), (own[3], t[3], pure_a, pure_b, mixed_a, mixed_b)
+    )
+
+    keep = after(keep, q2a)
+    w_sum = [
+        (keep[a:b] + own_got[a:b].astype(f32) + w.astype(f32)).astype(bf16)
+        for (a, b), w in zip(SHARES, (w_recv,))
+    ]
+    w_sum_other = [core(w, f"w_sum{i}") for i, w in enumerate(w_sum)]
     weight_grad = join(w_sum, w_sum_other)
     return weight_grad, hidden_grad, stream_grad
 

time: 190 us -> 160 us (0.84)
  Pallas kernels: 47.7 us -> 22.2 us
  starting transfers between devices: 31.5 us -> 42.1 us
  other arithmetic: 9.17 us -> 3.13 us
  waiting for transfers between devices: 83.6 us -> 78.1 us
  local copies, waits for them, and re-layouts: 14.7 us -> 12.3 us
    pallas_call x11 -> x13, Pallas kernels: 42.8 us -> 22.2 us  [call(): pl.pallas_call(body, out_shape=out_shape, scratch_shapes=list(scratch), c...]
    ppermute x31 -> x34, starting transfers between devices: 31.5 us -> 42.1 us  [send(): return lax.ppermute(a, axis, perm)]
    ppermute x31 -> x34, waiting for transfers between devices: 83.6 us -> 78.1 us  [send(): return lax.ppermute(a, axis, perm)]
    pallas_call x1 -> x0, Pallas kernels: 4.89 us -> none  [join(): pl.pallas_call(join_body, grid=(rows // tile,), in_specs=[pl.BlockSpec((t...]
    convert_element_type x2, other arithmetic: 4.42 us -> 1.27 us  [the longest x1 0.66 us: per_device(): (keep[a:b] + own_got[a:b].astype(f32) + w.astype(f32)).astype(bf16)]
    unnamed x50 -> x28, local copies, waits for them, and re-layouts: 7.41 us -> 4.77 us
  transfers between devices with their start and end apart: 31 -> 34, of which waited for: 19 -> 18; matrix products, arithmetic and copies ran while one was open for 7% -> 6% of each run, Pallas kernels for 16% -> 9%
where the time goes in v3:
time: 160 us; the launch traced here: 159 us
  waiting for transfers between devices  78.1 us (49%)
  starting transfers between devices  42.1 us (26%)
  Pallas kernels  22.2 us (14%)
  local copies, waits for them, and re-layouts  12.3 us (8%)
  other arithmetic  3.13 us (2%)
    ppermute x34, waiting for transfers between devices, send(): return lax.ppermute(a, axis, perm)  78.1 us
    ppermute x34, starting transfers between devices, send(): return lax.ppermute(a, axis, perm)  42.1 us
    pallas_call x13, Pallas kernels, call(): pl.pallas_call(body, out_shape=out_shape, scratch_shapes=list(scratch), c...  22.2 us
    unnamed x28, local copies, waits for them, and re-layouts  4.77 us
  transfers between devices with their start and end apart: 34, of which 18 were waited for; matrix products, arithmetic and copies ran while one was open for 6% of the time, Pallas kernels for 9%

profile of v3, /device:TPU:6, one launch (start us, length us, event | category | flops | bytes accessed | tf_op | source)
XLA Modules:
  0.0 159.3 jit_solution(7192389372754263353)
XLA Ops:
  0.6 1.6 %prep_body.1 = bf16[144,512]{1,0:T(8,128)(2,1)} custom-call(bf16[128,512]{1,0:T(8,128)(2,1)} %stream.2, f32[1,512]{1,0:T(1,128)} %bitcast.2, f32[1,512]{1,0:T(1,128)} %bitcast.3, f32[1,128]{1,0:T(1,128)} %reward.1, s32[1,128]{1,0:T(1,128)} %segment.1), custom_call_target="tpu_custom_call" | custom-call | tf_op jit(solution)/shard_map/prep_body/pallas_call | solution.py:55
  2.3 3.1 %collective-permute-start.2 = (bf16[144,512]{1,0:T(8,128)(2,1)}, bf16[144,512]{1,0:T(8,128)(2,1)S(1)}, u32[]{:S(2)}, u32[]{:S(2)}) collective-permute-start(bf16[144,512]{1,0:T(8,128)(2,1)} %prep_body.1), channel_id=1, source_target_pairs={{0,3},{1,2},{2,1},{3,0},{4,7},{5,6},{6,5},{7,4},{8,11},{9,10},{10,... | collective-permute-start | bytes 442376 | tf_op jit(solution)/shard_map/payload_mate/ppermute | solution.py:29
  5.5 6.3 %collective-permute-start.1 = (bf16[64,3696]{1,0:T(8,128)(2,1)}, bf16[64,3696]{1,0:T(8,128)(2,1)S(1)}, u32[]{:S(2)}, u32[]{:S(2)}) collective-permute-start(bf16[64,3696]{1,0:T(8,128)(2,1)} %refs_4_.3), channel_id=1, source_target_pairs={{0,12},{1,13},{2,14},{3,15},{4,0},{5,1},{6,2},{7,3},{8,4},{9,5},{1... | collective-permute-start | bytes 1419272 | tf_op jit(solution)/shard_map/up/ppermute | solution.py:29
  11.8 0.9 pad_maximum_fusion.2.own
  12.8 0.9 collective-permute-start.3
  13.7 2.9 %constant_dynamic-slice_fusion = bf16[1856,512]{1,0:T(8,128)(2,1)} fusion(bf16[3696,512]{1,0:T(8,128)(2,1)} %refs_2_.1, s32[]{:T(128)S(6)} %select_n.3), kind=kLoop, calls=%fused_computation.10 | loop fusion | bytes 3801092 | tf_op jit(solution)/shard_map/dynamic_slice | solution.py:384
  16.6 1.1 collective-permute-start.15
  17.6 3.3 %collective-permute-done.3.other = bf16[144,1024]{1,0:T(8,128)(2,1)S(1)} collective-permute-done((bf16[144,1024]{1,0:T(8,128)(2,1)S(1)}, bf16[144,1024]{1,0:T(8,128)(2,1)S(1)}, u32[]{:S(2)}, u32[]{:S(2)}) %collective-permute-start.3) | collective-permute-done | bytes 294944 | tf_op jit(solution)/shard_map/block_x1/ppermute | solution.py:29
  21.1 0.6 collective-permute-start.9
  21.7 0.8 copy-done.10
  22.5 1.7 %collective-permute-start.5 = (f32[8,128]{1,0:T(8,128)S(1)}, f32[8,128]{1,0:T(8,128)S(1)}, u32[]{:S(2)}, u32[]{:S(2)}) collective-permute-start(f32[8,128]{1,0:T(8,128)S(1)} %get-tuple-element.47), channel_id=1, source_target_pairs={{0,1},{1,0},{2,3},{3,2},{4,5},{5,4},{6,7},{7,6},{8,9},{9,8},{10,11... | collective-permute-start | bytes 12296 | tf_op jit(solution)/shard_map/sums0/ppermute | solution.py:29
  24.2 1.8 %collective-permute-done.5 = f32[8,128]{1,0:T(8,128)S(1)} collective-permute-done((f32[8,128]{1,0:T(8,128)S(1)}, f32[8,128]{1,0:T(8,128)S(1)}, u32[]{:S(2)}, u32[]{:S(2)}) %collective-permute-start.5) | collective-permute-done | bytes 4128 | tf_op jit(solution)/shard_map/sums0/ppermute | solution.py:29
  26.1 6.0 %collective-permute-done.1.refs_2_ = bf16[64,3696]{1,0:T(8,128)(2,1)S(1)} collective-permute-done((bf16[64,3696]{1,0:T(8,128)(2,1)}, bf16[64,3696]{1,0:T(8,128)(2,1)S(1)}, u32[]{:S(2)}, u32[]{:S(2)}) %collective-permute-start.1) | collective-permute-done | bytes 473120 | tf_op jit(solution)/shard_map/up/ppermute | solution.py:29
  32.1 3.7 %collective-permute-done.refs_3_ = bf16[64,3696]{1,0:T(8,128)(2,1)S(1)} collective-permute-done((bf16[64,3696]{1,0:T(8,128)(2,1)}, bf16[64,3696]{1,0:T(8,128)(2,1)S(1)}, u32[]{:S(2)}, u32[]{:S(2)}) %collective-permute-start) | collective-permute-done | bytes 473120 | tf_op jit(solution)/shard_map/down/ppermute | solution.py:29
  35.8 0.7 slice.6
  36.5 1.0 collective-permute-start.7
  37.6 2.0 %collective-permute-start.6 = (bf16[32,3696]{1,0:T(8,128)(2,1)}, bf16[32,3696]{1,0:T(8,128)(2,1)S(1)}, u32[]{:S(2)}, u32[]{:S(2)}) collective-permute-start(bf16[32,3696]{1,0:T(8,128)(2,1)} %slice.6), channel_id=1, source_target_pairs={{0,4},{1,5},{2,6},{3,7},{4,8},{5,9},{6,10},{7,11},{8,12},{9,13},{1... | collective-permute-start | bytes 709640 | tf_op jit(solution)/shard_map/far_a/ppermute | solution.py:29
  39.7 1.3 copy.11
  41.0 1.7 %collective-permute-start.12 = (bf16[128,3696]{0,1:T(8,128)(2,1)}, bf16[128,3696]{0,1:T(8,128)(2,1)}, u32[]{:S(2)}, u32[]{:S(2)}) collective-permute-start(bf16[128,3696]{0,1:T(8,128)(2,1)} %copy.11), channel_id=1, source_target_pairs={{0,1},{1,0},{2,3},{3,2},{4,5},{5,4},{6,7},{7,6},{8,9},{9,8},{10,11... | collective-permute-start | bytes 2838536 | tf_op jit(solution)/shard_map/y12/ppermute | solution.py:29
  42.8 2.1 %collective-permute-start.10 = (f32[8,128]{1,0:T(8,128)S(1)}, f32[8,128]{1,0:T(8,128)S(1)}, u32[]{:S(2)}, u32[]{:S(2)}) collective-permute-start(f32[8,128]{1,0:T(8,128)S(1)} %add.22), channel_id=1, source_target_pairs={{0,12},{1,13},{2,14},{3,15},{4,8},{5,9},{6,10},{7,11},{8,4},{9,5},... | collective-permute-start | bytes 12296 | tf_op jit(solution)/shard_map/sums2/ppermute | solution.py:29
  44.9 1.0 constant_dynamic-update-slice_fusion.2.here
  45.9 2.9 %collective-permute-done.7.refs_1_ = bf16[32,3696]{1,0:T(8,128)(2,1)S(1)} collective-permute-done((bf16[32,3696]{1,0:T(8,128)(2,1)S(1)}, bf16[32,3696]{1,0:T(8,128)(2,1)S(1)}, u32[]{:S(2)}, u32[]{:S(2)}) %collective-permute-start.7) | collective-permute-done | bytes 236576 | tf_op jit(solution)/shard_map/far_b/ppermute | solution.py:29
  48.8 4.0 %collective-permute-done.6.refs_0_ = bf16[32,3696]{1,0:T(8,128)(2,1)S(1)} collective-permute-done((bf16[32,3696]{1,0:T(8,128)(2,1)}, bf16[32,3696]{1,0:T(8,128)(2,1)S(1)}, u32[]{:S(2)}, u32[]{:S(2)}) %collective-permute-start.6) | collective-permute-done | bytes 236576 | tf_op jit(solution)/shard_map/far_a/ppermute | solution.py:29
  52.8 0.8 pad_maximum_fusion.1
  53.6 1.8 %collective-permute-start.11 = (bf16[64,3696]{1,0:T(8,128)(2,1)}, bf16[64,3696]{1,0:T(8,128)(2,1)}, u32[]{:S(2)}, u32[]{:S(2)}) collective-permute-start(bf16[64,3696]{1,0:T(8,128)(2,1)} %pad_maximum_fusion.1), channel_id=1, source_target_pairs={{0,1},{1,0},{2,3},{3,2},{4,5},{5,4},{6,7},{7,6},{8,9},{9,8},{10,11... | collective-permute-start | bytes 1419272 | tf_op jit(solution)/shard_map/y0/ppermute | solution.py:29
  55.4 1.2 collective-permute-done.13
  56.6 0.5 collective-permute-start.14
  57.1 4.4 %collective-permute-done.14 = f32[24,128]{1,0:T(8,128)S(1)} collective-permute-done((f32[24,128]{1,0:T(8,128)S(1)}, f32[24,128]{1,0:T(8,128)S(1)}, u32[]{:S(2)}, u32[]{:S(2)}) %collective-permute-start.14) | collective-permute-done | bytes 12320 | tf_op jit(solution)/shard_map/tiny_x3/ppermute | solution.py:29
  62.2 3.2 %collective-permute-done.16.there = f32[48,128]{1,0:T(8,128)S(1)} collective-permute-done((f32[48,128]{1,0:T(8,128)S(1)}, f32[48,128]{1,0:T(8,128)S(1)}, u32[]{:S(2)}, u32[]{:S(2)}) %collective-permute-start.16) | collective-permute-done | bytes 24608 | tf_op jit(solution)/shard_map/tiny_zlo/ppermute | solution.py:29
  65.3 0.8 coefs_body.1.coefs
  66.1 0.5 collective-permute-start.18
  66.6 1.6 %copy.12.refs_6_ = bf16[128,3696]{1,0:T(8,128)(2,1)S(1)} copy(bf16[128,3696]{0,1:T(8,128)(2,1)} %collective-permute-done.12) | data formatting | bytes 1892352 | tf_op jit(solution)/shard_map/y12/ppermute | solution.py:29
  68.2 1.2 grad_body.1
  69.3 1.8 %collective-permute-done.18.coefs_mate = f32[8,128]{1,0:T(8,128)S(1)} collective-permute-done((f32[8,128]{1,0:T(8,128)S(1)}, f32[8,128]{1,0:T(8,128)S(1)}, u32[]{:S(2)}, u32[]{:S(2)}) %collective-permute-start.18) | collective-permute-done | bytes 4128 | tf_op jit(solution)/shard_map/coefs_mate/ppermute | solution.py:29
  71.2 0.9 copy-done.3
  72.1 0.9 copy-done.6
  73.1 1.0 copy-done.8
  74.1 1.0 copy-done.11
  75.1 3.2 %outer_mate.1 = (bf16[3696,256]{1,0:T(8,128)(2,1)S(1)}, f32[3696,256]{1,0:T(8,128)S(1)}) custom-call(bf16[32,3696]{1,0:T(8,128)(2,1)S(1)} %copy-done.6, bf16[32,3696]{1,0:T(8,128)(2,1)S(1)} %copy-done.3, bf16[64,3696]{1,0:T(8,128)(2,1)S(1)} %collective-permute-done.1.refs_2_, bf16[64,3696]{1,0:T(8,128)(2,1)S(1)} %collective-permute-done.refs_3_, ...), custom_call_target="tpu_custom_call" | custom-call | flops 1937768448 | bytes 8388608 | tf_op jit(solution)/shard_map/outer_mate/pallas_call | solution.py:55
  78.4 0.5 collective-permute-start.20
  78.9 5.1 %collective-permute-done.19 = bf16[3696,256]{1,0:T(8,128)(2,1)S(1)} collective-permute-done((bf16[3696,256]{1,0:T(8,128)(2,1)S(1)}, bf16[3696,256]{1,0:T(8,128)(2,1)S(1)}, u32[]{:S(2)}, u32[]{:S(2)}) %collective-permute-start.19) | collective-permute-done | bytes 1892384 | tf_op jit(solution)/shard_map/mate_got/ppermute | solution.py:29
  84.0 0.6 add_convert_fusion.1
  84.6 1.3 collective-permute-start.22
  86.0 3.2 %outer_own.1 = (bf16[3696,256]{1,0:T(8,128)(2,1)S(1)}, f32[3696,256]{1,0:T(8,128)S(1)}) custom-call(bf16[32,3696]{1,0:T(8,128)(2,1)S(1)} %copy-done.7, bf16[32,3696]{1,0:T(8,128)(2,1)S(1)} %copy-done.4, bf16[64,3696]{1,0:T(8,128)(2,1)S(1)} %collective-permute-done.1.refs_2_, bf16[64,3696]{1,0:T(8,128)(2,1)S(1)} %collective-permute-done.refs_3_, ...), custom_call_target="tpu_custom_call" | custom-call | flops 1937768448 | bytes 8388608 | tf_op jit(solution)/shard_map/outer_own/pallas_call | solution.py:55
  89.3 7.4 %inner_body.1 = (bf16[64,3696]{1,0:T(8,128)(2,1)S(1)}, bf16[64,3696]{1,0:T(8,128)(2,1)S(1)}, bf16[64,3696]{1,0:T(8,128)(2,1)S(1)}, bf16[64,3696]{1,0:T(8,128)(2,...) custom-call(bf16[256,1024]{1,0:T(8,128)(2,1)S(1)} %get-tuple-element., ...), custom_call_target="tpu_custom_call" | custom-call | flops 3875536896 | bytes 13631488 | tf_op jit(solution)/shard_map/inner_body/pallas_call | solution.py:55
  96.7 1.6 %collective-permute-start.24 = (bf16[64,3696]{1,0:T(8,128)(2,1)S(1)}, bf16[64,3696]{1,0:T(8,128)(2,1)S(1)}, u32[]{:S(2)}, u32[]{:S(2)}) collective-permute-start(bf16[64,3696]{1,0:T(8,128)(2,1)S(1)} %get-tuple-element.73), channel_id=1, source_target_pairs={{0,1},{1,0},{2,3},{3,2},{4,5},{5,4},{6,7},{7,6},{8,9},{9,8},{10,11... | collective-permute-start | bytes 1419272 | tf_op jit(solution)/shard_map/t0/ppermute | solution.py:29
  98.3 0.5 collective-permute-start.23
  98.8 11.8 %collective-permute-done.24.other = bf16[64,3696]{1,0:T(8,128)(2,1)S(1)} collective-permute-done((bf16[64,3696]{1,0:T(8,128)(2,1)S(1)}, bf16[64,3696]{1,0:T(8,128)(2,1)S(1)}, u32[]{:S(2)}, u32[]{:S(2)}) %collective-permute-start.24) | collective-permute-done | bytes 473120 | tf_op jit(solution)/shard_map/t0/ppermute | solution.py:29
  110.7 1.4 collective-permute-start.25
  112.1 2.8 %collective-permute-start.26 = (bf16[32,3696]{1,0:T(8,128)(2,1)S(1)}, bf16[32,3696]{1,0:T(8,128)(2,1)S(1)}, u32[]{:S(2)}, u32[]{:S(2)}) collective-permute-start(bf16[32,3696]{1,0:T(8,128)(2,1)S(1)} %get-tuple-element.76), channel_id=1, source_target_pairs={{0,12},{1,13},{2,14},{3,15},{4,0},{5,1},{6,2},{7,3},{8,4},{9,5},{1... | collective-permute-start | bytes 709640 | tf_op jit(solution)/shard_map/from_up/ppermute | solution.py:29
  114.9 4.1 %collective-permute-done.23.other = bf16[64,3696]{1,0:T(8,128)(2,1)S(1)} collective-permute-done((bf16[64,3696]{1,0:T(8,128)(2,1)S(1)}, bf16[64,3696]{1,0:T(8,128)(2,1)S(1)}, u32[]{:S(2)}, u32[]{:S(2)}) %collective-permute-start.23) | collective-permute-done | bytes 473120 | tf_op jit(solution)/shard_map/t1/ppermute | solution.py:29
  119.0 1.4 collective-permute-start.21
  120.4 2.1 %collective-permute-done.25.refs_0_ = bf16[32,3696]{1,0:T(8,128)(2,1)S(1)} collective-permute-done((bf16[32,3696]{1,0:T(8,128)(2,1)S(1)}, bf16[32,3696]{1,0:T(8,128)(2,1)S(1)}, u32[]{:S(2)}, u32[]{:S(2)}) %collective-permute-start.25) | collective-permute-done | bytes 236576 | tf_op jit(solution)/shard_map/from_down/ppermute | solution.py:29
  122.6 1.3 collective-permute-start.28
  123.9 2.9 %collective-permute-start.27 = (bf16[32,3696]{1,0:T(8,128)(2,1)S(1)}, bf16[32,3696]{1,0:T(8,128)(2,1)S(1)}, u32[]{:S(2)}, u32[]{:S(2)}) collective-permute-start(bf16[32,3696]{1,0:T(8,128)(2,1)S(1)} %get-tuple-element.78), channel_id=1, source_target_pairs={{0,12},{1,13},{2,14},{3,15},{4,0},{5,1},{6,2},{7,3},{8,4},{9,5},{1... | collective-permute-start | bytes 709640 | tf_op jit(solution)/shard_map/pure_a/ppermute | solution.py:29
  126.8 0.9 own_grad_body.1
  127.7 2.4 %collective-permute-done.21.other = bf16[64,3696]{1,0:T(8,128)(2,1)S(1)} collective-permute-done((bf16[64,3696]{1,0:T(8,128)(2,1)S(1)}, bf16[64,3696]{1,0:T(8,128)(2,1)S(1)}, u32[]{:S(2)}, u32[]{:S(2)}) %collective-permute-start.21) | collective-permute-done | bytes 473120 | tf_op jit(solution)/shard_map/t2/ppermute | solution.py:29
  130.1 5.4 %collective-permute-done.28.pure_b = bf16[32,3696]{1,0:T(8,128)(2,1)S(1)} collective-permute-done((bf16[32,3696]{1,0:T(8,128)(2,1)S(1)}, bf16[32,3696]{1,0:T(8,128)(2,1)S(1)}, u32[]{:S(2)}, u32[]{:S(2)}) %collective-permute-start.28) | collective-permute-done | bytes 236576 | tf_op jit(solution)/shard_map/pure_b/ppermute | solution.py:29
  135.7 0.7 add_convert_fusion.refs_0_
  136.5 4.5 %collective-permute-start.33 = (bf16[32,3696]{1,0:T(8,128)(2,1)S(1)}, bf16[32,3696]{1,0:T(8,128)(2,1)S(1)}, u32[]{:S(2)}, u32[]{:S(2)}) collective-permute-start(bf16[32,3696]{1,0:T(8,128)(2,1)S(1)} %get-tuple-element.88), channel_id=1, source_target_pairs={{0,12},{1,13},{2,14},{3,15},{4,0},{5,1},{6,2},{7,3},{8,4},{9,5},{1... | collective-permute-start | bytes 709640 | tf_op jit(solution)/shard_map/mixed_b/ppermute | solution.py:29
  141.0 8.7 %collective-permute-done.31.other = bf16[64,3696]{1,0:T(8,128)(2,1)S(1)} collective-permute-done((bf16[64,3696]{1,0:T(8,128)(2,1)S(1)}, bf16[64,3696]{1,0:T(8,128)(2,1)S(1)}, u32[]{:S(2)}, u32[]{:S(2)}) %collective-permute-start.31) | collective-permute-done | bytes 473120 | tf_op jit(solution)/shard_map/t3/ppermute | solution.py:29
  149.7 6.2 %collective-permute-done.32.mixed_a = bf16[32,3696]{1,0:T(8,128)(2,1)S(1)} collective-permute-done((bf16[32,3696]{1,0:T(8,128)(2,1)S(1)}, bf16[32,3696]{1,0:T(8,128)(2,1)S(1)}, u32[]{:S(2)}, u32[]{:S(2)}) %collective-permute-start.32) | collective-permute-done | bytes 236576 | tf_op jit(solution)/shard_map/mixed_a/ppermute | solution.py:29
  155.9 1.0 here_body.1
  156.9 2.4 %join_body.1 = bf16[3696,512]{1,0:T(8,128)(2,1)} custom-call(bf16[3696,256]{1,0:T(8,128)(2,1)S(1)} %add_convert_fusion.refs_0_, bf16[3696,256]{1,0:T(8,128)(2,1)S(1)} %collective-permute-done.30.refs_1_), custom_call_target="tpu_custom_call" | custom-call | tf_op jit(solution)/shard_map/join_body/pallas_call | solution.py:55
  (61 shorter events, 1.3 us)
Async XLA Ops:
  2.3 9.5 %collective-permute-start.2 = (bf16[144,512]{1,0:T(8,128)(2,1)}, bf16[144,512]{1,0:T(8,128)(2,1)S(1)}, u32[]{:S(2)}, u32[]{:S(2)}) collective-permute-start(bf16[144,512]{1,0:T(8,128)(2,1)} %prep_body.1), channel_id=1, source_target_pairs={{0,3},{1,2},{2,1},{3,0},{4,7},{5,6},{6,5},{7,4},{8,11},{9,10},{10,... | collective-permute-start | bytes 442376 | tf_op jit(solution)/shard_map/payload_mate/ppermute | solution.py:29
  5.4 16.3 %collective-permute-start.4 = (bf16[64,3696]{1,0:T(8,128)(2,1)}, bf16[64,3696]{1,0:T(8,128)(2,1)S(1)}, u32[]{:S(2)}, u32[]{:S(2)}) collective-permute-start(bf16[64,3696]{1,0:T(8,128)(2,1)} %refs_4_.3), channel_id=1, source_target_pairs={{0,1},{1,0},{2,3},{3,2},{4,5},{5,4},{6,7},{7,6},{8,9},{9,8},{10,11... | collective-permute-start | bytes 1419272 | tf_op jit(solution)/shard_map/y3/ppermute | solution.py:29
  5.5 26.5 %collective-permute-start.1 = (bf16[64,3696]{1,0:T(8,128)(2,1)}, bf16[64,3696]{1,0:T(8,128)(2,1)S(1)}, u32[]{:S(2)}, u32[]{:S(2)}) collective-permute-start(bf16[64,3696]{1,0:T(8,128)(2,1)} %refs_4_.3), channel_id=1, source_target_pairs={{0,12},{1,13},{2,14},{3,15},{4,0},{5,1},{6,2},{7,3},{8,4},{9,5},{1... | collective-permute-start | bytes 1419272 | tf_op jit(solution)/shard_map/up/ppermute | solution.py:29
  11.8 24.0 %collective-permute-start = (bf16[64,3696]{1,0:T(8,128)(2,1)}, bf16[64,3696]{1,0:T(8,128)(2,1)S(1)}, u32[]{:S(2)}, u32[]{:S(2)}) collective-permute-start(bf16[64,3696]{1,0:T(8,128)(2,1)} %refs_4_.3), channel_id=1, source_target_pairs={{0,4},{1,5},{2,6},{3,7},{4,8},{5,9},{6,10},{7,11},{8,12},{9,13},{1... | collective-permute-start | bytes 1419272 | tf_op jit(solution)/shard_map/down/ppermute | solution.py:29
  12.8 8.1 %collective-permute-start.3 = (bf16[144,1024]{1,0:T(8,128)(2,1)S(1)}, bf16[144,1024]{1,0:T(8,128)(2,1)S(1)}, u32[]{:S(2)}, u32[]{:S(2)}) collective-permute-start(bf16[144,1024]{1,0:T(8,128)(2,1)S(1)} %pad_maximum_fusion.2.own), channel_id=1, source_target_pairs={{0,16},{16,0},{32,48},{48,32},{64,80},{80,64},{96,112},{112,96},{1... | collective-permute-start | bytes 884744 | tf_op jit(solution)/shard_map/block_x1/ppermute | solution.py:29
  16.6 45.6 %collective-permute-start.15 = (bf16[1856,512]{1,0:T(8,128)(2,1)}, bf16[1856,512]{1,0:T(8,128)(2,1)}, u32[]{:S(2)}, u32[]{:S(2)}) collective-permute-start(bf16[1856,512]{1,0:T(8,128)(2,1)} %constant_dynamic-slice_fusion), channel_id=1, source_target_pairs={{0,3},{1,2},{2,1},{3,0},{4,7},{5,6},{6,5},{7,4},{8,11},{9,10},{10,... | collective-permute-start | bytes 5701640 | tf_op jit(solution)/shard_map/got/ppermute | solution.py:29
  21.1 21.7 %collective-permute-start.9 = (bf16[144,1024]{1,0:T(8,128)(2,1)S(1)}, bf16[144,1024]{1,0:T(8,128)(2,1)}, u32[]{:S(2)}, u32[]{:S(2)}) collective-permute-start(bf16[144,1024]{1,0:T(8,128)(2,1)S(1)} %get-tuple-element.51.block), channel_id=1, source_target_pairs={{0,48},{16,32},{32,16},{48,0},{64,112},{80,96},{96,80},{112,64},{1... | collective-permute-start | bytes 884744 | tf_op jit(solution)/shard_map/block_x3/ppermute | solution.py:29
  21.7 0.8 copy-start.10
  22.5 3.6 %collective-permute-start.5 = (f32[8,128]{1,0:T(8,128)S(1)}, f32[8,128]{1,0:T(8,128)S(1)}, u32[]{:S(2)}, u32[]{:S(2)}) collective-permute-start(f32[8,128]{1,0:T(8,128)S(1)} %get-tuple-element.47), channel_id=1, source_target_pairs={{0,1},{1,0},{2,3},{3,2},{4,5},{5,4},{6,7},{7,6},{8,9},{9,8},{10,11... | collective-permute-start | bytes 12296 | tf_op jit(solution)/shard_map/sums0/ppermute | solution.py:29
  35.8 5.2 %collective-permute-start.8 = (f32[8,128]{1,0:T(8,128)S(1)}, f32[8,128]{1,0:T(8,128)S(1)}, u32[]{:S(2)}, u32[]{:S(2)}) collective-permute-start(f32[8,128]{1,0:T(8,128)S(1)} %add.21), channel_id=1, source_target_pairs={{0,4},{1,5},{2,6},{3,7},{4,0},{5,1},{6,2},{7,3},{8,12},{9,13},{10,... | collective-permute-start | bytes 12296 | tf_op jit(solution)/shard_map/sums1/ppermute | solution.py:29
  36.5 12.2 %collective-permute-start.7 = (bf16[32,3696]{1,0:T(8,128)(2,1)S(1)}, bf16[32,3696]{1,0:T(8,128)(2,1)S(1)}, u32[]{:S(2)}, u32[]{:S(2)}) collective-permute-start(bf16[32,3696]{1,0:T(8,128)(2,1)S(1)} %slice.7), channel_id=1, source_target_pairs={{0,12},{1,13},{2,14},{3,15},{4,0},{5,1},{6,2},{7,3},{8,4},{9,5},{1... | collective-permute-start | bytes 709640 | tf_op jit(solution)/shard_map/far_b/ppermute | solution.py:29
  37.6 15.2 %collective-permute-start.6 = (bf16[32,3696]{1,0:T(8,128)(2,1)}, bf16[32,3696]{1,0:T(8,128)(2,1)S(1)}, u32[]{:S(2)}, u32[]{:S(2)}) collective-permute-start(bf16[32,3696]{1,0:T(8,128)(2,1)} %slice.6), channel_id=1, source_target_pairs={{0,4},{1,5},{2,6},{3,7},{4,8},{5,9},{6,10},{7,11},{8,12},{9,13},{1... | collective-permute-start | bytes 709640 | tf_op jit(solution)/shard_map/far_a/ppermute | solution.py:29
  41.0 25.5 %collective-permute-start.12 = (bf16[128,3696]{0,1:T(8,128)(2,1)}, bf16[128,3696]{0,1:T(8,128)(2,1)}, u32[]{:S(2)}, u32[]{:S(2)}) collective-permute-start(bf16[128,3696]{0,1:T(8,128)(2,1)} %copy.11), channel_id=1, source_target_pairs={{0,1},{1,0},{2,3},{3,2},{4,5},{5,4},{6,7},{7,6},{8,9},{9,8},{10,11... | collective-permute-start | bytes 2838536 | tf_op jit(solution)/shard_map/y12/ppermute | solution.py:29
  42.8 10.8 %collective-permute-start.10 = (f32[8,128]{1,0:T(8,128)S(1)}, f32[8,128]{1,0:T(8,128)S(1)}, u32[]{:S(2)}, u32[]{:S(2)}) collective-permute-start(f32[8,128]{1,0:T(8,128)S(1)} %add.22), channel_id=1, source_target_pairs={{0,12},{1,13},{2,14},{3,15},{4,8},{5,9},{6,10},{7,11},{8,4},{9,5},... | collective-permute-start | bytes 12296 | tf_op jit(solution)/shard_map/sums2/ppermute | solution.py:29
  48.8 17.8 %copy-start.2 = (bf16[32,3696]{1,0:T(8,128)(2,1)}, bf16[32,3696]{1,0:T(8,128)(2,1)S(1)}, u32[]{:S(2)}) copy-start(bf16[32,3696]{1,0:T(8,128)(2,1)S(1)} %collective-permute-done.7.refs_1_) | copy-start | bytes 709636
  48.8 19.4 %collective-permute-start.17 = (bf16[288,1024]{1,0:T(8,128)(2,1)S(1)}, bf16[288,1024]{1,0:T(8,128)(2,1)S(1)}, u32[]{:S(2)}, u32[]{:S(2)}) collective-permute-start(bf16[288,1024]{1,0:T(8,128)(2,1)S(1)} %constant_dynamic-update-slice_fusion.2.here), channel_id=1, source_target_pairs={{0,64},{16,80},{32,96},{48,112},{64,0},{80,16},{96,32},{112,48},{1... | collective-permute-start | bytes 1769480 | tf_op jit(solution)/shard_map/block_zlo/ppermute | solution.py:29
  52.8 13.8 %copy-start.5 = (bf16[32,3696]{1,0:T(8,128)(2,1)}, bf16[32,3696]{1,0:T(8,128)(2,1)S(1)}, u32[]{:S(2)}) copy-start(bf16[32,3696]{1,0:T(8,128)(2,1)S(1)} %collective-permute-done.6.refs_0_) | copy-start | bytes 709636
  53.6 17.6 %collective-permute-start.11 = (bf16[64,3696]{1,0:T(8,128)(2,1)}, bf16[64,3696]{1,0:T(8,128)(2,1)}, u32[]{:S(2)}, u32[]{:S(2)}) collective-permute-start(bf16[64,3696]{1,0:T(8,128)(2,1)} %pad_maximum_fusion.1), channel_id=1, source_target_pairs={{0,1},{1,0},{2,3},{3,2},{4,5},{5,4},{6,7},{7,6},{8,9},{9,8},{10,11... | collective-permute-start | bytes 1419272 | tf_op jit(solution)/shard_map/y0/ppermute | solution.py:29
  55.4 1.2 collective-permute-start.13
  56.6 4.9 %collective-permute-start.14 = (f32[24,128]{1,0:T(8,128)S(1)}, f32[24,128]{1,0:T(8,128)S(1)}, u32[]{:S(2)}, u32[]{:S(2)}) collective-permute-start(f32[24,128]{1,0:T(8,128)S(1)} %pad_maximum_fusion.3), channel_id=1, source_target_pairs={{0,48},{16,32},{32,16},{48,0},{64,112},{80,96},{96,80},{112,64},{1... | collective-permute-start | bytes 36872 | tf_op jit(solution)/shard_map/tiny_x3/ppermute | solution.py:29
  61.5 3.8 %collective-permute-start.16 = (f32[48,128]{1,0:T(8,128)S(1)}, f32[48,128]{1,0:T(8,128)S(1)}, u32[]{:S(2)}, u32[]{:S(2)}) collective-permute-start(f32[48,128]{1,0:T(8,128)S(1)} %constant_dynamic-update-slice_fusion.here), channel_id=1, source_target_pairs={{0,64},{16,80},{32,96},{48,112},{64,0},{80,16},{96,32},{112,48},{1... | collective-permute-start | bytes 73736 | tf_op jit(solution)/shard_map/tiny_zlo/ppermute | solution.py:29
  66.1 5.1 %collective-permute-start.18 = (f32[8,128]{1,0:T(8,128)S(1)}, f32[8,128]{1,0:T(8,128)S(1)}, u32[]{:S(2)}, u32[]{:S(2)}) collective-permute-start(f32[8,128]{1,0:T(8,128)S(1)} %coefs_body.1.coefs), channel_id=1, source_target_pairs={{0,3},{1,2},{2,1},{3,0},{4,7},{5,6},{6,5},{7,4},{8,11},{9,10},{10,... | collective-permute-start | bytes 12296 | tf_op jit(solution)/shard_map/coefs_mate/ppermute | solution.py:29
  71.2 0.9 copy-start.3
  72.1 0.9 copy-start.6
  73.1 1.0 copy-start.8
  74.1 1.0 copy-start.11
  78.3 5.7 %collective-permute-start.19 = (bf16[3696,256]{1,0:T(8,128)(2,1)S(1)}, bf16[3696,256]{1,0:T(8,128)(2,1)S(1)}, u32[]{:S(2)}, u32[]{:S(2)}) collective-permute-start(bf16[3696,256]{1,0:T(8,128)(2,1)S(1)} %get-tuple-element.63), channel_id=1, source_target_pairs={{0,128},{128,0},{1,129},{129,1},{2,130},{130,2},{3,131},{131,3},{4... | collective-permute-start | bytes 5677064 | tf_op jit(solution)/shard_map/mate_got/ppermute | solution.py:29
  78.4 10.8 %collective-permute-start.20 = (bf16[1856,512]{1,0:T(8,128)(2,1)}, bf16[1856,512]{1,0:T(8,128)(2,1)S(1)}, u32[]{:S(2)}, u32[]{:S(2)}) collective-permute-start(bf16[1856,512]{1,0:T(8,128)(2,1)} %collective-permute-done.15.refs_3_), channel_id=1, source_target_pairs={{0,128},{128,0},{1,129},{129,1},{2,130},{130,2},{3,131},{131,3},{4... | collective-permute-start | bytes 5701640 | tf_op jit(solution)/shard_map/got_other/ppermute | solution.py:29
  84.0 1.9 %copy-start.4 = (bf16[32,3696]{1,0:T(8,128)(2,1)S(1)}, bf16[32,3696]{1,0:T(8,128)(2,1)}, u32[]{:S(2)}) copy-start(bf16[32,3696]{1,0:T(8,128)(2,1)} %copy-done.2) | copy-start | bytes 709636
  84.0 1.9 %copy-start.7 = (bf16[32,3696]{1,0:T(8,128)(2,1)S(1)}, bf16[32,3696]{1,0:T(8,128)(2,1)}, u32[]{:S(2)}) copy-start(bf16[32,3696]{1,0:T(8,128)(2,1)} %copy-done.5) | copy-start | bytes 709636
  84.0 1.9 %copy-start.9 = (bf16[64,3696]{1,0:T(8,128)(2,1)S(1)}, bf16[64,3696]{1,0:T(8,128)(2,1)}, u32[]{:S(2)}) copy-start(bf16[64,3696]{1,0:T(8,128)(2,1)} %refs_4_.3) | copy-start | bytes 1419268
  84.0 1.9 %copy-start.12 = (bf16[64,3696]{1,0:T(8,128)(2,1)S(1)}, bf16[64,3696]{1,0:T(8,128)(2,1)}, u32[]{:S(2)}) copy-start(bf16[64,3696]{1,0:T(8,128)(2,1)} %copy-done.10) | copy-start | bytes 1419268
  84.6 4.7 %copy-start = (bf16[3696,512]{1,0:T(8,128)(2,1)S(1)}, bf16[3696,512]{1,0:T(8,128)(2,1)}, u32[]{:S(2)}) copy-start(bf16[3696,512]{1,0:T(8,128)(2,1)} %refs_2_.1) | copy-start | bytes 11354116
  84.6 50.9 %collective-permute-start.22 = (bf16[3696,256]{1,0:T(8,128)(2,1)S(1)}, bf16[3696,256]{1,0:T(8,128)(2,1)S(1)}, u32[]{:S(2)}, u32[]{:S(2)}) collective-permute-start(bf16[3696,256]{1,0:T(8,128)(2,1)S(1)} %add_convert_fusion.1), channel_id=1, source_target_pairs={{0,3},{1,2},{2,1},{3,0},{4,7},{5,6},{6,5},{7,4},{8,11},{9,10},{10,... | collective-permute-start | bytes 5677064 | tf_op jit(solution)/shard_map/w_recv/ppermute | solution.py:29
  89.2 46.5 %collective-permute-start.29 = (bf16[3696,256]{1,0:T(8,128)(2,1)S(1)}, bf16[3696,256]{1,0:T(8,128)(2,1)S(1)}, u32[]{:S(2)}, u32[]{:S(2)}) collective-permute-start(bf16[3696,256]{1,0:T(8,128)(2,1)S(1)} %get-tuple-element.84), channel_id=1, source_target_pairs={{0,128},{128,0},{1,129},{129,1},{2,130},{130,2},{3,131},{131,3},{4... | collective-permute-start | bytes 5677064 | tf_op jit(solution)/shard_map/own_got/ppermute | solution.py:29
  96.7 30.1 %copy-start.1 = (bf16[128,512]{1,0:T(8,128)(2,1)S(1)}, bf16[128,512]{1,0:T(8,128)(2,1)}, u32[]{:S(2)}) copy-start(bf16[128,512]{1,0:T(8,128)(2,1)} %stream.2) | copy-start | bytes 393220
  96.7 13.9 %collective-permute-start.24 = (bf16[64,3696]{1,0:T(8,128)(2,1)S(1)}, bf16[64,3696]{1,0:T(8,128)(2,1)S(1)}, u32[]{:S(2)}, u32[]{:S(2)}) collective-permute-start(bf16[64,3696]{1,0:T(8,128)(2,1)S(1)} %get-tuple-element.73), channel_id=1, source_target_pairs={{0,1},{1,0},{2,3},{3,2},{4,5},{5,4},{6,7},{7,6},{8,9},{9,8},{10,11... | collective-permute-start | bytes 1419272 | tf_op jit(solution)/shard_map/t0/ppermute | solution.py:29
  98.3 20.7 %collective-permute-start.23 = (bf16[64,3696]{1,0:T(8,128)(2,1)S(1)}, bf16[64,3696]{1,0:T(8,128)(2,1)S(1)}, u32[]{:S(2)}, u32[]{:S(2)}) collective-permute-start(bf16[64,3696]{1,0:T(8,128)(2,1)S(1)} %get-tuple-element.71), channel_id=1, source_target_pairs={{0,1},{1,0},{2,3},{3,2},{4,5},{5,4},{6,7},{7,6},{8,9},{9,8},{10,11... | collective-permute-start | bytes 1419272 | tf_op jit(solution)/shard_map/t1/ppermute | solution.py:29
  110.7 11.8 %collective-permute-start.25 = (bf16[32,3696]{1,0:T(8,128)(2,1)S(1)}, bf16[32,3696]{1,0:T(8,128)(2,1)S(1)}, u32[]{:S(2)}, u32[]{:S(2)}) collective-permute-start(bf16[32,3696]{1,0:T(8,128)(2,1)S(1)} %get-tuple-element.75), channel_id=1, source_target_pairs={{0,4},{1,5},{2,6},{3,7},{4,8},{5,9},{6,10},{7,11},{8,12},{9,13},{1... | collective-permute-start | bytes 709640 | tf_op jit(solution)/shard_map/from_down/ppermute | solution.py:29
  112.1 10.4 %collective-permute-start.26 = (bf16[32,3696]{1,0:T(8,128)(2,1)S(1)}, bf16[32,3696]{1,0:T(8,128)(2,1)S(1)}, u32[]{:S(2)}, u32[]{:S(2)}) collective-permute-start(bf16[32,3696]{1,0:T(8,128)(2,1)S(1)} %get-tuple-element.76), channel_id=1, source_target_pairs={{0,12},{1,13},{2,14},{3,15},{4,0},{5,1},{6,2},{7,3},{8,4},{9,5},{1... | collective-permute-start | bytes 709640 | tf_op jit(solution)/shard_map/from_up/ppermute | solution.py:29
  119.0 11.1 %collective-permute-start.21 = (bf16[64,3696]{1,0:T(8,128)(2,1)S(1)}, bf16[64,3696]{1,0:T(8,128)(2,1)S(1)}, u32[]{:S(2)}, u32[]{:S(2)}) collective-permute-start(bf16[64,3696]{1,0:T(8,128)(2,1)S(1)} %get-tuple-element.68), channel_id=1, source_target_pairs={{0,1},{1,0},{2,3},{3,2},{4,5},{5,4},{6,7},{7,6},{8,9},{9,8},{10,11... | collective-permute-start | bytes 1419272 | tf_op jit(solution)/shard_map/t2/ppermute | solution.py:29
  122.6 12.9 %collective-permute-start.28 = (bf16[32,3696]{1,0:T(8,128)(2,1)S(1)}, bf16[32,3696]{1,0:T(8,128)(2,1)S(1)}, u32[]{:S(2)}, u32[]{:S(2)}) collective-permute-start(bf16[32,3696]{1,0:T(8,128)(2,1)S(1)} %get-tuple-element.79), channel_id=1, source_target_pairs={{0,4},{1,5},{2,6},{3,7},{4,8},{5,9},{6,10},{7,11},{8,12},{9,13},{1... | collective-permute-start | bytes 709640 | tf_op jit(solution)/shard_map/pure_b/ppermute | solution.py:29
  123.9 11.6 %collective-permute-start.27 = (bf16[32,3696]{1,0:T(8,128)(2,1)S(1)}, bf16[32,3696]{1,0:T(8,128)(2,1)S(1)}, u32[]{:S(2)}, u32[]{:S(2)}) collective-permute-start(bf16[32,3696]{1,0:T(8,128)(2,1)S(1)} %get-tuple-element.78), channel_id=1, source_target_pairs={{0,12},{1,13},{2,14},{3,15},{4,0},{5,1},{6,2},{7,3},{8,4},{9,5},{1... | collective-permute-start | bytes 709640 | tf_op jit(solution)/shard_map/pure_a/ppermute | solution.py:29
  136.3 20.6 %collective-permute-start.30 = (bf16[3696,256]{1,0:T(8,128)(2,1)S(1)}, bf16[3696,256]{1,0:T(8,128)(2,1)S(1)}, u32[]{:S(2)}, u32[]{:S(2)}) collective-permute-start(bf16[3696,256]{1,0:T(8,128)(2,1)S(1)} %add_convert_fusion.refs_0_), channel_id=1, source_target_pairs={{0,128},{128,0},{1,129},{129,1},{2,130},{130,2},{3,131},{131,3},{4... | collective-permute-start | bytes 5677064 | tf_op jit(solution)/shard_map/w_sum0/ppermute | solution.py:29
  136.4 13.3 %collective-permute-start.31 = (bf16[64,3696]{1,0:T(8,128)(2,1)S(1)}, bf16[64,3696]{1,0:T(8,128)(2,1)S(1)}, u32[]{:S(2)}, u32[]{:S(2)}) collective-permute-start(bf16[64,3696]{1,0:T(8,128)(2,1)S(1)} %get-tuple-element.87), channel_id=1, source_target_pairs={{0,1},{1,0},{2,3},{3,2},{4,5},{5,4},{6,7},{7,6},{8,9},{9,8},{10,11... | collective-permute-start | bytes 1419272 | tf_op jit(solution)/shard_map/t3/ppermute | solution.py:29
  136.5 13.2 %collective-permute-start.33 = (bf16[32,3696]{1,0:T(8,128)(2,1)S(1)}, bf16[32,3696]{1,0:T(8,128)(2,1)S(1)}, u32[]{:S(2)}, u32[]{:S(2)}) collective-permute-start(bf16[32,3696]{1,0:T(8,128)(2,1)S(1)} %get-tuple-element.88), channel_id=1, source_target_pairs={{0,12},{1,13},{2,14},{3,15},{4,0},{5,1},{6,2},{7,3},{8,4},{9,5},{1... | collective-permute-start | bytes 709640 | tf_op jit(solution)/shard_map/mixed_b/ppermute | solution.py:29
  141.0 14.9 %collective-permute-start.32 = (bf16[32,3696]{1,0:T(8,128)(2,1)S(1)}, bf16[32,3696]{1,0:T(8,128)(2,1)S(1)}, u32[]{:S(2)}, u32[]{:S(2)}) collective-permute-start(bf16[32,3696]{1,0:T(8,128)(2,1)S(1)} %get-tuple-element.82), channel_id=1, source_target_pairs={{0,4},{1,5},{2,6},{3,7},{4,8},{5,9},{6,10},{7,11},{8,12},{9,13},{1... | collective-permute-start | bytes 709640 | tf_op jit(solution)/shard_map/mixed_a/ppermute | solution.py:29

commit v4 on v3

--- a/solution.py
+++ b/solution.py
@@ -273,10 +273,10 @@
                 own[n][:, f:e] = out[256 + low : 256 + high]
 
 
-def outer_body(*refs, first):
-    pieces, (g_own, g_other), (give, keep, h_v, g_v) = refs[:8], refs[8:10], refs[10:]
+def outer_body(*refs, first, split):
+    (far_a, far_b, up, down, here, y0, y12, y3), (g_own, g_other) = refs[:8], refs[8:10]
+    *outs, h_v, g_v = refs[10:]
     p = lax.axis_index("dp")
-    far_a, far_b, up, down, here, y0, y12, y3 = pieces
     for at, src in (
         (0, far_a[...]),
         (32, far_b[...]),
@@ -292,7 +292,7 @@
         (448, y3[...]),
     ):
         h_v[at : at + src.shape[0]] = src
-    for n, side in enumerate((1 - p, p)):
+    for n, side in enumerate((1 - p, p) if split else (0, 1)):
         start = pl.multiple_of(first + 256 * side, 256)
         g_v[:256, 256 * n : 256 * n + 256] = g_own[:, pl.ds(start, 256)]
         g_v[256:, 256 * n : 256 * n + 256] = g_other[:, pl.ds(start, 256)]
@@ -301,14 +301,18 @@
         out = lax.dot_general(
             h_v[:, f:e], g_v[...], (((0,), (0,)), ((), ())), preferred_element_type=f32
         )
-        give[f:e] = out[:, :256].astype(bf16)
-        keep[f:e] = out[:, 256:]
-
-
-def outer(pieces, g_own, g_other, first, name):
+        if split:
+            outs[0][f:e] = out[:, :256].astype(bf16)
+            outs[1][f:e] = out[:, 256:]
+        else:
+            outs[0][f:e] = out
+
+
+def outer(pieces, g_own, g_other, first, split, name):
+    out = [sds((3696, 256), bf16), sds((3696, 256), f32)] if split else sds((3696, 512), f32)
     return call(
-        functools.partial(outer_body, first=first),
-        [sds((3696, 256), bf16), sds((3696, 256), f32)],
+        functools.partial(outer_body, first=first, split=split),
+        out,
         (*pieces, g_own, g_other),
         scratch=[pltpu.VMEM((512, 3696), bf16), pltpu.VMEM((512, 512), bf16)],
         flops=512 * 1024 * 3696,
@@ -339,20 +343,12 @@
         out[at : at + 32] = part.astype(bf16)
 
 
-SHARES = ((0, 3696),)
-
-
-def join_body(*refs):
+def merge_body(partial, recv, out):
     p = lax.axis_index("dp")
-    out = refs[-1]
-    n = len(SHARES)
-    for (a, b), mine, other in zip(SHARES, refs[:n], refs[n : 2 * n]):
-        out[a:b, pl.ds(pl.multiple_of(256 * p, 256), 256)] = mine[...]
-        out[a:b, pl.ds(pl.multiple_of(256 * (1 - p), 256), 256)] = other[...]
-
-
-def join(mine, other):
-    return call(join_body, sds((3696, 512), bf16), (*mine, *other))
+    mine = pl.ds(pl.multiple_of(256 * p, 256), 256)
+    rest = pl.ds(pl.multiple_of(256 * (1 - p), 256), 256)
+    out[:, mine] = (partial[:, mine] + recv[...].astype(f32)).astype(bf16)
+    out[:, rest] = partial[:, rest].astype(bf16)
 
 
 def per_device(stream, hidden, w_down, norm_gain, value_head, value_bias, rewards, segments):
@@ -377,9 +373,10 @@
         grant=56,
     )
     payload_mate = col(payload, MATE, "payload_mate")
-    y3 = col(hidden, PAIR, "y3")
-    down = col(hidden, ZUP, "down")
-    up = col(hidden, ZDOWN, "up")
+    ready = after(hidden, payload)
+    y3 = col(ready, PAIR, "y3")
+    down = col(ready, ZUP, "down")
+    up = col(ready, ZDOWN, "up")
 
     w_half = lax.dynamic_slice_in_dim(w_down, p * HIGH, LO, 0)
     got = col(after(w_half, payload_mate), MATE, "got")
@@ -426,15 +423,12 @@
     )
 
     pieces = (far_a, far_b, up, down, hidden, y0, y12, y3)
-    mate_give, mate_keep = outer(pieces, after(g_own, coefs_mate), g_other, 512, "outer_mate")
+    mate_give, mate_keep = outer(pieces, after(g_own, coefs_mate), g_other, 512, True, "outer_mate")
     mate_got = core(mate_give, "mate_got")
-    w_send = [(mate_keep[a:b] + mate_got[a:b].astype(f32)).astype(bf16) for a, b in SHARES]
-    w_recv = col(w_send[0], MATE, "w_recv")
-
     outs = call(
         inner_body,
         [sds((b - a, 3696), d) for d in (bf16, f32) for a, b in PARTS],
-        (after(g_own, w_send[0]), g_other, w_down, got, got_other),
+        (after(g_own, mate_keep), g_other, w_down, got, got_other),
         in_specs=[vmem] * 2 + [hbm] * 3,
         scratch=[
             pltpu.VMEM((3696, 512), bf16),
@@ -446,35 +440,31 @@
         grant=28,
     )
     sent, own = outs[:4], outs[4:]
-    t = [col(sent[0], PAIR, "t0")]
-    t += [col(after(sent[i], mate_got), PAIR, f"t{i}") for i in (1, 2)]
+    t = [col(a, PAIR, f"t{i}") for i, a in enumerate(sent)]
+    w_send = (after(mate_keep, own[0]) + mate_got.astype(f32)).astype(bf16)
+    w_recv = col(w_send, MATE, "w_recv")
 
     stream_grad = call(
         own_grad_body, sds((128, 512), bf16), (after(stream, own[0]), near, coefs, coefs_mate)
     )
-    q0a, q0b = fold(own[0], after(t[0], w_send[0]))
+    q0a, q0b = fold(own[0], after(t[0], w_send))
     from_down = col(q0a, ZUP, "from_down")
     from_up = col(q0b, ZDOWN, "from_up")
-    q1b, q1a = fold(own[1], after(t[1], from_down, from_up))
-    t.append(col(after(sent[3], q1a), PAIR, "t3"))
-    give, keep = outer(pieces, g_own, g_other, 0, "outer_own")
-    own_got = core(give, "own_got")
+    partial = outer(pieces, after(g_own, q0a), g_other, 0, False, "outer_own")
+    q1b, q1a = fold(own[1], after(t[1], partial, from_down, from_up))
     pure_b = col(q1b, ZUP, "pure_b")
     pure_a = col(q1a, ZDOWN, "pure_a")
     q2a, q2b = fold(own[2], after(t[2], w_recv, pure_a, pure_b, stream_grad), from_down, from_up)
     mixed_a = col(q2a, ZUP, "mixed_a")
     mixed_b = col(q2b, ZDOWN, "mixed_b")
+    part = call(merge_body, sds((3696, 512), bf16), (after(partial, q2a), w_recv))
+    part_other = core(part, "part")
+    weight_grad = (part.astype(f32) + part_other.astype(f32)).astype(bf16)
     hidden_grad = call(
-        here_body, sds((64, 3696), bf16), (own[3], t[3], pure_a, pure_b, mixed_a, mixed_b)
-    )
-
-    keep = after(keep, q2a)
-    w_sum = [
-        (keep[a:b] + own_got[a:b].astype(f32) + w.astype(f32)).astype(bf16)
-        for (a, b), w in zip(SHARES, (w_recv,))
-    ]
-    w_sum_other = [core(w, f"w_sum{i}") for i, w in enumerate(w_sum)]
-    weight_grad = join(w_sum, w_sum_other)
+        here_body,
+        sds((64, 3696), bf16),
+        (after(own[3], weight_grad), t[3], pure_a, pure_b, mixed_a, mixed_b),
+    )
     return weight_grad, hidden_grad, stream_grad
 
 

time: 160 us -> 154 us (0.963)
  waiting for transfers between devices: 78.1 us -> 74.1 us
  local copies, waits for them, and re-layouts: 12.3 us -> 10.4 us
    ppermute x34 -> x33, waiting for transfers between devices: 78.1 us -> 74.1 us  [send(): return lax.ppermute(a, axis, perm)]
    convert_element_type x2, other arithmetic: 1.27 us -> 3.59 us  [the longest x1 2.98 us: per_device(): weight_grad = (part.astype(f32) + part_other.astype(f32)).astype(bf16)]
    unnamed x28 -> x18, local copies, waits for them, and re-layouts: 4.77 us -> 2.87 us
    ppermute x34 -> x33, starting transfers between devices: 42.1 us -> 41.3 us  [send(): return lax.ppermute(a, axis, perm)]
  transfers between devices with their start and end apart: 34 -> 33, of which waited for: 18 -> 19; matrix products, arithmetic and copies ran while one was open for 6% -> 7% of each run, Pallas kernels for 9% -> 12%
where the time goes in v4:
time: 154 us; the launch traced here: 153 us
  waiting for transfers between devices  74.1 us (48%)
  starting transfers between devices  41.3 us (27%)
  Pallas kernels  21.5 us (14%)
  local copies, waits for them, and re-layouts  10.4 us (7%)
  other arithmetic  4.5 us (3%)
    ppermute x33, waiting for transfers between devices, send(): return lax.ppermute(a, axis, perm)  74.1 us
    ppermute x33, starting transfers between devices, send(): return lax.ppermute(a, axis, perm)  41.3 us
    pallas_call x13, Pallas kernels, call(): pl.pallas_call(body, out_shape=out_shape, scratch_shapes=list(scratch), c...  21.5 us
  transfers between devices with their start and end apart: 33, of which 19 were waited for; matrix products, arithmetic and copies ran while one was open for 7% of the time, Pallas kernels for 12%

profile of v4, /device:TPU:6, one launch (start us, length us, event | category | flops | bytes accessed | tf_op | source)
XLA Modules:
  0.0 153.3 jit_solution(15541757011942491742)
XLA Ops:
  0.6 1.6 %prep_body.1 = bf16[144,512]{1,0:T(8,128)(2,1)} custom-call(bf16[128,512]{1,0:T(8,128)(2,1)} %stream.2, f32[1,512]{1,0:T(1,128)} %bitcast.2, f32[1,512]{1,0:T(1,128)} %bitcast.3, f32[1,128]{1,0:T(1,128)} %reward.1, s32[1,128]{1,0:T(1,128)} %segment.1), custom_call_target="tpu_custom_call" | custom-call | tf_op jit(solution)/shard_map/prep_body/pallas_call | solution.py:55
  2.3 3.1 %collective-permute-start.2 = (bf16[144,512]{1,0:T(8,128)(2,1)}, bf16[144,512]{1,0:T(8,128)(2,1)S(1)}, u32[]{:S(2)}, u32[]{:S(2)}) collective-permute-start(bf16[144,512]{1,0:T(8,128)(2,1)} %prep_body.1), channel_id=1, source_target_pairs={{0,3},{1,2},{2,1},{3,0},{4,7},{5,6},{6,5},{7,4},{8,11},{9,10},{10,... | collective-permute-start | bytes 442376 | tf_op jit(solution)/shard_map/payload_mate/ppermute | solution.py:29
  5.5 6.3 %collective-permute-start.1 = (bf16[64,3696]{1,0:T(8,128)(2,1)}, bf16[64,3696]{1,0:T(8,128)(2,1)S(1)}, u32[]{:S(2)}, u32[]{:S(2)}) collective-permute-start(bf16[64,3696]{1,0:T(8,128)(2,1)} %refs_4_.3), channel_id=1, source_target_pairs={{0,12},{1,13},{2,14},{3,15},{4,0},{5,1},{6,2},{7,3},{8,4},{9,5},{1... | collective-permute-start | bytes 1419272 | tf_op jit(solution)/shard_map/up/ppermute | solution.py:29
  11.8 2.9 %constant_dynamic-slice_fusion = bf16[1856,512]{1,0:T(8,128)(2,1)} fusion(bf16[3696,512]{1,0:T(8,128)(2,1)} %refs_2_.1, s32[]{:T(128)S(6)} %select_n.3), kind=kLoop, calls=%fused_computation.10 | loop fusion | bytes 3801092 | tf_op jit(solution)/shard_map/dynamic_slice | solution.py:381
  14.7 1.1 collective-permute-start.15
  15.8 0.9 collective-permute-start.3
  16.7 6.8 %collective-permute-done.3.other = bf16[144,1024]{1,0:T(8,128)(2,1)S(1)} collective-permute-done((bf16[144,1024]{1,0:T(8,128)(2,1)S(1)}, bf16[144,1024]{1,0:T(8,128)(2,1)S(1)}, u32[]{:S(2)}, u32[]{:S(2)}) %collective-permute-start.3) | collective-permute-done | bytes 294944 | tf_op jit(solution)/shard_map/block_x1/ppermute | solution.py:29
  23.5 0.2 pick_body.1
  23.7 0.6 collective-permute-start.9
  24.3 0.8 copy-done.4
  25.1 1.1 collective-permute-start.5
  26.2 2.5 %collective-permute-done.5 = f32[8,128]{1,0:T(8,128)S(1)} collective-permute-done((f32[8,128]{1,0:T(8,128)S(1)}, f32[8,128]{1,0:T(8,128)S(1)}, u32[]{:S(2)}, u32[]{:S(2)}) %collective-permute-start.5) | collective-permute-done | bytes 4128 | tf_op jit(solution)/shard_map/sums0/ppermute | solution.py:29
  28.7 3.4 %collective-permute-done.1.refs_2_ = bf16[64,3696]{1,0:T(8,128)(2,1)S(1)} collective-permute-done((bf16[64,3696]{1,0:T(8,128)(2,1)}, bf16[64,3696]{1,0:T(8,128)(2,1)S(1)}, u32[]{:S(2)}, u32[]{:S(2)}) %collective-permute-start.1) | collective-permute-done | bytes 473120 | tf_op jit(solution)/shard_map/up/ppermute | solution.py:29
  32.1 3.7 %collective-permute-done.refs_3_ = bf16[64,3696]{1,0:T(8,128)(2,1)S(1)} collective-permute-done((bf16[64,3696]{1,0:T(8,128)(2,1)}, bf16[64,3696]{1,0:T(8,128)(2,1)S(1)}, u32[]{:S(2)}, u32[]{:S(2)}) %collective-permute-start) | collective-permute-done | bytes 473120 | tf_op jit(solution)/shard_map/down/ppermute | solution.py:29
  35.8 0.7 slice.7
  36.5 1.0 collective-permute-start.7
  37.5 2.0 %collective-permute-start.6 = (bf16[32,3696]{1,0:T(8,128)(2,1)S(1)}, bf16[32,3696]{1,0:T(8,128)(2,1)S(1)}, u32[]{:S(2)}, u32[]{:S(2)}) collective-permute-start(bf16[32,3696]{1,0:T(8,128)(2,1)S(1)} %slice.6), channel_id=1, source_target_pairs={{0,4},{1,5},{2,6},{3,7},{4,8},{5,9},{6,10},{7,11},{8,12},{9,13},{1... | collective-permute-start | bytes 709640 | tf_op jit(solution)/shard_map/far_a/ppermute | solution.py:29
  39.5 1.4 copy.11
  40.9 1.8 %collective-permute-start.12 = (bf16[128,3696]{0,1:T(8,128)(2,1)}, bf16[128,3696]{0,1:T(8,128)(2,1)}, u32[]{:S(2)}, u32[]{:S(2)}) collective-permute-start(bf16[128,3696]{0,1:T(8,128)(2,1)} %copy.11), channel_id=1, source_target_pairs={{0,1},{1,0},{2,3},{3,2},{4,5},{5,4},{6,7},{7,6},{8,9},{9,8},{10,11... | collective-permute-start | bytes 2838536 | tf_op jit(solution)/shard_map/y12/ppermute | solution.py:29
  42.8 1.0 constant_dynamic-update-slice_fusion.2.here
  43.7 5.1 %collective-permute-done.7.refs_1_ = bf16[32,3696]{1,0:T(8,128)(2,1)S(1)} collective-permute-done((bf16[32,3696]{1,0:T(8,128)(2,1)}, bf16[32,3696]{1,0:T(8,128)(2,1)S(1)}, u32[]{:S(2)}, u32[]{:S(2)}) %collective-permute-start.7) | collective-permute-done | bytes 236576 | tf_op jit(solution)/shard_map/far_b/ppermute | solution.py:29
  48.8 2.6 %collective-permute-start.10 = (f32[8,128]{1,0:T(8,128)S(1)}, f32[8,128]{1,0:T(8,128)S(1)}, u32[]{:S(2)}, u32[]{:S(2)}) collective-permute-start(f32[8,128]{1,0:T(8,128)S(1)} %add.19), channel_id=1, source_target_pairs={{0,12},{1,13},{2,14},{3,15},{4,8},{5,9},{6,10},{7,11},{8,4},{9,5},... | collective-permute-start | bytes 12296 | tf_op jit(solution)/shard_map/sums2/ppermute | solution.py:29
  51.4 0.8 pad_maximum_fusion.1
  52.2 2.4 %collective-permute-done.10 = f32[8,128]{1,0:T(8,128)S(1)} collective-permute-done((f32[8,128]{1,0:T(8,128)S(1)}, f32[8,128]{1,0:T(8,128)S(1)}, u32[]{:S(2)}, u32[]{:S(2)}) %collective-permute-start.10) | collective-permute-done | bytes 4128 | tf_op jit(solution)/shard_map/sums2/ppermute | solution.py:29
  54.6 1.7 %collective-permute-start.11 = (bf16[64,3696]{1,0:T(8,128)(2,1)}, bf16[64,3696]{1,0:T(8,128)(2,1)}, u32[]{:S(2)}, u32[]{:S(2)}) collective-permute-start(bf16[64,3696]{1,0:T(8,128)(2,1)} %pad_maximum_fusion.1), channel_id=1, source_target_pairs={{0,1},{1,0},{2,3},{3,2},{4,5},{5,4},{6,7},{7,6},{8,9},{9,8},{10,11... | collective-permute-start | bytes 1419272 | tf_op jit(solution)/shard_map/y0/ppermute | solution.py:29
  56.4 0.5 collective-permute-start.14
  56.9 4.4 %collective-permute-done.14 = f32[24,128]{1,0:T(8,128)S(1)} collective-permute-done((f32[24,128]{1,0:T(8,128)S(1)}, f32[24,128]{1,0:T(8,128)S(1)}, u32[]{:S(2)}, u32[]{:S(2)}) %collective-permute-start.14) | collective-permute-done | bytes 12320 | tf_op jit(solution)/shard_map/tiny_x3/ppermute | solution.py:29
  61.3 3.8 %collective-permute-done.16.there = f32[48,128]{1,0:T(8,128)S(1)} collective-permute-done((f32[48,128]{1,0:T(8,128)S(1)}, f32[48,128]{1,0:T(8,128)S(1)}, u32[]{:S(2)}, u32[]{:S(2)}) %collective-permute-start.16) | collective-permute-done | bytes 24608 | tf_op jit(solution)/shard_map/tiny_zlo/ppermute | solution.py:29
  65.8 0.8 coefs_body.1.coefs
  66.6 0.5 collective-permute-start.18
  67.1 1.6 %copy.13.refs_6_ = bf16[128,3696]{1,0:T(8,128)(2,1)S(1)} copy(bf16[128,3696]{0,1:T(8,128)(2,1)} %collective-permute-done.12) | data formatting | bytes 1892352 | tf_op jit(solution)/shard_map/y12/ppermute | solution.py:29
  68.7 2.2 %grad_body.1 = (bf16[256,1024]{1,0:T(8,128)(2,1)S(1)}, bf16[256,1024]{1,0:T(8,128)(2,1)S(1)}) custom-call(f32[8,128]{1,0:T(8,128)S(1)} %coefs_body.1.coefs, bf16[288,1024]{1,0:T(8,128)(2,1)S(1)} %constant_dynamic-update-slice_fusion.2.here, bf16[288,1024]{1,0:T(8,128)(2,1)} %collective-permute-done.17.there), custom_call_target="tpu_custom_call" | custom-call | bytes 4194304 | tf_op jit(solution)/shard_map/grad_body/pallas_call | solution.py:55
  70.9 0.6 collective-permute-done.18.coefs_mate
  71.5 3.3 %collective-permute-done.11.refs_5_ = bf16[64,3696]{1,0:T(8,128)(2,1)} collective-permute-done((bf16[64,3696]{1,0:T(8,128)(2,1)}, bf16[64,3696]{1,0:T(8,128)(2,1)}, u32[]{:S(2)}, u32[]{:S(2)}) %collective-permute-start.11) | collective-permute-done | bytes 473120 | tf_op jit(solution)/shard_map/y0/ppermute | solution.py:29
  74.8 1.0 copy-done.2
  75.8 1.0 copy-done.5
  76.9 3.2 %outer_mate.1 = (bf16[3696,256]{1,0:T(8,128)(2,1)S(1)}, f32[3696,256]{1,0:T(8,128)S(1)}) custom-call(bf16[32,3696]{1,0:T(8,128)(2,1)S(1)} %collective-permute-done.6.refs_0_, bf16[32,3696]{1,0:T(8,128)(2,1)S(1)} %collective-permute-done.7.refs_1_, bf16[64,3696]{1,0:T(8,128)(2,1)S(1)} %collective-permute-done.1.refs_2_, ...), custom_call_target="tpu_custom_call" | custom-call | flops 1937768448 | bytes 8388608 | tf_op jit(solution)/shard_map/outer_mate/pallas_call | solution.py:55
  80.2 7.4 %inner_body.1 = (bf16[64,3696]{1,0:T(8,128)(2,1)S(1)}, bf16[64,3696]{1,0:T(8,128)(2,1)S(1)}, bf16[64,3696]{1,0:T(8,128)(2,1)S(1)}, bf16[64,3696]{1,0:T(8,128)(2,...) custom-call(bf16[256,1024]{1,0:T(8,128)(2,1)S(1)} %get-tuple-element., ...), custom_call_target="tpu_custom_call" | custom-call | flops 3875536896 | bytes 13631488 | tf_op jit(solution)/shard_map/inner_body/pallas_call | solution.py:55
  87.6 0.6 add_convert_fusion.1
  88.2 1.0 collective-permute-start.23
  89.2 0.9 collective-permute-start.20
  90.2 1.1 collective-permute-start.24
  91.3 11.7 %collective-permute-done.20.other = bf16[64,3696]{1,0:T(8,128)(2,1)S(1)} collective-permute-done((bf16[64,3696]{1,0:T(8,128)(2,1)S(1)}, bf16[64,3696]{1,0:T(8,128)(2,1)S(1)}, u32[]{:S(2)}, u32[]{:S(2)}) %collective-permute-start.20) | collective-permute-done | bytes 473120 | tf_op jit(solution)/shard_map/t0/ppermute | solution.py:29
  103.0 2.2 %collective-permute-start.26 = (bf16[32,3696]{1,0:T(8,128)(2,1)S(1)}, bf16[32,3696]{1,0:T(8,128)(2,1)S(1)}, u32[]{:S(2)}, u32[]{:S(2)}) collective-permute-start(bf16[32,3696]{1,0:T(8,128)(2,1)S(1)} %get-tuple-element.75), channel_id=1, source_target_pairs={{0,12},{1,13},{2,14},{3,15},{4,0},{5,1},{6,2},{7,3},{8,4},{9,5},{1... | collective-permute-start | bytes 709640 | tf_op jit(solution)/shard_map/from_up/ppermute | solution.py:29
  105.3 2.0 %collective-permute-start.25 = (bf16[32,3696]{1,0:T(8,128)(2,1)S(1)}, bf16[32,3696]{1,0:T(8,128)(2,1)S(1)}, u32[]{:S(2)}, u32[]{:S(2)}) collective-permute-start(bf16[32,3696]{1,0:T(8,128)(2,1)S(1)} %get-tuple-element.69), channel_id=1, source_target_pairs={{0,4},{1,5},{2,6},{3,7},{4,8},{5,9},{6,10},{7,11},{8,12},{9,13},{1... | collective-permute-start | bytes 709640 | tf_op jit(solution)/shard_map/from_down/ppermute | solution.py:29
  107.3 0.9 collective-permute-start.22
  108.2 3.2 %outer_own.1.partial = f32[3696,512]{1,0:T(8,128)S(1)} custom-call(bf16[32,3696]{1,0:T(8,128)(2,1)S(1)} %collective-permute-done.6.refs_0_, bf16[32,3696]{1,0:T(8,128)(2,1)S(1)} %collective-permute-done.7.refs_1_, bf16[64,3696]{1,0:T(8,128)(2,1)S(1)} %collective-permute-done.1.refs_2_, bf16[64,3696]{1,0:T(8,128)(2,1)S(1)} %collective-permute-done.refs_3_, ...), custom_call_target="tpu_custom_call" | custom-call | flops 1937768448 | bytes 8388608 | tf_op jit(solution)/shard_map/outer_own/pallas_call | solution.py:55
  111.5 1.7 %collective-permute-done.24.other = bf16[64,3696]{1,0:T(8,128)(2,1)S(1)} collective-permute-done((bf16[64,3696]{1,0:T(8,128)(2,1)S(1)}, bf16[64,3696]{1,0:T(8,128)(2,1)S(1)}, u32[]{:S(2)}, u32[]{:S(2)}) %collective-permute-start.24) | collective-permute-done | bytes 473120 | tf_op jit(solution)/shard_map/t1/ppermute | solution.py:29
  113.1 3.8 %collective-permute-done.26.refs_1_ = bf16[32,3696]{1,0:T(8,128)(2,1)S(1)} collective-permute-done((bf16[32,3696]{1,0:T(8,128)(2,1)S(1)}, bf16[32,3696]{1,0:T(8,128)(2,1)S(1)}, u32[]{:S(2)}, u32[]{:S(2)}) %collective-permute-start.26) | collective-permute-done | bytes 236576 | tf_op jit(solution)/shard_map/from_up/ppermute | solution.py:29
  117.1 3.9 %collective-permute-start.28 = (bf16[32,3696]{1,0:T(8,128)(2,1)S(1)}, bf16[32,3696]{1,0:T(8,128)(2,1)S(1)}, u32[]{:S(2)}, u32[]{:S(2)}) collective-permute-start(bf16[32,3696]{1,0:T(8,128)(2,1)S(1)} %get-tuple-element.78), channel_id=1, source_target_pairs={{0,4},{1,5},{2,6},{3,7},{4,8},{5,9},{6,10},{7,11},{8,12},{9,13},{1... | collective-permute-start | bytes 709640 | tf_op jit(solution)/shard_map/pure_b/ppermute | solution.py:29
  121.0 0.9 own_grad_body.1
  121.9 0.7 collective-permute-done.22.other
  122.6 7.5 %collective-permute-done.27.pure_a = bf16[32,3696]{1,0:T(8,128)(2,1)S(1)} collective-permute-done((bf16[32,3696]{1,0:T(8,128)(2,1)S(1)}, bf16[32,3696]{1,0:T(8,128)(2,1)S(1)}, u32[]{:S(2)}, u32[]{:S(2)}) %collective-permute-start.27) | collective-permute-done | bytes 236576 | tf_op jit(solution)/shard_map/pure_a/ppermute | solution.py:29
  130.1 3.5 %collective-permute-done.28.pure_b = bf16[32,3696]{1,0:T(8,128)(2,1)S(1)} collective-permute-done((bf16[32,3696]{1,0:T(8,128)(2,1)S(1)}, bf16[32,3696]{1,0:T(8,128)(2,1)S(1)}, u32[]{:S(2)}, u32[]{:S(2)}) %collective-permute-start.28) | collective-permute-done | bytes 236576 | tf_op jit(solution)/shard_map/pure_b/ppermute | solution.py:29
  133.6 0.2 fold_body.5
  133.8 0.6 merge_body.1
  134.5 1.6 %collective-permute-start.30 = (bf16[64,3696]{1,0:T(8,128)(2,1)S(1)}, bf16[64,3696]{1,0:T(8,128)(2,1)S(1)}, u32[]{:S(2)}, u32[]{:S(2)}) collective-permute-start(bf16[64,3696]{1,0:T(8,128)(2,1)S(1)} %get-tuple-element.85), channel_id=1, source_target_pairs={{0,1},{1,0},{2,3},{3,2},{4,5},{5,4},{6,7},{7,6},{8,9},{9,8},{10,11... | collective-permute-start | bytes 1419272 | tf_op jit(solution)/shard_map/t3/ppermute | solution.py:29
  136.1 2.7 %collective-permute-start.31 = (bf16[32,3696]{1,0:T(8,128)(2,1)S(1)}, bf16[32,3696]{1,0:T(8,128)(2,1)S(1)}, u32[]{:S(2)}, u32[]{:S(2)}) collective-permute-start(bf16[32,3696]{1,0:T(8,128)(2,1)S(1)} %get-tuple-element.81), channel_id=1, source_target_pairs={{0,4},{1,5},{2,6},{3,7},{4,8},{5,9},{6,10},{7,11},{8,12},{9,13},{1... | collective-permute-start | bytes 709640 | tf_op jit(solution)/shard_map/mixed_a/ppermute | solution.py:29
  138.8 1.5 collective-permute-start.32
  140.2 0.8 collective-permute-done.29
  141.1 3.0 %add_convert_fusion = bf16[3696,512]{1,0:T(8,128)(2,1)} fusion(bf16[3696,512]{1,0:T(8,128)(2,1)S(1)} %collective-permute-done.29, bf16[3696,512]{1,0:T(8,128)(2,1)S(1)} %merge_body.1), kind=kLoop, calls=%fused_computation | loop fusion | flops 7569408 | bytes 11354112 | tf_op jit(solution)/shard_map/convert_element_type | solution.py:462
  144.0 3.8 %collective-permute-done.30.other = bf16[64,3696]{1,0:T(8,128)(2,1)S(1)} collective-permute-done((bf16[64,3696]{1,0:T(8,128)(2,1)S(1)}, bf16[64,3696]{1,0:T(8,128)(2,1)S(1)}, u32[]{:S(2)}, u32[]{:S(2)}) %collective-permute-start.30) | collective-permute-done | bytes 473120 | tf_op jit(solution)/shard_map/t3/ppermute | solution.py:29
  147.8 4.5 %collective-permute-done.32.mixed_b = bf16[32,3696]{1,0:T(8,128)(2,1)S(1)} collective-permute-done((bf16[32,3696]{1,0:T(8,128)(2,1)S(1)}, bf16[32,3696]{1,0:T(8,128)(2,1)S(1)}, u32[]{:S(2)}, u32[]{:S(2)}) %collective-permute-start.32) | collective-permute-done | bytes 236576 | tf_op jit(solution)/shard_map/mixed_b/ppermute | solution.py:29
  152.3 1.0 here_body.1
  (49 shorter events, 0.8 us)
Async XLA Ops:
  2.3 13.5 %copy-start.7 = (bf16[144,512]{1,0:T(8,128)(2,1)S(1)}, bf16[144,512]{1,0:T(8,128)(2,1)}, u32[]{:S(2)}) copy-start(bf16[144,512]{1,0:T(8,128)(2,1)} %prep_body.1) | copy-start | bytes 442372
  2.3 12.4 %collective-permute-start.2 = (bf16[144,512]{1,0:T(8,128)(2,1)}, bf16[144,512]{1,0:T(8,128)(2,1)S(1)}, u32[]{:S(2)}, u32[]{:S(2)}) collective-permute-start(bf16[144,512]{1,0:T(8,128)(2,1)} %prep_body.1), channel_id=1, source_target_pairs={{0,3},{1,2},{2,1},{3,0},{4,7},{5,6},{6,5},{7,4},{8,11},{9,10},{10,... | collective-permute-start | bytes 442376 | tf_op jit(solution)/shard_map/payload_mate/ppermute | solution.py:29
  5.4 18.9 %collective-permute-start.4 = (bf16[64,3696]{1,0:T(8,128)(2,1)}, bf16[64,3696]{1,0:T(8,128)(2,1)S(1)}, u32[]{:S(2)}, u32[]{:S(2)}) collective-permute-start(bf16[64,3696]{1,0:T(8,128)(2,1)} %refs_4_.3), channel_id=1, source_target_pairs={{0,1},{1,0},{2,3},{3,2},{4,5},{5,4},{6,7},{7,6},{8,9},{9,8},{10,11... | collective-permute-start | bytes 1419272 | tf_op jit(solution)/shard_map/y3/ppermute | solution.py:29
  5.5 26.5 %collective-permute-start.1 = (bf16[64,3696]{1,0:T(8,128)(2,1)}, bf16[64,3696]{1,0:T(8,128)(2,1)S(1)}, u32[]{:S(2)}, u32[]{:S(2)}) collective-permute-start(bf16[64,3696]{1,0:T(8,128)(2,1)} %refs_4_.3), channel_id=1, source_target_pairs={{0,12},{1,13},{2,14},{3,15},{4,0},{5,1},{6,2},{7,3},{8,4},{9,5},{1... | collective-permute-start | bytes 1419272 | tf_op jit(solution)/shard_map/up/ppermute | solution.py:29
  11.8 24.0 %collective-permute-start = (bf16[64,3696]{1,0:T(8,128)(2,1)}, bf16[64,3696]{1,0:T(8,128)(2,1)S(1)}, u32[]{:S(2)}, u32[]{:S(2)}) collective-permute-start(bf16[64,3696]{1,0:T(8,128)(2,1)} %refs_4_.3), channel_id=1, source_target_pairs={{0,4},{1,5},{2,6},{3,7},{4,8},{5,9},{6,10},{7,11},{8,12},{9,13},{1... | collective-permute-start | bytes 1419272 | tf_op jit(solution)/shard_map/down/ppermute | solution.py:29
  14.7 50.4 %collective-permute-start.15 = (bf16[1856,512]{1,0:T(8,128)(2,1)}, bf16[1856,512]{1,0:T(8,128)(2,1)}, u32[]{:S(2)}, u32[]{:S(2)}) collective-permute-start(bf16[1856,512]{1,0:T(8,128)(2,1)} %constant_dynamic-slice_fusion), channel_id=1, source_target_pairs={{0,3},{1,2},{2,1},{3,0},{4,7},{5,6},{6,5},{7,4},{8,11},{9,10},{10,... | collective-permute-start | bytes 5701640 | tf_op jit(solution)/shard_map/got/ppermute | solution.py:29
  15.8 7.7 %collective-permute-start.3 = (bf16[144,1024]{1,0:T(8,128)(2,1)S(1)}, bf16[144,1024]{1,0:T(8,128)(2,1)S(1)}, u32[]{:S(2)}, u32[]{:S(2)}) collective-permute-start(bf16[144,1024]{1,0:T(8,128)(2,1)S(1)} %pad_maximum_fusion.2.own), channel_id=1, source_target_pairs={{0,16},{16,0},{32,48},{48,32},{64,80},{80,64},{96,112},{112,96},{1... | collective-permute-start | bytes 884744 | tf_op jit(solution)/shard_map/block_x1/ppermute | solution.py:29
  23.7 17.2 %collective-permute-start.9 = (bf16[144,1024]{1,0:T(8,128)(2,1)S(1)}, bf16[144,1024]{1,0:T(8,128)(2,1)}, u32[]{:S(2)}, u32[]{:S(2)}) collective-permute-start(bf16[144,1024]{1,0:T(8,128)(2,1)S(1)} %get-tuple-element.51.block), channel_id=1, source_target_pairs={{0,48},{16,32},{32,16},{48,0},{64,112},{80,96},{96,80},{112,64},{1... | collective-permute-start | bytes 884744 | tf_op jit(solution)/shard_map/block_x3/ppermute | solution.py:29
  24.3 0.8 copy-start.4
  25.1 3.6 %collective-permute-start.5 = (f32[8,128]{1,0:T(8,128)S(1)}, f32[8,128]{1,0:T(8,128)S(1)}, u32[]{:S(2)}, u32[]{:S(2)}) collective-permute-start(f32[8,128]{1,0:T(8,128)S(1)} %get-tuple-element.47), channel_id=1, source_target_pairs={{0,1},{1,0},{2,3},{3,2},{4,5},{5,4},{6,7},{7,6},{8,9},{9,8},{10,11... | collective-permute-start | bytes 12296 | tf_op jit(solution)/shard_map/sums0/ppermute | solution.py:29
  35.8 5.1 %collective-permute-start.8 = (f32[8,128]{1,0:T(8,128)S(1)}, f32[8,128]{1,0:T(8,128)S(1)}, u32[]{:S(2)}, u32[]{:S(2)}) collective-permute-start(f32[8,128]{1,0:T(8,128)S(1)} %add.18), channel_id=1, source_target_pairs={{0,4},{1,5},{2,6},{3,7},{4,0},{5,1},{6,2},{7,3},{8,12},{9,13},{10,... | collective-permute-start | bytes 12296 | tf_op jit(solution)/shard_map/sums1/ppermute | solution.py:29
  36.5 12.3 %collective-permute-start.7 = (bf16[32,3696]{1,0:T(8,128)(2,1)}, bf16[32,3696]{1,0:T(8,128)(2,1)S(1)}, u32[]{:S(2)}, u32[]{:S(2)}) collective-permute-start(bf16[32,3696]{1,0:T(8,128)(2,1)} %slice.7), channel_id=1, source_target_pairs={{0,12},{1,13},{2,14},{3,15},{4,0},{5,1},{6,2},{7,3},{8,4},{9,5},{1... | collective-permute-start | bytes 709640 | tf_op jit(solution)/shard_map/far_b/ppermute | solution.py:29
  37.5 13.9 %collective-permute-start.6 = (bf16[32,3696]{1,0:T(8,128)(2,1)S(1)}, bf16[32,3696]{1,0:T(8,128)(2,1)S(1)}, u32[]{:S(2)}, u32[]{:S(2)}) collective-permute-start(bf16[32,3696]{1,0:T(8,128)(2,1)S(1)} %slice.6), channel_id=1, source_target_pairs={{0,4},{1,5},{2,6},{3,7},{4,8},{5,9},{6,10},{7,11},{8,12},{9,13},{1... | collective-permute-start | bytes 709640 | tf_op jit(solution)/shard_map/far_a/ppermute | solution.py:29
  40.9 15.5 %collective-permute-start.13 = (f32[8,128]{1,0:T(8,128)S(1)}, f32[8,128]{1,0:T(8,128)S(1)}, u32[]{:S(2)}, u32[]{:S(2)}) collective-permute-start(f32[8,128]{1,0:T(8,128)S(1)} %get-tuple-element.54), channel_id=1, source_target_pairs={{0,128},{128,0},{1,129},{129,1},{2,130},{130,2},{3,131},{131,3},{4... | collective-permute-start | bytes 12296 | tf_op jit(solution)/shard_map/owed_other/ppermute | solution.py:29
  40.9 26.1 %collective-permute-start.12 = (bf16[128,3696]{0,1:T(8,128)(2,1)}, bf16[128,3696]{0,1:T(8,128)(2,1)}, u32[]{:S(2)}, u32[]{:S(2)}) collective-permute-start(bf16[128,3696]{0,1:T(8,128)(2,1)} %copy.11), channel_id=1, source_target_pairs={{0,1},{1,0},{2,3},{3,2},{4,5},{5,4},{6,7},{7,6},{8,9},{9,8},{10,11... | collective-permute-start | bytes 2838536 | tf_op jit(solution)/shard_map/y12/ppermute | solution.py:29
  48.8 5.8 %collective-permute-start.10 = (f32[8,128]{1,0:T(8,128)S(1)}, f32[8,128]{1,0:T(8,128)S(1)}, u32[]{:S(2)}, u32[]{:S(2)}) collective-permute-start(f32[8,128]{1,0:T(8,128)S(1)} %add.19), channel_id=1, source_target_pairs={{0,12},{1,13},{2,14},{3,15},{4,8},{5,9},{6,10},{7,11},{8,4},{9,5},... | collective-permute-start | bytes 12296 | tf_op jit(solution)/shard_map/sums2/ppermute | solution.py:29
  51.4 17.3 %collective-permute-start.17 = (bf16[288,1024]{1,0:T(8,128)(2,1)S(1)}, bf16[288,1024]{1,0:T(8,128)(2,1)}, u32[]{:S(2)}, u32[]{:S(2)}) collective-permute-start(bf16[288,1024]{1,0:T(8,128)(2,1)S(1)} %constant_dynamic-update-slice_fusion.2.here), channel_id=1, source_target_pairs={{0,64},{16,80},{32,96},{48,112},{64,0},{80,16},{96,32},{112,48},{1... | collective-permute-start | bytes 1769480 | tf_op jit(solution)/shard_map/block_zlo/ppermute | solution.py:29
  54.6 20.2 %collective-permute-start.11 = (bf16[64,3696]{1,0:T(8,128)(2,1)}, bf16[64,3696]{1,0:T(8,128)(2,1)}, u32[]{:S(2)}, u32[]{:S(2)}) collective-permute-start(bf16[64,3696]{1,0:T(8,128)(2,1)} %pad_maximum_fusion.1), channel_id=1, source_target_pairs={{0,1},{1,0},{2,3},{3,2},{4,5},{5,4},{6,7},{7,6},{8,9},{9,8},{10,11... | collective-permute-start | bytes 1419272 | tf_op jit(solution)/shard_map/y0/ppermute | solution.py:29
  56.4 4.9 %collective-permute-start.14 = (f32[24,128]{1,0:T(8,128)S(1)}, f32[24,128]{1,0:T(8,128)S(1)}, u32[]{:S(2)}, u32[]{:S(2)}) collective-permute-start(f32[24,128]{1,0:T(8,128)S(1)} %pad_maximum_fusion.3), channel_id=1, source_target_pairs={{0,48},{16,32},{32,16},{48,0},{64,112},{80,96},{96,80},{112,64},{1... | collective-permute-start | bytes 36872 | tf_op jit(solution)/shard_map/tiny_x3/ppermute | solution.py:29
  61.3 3.8 %collective-permute-start.16 = (f32[48,128]{1,0:T(8,128)S(1)}, f32[48,128]{1,0:T(8,128)S(1)}, u32[]{:S(2)}, u32[]{:S(2)}) collective-permute-start(f32[48,128]{1,0:T(8,128)S(1)} %constant_dynamic-update-slice_fusion.here), channel_id=1, source_target_pairs={{0,64},{16,80},{32,96},{48,112},{64,0},{80,16},{96,32},{112,48},{1... | collective-permute-start | bytes 73736 | tf_op jit(solution)/shard_map/tiny_zlo/ppermute | solution.py:29
  65.1 15.1 %collective-permute-start.19 = (bf16[1856,512]{1,0:T(8,128)(2,1)}, bf16[1856,512]{1,0:T(8,128)(2,1)}, u32[]{:S(2)}, u32[]{:S(2)}) collective-permute-start(bf16[1856,512]{1,0:T(8,128)(2,1)} %collective-permute-done.15.refs_3_), channel_id=1, source_target_pairs={{0,128},{128,0},{1,129},{129,1},{2,130},{130,2},{3,131},{131,3},{4... | collective-permute-start | bytes 5701640 | tf_op jit(solution)/shard_map/got_other/ppermute | solution.py:29
  66.6 4.9 %collective-permute-start.18 = (f32[8,128]{1,0:T(8,128)S(1)}, f32[8,128]{1,0:T(8,128)S(1)}, u32[]{:S(2)}, u32[]{:S(2)}) collective-permute-start(f32[8,128]{1,0:T(8,128)S(1)} %coefs_body.1.coefs), channel_id=1, source_target_pairs={{0,3},{1,2},{2,1},{3,0},{4,7},{5,6},{6,5},{7,4},{8,11},{9,10},{10,... | collective-permute-start | bytes 12296 | tf_op jit(solution)/shard_map/coefs_mate/ppermute | solution.py:29
  70.9 9.3 %copy-start = (bf16[3696,512]{1,0:T(8,128)(2,1)S(1)}, bf16[3696,512]{1,0:T(8,128)(2,1)}, u32[]{:S(2)}) copy-start(bf16[3696,512]{1,0:T(8,128)(2,1)} %refs_2_.1) | copy-start | bytes 11354116
  74.8 1.0 copy-start.2
  75.8 1.0 copy-start.5
  80.1 7.5 %collective-permute-start.21 = (bf16[3696,256]{1,0:T(8,128)(2,1)S(1)}, bf16[3696,256]{1,0:T(8,128)(2,1)S(1)}, u32[]{:S(2)}, u32[]{:S(2)}) collective-permute-start(bf16[3696,256]{1,0:T(8,128)(2,1)S(1)} %get-tuple-element.67), channel_id=1, source_target_pairs={{0,128},{128,0},{1,129},{129,1},{2,130},{130,2},{3,131},{131,3},{4... | collective-permute-start | bytes 5677064 | tf_op jit(solution)/shard_map/mate_got/ppermute | solution.py:29
  87.6 20.6 %copy-start.3 = (bf16[64,3696]{1,0:T(8,128)(2,1)S(1)}, bf16[64,3696]{1,0:T(8,128)(2,1)}, u32[]{:S(2)}) copy-start(bf16[64,3696]{1,0:T(8,128)(2,1)} %refs_4_.3) | copy-start | bytes 1419268
  87.6 20.6 %copy-start.6 = (bf16[64,3696]{1,0:T(8,128)(2,1)S(1)}, bf16[64,3696]{1,0:T(8,128)(2,1)}, u32[]{:S(2)}) copy-start(bf16[64,3696]{1,0:T(8,128)(2,1)} %copy-done.4) | copy-start | bytes 1419268
  88.2 45.4 %collective-permute-start.23 = (bf16[3696,256]{1,0:T(8,128)(2,1)S(1)}, bf16[3696,256]{1,0:T(8,128)(2,1)S(1)}, u32[]{:S(2)}, u32[]{:S(2)}) collective-permute-start(bf16[3696,256]{1,0:T(8,128)(2,1)S(1)} %add_convert_fusion.1), channel_id=1, source_target_pairs={{0,3},{1,2},{2,1},{3,0},{4,7},{5,6},{6,5},{7,4},{8,11},{9,10},{10,... | collective-permute-start | bytes 5677064 | tf_op jit(solution)/shard_map/w_recv/ppermute | solution.py:29
  89.2 13.7 %collective-permute-start.20 = (bf16[64,3696]{1,0:T(8,128)(2,1)S(1)}, bf16[64,3696]{1,0:T(8,128)(2,1)S(1)}, u32[]{:S(2)}, u32[]{:S(2)}) collective-permute-start(bf16[64,3696]{1,0:T(8,128)(2,1)S(1)} %get-tuple-element.65), channel_id=1, source_target_pairs={{0,1},{1,0},{2,3},{3,2},{4,5},{5,4},{6,7},{7,6},{8,9},{9,8},{10,11... | collective-permute-start | bytes 1419272 | tf_op jit(solution)/shard_map/t0/ppermute | solution.py:29
  90.2 23.0 %collective-permute-start.24 = (bf16[64,3696]{1,0:T(8,128)(2,1)S(1)}, bf16[64,3696]{1,0:T(8,128)(2,1)S(1)}, u32[]{:S(2)}, u32[]{:S(2)}) collective-permute-start(bf16[64,3696]{1,0:T(8,128)(2,1)S(1)} %get-tuple-element.74), channel_id=1, source_target_pairs={{0,1},{1,0},{2,3},{3,2},{4,5},{5,4},{6,7},{7,6},{8,9},{9,8},{10,11... | collective-permute-start | bytes 1419272 | tf_op jit(solution)/shard_map/t1/ppermute | solution.py:29
  103.0 13.9 %collective-permute-start.26 = (bf16[32,3696]{1,0:T(8,128)(2,1)S(1)}, bf16[32,3696]{1,0:T(8,128)(2,1)S(1)}, u32[]{:S(2)}, u32[]{:S(2)}) collective-permute-start(bf16[32,3696]{1,0:T(8,128)(2,1)S(1)} %get-tuple-element.75), channel_id=1, source_target_pairs={{0,12},{1,13},{2,14},{3,15},{4,0},{5,1},{6,2},{7,3},{8,4},{9,5},{1... | collective-permute-start | bytes 709640 | tf_op jit(solution)/shard_map/from_up/ppermute | solution.py:29
  105.3 11.7 %collective-permute-start.25 = (bf16[32,3696]{1,0:T(8,128)(2,1)S(1)}, bf16[32,3696]{1,0:T(8,128)(2,1)S(1)}, u32[]{:S(2)}, u32[]{:S(2)}) collective-permute-start(bf16[32,3696]{1,0:T(8,128)(2,1)S(1)} %get-tuple-element.69), channel_id=1, source_target_pairs={{0,4},{1,5},{2,6},{3,7},{4,8},{5,9},{6,10},{7,11},{8,12},{9,13},{1... | collective-permute-start | bytes 709640 | tf_op jit(solution)/shard_map/from_down/ppermute | solution.py:29
  107.3 13.7 %copy-start.1 = (bf16[128,512]{1,0:T(8,128)(2,1)S(1)}, bf16[128,512]{1,0:T(8,128)(2,1)}, u32[]{:S(2)}) copy-start(bf16[128,512]{1,0:T(8,128)(2,1)} %stream.2) | copy-start | bytes 393220
  107.3 15.2 %collective-permute-start.22 = (bf16[64,3696]{1,0:T(8,128)(2,1)S(1)}, bf16[64,3696]{1,0:T(8,128)(2,1)S(1)}, u32[]{:S(2)}, u32[]{:S(2)}) collective-permute-start(bf16[64,3696]{1,0:T(8,128)(2,1)S(1)} %get-tuple-element.72), channel_id=1, source_target_pairs={{0,1},{1,0},{2,3},{3,2},{4,5},{5,4},{6,7},{7,6},{8,9},{9,8},{10,11... | collective-permute-start | bytes 1419272 | tf_op jit(solution)/shard_map/t2/ppermute | solution.py:29
  117.0 13.1 %collective-permute-start.27 = (bf16[32,3696]{1,0:T(8,128)(2,1)S(1)}, bf16[32,3696]{1,0:T(8,128)(2,1)S(1)}, u32[]{:S(2)}, u32[]{:S(2)}) collective-permute-start(bf16[32,3696]{1,0:T(8,128)(2,1)S(1)} %get-tuple-element.77), channel_id=1, source_target_pairs={{0,12},{1,13},{2,14},{3,15},{4,0},{5,1},{6,2},{7,3},{8,4},{9,5},{1... | collective-permute-start | bytes 709640 | tf_op jit(solution)/shard_map/pure_a/ppermute | solution.py:29
  117.1 16.5 %collective-permute-start.28 = (bf16[32,3696]{1,0:T(8,128)(2,1)S(1)}, bf16[32,3696]{1,0:T(8,128)(2,1)S(1)}, u32[]{:S(2)}, u32[]{:S(2)}) collective-permute-start(bf16[32,3696]{1,0:T(8,128)(2,1)S(1)} %get-tuple-element.78), channel_id=1, source_target_pairs={{0,4},{1,5},{2,6},{3,7},{4,8},{5,9},{6,10},{7,11},{8,12},{9,13},{1... | collective-permute-start | bytes 709640 | tf_op jit(solution)/shard_map/pure_b/ppermute | solution.py:29
  134.4 6.7 %collective-permute-start.29 = (bf16[3696,512]{1,0:T(8,128)(2,1)S(1)}, bf16[3696,512]{1,0:T(8,128)(2,1)S(1)}, u32[]{:S(2)}, u32[]{:S(2)}) collective-permute-start(bf16[3696,512]{1,0:T(8,128)(2,1)S(1)} %merge_body.1), channel_id=1, source_target_pairs={{0,128},{128,0},{1,129},{129,1},{2,130},{130,2},{3,131},{131,3},{4... | collective-permute-start | bytes 11354120 | tf_op jit(solution)/shard_map/part/ppermute | solution.py:29
  134.5 13.3 %collective-permute-start.30 = (bf16[64,3696]{1,0:T(8,128)(2,1)S(1)}, bf16[64,3696]{1,0:T(8,128)(2,1)S(1)}, u32[]{:S(2)}, u32[]{:S(2)}) collective-permute-start(bf16[64,3696]{1,0:T(8,128)(2,1)S(1)} %get-tuple-element.85), channel_id=1, source_target_pairs={{0,1},{1,0},{2,3},{3,2},{4,5},{5,4},{6,7},{7,6},{8,9},{9,8},{10,11... | collective-permute-start | bytes 1419272 | tf_op jit(solution)/shard_map/t3/ppermute | solution.py:29
  136.1 16.2 %collective-permute-start.31 = (bf16[32,3696]{1,0:T(8,128)(2,1)S(1)}, bf16[32,3696]{1,0:T(8,128)(2,1)S(1)}, u32[]{:S(2)}, u32[]{:S(2)}) collective-permute-start(bf16[32,3696]{1,0:T(8,128)(2,1)S(1)} %get-tuple-element.81), channel_id=1, source_target_pairs={{0,4},{1,5},{2,6},{3,7},{4,8},{5,9},{6,10},{7,11},{8,12},{9,13},{1... | collective-permute-start | bytes 709640 | tf_op jit(solution)/shard_map/mixed_a/ppermute | solution.py:29
  138.8 13.5 %collective-permute-start.32 = (bf16[32,3696]{1,0:T(8,128)(2,1)S(1)}, bf16[32,3696]{1,0:T(8,128)(2,1)S(1)}, u32[]{:S(2)}, u32[]{:S(2)}) collective-permute-start(bf16[32,3696]{1,0:T(8,128)(2,1)S(1)} %get-tuple-element.86), channel_id=1, source_target_pairs={{0,12},{1,13},{2,14},{3,15},{4,0},{5,1},{6,2},{7,3},{8,4},{9,5},{1... | collective-permute-start | bytes 709640 | tf_op jit(solution)/shard_map/mixed_b/ppermute | solution.py:29

commit v5 on v4

--- a/solution.py
+++ b/solution.py
@@ -67,7 +67,7 @@
     return r % 4, r // 4, c % 4, c // 4
 
 
-def prep_body(stream, gain, head, reward, segment, out, s_v, g_v, h_v, r_v, i_v, sems):
+def prep_body(stream, gain, head, reward, segment, out, owed, s_v, g_v, h_v, r_v, i_v, sems):
     moves = [
         pltpu.make_async_copy(src, dst, sems.at[i])
         for i, (src, dst) in enumerate(
@@ -92,6 +92,20 @@
     for i, a in enumerate(rows):
         extra = jnp.where(line == i, jnp.broadcast_to(a, (16, 512)), extra)
     out[128:144] = extra.astype(bf16)
+    owed[...] = jnp.zeros(owed.shape, f32)
+    for i, a in enumerate(rows[3:]):
+        for j in range(4):
+            owed[4 * i + j : 4 * i + j + 1] = a[:, 128 * j : 128 * j + 128]
+
+
+def wide_body(own, mate, owed, out):
+    out[:, :512] = own[...]
+    out[:, 512:] = mate[...]
+    extra = own[128:144].astype(f32)
+    theirs = jnp.concatenate([owed[i : i + 1] for i in range(4)], 1)
+    line = lax.broadcasted_iota(jnp.int32, extra.shape, 0)
+    extra = jnp.where(line == 4, jnp.broadcast_to(theirs, extra.shape), extra)
+    out[128:144, :512] = extra.astype(bf16)
 
 
 def pick_body(own, other, out, sums, owed):
@@ -109,10 +123,10 @@
     even = lax.rem(x, 2) == 0
     first = jnp.where(even, mine, theirs)
     second = jnp.where(even, theirs, mine)
-    for i, a in enumerate((first[3:4], second[3:4])):
-        owed[i : i + 1] = a[:, 0:128] + a[:, 128:256] + a[:, 256:384]
-        owed[2 + i : 3 + i] = a[:, 384:512]
-    owed[4:8] = jnp.zeros((4, 128), f32)
+    for i, a in enumerate((first[3:4], second[3:4], first[4:5], second[4:5])):
+        at = (0, 1, 4, 5)[i]
+        owed[at : at + 1] = a[:, 0:128] + a[:, 128:256] + a[:, 256:384]
+        owed[2 + at : 3 + at] = a[:, 384:512]
     out[128:144] = mine.astype(bf16)
     gw = gains_of(own)
 
@@ -135,7 +149,7 @@
     x, zlo, y, _ = place()
 
     def side(src, at):
-        near, away = src[at : at + 2], src[24 + at : 26 + at]
+        near, away = src[at : at + 2], src[16 + at : 18 + at]
         low, high = jnp.where(x // 2 == 0, near, away), jnp.where(x // 2 == 0, away, near)
         return jnp.concatenate([low, high], 0)
 
@@ -143,8 +157,8 @@
         mine, theirs = side(here, at), side(there, at)
         return jnp.where(zlo == 0, mine, theirs), jnp.where(zlo == 0, theirs, mine)
 
-    value = jnp.concatenate([*rows(8), *rows(16)], 0)
-    segment = jnp.concatenate([*rows(10), *rows(18)], 0)
+    value = jnp.concatenate([*rows(8), *rows(12)], 0)
+    segment = jnp.concatenate([*rows(10), *rows(14)], 0)
     shape = value.shape
     line = lax.broadcasted_iota(jnp.int32, shape, 0) % 8
     lane = lax.broadcasted_iota(jnp.int32, shape, 1)
@@ -172,7 +186,7 @@
         b = x // 2 if i % 2 == 0 else 1 - x // 2
         wanted.append(target[pl.ds(4 * zl + 2 * b + y // 2, 1)])
         src = (here, there)[i // 2]
-        at = 24 * (i % 2)
+        at = 16 * (i % 2)
         sq.append(src[at : at + 1])
         lin.append(src[at + 1 : at + 2])
     wanted, sq, lin = (jnp.concatenate(a, 0) for a in (wanted, sq, lin))
@@ -233,10 +247,8 @@
 CHUNKS = ((0, 1024), (1024, 2048), (2048, 3072), (3072, 3696))
 HIGH = 3696 - LO
 SPANS = ((0, LO), (LO, 3696))
-PARTS = ((0, 64), (64, 128), (128, 192), (192, 256))
-def inner_body(*refs):
-    g_own, g_other, w, got, other = refs[:5]
-    sent, own, (w_v, m_v, sems) = refs[5:9], refs[9:13], refs[13:]
+def inner_body(g, w, got, other, *refs):
+    out, (w_v, m_v, sems) = refs[:4], refs[4:]
     p = lax.axis_index("dp")
     for i, (a, b) in enumerate(CHUNKS):
         pltpu.make_async_copy(w.at[a:b], w_v.at[a:b], sems.at[i]).start()
@@ -256,8 +268,7 @@
         for j in range(2):
             mate_copy(j, other, got).start()
 
-    left = jnp.concatenate([g_other[:, :512], g_own[:, :512]], 0)
-    right = jnp.concatenate([g_other[:, 512:], g_own[:, 512:]], 0)
+    left, right = g[:, :512], g[:, 512:]
     nt = (((1,), (1,)), ((), ()))
     waits = ((0,), (1,), (), ())
     for i, (a, b) in enumerate(CHUNKS):
@@ -266,11 +277,29 @@
             mate_copy(j, other, other).wait()
         for f in range(a, b, 512):
             e = min(f + 512, b)
-            out = lax.dot_general(left, w_v[f:e], nt, preferred_element_type=f32)
-            out = out + lax.dot_general(right, m_v[f:e], nt, preferred_element_type=f32)
-            for n, (low, high) in enumerate(PARTS):
-                sent[n][:, f:e] = out[low:high].astype(bf16)
-                own[n][:, f:e] = out[256 + low : 256 + high]
+            made = lax.dot_general(left, w_v[f:e], nt, preferred_element_type=f32)
+            made = made + lax.dot_general(right, m_v[f:e], nt, preferred_element_type=f32)
+            for n, o in enumerate(out):
+                o[:, f:e] = made[64 * n : 64 * n + 64].astype(o.dtype)
+
+
+def inner(g, w, got, other, dtype, name):
+    hbm = pl.BlockSpec(memory_space=pl.ANY)
+    return call(
+        inner_body,
+        [sds((64, 3696), dtype)] * 4,
+        (g, w, got, other),
+        in_specs=[pl.BlockSpec(memory_space=pltpu.VMEM)] + [hbm] * 3,
+        scratch=[
+            pltpu.VMEM((3696, 512), bf16),
+            pltpu.VMEM((3696, 512), bf16),
+            pltpu.SemaphoreType.DMA((6,)),
+        ],
+        flops=2 * 256 * 1024 * 3696,
+        moved=10 << 20,
+        name=name,
+        grant=24,
+    )
 
 
 def outer_body(*refs, first, split):
@@ -357,9 +386,9 @@
     vmem = pl.BlockSpec(memory_space=pltpu.VMEM)
     hbm = pl.BlockSpec(memory_space=pl.ANY)
 
-    payload = call(
+    payload, owed = call(
         prep_body,
-        sds((144, 512), bf16),
+        (sds((144, 512), bf16), sds((8, 128), f32)),
         (stream, norm_gain[None], value_head[None], rewards, segments),
         in_specs=[hbm] * 5,
         scratch=[
@@ -381,7 +410,8 @@
     w_half = lax.dynamic_slice_in_dim(w_down, p * HIGH, LO, 0)
     got = col(after(w_half, payload_mate), MATE, "got")
 
-    block = jnp.concatenate([payload, payload_mate], 1)
+    owed_other = core(owed, "owed_other")
+    block = call(wide_body, sds((144, 1024), bf16), (payload, payload_mate, owed_other))
     near, sums, owed = call(
         pick_body,
         (sds((144, 1024), bf16), sds((8, 128), f32), sds((8, 128), f32)),
@@ -390,7 +420,6 @@
     away = row(near, XTHREE, "block_x3")
     here = jnp.concatenate([near, away], 0)
     there = row(here, ZLO, "block_zlo")
-    owed_other = core(owed, "owed_other")
 
     gates = ((y3,), (down, up), (away,))
     for i, perm in enumerate((PAIR, ZONE, ZTHREE)):
@@ -398,11 +427,12 @@
         sums = sums + col(sums, perm, f"sums{i}")
         if i == 0:
             down, up = lax.optimization_barrier((down, up, sums))[:2]
-            far_a = col(down[:32], ZUP, "far_a")
             far_b = col(up[32:], ZDOWN, "far_b")
             y12 = col(jnp.concatenate([up, down], 0), PAIR, "y12")
+        if i == 1:
+            far_a = col(after(down[:32], sums), ZUP, "far_a")
     y0 = col(after(jnp.concatenate([far_a, far_b], 0), sums), PAIR, "y0")
-    tiny = jnp.concatenate([sums, owed, owed_other], 0)
+    tiny = jnp.concatenate([sums, owed], 0)
     tiny = after(tiny, far_a, far_b)
     tiny = jnp.concatenate([tiny, row(tiny, XTHREE, "tiny_x3")], 0)
     tiny_zlo = row(tiny, ZLO, "tiny_zlo")
@@ -425,45 +455,35 @@
     pieces = (far_a, far_b, up, down, hidden, y0, y12, y3)
     mate_give, mate_keep = outer(pieces, after(g_own, coefs_mate), g_other, 512, True, "outer_mate")
     mate_got = core(mate_give, "mate_got")
-    outs = call(
-        inner_body,
-        [sds((b - a, 3696), d) for d in (bf16, f32) for a, b in PARTS],
-        (after(g_own, mate_keep), g_other, w_down, got, got_other),
-        in_specs=[vmem] * 2 + [hbm] * 3,
-        scratch=[
-            pltpu.VMEM((3696, 512), bf16),
-            pltpu.VMEM((3696, 512), bf16),
-            pltpu.SemaphoreType.DMA((6,)),
-        ],
-        flops=2 * 512 * 1024 * 3696,
-        moved=13 << 20,
-        grant=28,
-    )
-    sent, own = outs[:4], outs[4:]
+    sent = inner(after(g_other, mate_keep), w_down, got, got_other, bf16, "inner_sent")
+    own = inner(after(g_own, sent[0]), w_down, got, got_other, f32, "inner_own")
     t = [col(a, PAIR, f"t{i}") for i, a in enumerate(sent)]
-    w_send = (after(mate_keep, own[0]) + mate_got.astype(f32)).astype(bf16)
+    w_send = (after(mate_keep, sent[0]) + mate_got.astype(f32)).astype(bf16)
     w_recv = col(w_send, MATE, "w_recv")
 
-    stream_grad = call(
-        own_grad_body, sds((128, 512), bf16), (after(stream, own[0]), near, coefs, coefs_mate)
-    )
     q0a, q0b = fold(own[0], after(t[0], w_send))
     from_down = col(q0a, ZUP, "from_down")
     from_up = col(q0b, ZDOWN, "from_up")
+    stream_grad = call(
+        own_grad_body, sds((128, 512), bf16), (after(stream, q0a), near, coefs, coefs_mate)
+    )
     partial = outer(pieces, after(g_own, q0a), g_other, 0, False, "outer_own")
-    q1b, q1a = fold(own[1], after(t[1], partial, from_down, from_up))
+    q1b, q1a = fold(own[1], after(t[1], partial, from_up))
     pure_b = col(q1b, ZUP, "pure_b")
     pure_a = col(q1a, ZDOWN, "pure_a")
-    q2a, q2b = fold(own[2], after(t[2], w_recv, pure_a, pure_b, stream_grad), from_down, from_up)
+    q2a, q2b = fold(own[2], after(t[2], stream_grad), from_down, from_up)
+    q2a, q2b, pure_a, pure_b = lax.optimization_barrier((q2a, q2b, pure_a, pure_b))
     mixed_a = col(q2a, ZUP, "mixed_a")
     mixed_b = col(q2b, ZDOWN, "mixed_b")
-    part = call(merge_body, sds((3696, 512), bf16), (after(partial, q2a), w_recv))
+    part = call(
+        merge_body, sds((3696, 512), bf16), (after(partial, mixed_a, mixed_b, t[3]), w_recv)
+    )
     part_other = core(part, "part")
     weight_grad = (part.astype(f32) + part_other.astype(f32)).astype(bf16)
     hidden_grad = call(
         here_body,
         sds((64, 3696), bf16),
-        (after(own[3], weight_grad), t[3], pure_a, pure_b, mixed_a, mixed_b),
+        (own[3], t[3], pure_a, pure_b, mixed_a, mixed_b),
     )
     return weight_grad, hidden_grad, stream_grad
 

time: 154 us -> 158 us (1.026)
  waiting for transfers between devices: 74.1 us -> 66.8 us
  local copies, waits for them, and re-layouts: 10.4 us -> 14.5 us
  Pallas kernels: 21.5 us -> 23.6 us
  starting transfers between devices: 41.3 us -> 43.1 us
  other arithmetic: 4.5 us -> 6.29 us
    ppermute x33, waiting for transfers between devices: 74.1 us -> 66.8 us  [send(): return lax.ppermute(a, axis, perm)]
    pallas_call x13 -> x15, Pallas kernels: 21.5 us -> 23.6 us  [call(): pl.pallas_call(body, out_shape=out_shape, scratch_shapes=list(scratch), c...]
    unnamed x18 -> x26, local copies, waits for them, and re-layouts: 2.87 us -> 4.67 us
    ppermute x33, starting transfers between devices: 41.3 us -> 43.1 us  [send(): return lax.ppermute(a, axis, perm)]
  transfers between devices with their start and end apart: 33 -> 33, of which waited for: 19 -> 19; matrix products, arithmetic and copies ran while one was open for 7% -> 9% of each run, Pallas kernels for 12% -> 14%
where the time goes in v5:
time: 158 us; the launch traced here: 156 us
  waiting for transfers between devices  66.8 us (42%)
  starting transfers between devices  43.1 us (27%)
  Pallas kernels  23.6 us (15%)
  local copies, waits for them, and re-layouts  14.5 us (9%)
  other arithmetic  6.29 us (4%)
    ppermute x33, waiting for transfers between devices, send(): return lax.ppermute(a, axis, perm)  66.8 us
    ppermute x33, starting transfers between devices, send(): return lax.ppermute(a, axis, perm)  43.1 us
    pallas_call x15, Pallas kernels, call(): pl.pallas_call(body, out_shape=out_shape, scratch_shapes=list(scratch), c...  23.6 us
    unnamed x26, local copies, waits for them, and re-layouts  4.67 us
  transfers between devices with their start and end apart: 33, of which 19 were waited for; matrix products, arithmetic and copies ran while one was open for 9% of the time, Pallas kernels for 14%

profile of v5, /device:TPU:6, one launch (start us, length us, event | category | flops | bytes accessed | tf_op | source)
XLA Modules:
  0.0 155.9 jit_solution(16064969258851371500)
XLA Ops:
  0.6 1.7 %prep_body.1 = (bf16[144,512]{1,0:T(8,128)(2,1)}, f32[8,128]{1,0:T(8,128)}) custom-call(bf16[128,512]{1,0:T(8,128)(2,1)} %stream.2, f32[1,512]{1,0:T(1,128)} %bitcast.2, f32[1,512]{1,0:T(1,128)} %bitcast.3, f32[1,128]{1,0:T(1,128)} %reward.1, s32[1,128]{1,0:T(1,128)} %segment.1), custom_call_target="tpu_custom_call" | custom-call | tf_op jit(solution)/shard_map/prep_body/pallas_call | solution.py:55
  2.3 3.1 %collective-permute-start.2 = (bf16[144,512]{1,0:T(8,128)(2,1)}, bf16[144,512]{1,0:T(8,128)(2,1)S(1)}, u32[]{:S(2)}, u32[]{:S(2)}) collective-permute-start(bf16[144,512]{1,0:T(8,128)(2,1)} %get-tuple-element.52.own), channel_id=1, source_target_pairs={{0,3},{1,2},{2,1},{3,0},{4,7},{5,6},{6,5},{7,4},{8,11},{9,10},{10,... | collective-permute-start | bytes 442376 | tf_op jit(solution)/shard_map/payload_mate/ppermute | solution.py:29
  5.5 3.3 %collective-permute-start = (bf16[64,3696]{1,0:T(8,128)(2,1)}, bf16[64,3696]{1,0:T(8,128)(2,1)S(1)}, u32[]{:S(2)}, u32[]{:S(2)}) collective-permute-start(bf16[64,3696]{1,0:T(8,128)(2,1)} %refs_4_.3), channel_id=1, source_target_pairs={{0,4},{1,5},{2,6},{3,7},{4,8},{5,9},{6,10},{7,11},{8,12},{9,13},{1... | collective-permute-start | bytes 1419272 | tf_op jit(solution)/shard_map/down/ppermute | solution.py:29
  8.8 3.0 %collective-permute-start.1 = (bf16[64,3696]{1,0:T(8,128)(2,1)}, bf16[64,3696]{1,0:T(8,128)(2,1)S(1)}, u32[]{:S(2)}, u32[]{:S(2)}) collective-permute-start(bf16[64,3696]{1,0:T(8,128)(2,1)} %refs_4_.3), channel_id=1, source_target_pairs={{0,12},{1,13},{2,14},{3,15},{4,0},{5,1},{6,2},{7,3},{8,4},{9,5},{1... | collective-permute-start | bytes 1419272 | tf_op jit(solution)/shard_map/up/ppermute | solution.py:29
  11.9 0.9 copy-done.11
  12.8 0.9 collective-permute-start.4
  13.7 2.9 %constant_dynamic-slice_fusion = bf16[1856,512]{1,0:T(8,128)(2,1)} fusion(bf16[3696,512]{1,0:T(8,128)(2,1)} %w.3, s32[]{:T(128)S(6)} %select_n.3), kind=kLoop, calls=%fused_computation.9 | loop fusion | bytes 3801092 | tf_op jit(solution)/shard_map/dynamic_slice | solution.py:410
  16.6 1.0 collective-permute-start.15
  17.7 4.2 %collective-permute-done.4.other = bf16[144,1024]{1,0:T(8,128)(2,1)S(1)} collective-permute-done((bf16[144,1024]{1,0:T(8,128)(2,1)S(1)}, bf16[144,1024]{1,0:T(8,128)(2,1)S(1)}, u32[]{:S(2)}, u32[]{:S(2)}) %collective-permute-start.4) | collective-permute-done | bytes 294944 | tf_op jit(solution)/shard_map/block_x1/ppermute | solution.py:29
  22.1 1.8 %collective-permute-start.6 = (f32[8,128]{1,0:T(8,128)S(1)}, f32[8,128]{1,0:T(8,128)S(1)}, u32[]{:S(2)}, u32[]{:S(2)}) collective-permute-start(f32[8,128]{1,0:T(8,128)S(1)} %get-tuple-element.56), channel_id=1, source_target_pairs={{0,1},{1,0},{2,3},{3,2},{4,5},{5,4},{6,7},{7,6},{8,9},{9,8},{10,11... | collective-permute-start | bytes 12296 | tf_op jit(solution)/shard_map/sums0/ppermute | solution.py:29
  24.4 1.4 collective-permute-done.6
  25.8 1.7 %collective-permute-done.refs_3_ = bf16[64,3696]{1,0:T(8,128)(2,1)S(1)} collective-permute-done((bf16[64,3696]{1,0:T(8,128)(2,1)}, bf16[64,3696]{1,0:T(8,128)(2,1)S(1)}, u32[]{:S(2)}, u32[]{:S(2)}) %collective-permute-start) | collective-permute-done | bytes 473120 | tf_op jit(solution)/shard_map/down/ppermute | solution.py:29
  27.5 7.3 %collective-permute-done.1.refs_2_ = bf16[64,3696]{1,0:T(8,128)(2,1)S(1)} collective-permute-done((bf16[64,3696]{1,0:T(8,128)(2,1)}, bf16[64,3696]{1,0:T(8,128)(2,1)S(1)}, u32[]{:S(2)}, u32[]{:S(2)}) %collective-permute-start.1) | collective-permute-done | bytes 473120 | tf_op jit(solution)/shard_map/up/ppermute | solution.py:29
  34.8 3.8 %collective-permute-start.7 = (f32[8,128]{1,0:T(8,128)S(1)}, f32[8,128]{1,0:T(8,128)S(1)}, u32[]{:S(2)}, u32[]{:S(2)}) collective-permute-start(f32[8,128]{1,0:T(8,128)S(1)} %add.18), channel_id=1, source_target_pairs={{0,4},{1,5},{2,6},{3,7},{4,0},{5,1},{6,2},{7,3},{8,12},{9,13},{10,... | collective-permute-start | bytes 12296 | tf_op jit(solution)/shard_map/sums1/ppermute | solution.py:29
  38.6 0.7 constant_dynamic-update-slice_fusion.3
  39.3 0.7 slice.6
  40.1 0.7 slice.7
  41.2 2.5 %collective-permute-start.8 = (bf16[32,3696]{1,0:T(8,128)(2,1)}, bf16[32,3696]{1,0:T(8,128)(2,1)}, u32[]{:S(2)}, u32[]{:S(2)}) collective-permute-start(bf16[32,3696]{1,0:T(8,128)(2,1)} %slice.6), channel_id=1, source_target_pairs={{0,4},{1,5},{2,6},{3,7},{4,8},{5,9},{6,10},{7,11},{8,12},{9,13},{1... | collective-permute-start | bytes 709640 | tf_op jit(solution)/shard_map/far_a/ppermute | solution.py:29
  43.7 1.0 pad_maximum_fusion
  44.8 2.2 %copy.11 = bf16[128,3696]{0,1:T(8,128)(2,1)} copy(bf16[128,3696]{1,0:T(8,128)(2,1)} %pad_maximum_fusion) | data formatting | bytes 1892352 | tf_op jit(solution)/shard_map/concatenate | solution.py:431
  47.0 1.7 %collective-permute-start.13 = (bf16[128,3696]{0,1:T(8,128)(2,1)}, bf16[128,3696]{0,1:T(8,128)(2,1)}, u32[]{:S(2)}, u32[]{:S(2)}) collective-permute-start(bf16[128,3696]{0,1:T(8,128)(2,1)} %copy.11), channel_id=1, source_target_pairs={{0,1},{1,0},{2,3},{3,2},{4,5},{5,4},{6,7},{7,6},{8,9},{9,8},{10,11... | collective-permute-start | bytes 2838536 | tf_op jit(solution)/shard_map/y12/ppermute | solution.py:29
  48.7 1.6 %collective-permute-start.11 = (f32[8,128]{1,0:T(8,128)S(1)}, f32[8,128]{1,0:T(8,128)S(1)}, u32[]{:S(2)}, u32[]{:S(2)}) collective-permute-start(f32[8,128]{1,0:T(8,128)S(1)} %add.19), channel_id=1, source_target_pairs={{0,12},{1,13},{2,14},{3,15},{4,8},{5,9},{6,10},{7,11},{8,4},{9,5},... | collective-permute-start | bytes 12296 | tf_op jit(solution)/shard_map/sums2/ppermute | solution.py:29
  50.4 1.7 %constant_dynamic-update-slice_fusion.2.here = bf16[288,1024]{1,0:T(8,128)(2,1)} fusion(bf16[288,1024]{1,0:T(8,128)(2,1)} %constant_dynamic-update-slice_fusion.3, bf16[144,1024]{1,0:T(8,128)(2,1)} %collective-permute-done.10), kind=kLoop, calls=%fused_computation.6 | loop fusion | bytes 589824 | tf_op jit(solution)/shard_map/concatenate | solution.py:421
  52.3 1.0 collective-permute-done.8.refs_0_
  53.4 1.8 %pad_maximum_fusion.1 = bf16[64,3696]{1,0:T(8,128)(2,1)} fusion(bf16[32,3696]{1,0:T(8,128)(2,1)S(1)} %collective-permute-done.9.refs_1_, bf16[32,3696]{1,0:T(8,128)(2,1)} %collective-permute-done.8.refs_0_), kind=kLoop, calls=%fused_computation.3 | loop fusion | flops 946176 | bytes 946176 | tf_op jit(solution)/shard_map/concatenate | solution.py:434
  55.2 1.7 %collective-permute-start.12 = (bf16[64,3696]{1,0:T(8,128)(2,1)}, bf16[64,3696]{1,0:T(8,128)(2,1)}, u32[]{:S(2)}, u32[]{:S(2)}) collective-permute-start(bf16[64,3696]{1,0:T(8,128)(2,1)} %pad_maximum_fusion.1), channel_id=1, source_target_pairs={{0,1},{1,0},{2,3},{3,2},{4,5},{5,4},{6,7},{7,6},{8,9},{9,8},{10,11... | collective-permute-start | bytes 1419272 | tf_op jit(solution)/shard_map/y0/ppermute | solution.py:29
  57.4 4.4 %collective-permute-done.14 = f32[16,128]{1,0:T(8,128)S(1)} collective-permute-done((f32[16,128]{1,0:T(8,128)S(1)}, f32[16,128]{1,0:T(8,128)S(1)}, u32[]{:S(2)}, u32[]{:S(2)}) %collective-permute-start.14) | collective-permute-done | bytes 8224 | tf_op jit(solution)/shard_map/tiny_x3/ppermute | solution.py:29
  61.9 4.1 %collective-permute-done.16.there = f32[32,128]{1,0:T(8,128)S(1)} collective-permute-done((f32[32,128]{1,0:T(8,128)S(1)}, f32[32,128]{1,0:T(8,128)S(1)}, u32[]{:S(2)}, u32[]{:S(2)}) %collective-permute-start.16) | collective-permute-done | bytes 16416 | tf_op jit(solution)/shard_map/tiny_zlo/ppermute | solution.py:29
  66.6 0.8 coefs_body.1.coefs
  67.4 0.6 collective-permute-start.18
  68.0 3.2 %collective-permute-done.13 = bf16[128,3696]{0,1:T(8,128)(2,1)} collective-permute-done((bf16[128,3696]{0,1:T(8,128)(2,1)}, bf16[128,3696]{0,1:T(8,128)(2,1)}, u32[]{:S(2)}, u32[]{:S(2)}) %collective-permute-start.13) | collective-permute-done | bytes 946208 | tf_op jit(solution)/shard_map/y12/ppermute | solution.py:29
  71.2 1.6 %copy.13.refs_6_ = bf16[128,3696]{1,0:T(8,128)(2,1)S(1)} copy(bf16[128,3696]{0,1:T(8,128)(2,1)} %collective-permute-done.13) | data formatting | bytes 1892352 | tf_op jit(solution)/shard_map/y12/ppermute | solution.py:29
  72.8 2.4 %grad_body.1 = (bf16[256,1024]{1,0:T(8,128)(2,1)S(1)}, bf16[256,1024]{1,0:T(8,128)(2,1)S(1)}) custom-call(f32[8,128]{1,0:T(8,128)S(1)} %coefs_body.1.coefs, bf16[288,1024]{1,0:T(8,128)(2,1)} %constant_dynamic-update-slice_fusion.2.here, bf16[288,1024]{1,0:T(8,128)(2,1)} %collective-permute-done.17.there), custom_call_target="tpu_custom_call" | custom-call | bytes 4194304 | tf_op jit(solution)/shard_map/grad_body/pallas_call | solution.py:55
  75.2 3.8 %collective-permute-done.12.refs_5_ = bf16[64,3696]{1,0:T(8,128)(2,1)} collective-permute-done((bf16[64,3696]{1,0:T(8,128)(2,1)}, bf16[64,3696]{1,0:T(8,128)(2,1)}, u32[]{:S(2)}, u32[]{:S(2)}) %collective-permute-start.12) | collective-permute-done | bytes 473120 | tf_op jit(solution)/shard_map/y0/ppermute | solution.py:29
  79.0 1.0 copy-done.2
  80.1 0.9 copy-done.7
  81.0 1.0 copy-done.9
  82.0 3.5 %outer_mate.1 = (bf16[3696,256]{1,0:T(8,128)(2,1)S(1)}, f32[3696,256]{1,0:T(8,128)S(1)}) custom-call(bf16[32,3696]{1,0:T(8,128)(2,1)} %collective-permute-done.8.refs_0_, bf16[32,3696]{1,0:T(8,128)(2,1)S(1)} %copy-done.7, bf16[64,3696]{1,0:T(8,128)(2,1)S(1)} %copy-done.2, bf16[64,3696]{1,0:T(8,128)(2,1)S(1)} %collective-permute-done.refs_3_, ...), custom_call_target="tpu_custom_call" | custom-call | flops 1937768448 | bytes 8388608 | tf_op jit(solution)/shard_map/outer_mate/pallas_call | solution.py:55
  85.6 4.4 %inner_sent.1 = (bf16[64,3696]{1,0:T(8,128)(2,1)S(1)}, bf16[64,3696]{1,0:T(8,128)(2,1)S(1)}, bf16[64,3696]{1,0:T(8,128)(2,1)S(1)}, bf16[64,3696]{1,0:T(8,128)(2,1)S(1)}) custom-call(bf16[256,1024]{1,0:T(8,128)(2,1)S(1)} %get-tuple-element.72.refs_9_.g, bf16[3696,512]{1,0:T(8,128)(2,1)S(1)} %copy-done, bf16[1856,512]{1,0:T(8,128)(2,1)S(1)} %collective-permute-done.15.got, ...), custom_call_target="tpu_custom_call" | custom-call | flops 1937768448 | bytes 10485760 | tf_op jit(solution)/shard_map/inner_sent/pallas_call | solution.py:55
  90.6 1.0 collective-permute-start.31
  91.5 0.9 collective-permute-start.20
  92.5 1.1 collective-permute-start.25
  93.6 0.9 collective-permute-start.22
  94.5 4.4 %inner_own.1 = (f32[64,3696]{1,0:T(8,128)S(1)}, f32[64,3696]{1,0:T(8,128)S(1)}, f32[64,3696]{1,0:T(8,128)S(1)}, f32[64,3696]{1,0:T(8,128)S(1)}) custom-call(bf16[256,1024]{1,0:T(8,128)(2,1)S(1)} %get-tuple-element.81.refs_8_.g, bf16[3696,512]{1,0:T(8,128)(2,1)S(1)} %copy-done, bf16[1856,512]{1,0:T(8,128)(2,1)S(1)} %collective-permute-done.15.got, ...), custom_call_target="tpu_custom_call" | custom-call | flops 1937768448 | bytes 10485760 | tf_op jit(solution)/shard_map/inner_own/pallas_call | solution.py:55
  98.9 6.4 %collective-permute-done.20.other = bf16[64,3696]{1,0:T(8,128)(2,1)S(1)} collective-permute-done((bf16[64,3696]{1,0:T(8,128)(2,1)S(1)}, bf16[64,3696]{1,0:T(8,128)(2,1)S(1)}, u32[]{:S(2)}, u32[]{:S(2)}) %collective-permute-start.20) | collective-permute-done | bytes 473120 | tf_op jit(solution)/shard_map/t0/ppermute | solution.py:29
  105.4 1.9 %collective-permute-start.24 = (bf16[32,3696]{1,0:T(8,128)(2,1)S(1)}, bf16[32,3696]{1,0:T(8,128)(2,1)S(1)}, u32[]{:S(2)}, u32[]{:S(2)}) collective-permute-start(bf16[32,3696]{1,0:T(8,128)(2,1)S(1)} %get-tuple-element.86), channel_id=1, source_target_pairs={{0,12},{1,13},{2,14},{3,15},{4,0},{5,1},{6,2},{7,3},{8,4},{9,5},{1... | collective-permute-start | bytes 709640 | tf_op jit(solution)/shard_map/from_up/ppermute | solution.py:29
  107.3 1.3 collective-permute-start.23
  108.6 3.5 %outer_own.1.partial = f32[3696,512]{1,0:T(8,128)S(1)} custom-call(bf16[32,3696]{1,0:T(8,128)(2,1)} %collective-permute-done.8.refs_0_, bf16[32,3696]{1,0:T(8,128)(2,1)S(1)} %copy-done.7, bf16[64,3696]{1,0:T(8,128)(2,1)S(1)} %copy-done.3, bf16[64,3696]{1,0:T(8,128)(2,1)S(1)} %collective-permute-done.refs_3_, bf16[64,3696]{1,0:T(8,128)(2,1)S(1)} %copy-done.10, ...), custom_call_target="tpu_custom_call" | custom-call | flops 1937768448 | bytes 8388608 | tf_op jit(solution)/shard_map/outer_own/pallas_call | solution.py:55
  112.1 3.4 %collective-permute-done.25.other = bf16[64,3696]{1,0:T(8,128)(2,1)S(1)} collective-permute-done((bf16[64,3696]{1,0:T(8,128)(2,1)S(1)}, bf16[64,3696]{1,0:T(8,128)(2,1)S(1)}, u32[]{:S(2)}, u32[]{:S(2)}) %collective-permute-start.25) | collective-permute-done | bytes 473120 | tf_op jit(solution)/shard_map/t1/ppermute | solution.py:29
  115.5 1.1 collective-permute-done.24.refs_1_
  116.7 3.7 %collective-permute-start.26 = (bf16[32,3696]{1,0:T(8,128)(2,1)S(1)}, bf16[32,3696]{1,0:T(8,128)(2,1)S(1)}, u32[]{:S(2)}, u32[]{:S(2)}) collective-permute-start(bf16[32,3696]{1,0:T(8,128)(2,1)S(1)} %get-tuple-element.92), channel_id=1, source_target_pairs={{0,12},{1,13},{2,14},{3,15},{4,0},{5,1},{6,2},{7,3},{8,4},{9,5},{1... | collective-permute-start | bytes 709640 | tf_op jit(solution)/shard_map/pure_a/ppermute | solution.py:29
  120.4 5.1 %collective-permute-done.22.other = bf16[64,3696]{1,0:T(8,128)(2,1)S(1)} collective-permute-done((bf16[64,3696]{1,0:T(8,128)(2,1)S(1)}, bf16[64,3696]{1,0:T(8,128)(2,1)S(1)}, u32[]{:S(2)}, u32[]{:S(2)}) %collective-permute-start.22) | collective-permute-done | bytes 473120 | tf_op jit(solution)/shard_map/t2/ppermute | solution.py:29
  125.5 0.9 collective-permute-start.30
  126.4 0.9 own_grad_body.1
  127.5 1.9 %collective-permute-done.26.pure_a = bf16[32,3696]{1,0:T(8,128)(2,1)S(1)} collective-permute-done((bf16[32,3696]{1,0:T(8,128)(2,1)S(1)}, bf16[32,3696]{1,0:T(8,128)(2,1)S(1)}, u32[]{:S(2)}, u32[]{:S(2)}) %collective-permute-start.26) | collective-permute-done | bytes 236576 | tf_op jit(solution)/shard_map/pure_a/ppermute | solution.py:29
  129.3 0.7 collective-permute-done.27.pure_b
  130.0 4.1 %collective-permute-start.28 = (bf16[32,3696]{1,0:T(8,128)(2,1)S(1)}, bf16[32,3696]{1,0:T(8,128)(2,1)S(1)}, u32[]{:S(2)}, u32[]{:S(2)}) collective-permute-start(bf16[32,3696]{1,0:T(8,128)(2,1)S(1)} %get-tuple-element.94), channel_id=1, source_target_pairs={{0,4},{1,5},{2,6},{3,7},{4,8},{5,9},{6,10},{7,11},{8,12},{9,13},{1... | collective-permute-start | bytes 709640 | tf_op jit(solution)/shard_map/mixed_a/ppermute | solution.py:29
  134.1 4.2 %collective-permute-done.30.other = bf16[64,3696]{1,0:T(8,128)(2,1)S(1)} collective-permute-done((bf16[64,3696]{1,0:T(8,128)(2,1)S(1)}, bf16[64,3696]{1,0:T(8,128)(2,1)S(1)}, u32[]{:S(2)}, u32[]{:S(2)}) %collective-permute-start.30) | collective-permute-done | bytes 473120 | tf_op jit(solution)/shard_map/t3/ppermute | solution.py:29
  138.3 1.9 %collective-permute-done.28.mixed_a = bf16[32,3696]{1,0:T(8,128)(2,1)S(1)} collective-permute-done((bf16[32,3696]{1,0:T(8,128)(2,1)S(1)}, bf16[32,3696]{1,0:T(8,128)(2,1)S(1)}, u32[]{:S(2)}, u32[]{:S(2)}) %collective-permute-start.28) | collective-permute-done | bytes 236576 | tf_op jit(solution)/shard_map/mixed_a/ppermute | solution.py:29
  140.3 5.4 %collective-permute-done.29.mixed_b = bf16[32,3696]{1,0:T(8,128)(2,1)S(1)} collective-permute-done((bf16[32,3696]{1,0:T(8,128)(2,1)S(1)}, bf16[32,3696]{1,0:T(8,128)(2,1)S(1)}, u32[]{:S(2)}, u32[]{:S(2)}) %collective-permute-start.29) | collective-permute-done | bytes 236576 | tf_op jit(solution)/shard_map/mixed_b/ppermute | solution.py:29
  145.7 0.6 merge_body.1
  146.4 1.0 here_body.1
  147.4 5.6 %collective-permute-done.32 = bf16[3696,512]{1,0:T(8,128)(2,1)S(1)} collective-permute-done((bf16[3696,512]{1,0:T(8,128)(2,1)S(1)}, bf16[3696,512]{1,0:T(8,128)(2,1)S(1)}, u32[]{:S(2)}, u32[]{:S(2)}) %collective-permute-start.32) | collective-permute-done | bytes 3784736 | tf_op jit(solution)/shard_map/part/ppermute | solution.py:29
  152.9 3.0 %add_convert_fusion = bf16[3696,512]{1,0:T(8,128)(2,1)} fusion(bf16[3696,512]{1,0:T(8,128)(2,1)S(1)} %collective-permute-done.32, bf16[3696,512]{1,0:T(8,128)(2,1)S(1)} %merge_body.1), kind=kLoop, calls=%fused_computation | loop fusion | flops 7569408 | bytes 11354112 | tf_op jit(solution)/shard_map/convert_element_type | solution.py:482
  (58 shorter events, 3.2 us)
Async XLA Ops:
  2.3 9.6 %collective-permute-start.2 = (bf16[144,512]{1,0:T(8,128)(2,1)}, bf16[144,512]{1,0:T(8,128)(2,1)S(1)}, u32[]{:S(2)}, u32[]{:S(2)}) collective-permute-start(bf16[144,512]{1,0:T(8,128)(2,1)} %get-tuple-element.52.own), channel_id=1, source_target_pairs={{0,3},{1,2},{2,1},{3,0},{4,7},{5,6},{6,5},{7,4},{8,11},{9,10},{10,... | collective-permute-start | bytes 442376 | tf_op jit(solution)/shard_map/payload_mate/ppermute | solution.py:29
  5.4 6.5 %collective-permute-start.3 = (f32[8,128]{1,0:T(8,128)}, f32[8,128]{1,0:T(8,128)S(1)}, u32[]{:S(2)}, u32[]{:S(2)}) collective-permute-start(f32[8,128]{1,0:T(8,128)} %get-tuple-element.54), channel_id=1, source_target_pairs={{0,128},{128,0},{1,129},{129,1},{2,130},{130,2},{3,131},{131,3},{4... | collective-permute-start | bytes 12296 | tf_op jit(solution)/shard_map/owed_other/ppermute | solution.py:29
  5.4 16.7 %collective-permute-start.5 = (bf16[64,3696]{1,0:T(8,128)(2,1)}, bf16[64,3696]{1,0:T(8,128)(2,1)}, u32[]{:S(2)}, u32[]{:S(2)}) collective-permute-start(bf16[64,3696]{1,0:T(8,128)(2,1)} %refs_4_.3), channel_id=1, source_target_pairs={{0,1},{1,0},{2,3},{3,2},{4,5},{5,4},{6,7},{7,6},{8,9},{9,8},{10,11... | collective-permute-start | bytes 1419272 | tf_op jit(solution)/shard_map/y3/ppermute | solution.py:29
  5.5 22.0 %collective-permute-start = (bf16[64,3696]{1,0:T(8,128)(2,1)}, bf16[64,3696]{1,0:T(8,128)(2,1)S(1)}, u32[]{:S(2)}, u32[]{:S(2)}) collective-permute-start(bf16[64,3696]{1,0:T(8,128)(2,1)} %refs_4_.3), channel_id=1, source_target_pairs={{0,4},{1,5},{2,6},{3,7},{4,8},{5,9},{6,10},{7,11},{8,12},{9,13},{1... | collective-permute-start | bytes 1419272 | tf_op jit(solution)/shard_map/down/ppermute | solution.py:29
  8.8 26.0 %collective-permute-start.1 = (bf16[64,3696]{1,0:T(8,128)(2,1)}, bf16[64,3696]{1,0:T(8,128)(2,1)S(1)}, u32[]{:S(2)}, u32[]{:S(2)}) collective-permute-start(bf16[64,3696]{1,0:T(8,128)(2,1)} %refs_4_.3), channel_id=1, source_target_pairs={{0,12},{1,13},{2,14},{3,15},{4,0},{5,1},{6,2},{7,3},{8,4},{9,5},{1... | collective-permute-start | bytes 1419272 | tf_op jit(solution)/shard_map/up/ppermute | solution.py:29
  11.9 0.9 copy-start.11
  12.8 9.1 %collective-permute-start.4 = (bf16[144,1024]{1,0:T(8,128)(2,1)S(1)}, bf16[144,1024]{1,0:T(8,128)(2,1)S(1)}, u32[]{:S(2)}, u32[]{:S(2)}) collective-permute-start(bf16[144,1024]{1,0:T(8,128)(2,1)S(1)} %wide_body.1.own), channel_id=1, source_target_pairs={{0,16},{16,0},{32,48},{48,32},{64,80},{80,64},{96,112},{112,96},{1... | collective-permute-start | bytes 884744 | tf_op jit(solution)/shard_map/block_x1/ppermute | solution.py:29
  16.6 49.4 %collective-permute-start.15 = (bf16[1856,512]{1,0:T(8,128)(2,1)}, bf16[1856,512]{1,0:T(8,128)(2,1)S(1)}, u32[]{:S(2)}, u32[]{:S(2)}) collective-permute-start(bf16[1856,512]{1,0:T(8,128)(2,1)} %constant_dynamic-slice_fusion), channel_id=1, source_target_pairs={{0,3},{1,2},{2,1},{3,0},{4,7},{5,6},{6,5},{7,4},{8,11},{9,10},{10,... | collective-permute-start | bytes 5701640 | tf_op jit(solution)/shard_map/got/ppermute | solution.py:29
  22.1 45.9 %copy-start.4 = (bf16[144,1024]{1,0:T(8,128)(2,1)}, bf16[144,1024]{1,0:T(8,128)(2,1)S(1)}, u32[]{:S(2)}) copy-start(bf16[144,1024]{1,0:T(8,128)(2,1)S(1)} %get-tuple-element.61.block) | copy-start | bytes 884740
  22.1 3.7 %collective-permute-start.6 = (f32[8,128]{1,0:T(8,128)S(1)}, f32[8,128]{1,0:T(8,128)S(1)}, u32[]{:S(2)}, u32[]{:S(2)}) collective-permute-start(f32[8,128]{1,0:T(8,128)S(1)} %get-tuple-element.56), channel_id=1, source_target_pairs={{0,1},{1,0},{2,3},{3,2},{4,5},{5,4},{6,7},{7,6},{8,9},{9,8},{10,11... | collective-permute-start | bytes 12296 | tf_op jit(solution)/shard_map/sums0/ppermute | solution.py:29
  23.9 24.8 %collective-permute-start.10 = (bf16[144,1024]{1,0:T(8,128)(2,1)S(1)}, bf16[144,1024]{1,0:T(8,128)(2,1)}, u32[]{:S(2)}, u32[]{:S(2)}) collective-permute-start(bf16[144,1024]{1,0:T(8,128)(2,1)S(1)} %get-tuple-element.61.block), channel_id=1, source_target_pairs={{0,48},{16,32},{32,16},{48,0},{64,112},{80,96},{96,80},{112,64},{1... | collective-permute-start | bytes 884744 | tf_op jit(solution)/shard_map/block_x3/ppermute | solution.py:29
  34.8 33.2 %copy-start.1 = (bf16[64,3696]{1,0:T(8,128)(2,1)}, bf16[64,3696]{1,0:T(8,128)(2,1)S(1)}, u32[]{:S(2)}) copy-start(bf16[64,3696]{1,0:T(8,128)(2,1)S(1)} %collective-permute-done.1.refs_2_) | copy-start | bytes 1419268
  34.8 6.4 %collective-permute-start.7 = (f32[8,128]{1,0:T(8,128)S(1)}, f32[8,128]{1,0:T(8,128)S(1)}, u32[]{:S(2)}, u32[]{:S(2)}) collective-permute-start(f32[8,128]{1,0:T(8,128)S(1)} %add.18), channel_id=1, source_target_pairs={{0,4},{1,5},{2,6},{3,7},{4,0},{5,1},{6,2},{7,3},{8,12},{9,13},{10,... | collective-permute-start | bytes 12296 | tf_op jit(solution)/shard_map/sums1/ppermute | solution.py:29
  40.8 11.3 %collective-permute-start.9 = (bf16[32,3696]{1,0:T(8,128)(2,1)}, bf16[32,3696]{1,0:T(8,128)(2,1)S(1)}, u32[]{:S(2)}, u32[]{:S(2)}) collective-permute-start(bf16[32,3696]{1,0:T(8,128)(2,1)} %slice.7), channel_id=1, source_target_pairs={{0,12},{1,13},{2,14},{3,15},{4,0},{5,1},{6,2},{7,3},{8,4},{9,5},{1... | collective-permute-start | bytes 709640 | tf_op jit(solution)/shard_map/far_b/ppermute | solution.py:29
  41.2 12.2 %collective-permute-start.8 = (bf16[32,3696]{1,0:T(8,128)(2,1)}, bf16[32,3696]{1,0:T(8,128)(2,1)}, u32[]{:S(2)}, u32[]{:S(2)}) collective-permute-start(bf16[32,3696]{1,0:T(8,128)(2,1)} %slice.6), channel_id=1, source_target_pairs={{0,4},{1,5},{2,6},{3,7},{4,8},{5,9},{6,10},{7,11},{8,12},{9,13},{1... | collective-permute-start | bytes 709640 | tf_op jit(solution)/shard_map/far_a/ppermute | solution.py:29
  47.0 24.2 %collective-permute-start.13 = (bf16[128,3696]{0,1:T(8,128)(2,1)}, bf16[128,3696]{0,1:T(8,128)(2,1)}, u32[]{:S(2)}, u32[]{:S(2)}) collective-permute-start(bf16[128,3696]{0,1:T(8,128)(2,1)} %copy.11), channel_id=1, source_target_pairs={{0,1},{1,0},{2,3},{3,2},{4,5},{5,4},{6,7},{7,6},{8,9},{9,8},{10,11... | collective-permute-start | bytes 2838536 | tf_op jit(solution)/shard_map/y12/ppermute | solution.py:29
  48.7 6.5 %collective-permute-start.11 = (f32[8,128]{1,0:T(8,128)S(1)}, f32[8,128]{1,0:T(8,128)S(1)}, u32[]{:S(2)}, u32[]{:S(2)}) collective-permute-start(f32[8,128]{1,0:T(8,128)S(1)} %add.19), channel_id=1, source_target_pairs={{0,12},{1,13},{2,14},{3,15},{4,8},{5,9},{6,10},{7,11},{8,4},{9,5},... | collective-permute-start | bytes 12296 | tf_op jit(solution)/shard_map/sums2/ppermute | solution.py:29
  52.1 15.9 %copy-start.6 = (bf16[32,3696]{1,0:T(8,128)(2,1)}, bf16[32,3696]{1,0:T(8,128)(2,1)S(1)}, u32[]{:S(2)}) copy-start(bf16[32,3696]{1,0:T(8,128)(2,1)S(1)} %collective-permute-done.9.refs_1_) | copy-start | bytes 709636
  52.1 20.7 %collective-permute-start.17 = (bf16[288,1024]{1,0:T(8,128)(2,1)}, bf16[288,1024]{1,0:T(8,128)(2,1)}, u32[]{:S(2)}, u32[]{:S(2)}) collective-permute-start(bf16[288,1024]{1,0:T(8,128)(2,1)} %constant_dynamic-update-slice_fusion.2.here), channel_id=1, source_target_pairs={{0,64},{16,80},{32,96},{48,112},{64,0},{80,16},{96,32},{112,48},{1... | collective-permute-start | bytes 1769480 | tf_op jit(solution)/shard_map/block_zlo/ppermute | solution.py:29
  55.2 23.9 %collective-permute-start.12 = (bf16[64,3696]{1,0:T(8,128)(2,1)}, bf16[64,3696]{1,0:T(8,128)(2,1)}, u32[]{:S(2)}, u32[]{:S(2)}) collective-permute-start(bf16[64,3696]{1,0:T(8,128)(2,1)} %pad_maximum_fusion.1), channel_id=1, source_target_pairs={{0,1},{1,0},{2,3},{3,2},{4,5},{5,4},{6,7},{7,6},{8,9},{9,8},{10,11... | collective-permute-start | bytes 1419272 | tf_op jit(solution)/shard_map/y0/ppermute | solution.py:29
  56.9 4.9 %collective-permute-start.14 = (f32[16,128]{1,0:T(8,128)S(1)}, f32[16,128]{1,0:T(8,128)S(1)}, u32[]{:S(2)}, u32[]{:S(2)}) collective-permute-start(f32[16,128]{1,0:T(8,128)S(1)} %pad_maximum_fusion.2), channel_id=1, source_target_pairs={{0,48},{16,32},{32,16},{48,0},{64,112},{80,96},{96,80},{112,64},{1... | collective-permute-start | bytes 24584 | tf_op jit(solution)/shard_map/tiny_x3/ppermute | solution.py:29
  61.8 4.2 %collective-permute-start.16 = (f32[32,128]{1,0:T(8,128)S(1)}, f32[32,128]{1,0:T(8,128)S(1)}, u32[]{:S(2)}, u32[]{:S(2)}) collective-permute-start(f32[32,128]{1,0:T(8,128)S(1)} %constant_dynamic-update-slice_fusion.here), channel_id=1, source_target_pairs={{0,64},{16,80},{32,96},{48,112},{64,0},{80,16},{96,32},{112,48},{1... | collective-permute-start | bytes 49160 | tf_op jit(solution)/shard_map/tiny_zlo/ppermute | solution.py:29
  66.0 19.6 %collective-permute-start.19 = (bf16[1856,512]{1,0:T(8,128)(2,1)S(1)}, bf16[1856,512]{1,0:T(8,128)(2,1)}, u32[]{:S(2)}, u32[]{:S(2)}) collective-permute-start(bf16[1856,512]{1,0:T(8,128)(2,1)S(1)} %collective-permute-done.15.got), channel_id=1, source_target_pairs={{0,128},{128,0},{1,129},{129,1},{2,130},{130,2},{3,131},{131,3},{4... | collective-permute-start | bytes 5701640 | tf_op jit(solution)/shard_map/got_other/ppermute | solution.py:29
  67.4 7.8 %collective-permute-start.18 = (f32[8,128]{1,0:T(8,128)S(1)}, f32[8,128]{1,0:T(8,128)S(1)}, u32[]{:S(2)}, u32[]{:S(2)}) collective-permute-start(f32[8,128]{1,0:T(8,128)S(1)} %coefs_body.1.coefs), channel_id=1, source_target_pairs={{0,3},{1,2},{2,1},{3,0},{4,7},{5,6},{6,5},{7,4},{8,11},{9,10},{10,... | collective-permute-start | bytes 12296 | tf_op jit(solution)/shard_map/coefs_mate/ppermute | solution.py:29
  75.2 10.4 %copy-start = (bf16[3696,512]{1,0:T(8,128)(2,1)S(1)}, bf16[3696,512]{1,0:T(8,128)(2,1)}, u32[]{:S(2)}) copy-start(bf16[3696,512]{1,0:T(8,128)(2,1)} %w.3) | copy-start | bytes 11354116
  79.0 1.0 copy-start.2
  80.1 0.9 copy-start.7
  81.0 1.0 copy-start.9
  85.5 4.5 %collective-permute-start.21 = (bf16[3696,256]{1,0:T(8,128)(2,1)S(1)}, bf16[3696,256]{1,0:T(8,128)(2,1)S(1)}, u32[]{:S(2)}, u32[]{:S(2)}) collective-permute-start(bf16[3696,256]{1,0:T(8,128)(2,1)S(1)} %get-tuple-element.78), channel_id=1, source_target_pairs={{0,128},{128,0},{1,129},{129,1},{2,130},{130,2},{3,131},{131,3},{4... | collective-permute-start | bytes 5677064 | tf_op jit(solution)/shard_map/mate_got/ppermute | solution.py:29
  90.6 55.1 %collective-permute-start.31 = (bf16[3696,256]{1,0:T(8,128)(2,1)S(1)}, bf16[3696,256]{1,0:T(8,128)(2,1)S(1)}, u32[]{:S(2)}, u32[]{:S(2)}) collective-permute-start(bf16[3696,256]{1,0:T(8,128)(2,1)S(1)} %add_convert_fusion.1), channel_id=1, source_target_pairs={{0,3},{1,2},{2,1},{3,0},{4,7},{5,6},{6,5},{7,4},{8,11},{9,10},{10,... | collective-permute-start | bytes 5677064 | tf_op jit(solution)/shard_map/w_recv/ppermute | solution.py:29
  91.5 13.7 %collective-permute-start.20 = (bf16[64,3696]{1,0:T(8,128)(2,1)S(1)}, bf16[64,3696]{1,0:T(8,128)(2,1)S(1)}, u32[]{:S(2)}, u32[]{:S(2)}) collective-permute-start(bf16[64,3696]{1,0:T(8,128)(2,1)S(1)} %get-tuple-element.74), channel_id=1, source_target_pairs={{0,1},{1,0},{2,3},{3,2},{4,5},{5,4},{6,7},{7,6},{8,9},{9,8},{10,11... | collective-permute-start | bytes 1419272 | tf_op jit(solution)/shard_map/t0/ppermute | solution.py:29
  92.5 23.0 %collective-permute-start.25 = (bf16[64,3696]{1,0:T(8,128)(2,1)S(1)}, bf16[64,3696]{1,0:T(8,128)(2,1)S(1)}, u32[]{:S(2)}, u32[]{:S(2)}) collective-permute-start(bf16[64,3696]{1,0:T(8,128)(2,1)S(1)} %get-tuple-element.90), channel_id=1, source_target_pairs={{0,1},{1,0},{2,3},{3,2},{4,5},{5,4},{6,7},{7,6},{8,9},{9,8},{10,11... | collective-permute-start | bytes 1419272 | tf_op jit(solution)/shard_map/t1/ppermute | solution.py:29
  93.6 15.0 %copy-start.3 = (bf16[64,3696]{1,0:T(8,128)(2,1)S(1)}, bf16[64,3696]{1,0:T(8,128)(2,1)}, u32[]{:S(2)}) copy-start(bf16[64,3696]{1,0:T(8,128)(2,1)} %copy-done.1) | copy-start | bytes 1419268
  93.6 15.0 %copy-start.10 = (bf16[64,3696]{1,0:T(8,128)(2,1)S(1)}, bf16[64,3696]{1,0:T(8,128)(2,1)}, u32[]{:S(2)}) copy-start(bf16[64,3696]{1,0:T(8,128)(2,1)} %refs_4_.3) | copy-start | bytes 1419268
  93.6 32.0 %collective-permute-start.22 = (bf16[64,3696]{1,0:T(8,128)(2,1)S(1)}, bf16[64,3696]{1,0:T(8,128)(2,1)S(1)}, u32[]{:S(2)}, u32[]{:S(2)}) collective-permute-start(bf16[64,3696]{1,0:T(8,128)(2,1)S(1)} %get-tuple-element.83), channel_id=1, source_target_pairs={{0,1},{1,0},{2,3},{3,2},{4,5},{5,4},{6,7},{7,6},{8,9},{9,8},{10,11... | collective-permute-start | bytes 1419272 | tf_op jit(solution)/shard_map/t2/ppermute | solution.py:29
  105.4 11.2 %collective-permute-start.24 = (bf16[32,3696]{1,0:T(8,128)(2,1)S(1)}, bf16[32,3696]{1,0:T(8,128)(2,1)S(1)}, u32[]{:S(2)}, u32[]{:S(2)}) collective-permute-start(bf16[32,3696]{1,0:T(8,128)(2,1)S(1)} %get-tuple-element.86), channel_id=1, source_target_pairs={{0,12},{1,13},{2,14},{3,15},{4,0},{5,1},{6,2},{7,3},{8,4},{9,5},{1... | collective-permute-start | bytes 709640 | tf_op jit(solution)/shard_map/from_up/ppermute | solution.py:29
  107.3 19.1 %copy-start.5 = (bf16[144,1024]{1,0:T(8,128)(2,1)S(1)}, bf16[144,1024]{1,0:T(8,128)(2,1)}, u32[]{:S(2)}) copy-start(bf16[144,1024]{1,0:T(8,128)(2,1)} %copy-done.4) | copy-start | bytes 884740
  107.3 19.1 %copy-start.8 = (bf16[128,512]{1,0:T(8,128)(2,1)S(1)}, bf16[128,512]{1,0:T(8,128)(2,1)}, u32[]{:S(2)}) copy-start(bf16[128,512]{1,0:T(8,128)(2,1)} %stream.2) | copy-start | bytes 393220
  107.3 20.0 %collective-permute-start.23 = (bf16[32,3696]{1,0:T(8,128)(2,1)S(1)}, bf16[32,3696]{1,0:T(8,128)(2,1)S(1)}, u32[]{:S(2)}, u32[]{:S(2)}) collective-permute-start(bf16[32,3696]{1,0:T(8,128)(2,1)S(1)} %get-tuple-element.80), channel_id=1, source_target_pairs={{0,4},{1,5},{2,6},{3,7},{4,8},{5,9},{6,10},{7,11},{8,12},{9,13},{1... | collective-permute-start | bytes 709640 | tf_op jit(solution)/shard_map/from_down/ppermute | solution.py:29
  116.7 12.7 %collective-permute-start.26 = (bf16[32,3696]{1,0:T(8,128)(2,1)S(1)}, bf16[32,3696]{1,0:T(8,128)(2,1)S(1)}, u32[]{:S(2)}, u32[]{:S(2)}) collective-permute-start(bf16[32,3696]{1,0:T(8,128)(2,1)S(1)} %get-tuple-element.92), channel_id=1, source_target_pairs={{0,12},{1,13},{2,14},{3,15},{4,0},{5,1},{6,2},{7,3},{8,4},{9,5},{1... | collective-permute-start | bytes 709640 | tf_op jit(solution)/shard_map/pure_a/ppermute | solution.py:29
  120.4 9.6 %collective-permute-start.27 = (bf16[32,3696]{1,0:T(8,128)(2,1)S(1)}, bf16[32,3696]{1,0:T(8,128)(2,1)S(1)}, u32[]{:S(2)}, u32[]{:S(2)}) collective-permute-start(bf16[32,3696]{1,0:T(8,128)(2,1)S(1)} %get-tuple-element.93), channel_id=1, source_target_pairs={{0,4},{1,5},{2,6},{3,7},{4,8},{5,9},{6,10},{7,11},{8,12},{9,13},{1... | collective-permute-start | bytes 709640 | tf_op jit(solution)/shard_map/pure_b/ppermute | solution.py:29
  125.5 12.8 %collective-permute-start.30 = (bf16[64,3696]{1,0:T(8,128)(2,1)S(1)}, bf16[64,3696]{1,0:T(8,128)(2,1)S(1)}, u32[]{:S(2)}, u32[]{:S(2)}) collective-permute-start(bf16[64,3696]{1,0:T(8,128)(2,1)S(1)} %get-tuple-element.96), channel_id=1, source_target_pairs={{0,1},{1,0},{2,3},{3,2},{4,5},{5,4},{6,7},{7,6},{8,9},{9,8},{10,11... | collective-permute-start | bytes 1419272 | tf_op jit(solution)/shard_map/t3/ppermute | solution.py:29
  130.0 10.2 %collective-permute-start.28 = (bf16[32,3696]{1,0:T(8,128)(2,1)S(1)}, bf16[32,3696]{1,0:T(8,128)(2,1)S(1)}, u32[]{:S(2)}, u32[]{:S(2)}) collective-permute-start(bf16[32,3696]{1,0:T(8,128)(2,1)S(1)} %get-tuple-element.94), channel_id=1, source_target_pairs={{0,4},{1,5},{2,6},{3,7},{4,8},{5,9},{6,10},{7,11},{8,12},{9,13},{1... | collective-permute-start | bytes 709640 | tf_op jit(solution)/shard_map/mixed_a/ppermute | solution.py:29
  134.1 11.5 %collective-permute-start.29 = (bf16[32,3696]{1,0:T(8,128)(2,1)S(1)}, bf16[32,3696]{1,0:T(8,128)(2,1)S(1)}, u32[]{:S(2)}, u32[]{:S(2)}) collective-permute-start(bf16[32,3696]{1,0:T(8,128)(2,1)S(1)} %get-tuple-element.95), channel_id=1, source_target_pairs={{0,12},{1,13},{2,14},{3,15},{4,0},{5,1},{6,2},{7,3},{8,4},{9,5},{1... | collective-permute-start | bytes 709640 | tf_op jit(solution)/shard_map/mixed_b/ppermute | solution.py:29
  146.3 6.7 %collective-permute-start.32 = (bf16[3696,512]{1,0:T(8,128)(2,1)S(1)}, bf16[3696,512]{1,0:T(8,128)(2,1)S(1)}, u32[]{:S(2)}, u32[]{:S(2)}) collective-permute-start(bf16[3696,512]{1,0:T(8,128)(2,1)S(1)} %merge_body.1), channel_id=1, source_target_pairs={{0,128},{128,0},{1,129},{129,1},{2,130},{130,2},{3,131},{131,3},{4... | collective-permute-start | bytes 11354120 | tf_op jit(solution)/shard_map/part/ppermute | solution.py:29

commit v6 on v5

--- a/solution.py
+++ b/solution.py
@@ -67,7 +67,7 @@
     return r % 4, r // 4, c % 4, c // 4
 
 
-def prep_body(stream, gain, head, reward, segment, out, owed, s_v, g_v, h_v, r_v, i_v, sems):
+def prep_body(stream, gain, head, reward, segment, out, s_v, g_v, h_v, r_v, i_v, sems):
     moves = [
         pltpu.make_async_copy(src, dst, sems.at[i])
         for i, (src, dst) in enumerate(
@@ -92,20 +92,6 @@
     for i, a in enumerate(rows):
         extra = jnp.where(line == i, jnp.broadcast_to(a, (16, 512)), extra)
     out[128:144] = extra.astype(bf16)
-    owed[...] = jnp.zeros(owed.shape, f32)
-    for i, a in enumerate(rows[3:]):
-        for j in range(4):
-            owed[4 * i + j : 4 * i + j + 1] = a[:, 128 * j : 128 * j + 128]
-
-
-def wide_body(own, mate, owed, out):
-    out[:, :512] = own[...]
-    out[:, 512:] = mate[...]
-    extra = own[128:144].astype(f32)
-    theirs = jnp.concatenate([owed[i : i + 1] for i in range(4)], 1)
-    line = lax.broadcasted_iota(jnp.int32, extra.shape, 0)
-    extra = jnp.where(line == 4, jnp.broadcast_to(theirs, extra.shape), extra)
-    out[128:144, :512] = extra.astype(bf16)
 
 
 def pick_body(own, other, out, sums, owed):
@@ -123,10 +109,10 @@
     even = lax.rem(x, 2) == 0
     first = jnp.where(even, mine, theirs)
     second = jnp.where(even, theirs, mine)
-    for i, a in enumerate((first[3:4], second[3:4], first[4:5], second[4:5])):
-        at = (0, 1, 4, 5)[i]
-        owed[at : at + 1] = a[:, 0:128] + a[:, 128:256] + a[:, 256:384]
-        owed[2 + at : 3 + at] = a[:, 384:512]
+    for i, a in enumerate((first[3:4], second[3:4])):
+        owed[i : i + 1] = a[:, 0:128] + a[:, 128:256] + a[:, 256:384]
+        owed[2 + i : 3 + i] = a[:, 384:512]
+    owed[4:8] = jnp.zeros((4, 128), f32)
     out[128:144] = mine.astype(bf16)
     gw = gains_of(own)
 
@@ -149,7 +135,7 @@
     x, zlo, y, _ = place()
 
     def side(src, at):
-        near, away = src[at : at + 2], src[16 + at : 18 + at]
+        near, away = src[at : at + 2], src[24 + at : 26 + at]
         low, high = jnp.where(x // 2 == 0, near, away), jnp.where(x // 2 == 0, away, near)
         return jnp.concatenate([low, high], 0)
 
@@ -157,8 +143,8 @@
         mine, theirs = side(here, at), side(there, at)
         return jnp.where(zlo == 0, mine, theirs), jnp.where(zlo == 0, theirs, mine)
 
-    value = jnp.concatenate([*rows(8), *rows(12)], 0)
-    segment = jnp.concatenate([*rows(10), *rows(14)], 0)
+    value = jnp.concatenate([*rows(8), *rows(16)], 0)
+    segment = jnp.concatenate([*rows(10), *rows(18)], 0)
     shape = value.shape
     line = lax.broadcasted_iota(jnp.int32, shape, 0) % 8
     lane = lax.broadcasted_iota(jnp.int32, shape, 1)
@@ -186,7 +172,7 @@
         b = x // 2 if i % 2 == 0 else 1 - x // 2
         wanted.append(target[pl.ds(4 * zl + 2 * b + y // 2, 1)])
         src = (here, there)[i // 2]
-        at = 16 * (i % 2)
+        at = 24 * (i % 2)
         sq.append(src[at : at + 1])
         lin.append(src[at + 1 : at + 2])
     wanted, sq, lin = (jnp.concatenate(a, 0) for a in (wanted, sq, lin))
@@ -304,27 +290,34 @@
 
 def outer_body(*refs, first, split):
     (far_a, far_b, up, down, here, y0, y12, y3), (g_own, g_other) = refs[:8], refs[8:10]
-    *outs, h_v, g_v = refs[10:]
+    *outs, h_v, g_v, sems = refs[10:]
     p = lax.axis_index("dp")
-    for at, src in (
-        (0, far_a[...]),
-        (32, far_b[...]),
-        (64, up[32:64]),
-        (96, down[0:32]),
-        (128, up[0:32]),
-        (160, down[32:64]),
-        (192, here[...]),
-        (256, y0[...]),
-        (320, y12[32:96]),
-        (384, y12[0:32]),
-        (416, y12[96:128]),
-        (448, y3[...]),
-    ):
-        h_v[at : at + src.shape[0]] = src
+    moves = (
+        (0, far_a, 0, 32),
+        (32, far_b, 0, 32),
+        (64, up, 32, 64),
+        (96, down, 0, 32),
+        (128, up, 0, 32),
+        (160, down, 32, 64),
+        (192, here, 0, 64),
+        (256, y0, 0, 64),
+        (320, y12, 32, 96),
+        (384, y12, 0, 32),
+        (416, y12, 96, 128),
+        (448, y3, 0, 64),
+    )
+    moves = [
+        pltpu.make_async_copy(src.at[a:b], h_v.at[at : at + b - a], sems.at[i])
+        for i, (at, src, a, b) in enumerate(moves)
+    ]
+    for m in moves:
+        m.start()
     for n, side in enumerate((1 - p, p) if split else (0, 1)):
         start = pl.multiple_of(first + 256 * side, 256)
         g_v[:256, 256 * n : 256 * n + 256] = g_own[:, pl.ds(start, 256)]
         g_v[256:, 256 * n : 256 * n + 256] = g_other[:, pl.ds(start, 256)]
+    for m in moves:
+        m.wait()
     for f in range(0, 3696, 512):
         e = min(f + 512, 3696)
         out = lax.dot_general(
@@ -343,7 +336,13 @@
         functools.partial(outer_body, first=first, split=split),
         out,
         (*pieces, g_own, g_other),
-        scratch=[pltpu.VMEM((512, 3696), bf16), pltpu.VMEM((512, 512), bf16)],
+        in_specs=[pl.BlockSpec(memory_space=pl.ANY)] * 8
+        + [pl.BlockSpec(memory_space=pltpu.VMEM)] * 2,
+        scratch=[
+            pltpu.VMEM((512, 3696), bf16),
+            pltpu.VMEM((512, 512), bf16),
+            pltpu.SemaphoreType.DMA((12,)),
+        ],
         flops=512 * 1024 * 3696,
         moved=8 << 20,
         name=name,
@@ -386,9 +385,9 @@
     vmem = pl.BlockSpec(memory_space=pltpu.VMEM)
     hbm = pl.BlockSpec(memory_space=pl.ANY)
 
-    payload, owed = call(
+    payload = call(
         prep_body,
-        (sds((144, 512), bf16), sds((8, 128), f32)),
+        sds((144, 512), bf16),
         (stream, norm_gain[None], value_head[None], rewards, segments),
         in_specs=[hbm] * 5,
         scratch=[
@@ -410,8 +409,7 @@
     w_half = lax.dynamic_slice_in_dim(w_down, p * HIGH, LO, 0)
     got = col(after(w_half, payload_mate), MATE, "got")
 
-    owed_other = core(owed, "owed_other")
-    block = call(wide_body, sds((144, 1024), bf16), (payload, payload_mate, owed_other))
+    block = jnp.concatenate([payload, payload_mate], 1)
     near, sums, owed = call(
         pick_body,
         (sds((144, 1024), bf16), sds((8, 128), f32), sds((8, 128), f32)),
@@ -420,6 +418,7 @@
     away = row(near, XTHREE, "block_x3")
     here = jnp.concatenate([near, away], 0)
     there = row(here, ZLO, "block_zlo")
+    owed_other = core(owed, "owed_other")
 
     gates = ((y3,), (down, up), (away,))
     for i, perm in enumerate((PAIR, ZONE, ZTHREE)):
@@ -427,12 +426,11 @@
         sums = sums + col(sums, perm, f"sums{i}")
         if i == 0:
             down, up = lax.optimization_barrier((down, up, sums))[:2]
+            far_a = col(down[:32], ZUP, "far_a")
             far_b = col(up[32:], ZDOWN, "far_b")
             y12 = col(jnp.concatenate([up, down], 0), PAIR, "y12")
-        if i == 1:
-            far_a = col(after(down[:32], sums), ZUP, "far_a")
     y0 = col(after(jnp.concatenate([far_a, far_b], 0), sums), PAIR, "y0")
-    tiny = jnp.concatenate([sums, owed], 0)
+    tiny = jnp.concatenate([sums, owed, owed_other], 0)
     tiny = after(tiny, far_a, far_b)
     tiny = jnp.concatenate([tiny, row(tiny, XTHREE, "tiny_x3")], 0)
     tiny_zlo = row(tiny, ZLO, "tiny_zlo")
@@ -476,7 +474,7 @@
     mixed_a = col(q2a, ZUP, "mixed_a")
     mixed_b = col(q2b, ZDOWN, "mixed_b")
     part = call(
-        merge_body, sds((3696, 512), bf16), (after(partial, mixed_a, mixed_b, t[3]), w_recv)
+        merge_body, sds((3696, 512), bf16), (after(partial, q2a), w_recv)
     )
     part_other = core(part, "part")
     weight_grad = (part.astype(f32) + part_other.astype(f32)).astype(bf16)

time: 158 us -> 156 us (0.987)
  waiting for transfers between devices: 66.8 us -> 60.4 us
  Pallas kernels: 23.6 us -> 28.7 us
    ppermute x33, waiting for transfers between devices: 66.8 us -> 60.4 us  [send(): return lax.ppermute(a, axis, perm)]
    pallas_call x15 -> x14, Pallas kernels: 23.6 us -> 28.7 us  [call(): pl.pallas_call(body, out_shape=out_shape, scratch_shapes=list(scratch), c...]
    unnamed x26 -> x24, local copies, waits for them, and re-layouts: 4.67 us -> 3.75 us
  transfers between devices with their start and end apart: 33 -> 33, of which waited for: 19 -> 17; matrix products, arithmetic and copies ran while one was open for 9% -> 9% of each run, Pallas kernels for 14% -> 17%
where the time goes in v6:
time: 156 us; the launch traced here: 155 us
  waiting for transfers between devices  60.4 us (39%)
  starting transfers between devices  43.9 us (28%)
  Pallas kernels  28.7 us (18%)
  local copies, waits for them, and re-layouts  13.6 us (9%)
  other arithmetic  7.19 us (5%)
    ppermute x33, waiting for transfers between devices, send(): return lax.ppermute(a, axis, perm)  60.4 us
    ppermute x33, starting transfers between devices, send(): return lax.ppermute(a, axis, perm)  43.9 us
    pallas_call x14, Pallas kernels, call(): pl.pallas_call(body, out_shape=out_shape, scratch_shapes=list(scratch), c...  28.7 us
    unnamed x24, local copies, waits for them, and re-layouts  3.75 us
  transfers between devices with their start and end apart: 33, of which 17 were waited for; matrix products, arithmetic and copies ran while one was open for 9% of the time, Pallas kernels for 17%

profile of v6, /device:TPU:6, one launch (start us, length us, event | category | flops | bytes accessed | tf_op | source)
XLA Modules:
  0.0 155.2 jit_solution(7849954672648756662)
XLA Ops:
  0.6 1.6 %prep_body.1 = bf16[144,512]{1,0:T(8,128)(2,1)} custom-call(bf16[128,512]{1,0:T(8,128)(2,1)} %stream.2, f32[1,512]{1,0:T(1,128)} %bitcast.2, f32[1,512]{1,0:T(1,128)} %bitcast.3, f32[1,128]{1,0:T(1,128)} %reward.1, s32[1,128]{1,0:T(1,128)} %segment.1), custom_call_target="tpu_custom_call" | custom-call | tf_op jit(solution)/shard_map/prep_body/pallas_call | solution.py:55
  2.3 3.1 %collective-permute-start.2 = (bf16[144,512]{1,0:T(8,128)(2,1)}, bf16[144,512]{1,0:T(8,128)(2,1)S(1)}, u32[]{:S(2)}, u32[]{:S(2)}) collective-permute-start(bf16[144,512]{1,0:T(8,128)(2,1)} %prep_body.1), channel_id=1, source_target_pairs={{0,3},{1,2},{2,1},{3,0},{4,7},{5,6},{6,5},{7,4},{8,11},{9,10},{10,... | collective-permute-start | bytes 442376 | tf_op jit(solution)/shard_map/payload_mate/ppermute | solution.py:29
  5.5 3.3 %collective-permute-start = (bf16[64,3696]{1,0:T(8,128)(2,1)}, bf16[64,3696]{1,0:T(8,128)(2,1)S(1)}, u32[]{:S(2)}, u32[]{:S(2)}) collective-permute-start(bf16[64,3696]{1,0:T(8,128)(2,1)} %refs_4_.3), channel_id=1, source_target_pairs={{0,4},{1,5},{2,6},{3,7},{4,8},{5,9},{6,10},{7,11},{8,12},{9,13},{1... | collective-permute-start | bytes 1419272 | tf_op jit(solution)/shard_map/down/ppermute | solution.py:29
  8.8 3.0 %collective-permute-start.1 = (bf16[64,3696]{1,0:T(8,128)(2,1)}, bf16[64,3696]{1,0:T(8,128)(2,1)S(1)}, u32[]{:S(2)}, u32[]{:S(2)}) collective-permute-start(bf16[64,3696]{1,0:T(8,128)(2,1)} %refs_4_.3), channel_id=1, source_target_pairs={{0,12},{1,13},{2,14},{3,15},{4,0},{5,1},{6,2},{7,3},{8,4},{9,5},{1... | collective-permute-start | bytes 1419272 | tf_op jit(solution)/shard_map/up/ppermute | solution.py:29
  11.8 0.9 pad_maximum_fusion.2.own
  12.8 0.9 collective-permute-start.3
  13.7 2.9 %constant_dynamic-slice_fusion = bf16[1856,512]{1,0:T(8,128)(2,1)} fusion(bf16[3696,512]{1,0:T(8,128)(2,1)} %w.3, s32[]{:T(128)S(6)} %select_n.3), kind=kLoop, calls=%fused_computation.10 | loop fusion | bytes 3801092 | tf_op jit(solution)/shard_map/dynamic_slice | solution.py:409
  16.6 1.1 collective-permute-start.15
  17.6 3.3 %collective-permute-done.3.other = bf16[144,1024]{1,0:T(8,128)(2,1)S(1)} collective-permute-done((bf16[144,1024]{1,0:T(8,128)(2,1)S(1)}, bf16[144,1024]{1,0:T(8,128)(2,1)S(1)}, u32[]{:S(2)}, u32[]{:S(2)}) %collective-permute-start.3) | collective-permute-done | bytes 294944 | tf_op jit(solution)/shard_map/block_x1/ppermute | solution.py:29
  21.1 0.6 collective-permute-start.9
  21.7 1.7 %collective-permute-start.5 = (f32[8,128]{1,0:T(8,128)S(1)}, f32[8,128]{1,0:T(8,128)S(1)}, u32[]{:S(2)}, u32[]{:S(2)}) collective-permute-start(f32[8,128]{1,0:T(8,128)S(1)} %get-tuple-element.51), channel_id=1, source_target_pairs={{0,1},{1,0},{2,3},{3,2},{4,5},{5,4},{6,7},{7,6},{8,9},{9,8},{10,11... | collective-permute-start | bytes 12296 | tf_op jit(solution)/shard_map/sums0/ppermute | solution.py:29
  23.4 0.7 constant_dynamic-update-slice_fusion.3
  24.2 1.1 collective-permute-done.5
  25.3 1.3 collective-permute-done.refs_3_
  26.6 7.3 %collective-permute-done.1.refs_2_ = bf16[64,3696]{1,0:T(8,128)(2,1)S(1)} collective-permute-done((bf16[64,3696]{1,0:T(8,128)(2,1)}, bf16[64,3696]{1,0:T(8,128)(2,1)S(1)}, u32[]{:S(2)}, u32[]{:S(2)}) %collective-permute-start.1) | collective-permute-done | bytes 473120 | tf_op jit(solution)/shard_map/up/ppermute | solution.py:29
  33.9 3.8 %collective-permute-start.8 = (f32[8,128]{1,0:T(8,128)S(1)}, f32[8,128]{1,0:T(8,128)S(1)}, u32[]{:S(2)}, u32[]{:S(2)}) collective-permute-start(f32[8,128]{1,0:T(8,128)S(1)} %add.18), channel_id=1, source_target_pairs={{0,4},{1,5},{2,6},{3,7},{4,0},{5,1},{6,2},{7,3},{8,12},{9,13},{10,... | collective-permute-start | bytes 12296 | tf_op jit(solution)/shard_map/sums1/ppermute | solution.py:29
  37.6 0.7 slice.6
  38.4 0.7 slice.7
  39.2 4.1 %collective-permute-start.7 = (bf16[32,3696]{1,0:T(8,128)(2,1)}, bf16[32,3696]{1,0:T(8,128)(2,1)}, u32[]{:S(2)}, u32[]{:S(2)}) collective-permute-start(bf16[32,3696]{1,0:T(8,128)(2,1)} %slice.7), channel_id=1, source_target_pairs={{0,12},{1,13},{2,14},{3,15},{4,0},{5,1},{6,2},{7,3},{8,4},{9,5},{1... | collective-permute-start | bytes 709640 | tf_op jit(solution)/shard_map/far_b/ppermute | solution.py:29
  43.2 1.0 pad_maximum_fusion
  44.3 2.2 %copy.11 = bf16[128,3696]{0,1:T(8,128)(2,1)} copy(bf16[128,3696]{1,0:T(8,128)(2,1)} %pad_maximum_fusion) | data formatting | bytes 1892352 | tf_op jit(solution)/shard_map/concatenate | solution.py:431
  46.5 1.7 %collective-permute-start.12 = (bf16[128,3696]{0,1:T(8,128)(2,1)}, bf16[128,3696]{0,1:T(8,128)(2,1)}, u32[]{:S(2)}, u32[]{:S(2)}) collective-permute-start(bf16[128,3696]{0,1:T(8,128)(2,1)} %copy.11), channel_id=1, source_target_pairs={{0,1},{1,0},{2,3},{3,2},{4,5},{5,4},{6,7},{7,6},{8,9},{9,8},{10,11... | collective-permute-start | bytes 2838536 | tf_op jit(solution)/shard_map/y12/ppermute | solution.py:29
  48.2 1.7 %constant_dynamic-update-slice_fusion.2.here = bf16[288,1024]{1,0:T(8,128)(2,1)} fusion(bf16[288,1024]{1,0:T(8,128)(2,1)} %constant_dynamic-update-slice_fusion.3, bf16[144,1024]{1,0:T(8,128)(2,1)} %collective-permute-done.9), kind=kLoop, calls=%fused_computation.8 | loop fusion | bytes 589824 | tf_op jit(solution)/shard_map/concatenate | solution.py:419
  50.0 2.5 %collective-permute-start.17 = (bf16[288,1024]{1,0:T(8,128)(2,1)}, bf16[288,1024]{1,0:T(8,128)(2,1)}, u32[]{:S(2)}, u32[]{:S(2)}) collective-permute-start(bf16[288,1024]{1,0:T(8,128)(2,1)} %constant_dynamic-update-slice_fusion.2.here), channel_id=1, source_target_pairs={{0,64},{16,80},{32,96},{48,112},{64,0},{80,16},{96,32},{112,48},{1... | collective-permute-start | bytes 1769480 | tf_op jit(solution)/shard_map/block_zlo/ppermute | solution.py:29
  52.5 1.8 %pad_maximum_fusion.1 = bf16[64,3696]{1,0:T(8,128)(2,1)} fusion(bf16[32,3696]{1,0:T(8,128)(2,1)} %collective-permute-done.7.refs_1_, bf16[32,3696]{1,0:T(8,128)(2,1)S(1)} %collective-permute-done.6.refs_0_), kind=kLoop, calls=%fused_computation.3 | loop fusion | flops 946176 | bytes 946176 | tf_op jit(solution)/shard_map/concatenate | solution.py:432
  54.3 1.8 %collective-permute-start.11 = (bf16[64,3696]{1,0:T(8,128)(2,1)}, bf16[64,3696]{1,0:T(8,128)(2,1)}, u32[]{:S(2)}, u32[]{:S(2)}) collective-permute-start(bf16[64,3696]{1,0:T(8,128)(2,1)} %pad_maximum_fusion.1), channel_id=1, source_target_pairs={{0,1},{1,0},{2,3},{3,2},{4,5},{5,4},{6,7},{7,6},{8,9},{9,8},{10,11... | collective-permute-start | bytes 1419272 | tf_op jit(solution)/shard_map/y0/ppermute | solution.py:29
  56.0 1.2 collective-permute-done.13
  57.2 0.5 collective-permute-start.14
  57.7 4.4 %collective-permute-done.14 = f32[24,128]{1,0:T(8,128)S(1)} collective-permute-done((f32[24,128]{1,0:T(8,128)S(1)}, f32[24,128]{1,0:T(8,128)S(1)}, u32[]{:S(2)}, u32[]{:S(2)}) %collective-permute-start.14) | collective-permute-done | bytes 12320 | tf_op jit(solution)/shard_map/tiny_x3/ppermute | solution.py:29
  62.5 3.5 %collective-permute-done.16.there = f32[48,128]{1,0:T(8,128)S(1)} collective-permute-done((f32[48,128]{1,0:T(8,128)S(1)}, f32[48,128]{1,0:T(8,128)S(1)}, u32[]{:S(2)}, u32[]{:S(2)}) %collective-permute-start.16) | collective-permute-done | bytes 24608 | tf_op jit(solution)/shard_map/tiny_zlo/ppermute | solution.py:29
  66.6 0.8 coefs_body.1.coefs
  67.4 0.5 collective-permute-start.18
  67.9 2.8 %collective-permute-done.12 = bf16[128,3696]{0,1:T(8,128)(2,1)} collective-permute-done((bf16[128,3696]{0,1:T(8,128)(2,1)}, bf16[128,3696]{0,1:T(8,128)(2,1)}, u32[]{:S(2)}, u32[]{:S(2)}) %collective-permute-start.12) | collective-permute-done | bytes 946208 | tf_op jit(solution)/shard_map/y12/ppermute | solution.py:29
  70.7 1.6 %copy.13.refs_6_ = bf16[128,3696]{1,0:T(8,128)(2,1)S(1)} copy(bf16[128,3696]{0,1:T(8,128)(2,1)} %collective-permute-done.12) | data formatting | bytes 1892352 | tf_op jit(solution)/shard_map/y12/ppermute | solution.py:29
  72.3 2.4 %grad_body.1 = (bf16[256,1024]{1,0:T(8,128)(2,1)S(1)}, bf16[256,1024]{1,0:T(8,128)(2,1)S(1)}) custom-call(f32[8,128]{1,0:T(8,128)S(1)} %coefs_body.1.coefs, bf16[288,1024]{1,0:T(8,128)(2,1)} %constant_dynamic-update-slice_fusion.2.here, bf16[288,1024]{1,0:T(8,128)(2,1)} %collective-permute-done.17.there), custom_call_target="tpu_custom_call" | custom-call | bytes 4194304 | tf_op jit(solution)/shard_map/grad_body/pallas_call | solution.py:55
  74.7 3.3 %collective-permute-done.11.refs_5_ = bf16[64,3696]{1,0:T(8,128)(2,1)} collective-permute-done((bf16[64,3696]{1,0:T(8,128)(2,1)}, bf16[64,3696]{1,0:T(8,128)(2,1)}, u32[]{:S(2)}, u32[]{:S(2)}) %collective-permute-start.11) | collective-permute-done | bytes 473120 | tf_op jit(solution)/shard_map/y0/ppermute | solution.py:29
  78.0 1.0 copy-done.2
  79.0 0.9 copy-done.7
  80.0 1.0 copy-done.9
  81.0 6.0 %outer_mate.1 = (bf16[3696,256]{1,0:T(8,128)(2,1)S(1)}, f32[3696,256]{1,0:T(8,128)S(1)}) custom-call(bf16[32,3696]{1,0:T(8,128)(2,1)S(1)} %copy-done.7, bf16[32,3696]{1,0:T(8,128)(2,1)} %collective-permute-done.7.refs_1_, bf16[64,3696]{1,0:T(8,128)(2,1)S(1)} %copy-done.2, bf16[64,3696]{1,0:T(8,128)(2,1)S(1)} %collective-permute-done.refs_3_, ...), custom_call_target="tpu_custom_call" | custom-call | flops 1937768448 | bytes 8388608 | tf_op jit(solution)/shard_map/outer_mate/pallas_call | solution.py:55
  87.1 4.4 %inner_sent.1 = (bf16[64,3696]{1,0:T(8,128)(2,1)S(1)}, bf16[64,3696]{1,0:T(8,128)(2,1)S(1)}, bf16[64,3696]{1,0:T(8,128)(2,1)S(1)}, bf16[64,3696]{1,0:T(8,128)(2,1)S(1)}) custom-call(bf16[256,1024]{1,0:T(8,128)(2,1)S(1)} %get-tuple-element.66.refs_9_.g, bf16[3696,512]{1,0:T(8,128)(2,1)S(1)} %copy-done, bf16[1856,512]{1,0:T(8,128)(2,1)S(1)} %collective-permute-done.15.got, ...), custom_call_target="tpu_custom_call" | custom-call | flops 1937768448 | bytes 10485760 | tf_op jit(solution)/shard_map/inner_sent/pallas_call | solution.py:55
  91.6 0.5 add_convert_fusion.1
  92.1 1.0 collective-permute-start.28
  93.1 0.9 collective-permute-start.20
  94.0 1.1 collective-permute-start.25
  95.1 4.4 %inner_own.1 = (f32[64,3696]{1,0:T(8,128)S(1)}, f32[64,3696]{1,0:T(8,128)S(1)}, f32[64,3696]{1,0:T(8,128)S(1)}, f32[64,3696]{1,0:T(8,128)S(1)}) custom-call(bf16[256,1024]{1,0:T(8,128)(2,1)S(1)} %get-tuple-element.75.refs_8_.g, bf16[3696,512]{1,0:T(8,128)(2,1)S(1)} %copy-done, bf16[1856,512]{1,0:T(8,128)(2,1)S(1)} %collective-permute-done.15.got, ...), custom_call_target="tpu_custom_call" | custom-call | flops 1937768448 | bytes 10485760 | tf_op jit(solution)/shard_map/inner_own/pallas_call | solution.py:55
  99.5 7.3 %collective-permute-done.20.other = bf16[64,3696]{1,0:T(8,128)(2,1)S(1)} collective-permute-done((bf16[64,3696]{1,0:T(8,128)(2,1)S(1)}, bf16[64,3696]{1,0:T(8,128)(2,1)S(1)}, u32[]{:S(2)}, u32[]{:S(2)}) %collective-permute-start.20) | collective-permute-done | bytes 473120 | tf_op jit(solution)/shard_map/t0/ppermute | solution.py:29
  106.9 0.4 collective-permute-start.24
  107.2 0.8 collective-permute-start.22
  108.0 2.6 %collective-permute-start.23 = (bf16[32,3696]{1,0:T(8,128)(2,1)S(1)}, bf16[32,3696]{1,0:T(8,128)(2,1)S(1)}, u32[]{:S(2)}, u32[]{:S(2)}) collective-permute-start(bf16[32,3696]{1,0:T(8,128)(2,1)S(1)} %get-tuple-element.74), channel_id=1, source_target_pairs={{0,4},{1,5},{2,6},{3,7},{4,8},{5,9},{6,10},{7,11},{8,12},{9,13},{1... | collective-permute-start | bytes 709640 | tf_op jit(solution)/shard_map/from_down/ppermute | solution.py:29
  110.7 6.0 %outer_own.1.partial = f32[3696,512]{1,0:T(8,128)S(1)} custom-call(bf16[32,3696]{1,0:T(8,128)(2,1)S(1)} %copy-done.7, bf16[32,3696]{1,0:T(8,128)(2,1)} %collective-permute-done.7.refs_1_, bf16[64,3696]{1,0:T(8,128)(2,1)S(1)} %copy-done.3, bf16[64,3696]{1,0:T(8,128)(2,1)S(1)} %collective-permute-done.refs_3_, bf16[64,3696]{1,0:T(8,128)(2,1)S(1)} %copy-done.10, ...), custom_call_target="tpu_custom_call" | custom-call | flops 1937768448 | bytes 8388608 | tf_op jit(solution)/shard_map/outer_own/pallas_call | solution.py:55
  117.0 0.4 collective-permute-done.24.refs_1_
  117.5 2.7 %collective-permute-start.26 = (bf16[32,3696]{1,0:T(8,128)(2,1)S(1)}, bf16[32,3696]{1,0:T(8,128)(2,1)S(1)}, u32[]{:S(2)}, u32[]{:S(2)}) collective-permute-start(bf16[32,3696]{1,0:T(8,128)(2,1)S(1)} %get-tuple-element.86), channel_id=1, source_target_pairs={{0,12},{1,13},{2,14},{3,15},{4,0},{5,1},{6,2},{7,3},{8,4},{9,5},{1... | collective-permute-start | bytes 709640 | tf_op jit(solution)/shard_map/pure_a/ppermute | solution.py:29
  120.6 0.9 own_grad_body.1
  121.5 5.6 %collective-permute-done.22.other = bf16[64,3696]{1,0:T(8,128)(2,1)S(1)} collective-permute-done((bf16[64,3696]{1,0:T(8,128)(2,1)S(1)}, bf16[64,3696]{1,0:T(8,128)(2,1)S(1)}, u32[]{:S(2)}, u32[]{:S(2)}) %collective-permute-start.22) | collective-permute-done | bytes 473120 | tf_op jit(solution)/shard_map/t2/ppermute | solution.py:29
  127.2 2.6 %collective-permute-done.26.pure_a = bf16[32,3696]{1,0:T(8,128)(2,1)S(1)} collective-permute-done((bf16[32,3696]{1,0:T(8,128)(2,1)S(1)}, bf16[32,3696]{1,0:T(8,128)(2,1)S(1)}, u32[]{:S(2)}, u32[]{:S(2)}) %collective-permute-start.26) | collective-permute-done | bytes 236576 | tf_op jit(solution)/shard_map/pure_a/ppermute | solution.py:29
  129.9 2.7 %collective-permute-done.27.pure_b = bf16[32,3696]{1,0:T(8,128)(2,1)S(1)} collective-permute-done((bf16[32,3696]{1,0:T(8,128)(2,1)S(1)}, bf16[32,3696]{1,0:T(8,128)(2,1)S(1)}, u32[]{:S(2)}, u32[]{:S(2)}) %collective-permute-start.27) | collective-permute-done | bytes 236576 | tf_op jit(solution)/shard_map/pure_b/ppermute | solution.py:29
  132.6 4.8 %collective-permute-done.28.recv = bf16[3696,256]{1,0:T(8,128)(2,1)S(1)} collective-permute-done((bf16[3696,256]{1,0:T(8,128)(2,1)S(1)}, bf16[3696,256]{1,0:T(8,128)(2,1)S(1)}, u32[]{:S(2)}, u32[]{:S(2)}) %collective-permute-start.28) | collective-permute-done | bytes 1892384 | tf_op jit(solution)/shard_map/w_recv/ppermute | solution.py:29
  137.3 0.6 merge_body.1
  138.1 0.5 collective-permute-start.30
  138.7 4.1 %collective-permute-start.32 = (bf16[32,3696]{1,0:T(8,128)(2,1)S(1)}, bf16[32,3696]{1,0:T(8,128)(2,1)S(1)}, u32[]{:S(2)}, u32[]{:S(2)}) collective-permute-start(bf16[32,3696]{1,0:T(8,128)(2,1)S(1)} %get-tuple-element.94), channel_id=1, source_target_pairs={{0,12},{1,13},{2,14},{3,15},{4,0},{5,1},{6,2},{7,3},{8,4},{9,5},{1... | collective-permute-start | bytes 709640 | tf_op jit(solution)/shard_map/mixed_b/ppermute | solution.py:29
  142.8 8.5 %collective-permute-done.30.other = bf16[64,3696]{1,0:T(8,128)(2,1)S(1)} collective-permute-done((bf16[64,3696]{1,0:T(8,128)(2,1)S(1)}, bf16[64,3696]{1,0:T(8,128)(2,1)S(1)}, u32[]{:S(2)}, u32[]{:S(2)}) %collective-permute-start.30) | collective-permute-done | bytes 473120 | tf_op jit(solution)/shard_map/t3/ppermute | solution.py:29
  151.3 1.0 here_body.1
  152.3 3.0 %add_convert_fusion = bf16[3696,512]{1,0:T(8,128)(2,1)} fusion(bf16[3696,512]{1,0:T(8,128)(2,1)S(1)} %collective-permute-done.29, bf16[3696,512]{1,0:T(8,128)(2,1)S(1)} %merge_body.1), kind=kLoop, calls=%fused_computation | loop fusion | flops 7569408 | bytes 11354112 | tf_op jit(solution)/shard_map/convert_element_type | solution.py:480
  (56 shorter events, 2.1 us)
Async XLA Ops:
  2.3 9.5 %collective-permute-start.2 = (bf16[144,512]{1,0:T(8,128)(2,1)}, bf16[144,512]{1,0:T(8,128)(2,1)S(1)}, u32[]{:S(2)}, u32[]{:S(2)}) collective-permute-start(bf16[144,512]{1,0:T(8,128)(2,1)} %prep_body.1), channel_id=1, source_target_pairs={{0,3},{1,2},{2,1},{3,0},{4,7},{5,6},{6,5},{7,4},{8,11},{9,10},{10,... | collective-permute-start | bytes 442376 | tf_op jit(solution)/shard_map/payload_mate/ppermute | solution.py:29
  5.4 16.3 %collective-permute-start.4 = (bf16[64,3696]{1,0:T(8,128)(2,1)}, bf16[64,3696]{1,0:T(8,128)(2,1)}, u32[]{:S(2)}, u32[]{:S(2)}) collective-permute-start(bf16[64,3696]{1,0:T(8,128)(2,1)} %refs_4_.3), channel_id=1, source_target_pairs={{0,1},{1,0},{2,3},{3,2},{4,5},{5,4},{6,7},{7,6},{8,9},{9,8},{10,11... | collective-permute-start | bytes 1419272 | tf_op jit(solution)/shard_map/y3/ppermute | solution.py:29
  5.5 21.0 %collective-permute-start = (bf16[64,3696]{1,0:T(8,128)(2,1)}, bf16[64,3696]{1,0:T(8,128)(2,1)S(1)}, u32[]{:S(2)}, u32[]{:S(2)}) collective-permute-start(bf16[64,3696]{1,0:T(8,128)(2,1)} %refs_4_.3), channel_id=1, source_target_pairs={{0,4},{1,5},{2,6},{3,7},{4,8},{5,9},{6,10},{7,11},{8,12},{9,13},{1... | collective-permute-start | bytes 1419272 | tf_op jit(solution)/shard_map/down/ppermute | solution.py:29
  8.8 25.1 %collective-permute-start.1 = (bf16[64,3696]{1,0:T(8,128)(2,1)}, bf16[64,3696]{1,0:T(8,128)(2,1)S(1)}, u32[]{:S(2)}, u32[]{:S(2)}) collective-permute-start(bf16[64,3696]{1,0:T(8,128)(2,1)} %refs_4_.3), channel_id=1, source_target_pairs={{0,12},{1,13},{2,14},{3,15},{4,0},{5,1},{6,2},{7,3},{8,4},{9,5},{1... | collective-permute-start | bytes 1419272 | tf_op jit(solution)/shard_map/up/ppermute | solution.py:29
  12.8 8.1 %collective-permute-start.3 = (bf16[144,1024]{1,0:T(8,128)(2,1)S(1)}, bf16[144,1024]{1,0:T(8,128)(2,1)S(1)}, u32[]{:S(2)}, u32[]{:S(2)}) collective-permute-start(bf16[144,1024]{1,0:T(8,128)(2,1)S(1)} %pad_maximum_fusion.2.own), channel_id=1, source_target_pairs={{0,16},{16,0},{32,48},{48,32},{64,80},{80,64},{96,112},{112,96},{1... | collective-permute-start | bytes 884744 | tf_op jit(solution)/shard_map/block_x1/ppermute | solution.py:29
  16.6 49.3 %collective-permute-start.15 = (bf16[1856,512]{1,0:T(8,128)(2,1)}, bf16[1856,512]{1,0:T(8,128)(2,1)S(1)}, u32[]{:S(2)}, u32[]{:S(2)}) collective-permute-start(bf16[1856,512]{1,0:T(8,128)(2,1)} %constant_dynamic-slice_fusion), channel_id=1, source_target_pairs={{0,3},{1,2},{2,1},{3,0},{4,7},{5,6},{6,5},{7,4},{8,11},{9,10},{10,... | collective-permute-start | bytes 5701640 | tf_op jit(solution)/shard_map/got/ppermute | solution.py:29
  21.1 46.8 %copy-start.4 = (bf16[144,1024]{1,0:T(8,128)(2,1)}, bf16[144,1024]{1,0:T(8,128)(2,1)S(1)}, u32[]{:S(2)}) copy-start(bf16[144,1024]{1,0:T(8,128)(2,1)S(1)} %get-tuple-element.55.block) | copy-start | bytes 884740
  21.1 27.1 %collective-permute-start.9 = (bf16[144,1024]{1,0:T(8,128)(2,1)S(1)}, bf16[144,1024]{1,0:T(8,128)(2,1)}, u32[]{:S(2)}, u32[]{:S(2)}) collective-permute-start(bf16[144,1024]{1,0:T(8,128)(2,1)S(1)} %get-tuple-element.55.block), channel_id=1, source_target_pairs={{0,48},{16,32},{32,16},{48,0},{64,112},{80,96},{96,80},{112,64},{1... | collective-permute-start | bytes 884744 | tf_op jit(solution)/shard_map/block_x3/ppermute | solution.py:29
  21.7 3.6 %collective-permute-start.5 = (f32[8,128]{1,0:T(8,128)S(1)}, f32[8,128]{1,0:T(8,128)S(1)}, u32[]{:S(2)}, u32[]{:S(2)}) collective-permute-start(f32[8,128]{1,0:T(8,128)S(1)} %get-tuple-element.51), channel_id=1, source_target_pairs={{0,1},{1,0},{2,3},{3,2},{4,5},{5,4},{6,7},{7,6},{8,9},{9,8},{10,11... | collective-permute-start | bytes 12296 | tf_op jit(solution)/shard_map/sums0/ppermute | solution.py:29
  33.9 34.0 %copy-start.1 = (bf16[64,3696]{1,0:T(8,128)(2,1)}, bf16[64,3696]{1,0:T(8,128)(2,1)S(1)}, u32[]{:S(2)}) copy-start(bf16[64,3696]{1,0:T(8,128)(2,1)S(1)} %collective-permute-done.1.refs_2_) | copy-start | bytes 1419268
  33.9 12.6 %collective-permute-start.8 = (f32[8,128]{1,0:T(8,128)S(1)}, f32[8,128]{1,0:T(8,128)S(1)}, u32[]{:S(2)}, u32[]{:S(2)}) collective-permute-start(f32[8,128]{1,0:T(8,128)S(1)} %add.18), channel_id=1, source_target_pairs={{0,4},{1,5},{2,6},{3,7},{4,0},{5,1},{6,2},{7,3},{8,12},{9,13},{10,... | collective-permute-start | bytes 12296 | tf_op jit(solution)/shard_map/sums1/ppermute | solution.py:29
  38.4 11.6 %collective-permute-start.6 = (bf16[32,3696]{1,0:T(8,128)(2,1)}, bf16[32,3696]{1,0:T(8,128)(2,1)S(1)}, u32[]{:S(2)}, u32[]{:S(2)}) collective-permute-start(bf16[32,3696]{1,0:T(8,128)(2,1)} %slice.6), channel_id=1, source_target_pairs={{0,4},{1,5},{2,6},{3,7},{4,8},{5,9},{6,10},{7,11},{8,12},{9,13},{1... | collective-permute-start | bytes 709640 | tf_op jit(solution)/shard_map/far_a/ppermute | solution.py:29
  39.2 13.3 %collective-permute-start.7 = (bf16[32,3696]{1,0:T(8,128)(2,1)}, bf16[32,3696]{1,0:T(8,128)(2,1)}, u32[]{:S(2)}, u32[]{:S(2)}) collective-permute-start(bf16[32,3696]{1,0:T(8,128)(2,1)} %slice.7), channel_id=1, source_target_pairs={{0,12},{1,13},{2,14},{3,15},{4,0},{5,1},{6,2},{7,3},{8,4},{9,5},{1... | collective-permute-start | bytes 709640 | tf_op jit(solution)/shard_map/far_b/ppermute | solution.py:29
  46.5 24.2 %collective-permute-start.12 = (bf16[128,3696]{0,1:T(8,128)(2,1)}, bf16[128,3696]{0,1:T(8,128)(2,1)}, u32[]{:S(2)}, u32[]{:S(2)}) collective-permute-start(bf16[128,3696]{0,1:T(8,128)(2,1)} %copy.11), channel_id=1, source_target_pairs={{0,1},{1,0},{2,3},{3,2},{4,5},{5,4},{6,7},{7,6},{8,9},{9,8},{10,11... | collective-permute-start | bytes 2838536 | tf_op jit(solution)/shard_map/y12/ppermute | solution.py:29
  48.2 6.0 %collective-permute-start.10 = (f32[8,128]{1,0:T(8,128)S(1)}, f32[8,128]{1,0:T(8,128)S(1)}, u32[]{:S(2)}, u32[]{:S(2)}) collective-permute-start(f32[8,128]{1,0:T(8,128)S(1)} %add.19), channel_id=1, source_target_pairs={{0,12},{1,13},{2,14},{3,15},{4,8},{5,9},{6,10},{7,11},{8,4},{9,5},... | collective-permute-start | bytes 12296 | tf_op jit(solution)/shard_map/sums2/ppermute | solution.py:29
  50.0 17.9 %copy-start.6 = (bf16[32,3696]{1,0:T(8,128)(2,1)}, bf16[32,3696]{1,0:T(8,128)(2,1)S(1)}, u32[]{:S(2)}) copy-start(bf16[32,3696]{1,0:T(8,128)(2,1)S(1)} %collective-permute-done.6.refs_0_) | copy-start | bytes 709636
  50.0 22.3 %collective-permute-start.17 = (bf16[288,1024]{1,0:T(8,128)(2,1)}, bf16[288,1024]{1,0:T(8,128)(2,1)}, u32[]{:S(2)}, u32[]{:S(2)}) collective-permute-start(bf16[288,1024]{1,0:T(8,128)(2,1)} %constant_dynamic-update-slice_fusion.2.here), channel_id=1, source_target_pairs={{0,64},{16,80},{32,96},{48,112},{64,0},{80,16},{96,32},{112,48},{1... | collective-permute-start | bytes 1769480 | tf_op jit(solution)/shard_map/block_zlo/ppermute | solution.py:29
  54.3 23.7 %collective-permute-start.11 = (bf16[64,3696]{1,0:T(8,128)(2,1)}, bf16[64,3696]{1,0:T(8,128)(2,1)}, u32[]{:S(2)}, u32[]{:S(2)}) collective-permute-start(bf16[64,3696]{1,0:T(8,128)(2,1)} %pad_maximum_fusion.1), channel_id=1, source_target_pairs={{0,1},{1,0},{2,3},{3,2},{4,5},{5,4},{6,7},{7,6},{8,9},{9,8},{10,11... | collective-permute-start | bytes 1419272 | tf_op jit(solution)/shard_map/y0/ppermute | solution.py:29
  56.0 1.2 collective-permute-start.13
  57.2 4.9 %collective-permute-start.14 = (f32[24,128]{1,0:T(8,128)S(1)}, f32[24,128]{1,0:T(8,128)S(1)}, u32[]{:S(2)}, u32[]{:S(2)}) collective-permute-start(f32[24,128]{1,0:T(8,128)S(1)} %pad_maximum_fusion.3), channel_id=1, source_target_pairs={{0,48},{16,32},{32,16},{48,0},{64,112},{80,96},{96,80},{112,64},{1... | collective-permute-start | bytes 36872 | tf_op jit(solution)/shard_map/tiny_x3/ppermute | solution.py:29
  62.1 3.8 %collective-permute-start.16 = (f32[48,128]{1,0:T(8,128)S(1)}, f32[48,128]{1,0:T(8,128)S(1)}, u32[]{:S(2)}, u32[]{:S(2)}) collective-permute-start(f32[48,128]{1,0:T(8,128)S(1)} %constant_dynamic-update-slice_fusion.here), channel_id=1, source_target_pairs={{0,64},{16,80},{32,96},{48,112},{64,0},{80,16},{96,32},{112,48},{1... | collective-permute-start | bytes 73736 | tf_op jit(solution)/shard_map/tiny_zlo/ppermute | solution.py:29
  65.9 21.2 %collective-permute-start.19 = (bf16[1856,512]{1,0:T(8,128)(2,1)S(1)}, bf16[1856,512]{1,0:T(8,128)(2,1)}, u32[]{:S(2)}, u32[]{:S(2)}) collective-permute-start(bf16[1856,512]{1,0:T(8,128)(2,1)S(1)} %collective-permute-done.15.got), channel_id=1, source_target_pairs={{0,128},{128,0},{1,129},{129,1},{2,130},{130,2},{3,131},{131,3},{4... | collective-permute-start | bytes 5701640 | tf_op jit(solution)/shard_map/got_other/ppermute | solution.py:29
  67.4 7.3 %collective-permute-start.18 = (f32[8,128]{1,0:T(8,128)S(1)}, f32[8,128]{1,0:T(8,128)S(1)}, u32[]{:S(2)}, u32[]{:S(2)}) collective-permute-start(f32[8,128]{1,0:T(8,128)S(1)} %coefs_body.1.coefs), channel_id=1, source_target_pairs={{0,3},{1,2},{2,1},{3,0},{4,7},{5,6},{6,5},{7,4},{8,11},{9,10},{10,... | collective-permute-start | bytes 12296 | tf_op jit(solution)/shard_map/coefs_mate/ppermute | solution.py:29
  74.7 12.4 %copy-start = (bf16[3696,512]{1,0:T(8,128)(2,1)S(1)}, bf16[3696,512]{1,0:T(8,128)(2,1)}, u32[]{:S(2)}) copy-start(bf16[3696,512]{1,0:T(8,128)(2,1)} %w.3) | copy-start | bytes 11354116
  78.0 1.0 copy-start.2
  79.0 0.9 copy-start.7
  80.0 1.0 copy-start.9
  87.0 4.5 %collective-permute-start.21 = (bf16[3696,256]{1,0:T(8,128)(2,1)S(1)}, bf16[3696,256]{1,0:T(8,128)(2,1)S(1)}, u32[]{:S(2)}, u32[]{:S(2)}) collective-permute-start(bf16[3696,256]{1,0:T(8,128)(2,1)S(1)} %get-tuple-element.72), channel_id=1, source_target_pairs={{0,128},{128,0},{1,129},{129,1},{2,130},{130,2},{3,131},{131,3},{4... | collective-permute-start | bytes 5677064 | tf_op jit(solution)/shard_map/mate_got/ppermute | solution.py:29
  92.1 45.2 %collective-permute-start.28 = (bf16[3696,256]{1,0:T(8,128)(2,1)S(1)}, bf16[3696,256]{1,0:T(8,128)(2,1)S(1)}, u32[]{:S(2)}, u32[]{:S(2)}) collective-permute-start(bf16[3696,256]{1,0:T(8,128)(2,1)S(1)} %add_convert_fusion.1), channel_id=1, source_target_pairs={{0,3},{1,2},{2,1},{3,0},{4,7},{5,6},{6,5},{7,4},{8,11},{9,10},{10,... | collective-permute-start | bytes 5677064 | tf_op jit(solution)/shard_map/w_recv/ppermute | solution.py:29
  93.1 13.7 %collective-permute-start.20 = (bf16[64,3696]{1,0:T(8,128)(2,1)S(1)}, bf16[64,3696]{1,0:T(8,128)(2,1)S(1)}, u32[]{:S(2)}, u32[]{:S(2)}) collective-permute-start(bf16[64,3696]{1,0:T(8,128)(2,1)S(1)} %get-tuple-element.68), channel_id=1, source_target_pairs={{0,1},{1,0},{2,3},{3,2},{4,5},{5,4},{6,7},{7,6},{8,9},{9,8},{10,11... | collective-permute-start | bytes 1419272 | tf_op jit(solution)/shard_map/t0/ppermute | solution.py:29
  94.0 16.7 %copy-start.3 = (bf16[64,3696]{1,0:T(8,128)(2,1)S(1)}, bf16[64,3696]{1,0:T(8,128)(2,1)}, u32[]{:S(2)}) copy-start(bf16[64,3696]{1,0:T(8,128)(2,1)} %copy-done.1) | copy-start | bytes 1419268
  94.0 16.7 %copy-start.10 = (bf16[64,3696]{1,0:T(8,128)(2,1)S(1)}, bf16[64,3696]{1,0:T(8,128)(2,1)}, u32[]{:S(2)}) copy-start(bf16[64,3696]{1,0:T(8,128)(2,1)} %refs_4_.3) | copy-start | bytes 1419268
  94.0 23.0 %collective-permute-start.25 = (bf16[64,3696]{1,0:T(8,128)(2,1)S(1)}, bf16[64,3696]{1,0:T(8,128)(2,1)S(1)}, u32[]{:S(2)}, u32[]{:S(2)}) collective-permute-start(bf16[64,3696]{1,0:T(8,128)(2,1)S(1)} %get-tuple-element.84), channel_id=1, source_target_pairs={{0,1},{1,0},{2,3},{3,2},{4,5},{5,4},{6,7},{7,6},{8,9},{9,8},{10,11... | collective-permute-start | bytes 1419272 | tf_op jit(solution)/shard_map/t1/ppermute | solution.py:29
  106.9 10.5 %collective-permute-start.24 = (bf16[32,3696]{1,0:T(8,128)(2,1)S(1)}, bf16[32,3696]{1,0:T(8,128)(2,1)S(1)}, u32[]{:S(2)}, u32[]{:S(2)}) collective-permute-start(bf16[32,3696]{1,0:T(8,128)(2,1)S(1)} %get-tuple-element.80), channel_id=1, source_target_pairs={{0,12},{1,13},{2,14},{3,15},{4,0},{5,1},{6,2},{7,3},{8,4},{9,5},{1... | collective-permute-start | bytes 709640 | tf_op jit(solution)/shard_map/from_up/ppermute | solution.py:29
  107.2 19.8 %collective-permute-start.22 = (bf16[64,3696]{1,0:T(8,128)(2,1)S(1)}, bf16[64,3696]{1,0:T(8,128)(2,1)S(1)}, u32[]{:S(2)}, u32[]{:S(2)}) collective-permute-start(bf16[64,3696]{1,0:T(8,128)(2,1)S(1)} %get-tuple-element.77), channel_id=1, source_target_pairs={{0,1},{1,0},{2,3},{3,2},{4,5},{5,4},{6,7},{7,6},{8,9},{9,8},{10,11... | collective-permute-start | bytes 1419272 | tf_op jit(solution)/shard_map/t2/ppermute | solution.py:29
  108.0 12.6 %copy-start.5 = (bf16[144,1024]{1,0:T(8,128)(2,1)S(1)}, bf16[144,1024]{1,0:T(8,128)(2,1)}, u32[]{:S(2)}) copy-start(bf16[144,1024]{1,0:T(8,128)(2,1)} %copy-done.4) | copy-start | bytes 884740
  108.0 12.6 %copy-start.8 = (bf16[128,512]{1,0:T(8,128)(2,1)S(1)}, bf16[128,512]{1,0:T(8,128)(2,1)}, u32[]{:S(2)}) copy-start(bf16[128,512]{1,0:T(8,128)(2,1)} %stream.2) | copy-start | bytes 393220
  108.0 19.0 %collective-permute-start.23 = (bf16[32,3696]{1,0:T(8,128)(2,1)S(1)}, bf16[32,3696]{1,0:T(8,128)(2,1)S(1)}, u32[]{:S(2)}, u32[]{:S(2)}) collective-permute-start(bf16[32,3696]{1,0:T(8,128)(2,1)S(1)} %get-tuple-element.74), channel_id=1, source_target_pairs={{0,4},{1,5},{2,6},{3,7},{4,8},{5,9},{6,10},{7,11},{8,12},{9,13},{1... | collective-permute-start | bytes 709640 | tf_op jit(solution)/shard_map/from_down/ppermute | solution.py:29
  117.5 12.4 %collective-permute-start.26 = (bf16[32,3696]{1,0:T(8,128)(2,1)S(1)}, bf16[32,3696]{1,0:T(8,128)(2,1)S(1)}, u32[]{:S(2)}, u32[]{:S(2)}) collective-permute-start(bf16[32,3696]{1,0:T(8,128)(2,1)S(1)} %get-tuple-element.86), channel_id=1, source_target_pairs={{0,12},{1,13},{2,14},{3,15},{4,0},{5,1},{6,2},{7,3},{8,4},{9,5},{1... | collective-permute-start | bytes 709640 | tf_op jit(solution)/shard_map/pure_a/ppermute | solution.py:29
  120.2 12.3 %collective-permute-start.27 = (bf16[32,3696]{1,0:T(8,128)(2,1)S(1)}, bf16[32,3696]{1,0:T(8,128)(2,1)S(1)}, u32[]{:S(2)}, u32[]{:S(2)}) collective-permute-start(bf16[32,3696]{1,0:T(8,128)(2,1)S(1)} %get-tuple-element.87), channel_id=1, source_target_pairs={{0,4},{1,5},{2,6},{3,7},{4,8},{5,9},{6,10},{7,11},{8,12},{9,13},{1... | collective-permute-start | bytes 709640 | tf_op jit(solution)/shard_map/pure_b/ppermute | solution.py:29
  137.9 14.4 %collective-permute-start.29 = (bf16[3696,512]{1,0:T(8,128)(2,1)S(1)}, bf16[3696,512]{1,0:T(8,128)(2,1)S(1)}, u32[]{:S(2)}, u32[]{:S(2)}) collective-permute-start(bf16[3696,512]{1,0:T(8,128)(2,1)S(1)} %merge_body.1), channel_id=1, source_target_pairs={{0,128},{128,0},{1,129},{129,1},{2,130},{130,2},{3,131},{131,3},{4... | collective-permute-start | bytes 11354120 | tf_op jit(solution)/shard_map/part/ppermute | solution.py:29
  138.1 13.2 %collective-permute-start.30 = (bf16[64,3696]{1,0:T(8,128)(2,1)S(1)}, bf16[64,3696]{1,0:T(8,128)(2,1)S(1)}, u32[]{:S(2)}, u32[]{:S(2)}) collective-permute-start(bf16[64,3696]{1,0:T(8,128)(2,1)S(1)} %get-tuple-element.91), channel_id=1, source_target_pairs={{0,1},{1,0},{2,3},{3,2},{4,5},{5,4},{6,7},{7,6},{8,9},{9,8},{10,11... | collective-permute-start | bytes 1419272 | tf_op jit(solution)/shard_map/t3/ppermute | solution.py:29
  138.7 12.6 %collective-permute-start.31 = (bf16[32,3696]{1,0:T(8,128)(2,1)S(1)}, bf16[32,3696]{1,0:T(8,128)(2,1)S(1)}, u32[]{:S(2)}, u32[]{:S(2)}) collective-permute-start(bf16[32,3696]{1,0:T(8,128)(2,1)S(1)} %get-tuple-element.88), channel_id=1, source_target_pairs={{0,4},{1,5},{2,6},{3,7},{4,8},{5,9},{6,10},{7,11},{8,12},{9,13},{1... | collective-permute-start | bytes 709640 | tf_op jit(solution)/shard_map/mixed_a/ppermute | solution.py:29
  138.7 12.6 %collective-permute-start.32 = (bf16[32,3696]{1,0:T(8,128)(2,1)S(1)}, bf16[32,3696]{1,0:T(8,128)(2,1)S(1)}, u32[]{:S(2)}, u32[]{:S(2)}) collective-permute-start(bf16[32,3696]{1,0:T(8,128)(2,1)S(1)} %get-tuple-element.94), channel_id=1, source_target_pairs={{0,12},{1,13},{2,14},{3,15},{4,0},{5,1},{6,2},{7,3},{8,4},{9,5},{1... | collective-permute-start | bytes 709640 | tf_op jit(solution)/shard_map/mixed_b/ppermute | solution.py:29

commit v7 on v6

--- a/solution.py
+++ b/solution.py
@@ -290,34 +290,28 @@
 
 def outer_body(*refs, first, split):
     (far_a, far_b, up, down, here, y0, y12, y3), (g_own, g_other) = refs[:8], refs[8:10]
-    *outs, h_v, g_v, sems = refs[10:]
+    *outs, h_v, g_v = refs[10:]
     p = lax.axis_index("dp")
-    moves = (
-        (0, far_a, 0, 32),
-        (32, far_b, 0, 32),
-        (64, up, 32, 64),
-        (96, down, 0, 32),
-        (128, up, 0, 32),
-        (160, down, 32, 64),
-        (192, here, 0, 64),
-        (256, y0, 0, 64),
-        (320, y12, 32, 96),
-        (384, y12, 0, 32),
-        (416, y12, 96, 128),
-        (448, y3, 0, 64),
-    )
-    moves = [
-        pltpu.make_async_copy(src.at[a:b], h_v.at[at : at + b - a], sems.at[i])
-        for i, (at, src, a, b) in enumerate(moves)
-    ]
-    for m in moves:
-        m.start()
+    for at, src in (
+        (0, far_a[...]),
+        (32, far_b[...]),
+        (64, up[32:64]),
+        (96, down[0:32]),
+        (128, up[0:32]),
+        (160, down[32:64]),
+        (192, here[...]),
+        (256, y0[...]),
+        (320, y12[0, 32:64]),
+        (352, y12[1, 0:32]),
+        (384, y12[0, 0:32]),
+        (416, y12[1, 32:64]),
+        (448, y3[...]),
+    ):
+        h_v[at : at + src.shape[0]] = src
     for n, side in enumerate((1 - p, p) if split else (0, 1)):
         start = pl.multiple_of(first + 256 * side, 256)
         g_v[:256, 256 * n : 256 * n + 256] = g_own[:, pl.ds(start, 256)]
         g_v[256:, 256 * n : 256 * n + 256] = g_other[:, pl.ds(start, 256)]
-    for m in moves:
-        m.wait()
     for f in range(0, 3696, 512):
         e = min(f + 512, 3696)
         out = lax.dot_general(
@@ -336,13 +330,7 @@
         functools.partial(outer_body, first=first, split=split),
         out,
         (*pieces, g_own, g_other),
-        in_specs=[pl.BlockSpec(memory_space=pl.ANY)] * 8
-        + [pl.BlockSpec(memory_space=pltpu.VMEM)] * 2,
-        scratch=[
-            pltpu.VMEM((512, 3696), bf16),
-            pltpu.VMEM((512, 512), bf16),
-            pltpu.SemaphoreType.DMA((12,)),
-        ],
+        scratch=[pltpu.VMEM((512, 3696), bf16), pltpu.VMEM((512, 512), bf16)],
         flops=512 * 1024 * 3696,
         moved=8 << 20,
         name=name,
@@ -428,7 +416,7 @@
             down, up = lax.optimization_barrier((down, up, sums))[:2]
             far_a = col(down[:32], ZUP, "far_a")
             far_b = col(up[32:], ZDOWN, "far_b")
-            y12 = col(jnp.concatenate([up, down], 0), PAIR, "y12")
+            y12 = col(jnp.stack([up, down]), PAIR, "y12")
     y0 = col(after(jnp.concatenate([far_a, far_b], 0), sums), PAIR, "y0")
     tiny = jnp.concatenate([sums, owed, owed_other], 0)
     tiny = after(tiny, far_a, far_b)
@@ -481,7 +469,7 @@
     hidden_grad = call(
         here_body,
         sds((64, 3696), bf16),
-        (own[3], t[3], pure_a, pure_b, mixed_a, mixed_b),
+        (after(own[3], weight_grad), t[3], pure_a, pure_b, mixed_a, mixed_b),
     )
     return weight_grad, hidden_grad, stream_grad
 

time: 156 us -> 141 us (0.904)
  local copies, waits for them, and re-layouts: 13.6 us -> 1.74 us
  Pallas kernels: 28.7 us -> 18.9 us
  waiting for transfers between devices: 60.4 us -> 68.3 us
  other arithmetic: 7.19 us -> 4.66 us
    pallas_call x14, Pallas kernels: 28.7 us -> 18.9 us  [call(): pl.pallas_call(body, out_shape=out_shape, scratch_shapes=list(scratch), c...]
    ppermute x33, waiting for transfers between devices: 60.4 us -> 68.3 us  [send(): return lax.ppermute(a, axis, perm)]
    unnamed x24 -> x8, local copies, waits for them, and re-layouts: 3.75 us -> 0.04 us
    concatenate x1 -> x0, local copies, waits for them, and re-layouts: 2.21 us -> none  [per_device(): y12 = col(jnp.concatenate([up, down], 0), PAIR, 'y12')]
    concatenate x1, other arithmetic: 1.76 us -> 0.04 us  [per_device(): y0 = col(after(jnp.concatenate([far_a, far_b], 0), sums), PAIR, 'y0')]
    concatenate x1, local copies, waits for them, and re-layouts: 1.71 us -> 0.02 us  [per_device(): here = jnp.concatenate([near, away], 0)]
    ppermute x1 -> x0, local copies, waits for them, and re-layouts: 1.59 us -> none  [send(): return lax.ppermute(a, axis, perm)]
  transfers between devices with their start and end apart: 33 -> 33, of which waited for: 17 -> 18; matrix products, arithmetic and copies ran while one was open for 9% -> 4% of each run, Pallas kernels for 17% -> 11%
where the time goes in v7:
time: 141 us; the launch traced here: 140 us
  waiting for transfers between devices  68.3 us (48%)
  starting transfers between devices  45.2 us (32%)
  Pallas kernels  18.9 us (13%)
  other arithmetic  4.66 us (3%)
  local copies, waits for them, and re-layouts  1.74 us (1%)
  between operations  1.5 us (1%)
    ppermute x33, waiting for transfers between devices, send(): return lax.ppermute(a, axis, perm)  68.3 us
    ppermute x33, starting transfers between devices, send(): return lax.ppermute(a, axis, perm)  45.2 us
    pallas_call x14, Pallas kernels, call(): pl.pallas_call(body, out_shape=out_shape, scratch_shapes=list(scratch), c...  18.9 us
    convert_element_type x1, other arithmetic, per_device(): weight_grad = (part.astype(f32) + part_other.astype(f32)).astype(bf16)  2.97 us
  transfers between devices with their start and end apart: 33, of which 18 were waited for; matrix products, arithmetic and copies ran while one was open for 4% of the time, Pallas kernels for 11%

profile of v7, /device:TPU:6, one launch (start us, length us, event | category | flops | bytes accessed | tf_op | source)
XLA Modules:
  0.0 140.3 jit_solution(9148943616516076510)
XLA Ops:
  0.6 1.6 %prep_body.1 = bf16[144,512]{1,0:T(8,128)(2,1)} custom-call(bf16[128,512]{1,0:T(8,128)(2,1)} %stream.2, f32[1,512]{1,0:T(1,128)} %bitcast.6, f32[1,512]{1,0:T(1,128)} %bitcast.7, f32[1,128]{1,0:T(1,128)} %reward.1, s32[1,128]{1,0:T(1,128)} %segment.1), custom_call_target="tpu_custom_call" | custom-call | tf_op jit(solution)/shard_map/prep_body/pallas_call | solution.py:55
  2.3 3.1 %collective-permute-start.2 = (bf16[144,512]{1,0:T(8,128)(2,1)}, bf16[144,512]{1,0:T(8,128)(2,1)S(1)}, u32[]{:S(2)}, u32[]{:S(2)}) collective-permute-start(bf16[144,512]{1,0:T(8,128)(2,1)} %prep_body.1), channel_id=1, source_target_pairs={{0,3},{1,2},{2,1},{3,0},{4,7},{5,6},{6,5},{7,4},{8,11},{9,10},{10,... | collective-permute-start | bytes 442376 | tf_op jit(solution)/shard_map/payload_mate/ppermute | solution.py:29
  5.4 0.1 collective-permute-start.4
  5.5 3.3 %collective-permute-start = (bf16[64,3696]{1,0:T(8,128)(2,1)}, bf16[64,3696]{1,0:T(8,128)(2,1)S(1)}, u32[]{:S(2)}, u32[]{:S(2)}) collective-permute-start(bf16[64,3696]{1,0:T(8,128)(2,1)} %refs_4_.3), channel_id=1, source_target_pairs={{0,4},{1,5},{2,6},{3,7},{4,8},{5,9},{6,10},{7,11},{8,12},{9,13},{1... | collective-permute-start | bytes 1419272 | tf_op jit(solution)/shard_map/down/ppermute | solution.py:29
  8.8 3.0 %collective-permute-start.1 = (bf16[64,3696]{1,0:T(8,128)(2,1)}, bf16[64,3696]{1,0:T(8,128)(2,1)S(1)}, u32[]{:S(2)}, u32[]{:S(2)}) collective-permute-start(bf16[64,3696]{1,0:T(8,128)(2,1)} %refs_4_.3), channel_id=1, source_target_pairs={{0,12},{1,13},{2,14},{3,15},{4,0},{5,1},{6,2},{7,3},{8,4},{9,5},{1... | collective-permute-start | bytes 1419272 | tf_op jit(solution)/shard_map/up/ppermute | solution.py:29
  11.8 0.9 pad_maximum_fusion.2.own
  12.8 0.9 collective-permute-start.3
  13.7 1.6 %constant_dynamic-slice_fusion = bf16[1856,512]{1,0:T(8,128)(2,1)S(1)} fusion(bf16[3696,512]{1,0:T(8,128)(2,1)} %w.3, s32[]{:T(128)S(6)} %select_n.3), kind=kLoop, calls=%fused_computation.10 | loop fusion | bytes 3801092 | tf_op jit(solution)/shard_map/dynamic_slice | solution.py:397
  15.4 1.1 collective-permute-start.15
  16.5 4.4 %collective-permute-done.3.other = bf16[144,1024]{1,0:T(8,128)(2,1)S(1)} collective-permute-done((bf16[144,1024]{1,0:T(8,128)(2,1)S(1)}, bf16[144,1024]{1,0:T(8,128)(2,1)S(1)}, u32[]{:S(2)}, u32[]{:S(2)}) %collective-permute-start.3) | collective-permute-done | bytes 294944 | tf_op jit(solution)/shard_map/block_x1/ppermute | solution.py:29
  20.9 0.2 pick_body.1
  21.1 0.6 collective-permute-start.9
  21.7 1.7 %collective-permute-start.5 = (f32[8,128]{1,0:T(8,128)S(1)}, f32[8,128]{1,0:T(8,128)S(1)}, u32[]{:S(2)}, u32[]{:S(2)}) collective-permute-start(f32[8,128]{1,0:T(8,128)S(1)} %get-tuple-element.52), channel_id=1, source_target_pairs={{0,1},{1,0},{2,3},{3,2},{4,5},{5,4},{6,7},{7,6},{8,9},{9,8},{10,11... | collective-permute-start | bytes 12296 | tf_op jit(solution)/shard_map/sums0/ppermute | solution.py:29
  23.4 1.8 %collective-permute-done.5 = f32[8,128]{1,0:T(8,128)S(1)} collective-permute-done((f32[8,128]{1,0:T(8,128)S(1)}, f32[8,128]{1,0:T(8,128)S(1)}, u32[]{:S(2)}, u32[]{:S(2)}) %collective-permute-start.5) | collective-permute-done | bytes 4128 | tf_op jit(solution)/shard_map/sums0/ppermute | solution.py:29
  25.3 1.3 collective-permute-done.refs_3_
  26.6 7.3 %collective-permute-done.1.refs_2_ = bf16[64,3696]{1,0:T(8,128)(2,1)S(1)} collective-permute-done((bf16[64,3696]{1,0:T(8,128)(2,1)}, bf16[64,3696]{1,0:T(8,128)(2,1)S(1)}, u32[]{:S(2)}, u32[]{:S(2)}) %collective-permute-start.1) | collective-permute-done | bytes 473120 | tf_op jit(solution)/shard_map/up/ppermute | solution.py:29
  33.9 3.8 %collective-permute-start.8 = (f32[8,128]{1,0:T(8,128)S(1)}, f32[8,128]{1,0:T(8,128)S(1)}, u32[]{:S(2)}, u32[]{:S(2)}) collective-permute-start(f32[8,128]{1,0:T(8,128)S(1)} %add.18), channel_id=1, source_target_pairs={{0,4},{1,5},{2,6},{3,7},{4,0},{5,1},{6,2},{7,3},{8,12},{9,13},{10,... | collective-permute-start | bytes 12296 | tf_op jit(solution)/shard_map/sums1/ppermute | solution.py:29
  37.7 0.1 collective-permute-start.6
  37.8 4.2 %collective-permute-start.7 = (bf16[32,3696]{1,0:T(8,128)(2,1)S(1)}, bf16[32,3696]{1,0:T(8,128)(2,1)S(1)}, u32[]{:S(2)}, u32[]{:S(2)}) collective-permute-start(bf16[32,3696]{1,0:T(8,128)(2,1)S(1)} %slice.7), channel_id=1, source_target_pairs={{0,12},{1,13},{2,14},{3,15},{4,0},{5,1},{6,2},{7,3},{8,4},{9,5},{1... | collective-permute-start | bytes 709640 | tf_op jit(solution)/shard_map/far_b/ppermute | solution.py:29
  42.0 0.1 pad_maximum_fusion
  42.1 1.8 %collective-permute-start.12 = (bf16[2,64,3696]{2,1,0:T(8,128)(2,1)S(1)}, bf16[2,64,3696]{2,1,0:T(8,128)(2,1)S(1)}, u32[]{:S(2)}, u32[]{:S(2)}) collective-permute-start(bf16[2,64,3696]{2,1,0:T(8,128)(2,1)S(1)} %pad_maximum_fusion), channel_id=1, source_target_pairs={{0,1},{1,0},{2,3},{3,2},{4,5},{5,4},{6,7},{7,6},{8,9},{9,8},{10,11... | collective-permute-start | bytes 2838536 | tf_op jit(solution)/shard_map/y12/ppermute | solution.py:29
  44.0 4.5 %collective-permute-done.6.refs_0_ = bf16[32,3696]{1,0:T(8,128)(2,1)S(1)} collective-permute-done((bf16[32,3696]{1,0:T(8,128)(2,1)S(1)}, bf16[32,3696]{1,0:T(8,128)(2,1)S(1)}, u32[]{:S(2)}, u32[]{:S(2)}) %collective-permute-start.6) | collective-permute-done | bytes 236576 | tf_op jit(solution)/shard_map/far_a/ppermute | solution.py:29
  48.5 3.3 %collective-permute-start.17 = (bf16[288,1024]{1,0:T(8,128)(2,1)S(1)}, bf16[288,1024]{1,0:T(8,128)(2,1)S(1)}, u32[]{:S(2)}, u32[]{:S(2)}) collective-permute-start(bf16[288,1024]{1,0:T(8,128)(2,1)S(1)} %constant_dynamic-update-slice_fusion.2.here), channel_id=1, source_target_pairs={{0,64},{16,80},{32,96},{48,112},{64,0},{80,16},{96,32},{112,48},{1... | collective-permute-start | bytes 1769480 | tf_op jit(solution)/shard_map/block_zlo/ppermute | solution.py:29
  51.8 1.8 %collective-permute-start.11 = (bf16[64,3696]{1,0:T(8,128)(2,1)S(1)}, bf16[64,3696]{1,0:T(8,128)(2,1)S(1)}, u32[]{:S(2)}, u32[]{:S(2)}) collective-permute-start(bf16[64,3696]{1,0:T(8,128)(2,1)S(1)} %pad_maximum_fusion.1), channel_id=1, source_target_pairs={{0,1},{1,0},{2,3},{3,2},{4,5},{5,4},{6,7},{7,6},{8,9},{9,8},{10,11... | collective-permute-start | bytes 1419272 | tf_op jit(solution)/shard_map/y0/ppermute | solution.py:29
  53.6 1.2 collective-permute-done.13
  54.8 0.5 collective-permute-start.14
  55.3 4.4 %collective-permute-done.14 = f32[24,128]{1,0:T(8,128)S(1)} collective-permute-done((f32[24,128]{1,0:T(8,128)S(1)}, f32[24,128]{1,0:T(8,128)S(1)}, u32[]{:S(2)}, u32[]{:S(2)}) %collective-permute-start.14) | collective-permute-done | bytes 12320 | tf_op jit(solution)/shard_map/tiny_x3/ppermute | solution.py:29
  59.7 4.4 %collective-permute-done.16.there = f32[48,128]{1,0:T(8,128)S(1)} collective-permute-done((f32[48,128]{1,0:T(8,128)S(1)}, f32[48,128]{1,0:T(8,128)S(1)}, u32[]{:S(2)}, u32[]{:S(2)}) %collective-permute-start.16) | collective-permute-done | bytes 24608 | tf_op jit(solution)/shard_map/tiny_zlo/ppermute | solution.py:29
  64.7 0.8 coefs_body.1.coefs
  65.5 1.0 collective-permute-start.18
  66.5 1.2 grad_body.1
  67.7 2.7 %collective-permute-done.18.coefs_mate = f32[8,128]{1,0:T(8,128)S(1)} collective-permute-done((f32[8,128]{1,0:T(8,128)S(1)}, f32[8,128]{1,0:T(8,128)S(1)}, u32[]{:S(2)}, u32[]{:S(2)}) %collective-permute-start.18) | collective-permute-done | bytes 4128 | tf_op jit(solution)/shard_map/coefs_mate/ppermute | solution.py:29
  70.4 3.1 %collective-permute-done.11.refs_5_ = bf16[64,3696]{1,0:T(8,128)(2,1)S(1)} collective-permute-done((bf16[64,3696]{1,0:T(8,128)(2,1)S(1)}, bf16[64,3696]{1,0:T(8,128)(2,1)S(1)}, u32[]{:S(2)}, u32[]{:S(2)}) %collective-permute-start.11) | collective-permute-done | bytes 473120 | tf_op jit(solution)/shard_map/y0/ppermute | solution.py:29
  73.5 2.2 %outer_mate.1 = (bf16[3696,256]{1,0:T(8,128)(2,1)S(1)}, f32[3696,256]{1,0:T(8,128)S(1)}) custom-call(bf16[32,3696]{1,0:T(8,128)(2,1)S(1)} %collective-permute-done.6.refs_0_, bf16[32,3696]{1,0:T(8,128)(2,1)S(1)} %collective-permute-done.7.refs_1_, bf16[64,3696]{1,0:T(8,128)(2,1)S(1)} %collective-permute-done.1.refs_2_, ...), custom_call_target="tpu_custom_call" | custom-call | flops 1937768448 | bytes 8388608 | tf_op jit(solution)/shard_map/outer_mate/pallas_call | solution.py:55
  75.7 0.1 collective-permute-start.21
  75.8 4.0 %inner_sent.1 = (bf16[64,3696]{1,0:T(8,128)(2,1)S(1)}, bf16[64,3696]{1,0:T(8,128)(2,1)S(1)}, bf16[64,3696]{1,0:T(8,128)(2,1)S(1)}, bf16[64,3696]{1,0:T(8,128)(2,1)S(1)}) custom-call(bf16[256,1024]{1,0:T(8,128)(2,1)S(1)} %get-tuple-element.67.refs_9_.g, bf16[3696,512]{1,0:T(8,128)(2,1)S(1)} %copy-done, bf16[1856,512]{1,0:T(8,128)(2,1)S(1)} %collective-permute-done.15.got, ...), custom_call_target="tpu_custom_call" | custom-call | flops 1937768448 | bytes 10485760 | tf_op jit(solution)/shard_map/inner_sent/pallas_call | solution.py:55
  79.8 0.6 add_convert_fusion.1
  80.4 1.0 collective-permute-start.28
  81.4 0.9 collective-permute-start.20
  82.3 1.1 collective-permute-start.25
  83.4 4.0 %inner_own.1 = (f32[64,3696]{1,0:T(8,128)S(1)}, f32[64,3696]{1,0:T(8,128)S(1)}, f32[64,3696]{1,0:T(8,128)S(1)}, f32[64,3696]{1,0:T(8,128)S(1)}) custom-call(bf16[256,1024]{1,0:T(8,128)(2,1)S(1)} %get-tuple-element.76.refs_8_.g, bf16[3696,512]{1,0:T(8,128)(2,1)S(1)} %copy-done, bf16[1856,512]{1,0:T(8,128)(2,1)S(1)} %collective-permute-done.15.got, ...), custom_call_target="tpu_custom_call" | custom-call | flops 1937768448 | bytes 10485760 | tf_op jit(solution)/shard_map/inner_own/pallas_call | solution.py:55
  87.4 7.7 %collective-permute-done.20.other = bf16[64,3696]{1,0:T(8,128)(2,1)S(1)} collective-permute-done((bf16[64,3696]{1,0:T(8,128)(2,1)S(1)}, bf16[64,3696]{1,0:T(8,128)(2,1)S(1)}, u32[]{:S(2)}, u32[]{:S(2)}) %collective-permute-start.20) | collective-permute-done | bytes 473120 | tf_op jit(solution)/shard_map/t0/ppermute | solution.py:29
  95.1 0.1 fold_body.3
  95.2 0.4 collective-permute-start.24
  95.6 0.9 collective-permute-start.22
  96.5 2.6 %collective-permute-start.23 = (bf16[32,3696]{1,0:T(8,128)(2,1)S(1)}, bf16[32,3696]{1,0:T(8,128)(2,1)S(1)}, u32[]{:S(2)}, u32[]{:S(2)}) collective-permute-start(bf16[32,3696]{1,0:T(8,128)(2,1)S(1)} %get-tuple-element.75), channel_id=1, source_target_pairs={{0,4},{1,5},{2,6},{3,7},{4,8},{5,9},{6,10},{7,11},{8,12},{9,13},{1... | collective-permute-start | bytes 709640 | tf_op jit(solution)/shard_map/from_down/ppermute | solution.py:29
  99.1 2.2 %outer_own.1.partial = f32[3696,512]{1,0:T(8,128)S(1)} custom-call(bf16[32,3696]{1,0:T(8,128)(2,1)S(1)} %collective-permute-done.6.refs_0_, bf16[32,3696]{1,0:T(8,128)(2,1)S(1)} %collective-permute-done.7.refs_1_, bf16[64,3696]{1,0:T(8,128)(2,1)S(1)} %collective-permute-done.1.refs_2_, bf16[64,3696]{1,0:T(8,128)(2,1)S(1)} %collective-permute-done.refs_3_, ...), custom_call_target="tpu_custom_call" | custom-call | flops 1937768448 | bytes 8388608 | tf_op jit(solution)/shard_map/outer_own/pallas_call | solution.py:55
  101.3 4.0 %collective-permute-done.25.other = bf16[64,3696]{1,0:T(8,128)(2,1)S(1)} collective-permute-done((bf16[64,3696]{1,0:T(8,128)(2,1)S(1)}, bf16[64,3696]{1,0:T(8,128)(2,1)S(1)}, u32[]{:S(2)}, u32[]{:S(2)}) %collective-permute-start.25) | collective-permute-done | bytes 473120 | tf_op jit(solution)/shard_map/t1/ppermute | solution.py:29
  105.4 1.9 %collective-permute-start.26 = (bf16[32,3696]{1,0:T(8,128)(2,1)S(1)}, bf16[32,3696]{1,0:T(8,128)(2,1)S(1)}, u32[]{:S(2)}, u32[]{:S(2)}) collective-permute-start(bf16[32,3696]{1,0:T(8,128)(2,1)S(1)} %get-tuple-element.87), channel_id=1, source_target_pairs={{0,12},{1,13},{2,14},{3,15},{4,0},{5,1},{6,2},{7,3},{8,4},{9,5},{1... | collective-permute-start | bytes 709640 | tf_op jit(solution)/shard_map/pure_a/ppermute | solution.py:29
  107.3 1.1 collective-permute-start.27
  108.4 0.9 own_grad_body.1
  109.2 5.5 %collective-permute-done.22.other = bf16[64,3696]{1,0:T(8,128)(2,1)S(1)} collective-permute-done((bf16[64,3696]{1,0:T(8,128)(2,1)S(1)}, bf16[64,3696]{1,0:T(8,128)(2,1)S(1)}, u32[]{:S(2)}, u32[]{:S(2)}) %collective-permute-start.22) | collective-permute-done | bytes 473120 | tf_op jit(solution)/shard_map/t2/ppermute | solution.py:29
  114.7 0.2 fold_body.4
  114.9 1.3 collective-permute-done.26.pure_a
  116.2 3.6 %collective-permute-done.27.pure_b = bf16[32,3696]{1,0:T(8,128)(2,1)S(1)} collective-permute-done((bf16[32,3696]{1,0:T(8,128)(2,1)S(1)}, bf16[32,3696]{1,0:T(8,128)(2,1)S(1)}, u32[]{:S(2)}, u32[]{:S(2)}) %collective-permute-start.27) | collective-permute-done | bytes 236576 | tf_op jit(solution)/shard_map/pure_b/ppermute | solution.py:29
  119.8 5.5 %collective-permute-done.28.recv = bf16[3696,256]{1,0:T(8,128)(2,1)S(1)} collective-permute-done((bf16[3696,256]{1,0:T(8,128)(2,1)S(1)}, bf16[3696,256]{1,0:T(8,128)(2,1)S(1)}, u32[]{:S(2)}, u32[]{:S(2)}) %collective-permute-start.28) | collective-permute-done | bytes 1892384 | tf_op jit(solution)/shard_map/w_recv/ppermute | solution.py:29
  125.3 0.6 merge_body.1
  125.9 0.1 collective-permute-start.29
  126.0 0.6 collective-permute-start.30
  126.7 4.1 %collective-permute-start.32 = (bf16[32,3696]{1,0:T(8,128)(2,1)S(1)}, bf16[32,3696]{1,0:T(8,128)(2,1)S(1)}, u32[]{:S(2)}, u32[]{:S(2)}) collective-permute-start(bf16[32,3696]{1,0:T(8,128)(2,1)S(1)} %get-tuple-element.96), channel_id=1, source_target_pairs={{0,12},{1,13},{2,14},{3,15},{4,0},{5,1},{6,2},{7,3},{8,4},{9,5},{1... | collective-permute-start | bytes 709640 | tf_op jit(solution)/shard_map/mixed_b/ppermute | solution.py:29
  130.8 1.8 %collective-permute-done.29 = bf16[3696,512]{1,0:T(8,128)(2,1)S(1)} collective-permute-done((bf16[3696,512]{1,0:T(8,128)(2,1)S(1)}, bf16[3696,512]{1,0:T(8,128)(2,1)S(1)}, u32[]{:S(2)}, u32[]{:S(2)}) %collective-permute-start.29) | collective-permute-done | bytes 3784736 | tf_op jit(solution)/shard_map/part/ppermute | solution.py:29
  132.6 3.0 %add_convert_fusion = bf16[3696,512]{1,0:T(8,128)(2,1)} fusion(bf16[3696,512]{1,0:T(8,128)(2,1)S(1)} %collective-permute-done.29, bf16[3696,512]{1,0:T(8,128)(2,1)S(1)} %merge_body.1), kind=kLoop, calls=%fused_computation | loop fusion | flops 7569408 | bytes 11354112 | tf_op jit(solution)/shard_map/convert_element_type | solution.py:468
  135.6 3.8 %collective-permute-done.30.other = bf16[64,3696]{1,0:T(8,128)(2,1)S(1)} collective-permute-done((bf16[64,3696]{1,0:T(8,128)(2,1)S(1)}, bf16[64,3696]{1,0:T(8,128)(2,1)S(1)}, u32[]{:S(2)}, u32[]{:S(2)}) %collective-permute-start.30) | collective-permute-done | bytes 473120 | tf_op jit(solution)/shard_map/t3/ppermute | solution.py:29
  139.3 1.0 here_body.1
  (38 shorter events, 0.4 us)
Async XLA Ops:
  2.3 9.5 %collective-permute-start.2 = (bf16[144,512]{1,0:T(8,128)(2,1)}, bf16[144,512]{1,0:T(8,128)(2,1)S(1)}, u32[]{:S(2)}, u32[]{:S(2)}) collective-permute-start(bf16[144,512]{1,0:T(8,128)(2,1)} %prep_body.1), channel_id=1, source_target_pairs={{0,3},{1,2},{2,1},{3,0},{4,7},{5,6},{6,5},{7,4},{8,11},{9,10},{10,... | collective-permute-start | bytes 442376 | tf_op jit(solution)/shard_map/payload_mate/ppermute | solution.py:29
  5.4 16.3 %collective-permute-start.4 = (bf16[64,3696]{1,0:T(8,128)(2,1)}, bf16[64,3696]{1,0:T(8,128)(2,1)S(1)}, u32[]{:S(2)}, u32[]{:S(2)}) collective-permute-start(bf16[64,3696]{1,0:T(8,128)(2,1)} %refs_4_.3), channel_id=1, source_target_pairs={{0,1},{1,0},{2,3},{3,2},{4,5},{5,4},{6,7},{7,6},{8,9},{9,8},{10,11... | collective-permute-start | bytes 1419272 | tf_op jit(solution)/shard_map/y3/ppermute | solution.py:29
  5.5 21.0 %collective-permute-start = (bf16[64,3696]{1,0:T(8,128)(2,1)}, bf16[64,3696]{1,0:T(8,128)(2,1)S(1)}, u32[]{:S(2)}, u32[]{:S(2)}) collective-permute-start(bf16[64,3696]{1,0:T(8,128)(2,1)} %refs_4_.3), channel_id=1, source_target_pairs={{0,4},{1,5},{2,6},{3,7},{4,8},{5,9},{6,10},{7,11},{8,12},{9,13},{1... | collective-permute-start | bytes 1419272 | tf_op jit(solution)/shard_map/down/ppermute | solution.py:29
  8.8 25.1 %collective-permute-start.1 = (bf16[64,3696]{1,0:T(8,128)(2,1)}, bf16[64,3696]{1,0:T(8,128)(2,1)S(1)}, u32[]{:S(2)}, u32[]{:S(2)}) collective-permute-start(bf16[64,3696]{1,0:T(8,128)(2,1)} %refs_4_.3), channel_id=1, source_target_pairs={{0,12},{1,13},{2,14},{3,15},{4,0},{5,1},{6,2},{7,3},{8,4},{9,5},{1... | collective-permute-start | bytes 1419272 | tf_op jit(solution)/shard_map/up/ppermute | solution.py:29
  12.8 8.1 %collective-permute-start.3 = (bf16[144,1024]{1,0:T(8,128)(2,1)S(1)}, bf16[144,1024]{1,0:T(8,128)(2,1)S(1)}, u32[]{:S(2)}, u32[]{:S(2)}) collective-permute-start(bf16[144,1024]{1,0:T(8,128)(2,1)S(1)} %pad_maximum_fusion.2.own), channel_id=1, source_target_pairs={{0,16},{16,0},{32,48},{48,32},{64,80},{80,64},{96,112},{112,96},{1... | collective-permute-start | bytes 884744 | tf_op jit(solution)/shard_map/block_x1/ppermute | solution.py:29
  15.3 58.1 %copy-start.2 = (bf16[64,3696]{1,0:T(8,128)(2,1)S(1)}, bf16[64,3696]{1,0:T(8,128)(2,1)}, u32[]{:S(2)}) copy-start(bf16[64,3696]{1,0:T(8,128)(2,1)} %refs_4_.3) | copy-start | bytes 1419268
  15.4 48.7 %collective-permute-start.15 = (bf16[1856,512]{1,0:T(8,128)(2,1)S(1)}, bf16[1856,512]{1,0:T(8,128)(2,1)S(1)}, u32[]{:S(2)}, u32[]{:S(2)}) collective-permute-start(bf16[1856,512]{1,0:T(8,128)(2,1)S(1)} %constant_dynamic-slice_fusion), channel_id=1, source_target_pairs={{0,3},{1,2},{2,1},{3,0},{4,7},{5,6},{6,5},{7,4},{8,11},{9,10},{10,... | collective-permute-start | bytes 5701640 | tf_op jit(solution)/shard_map/got/ppermute | solution.py:29
  21.1 22.8 %collective-permute-start.9 = (bf16[144,1024]{1,0:T(8,128)(2,1)S(1)}, bf16[144,1024]{1,0:T(8,128)(2,1)S(1)}, u32[]{:S(2)}, u32[]{:S(2)}) collective-permute-start(bf16[144,1024]{1,0:T(8,128)(2,1)S(1)} %get-tuple-element.56.block), channel_id=1, source_target_pairs={{0,48},{16,32},{32,16},{48,0},{64,112},{80,96},{96,80},{112,64},{1... | collective-permute-start | bytes 884744 | tf_op jit(solution)/shard_map/block_x3/ppermute | solution.py:29
  21.7 3.6 %collective-permute-start.5 = (f32[8,128]{1,0:T(8,128)S(1)}, f32[8,128]{1,0:T(8,128)S(1)}, u32[]{:S(2)}, u32[]{:S(2)}) collective-permute-start(f32[8,128]{1,0:T(8,128)S(1)} %get-tuple-element.52), channel_id=1, source_target_pairs={{0,1},{1,0},{2,3},{3,2},{4,5},{5,4},{6,7},{7,6},{8,9},{9,8},{10,11... | collective-permute-start | bytes 12296 | tf_op jit(solution)/shard_map/sums0/ppermute | solution.py:29
  33.9 8.2 %collective-permute-start.8 = (f32[8,128]{1,0:T(8,128)S(1)}, f32[8,128]{1,0:T(8,128)S(1)}, u32[]{:S(2)}, u32[]{:S(2)}) collective-permute-start(f32[8,128]{1,0:T(8,128)S(1)} %add.18), channel_id=1, source_target_pairs={{0,4},{1,5},{2,6},{3,7},{4,0},{5,1},{6,2},{7,3},{8,12},{9,13},{10,... | collective-permute-start | bytes 12296 | tf_op jit(solution)/shard_map/sums1/ppermute | solution.py:29
  37.7 10.8 %collective-permute-start.6 = (bf16[32,3696]{1,0:T(8,128)(2,1)S(1)}, bf16[32,3696]{1,0:T(8,128)(2,1)S(1)}, u32[]{:S(2)}, u32[]{:S(2)}) collective-permute-start(bf16[32,3696]{1,0:T(8,128)(2,1)S(1)} %slice.6), channel_id=1, source_target_pairs={{0,4},{1,5},{2,6},{3,7},{4,8},{5,9},{6,10},{7,11},{8,12},{9,13},{1... | collective-permute-start | bytes 709640 | tf_op jit(solution)/shard_map/far_a/ppermute | solution.py:29
  37.8 14.0 %collective-permute-start.7 = (bf16[32,3696]{1,0:T(8,128)(2,1)S(1)}, bf16[32,3696]{1,0:T(8,128)(2,1)S(1)}, u32[]{:S(2)}, u32[]{:S(2)}) collective-permute-start(bf16[32,3696]{1,0:T(8,128)(2,1)S(1)} %slice.7), channel_id=1, source_target_pairs={{0,12},{1,13},{2,14},{3,15},{4,0},{5,1},{6,2},{7,3},{8,4},{9,5},{1... | collective-permute-start | bytes 709640 | tf_op jit(solution)/shard_map/far_b/ppermute | solution.py:29
  42.1 31.4 %collective-permute-start.12 = (bf16[2,64,3696]{2,1,0:T(8,128)(2,1)S(1)}, bf16[2,64,3696]{2,1,0:T(8,128)(2,1)S(1)}, u32[]{:S(2)}, u32[]{:S(2)}) collective-permute-start(bf16[2,64,3696]{2,1,0:T(8,128)(2,1)S(1)} %pad_maximum_fusion), channel_id=1, source_target_pairs={{0,1},{1,0},{2,3},{3,2},{4,5},{5,4},{6,7},{7,6},{8,9},{9,8},{10,11... | collective-permute-start | bytes 2838536 | tf_op jit(solution)/shard_map/y12/ppermute | solution.py:29
  43.9 7.9 %collective-permute-start.10 = (f32[8,128]{1,0:T(8,128)S(1)}, f32[8,128]{1,0:T(8,128)S(1)}, u32[]{:S(2)}, u32[]{:S(2)}) collective-permute-start(f32[8,128]{1,0:T(8,128)S(1)} %add.19), channel_id=1, source_target_pairs={{0,12},{1,13},{2,14},{3,15},{4,8},{5,9},{6,10},{7,11},{8,4},{9,5},... | collective-permute-start | bytes 12296 | tf_op jit(solution)/shard_map/sums2/ppermute | solution.py:29
  48.5 18.1 %collective-permute-start.17 = (bf16[288,1024]{1,0:T(8,128)(2,1)S(1)}, bf16[288,1024]{1,0:T(8,128)(2,1)S(1)}, u32[]{:S(2)}, u32[]{:S(2)}) collective-permute-start(bf16[288,1024]{1,0:T(8,128)(2,1)S(1)} %constant_dynamic-update-slice_fusion.2.here), channel_id=1, source_target_pairs={{0,64},{16,80},{32,96},{48,112},{64,0},{80,16},{96,32},{112,48},{1... | collective-permute-start | bytes 1769480 | tf_op jit(solution)/shard_map/block_zlo/ppermute | solution.py:29
  51.8 21.6 %collective-permute-start.11 = (bf16[64,3696]{1,0:T(8,128)(2,1)S(1)}, bf16[64,3696]{1,0:T(8,128)(2,1)S(1)}, u32[]{:S(2)}, u32[]{:S(2)}) collective-permute-start(bf16[64,3696]{1,0:T(8,128)(2,1)S(1)} %pad_maximum_fusion.1), channel_id=1, source_target_pairs={{0,1},{1,0},{2,3},{3,2},{4,5},{5,4},{6,7},{7,6},{8,9},{9,8},{10,11... | collective-permute-start | bytes 1419272 | tf_op jit(solution)/shard_map/y0/ppermute | solution.py:29
  53.6 1.2 collective-permute-start.13
  54.8 4.9 %collective-permute-start.14 = (f32[24,128]{1,0:T(8,128)S(1)}, f32[24,128]{1,0:T(8,128)S(1)}, u32[]{:S(2)}, u32[]{:S(2)}) collective-permute-start(f32[24,128]{1,0:T(8,128)S(1)} %pad_maximum_fusion.3), channel_id=1, source_target_pairs={{0,48},{16,32},{32,16},{48,0},{64,112},{80,96},{96,80},{112,64},{1... | collective-permute-start | bytes 36872 | tf_op jit(solution)/shard_map/tiny_x3/ppermute | solution.py:29
  59.7 4.4 %collective-permute-start.16 = (f32[48,128]{1,0:T(8,128)S(1)}, f32[48,128]{1,0:T(8,128)S(1)}, u32[]{:S(2)}, u32[]{:S(2)}) collective-permute-start(f32[48,128]{1,0:T(8,128)S(1)} %constant_dynamic-update-slice_fusion.here), channel_id=1, source_target_pairs={{0,64},{16,80},{32,96},{48,112},{64,0},{80,16},{96,32},{112,48},{1... | collective-permute-start | bytes 73736 | tf_op jit(solution)/shard_map/tiny_zlo/ppermute | solution.py:29
  64.1 11.7 %collective-permute-start.19 = (bf16[1856,512]{1,0:T(8,128)(2,1)S(1)}, bf16[1856,512]{1,0:T(8,128)(2,1)S(1)}, u32[]{:S(2)}, u32[]{:S(2)}) collective-permute-start(bf16[1856,512]{1,0:T(8,128)(2,1)S(1)} %collective-permute-done.15.got), channel_id=1, source_target_pairs={{0,128},{128,0},{1,129},{129,1},{2,130},{130,2},{3,131},{131,3},{4... | collective-permute-start | bytes 5701640 | tf_op jit(solution)/shard_map/got_other/ppermute | solution.py:29
  65.5 4.9 %collective-permute-start.18 = (f32[8,128]{1,0:T(8,128)S(1)}, f32[8,128]{1,0:T(8,128)S(1)}, u32[]{:S(2)}, u32[]{:S(2)}) collective-permute-start(f32[8,128]{1,0:T(8,128)S(1)} %coefs_body.1.coefs), channel_id=1, source_target_pairs={{0,3},{1,2},{2,1},{3,0},{4,7},{5,6},{6,5},{7,4},{8,11},{9,10},{10,... | collective-permute-start | bytes 12296 | tf_op jit(solution)/shard_map/coefs_mate/ppermute | solution.py:29
  67.7 8.1 %copy-start = (bf16[3696,512]{1,0:T(8,128)(2,1)S(1)}, bf16[3696,512]{1,0:T(8,128)(2,1)}, u32[]{:S(2)}) copy-start(bf16[3696,512]{1,0:T(8,128)(2,1)} %w.3) | copy-start | bytes 11354116
  75.7 4.1 %collective-permute-start.21 = (bf16[3696,256]{1,0:T(8,128)(2,1)S(1)}, bf16[3696,256]{1,0:T(8,128)(2,1)S(1)}, u32[]{:S(2)}, u32[]{:S(2)}) collective-permute-start(bf16[3696,256]{1,0:T(8,128)(2,1)S(1)} %get-tuple-element.73), channel_id=1, source_target_pairs={{0,128},{128,0},{1,129},{129,1},{2,130},{130,2},{3,131},{131,3},{4... | collective-permute-start | bytes 5677064 | tf_op jit(solution)/shard_map/mate_got/ppermute | solution.py:29
  80.4 44.9 %collective-permute-start.28 = (bf16[3696,256]{1,0:T(8,128)(2,1)S(1)}, bf16[3696,256]{1,0:T(8,128)(2,1)S(1)}, u32[]{:S(2)}, u32[]{:S(2)}) collective-permute-start(bf16[3696,256]{1,0:T(8,128)(2,1)S(1)} %add_convert_fusion.1), channel_id=1, source_target_pairs={{0,3},{1,2},{2,1},{3,0},{4,7},{5,6},{6,5},{7,4},{8,11},{9,10},{10,... | collective-permute-start | bytes 5677064 | tf_op jit(solution)/shard_map/w_recv/ppermute | solution.py:29
  81.4 13.7 %collective-permute-start.20 = (bf16[64,3696]{1,0:T(8,128)(2,1)S(1)}, bf16[64,3696]{1,0:T(8,128)(2,1)S(1)}, u32[]{:S(2)}, u32[]{:S(2)}) collective-permute-start(bf16[64,3696]{1,0:T(8,128)(2,1)S(1)} %get-tuple-element.69), channel_id=1, source_target_pairs={{0,1},{1,0},{2,3},{3,2},{4,5},{5,4},{6,7},{7,6},{8,9},{9,8},{10,11... | collective-permute-start | bytes 1419272 | tf_op jit(solution)/shard_map/t0/ppermute | solution.py:29
  82.3 23.0 %collective-permute-start.25 = (bf16[64,3696]{1,0:T(8,128)(2,1)S(1)}, bf16[64,3696]{1,0:T(8,128)(2,1)S(1)}, u32[]{:S(2)}, u32[]{:S(2)}) collective-permute-start(bf16[64,3696]{1,0:T(8,128)(2,1)S(1)} %get-tuple-element.85), channel_id=1, source_target_pairs={{0,1},{1,0},{2,3},{3,2},{4,5},{5,4},{6,7},{7,6},{8,9},{9,8},{10,11... | collective-permute-start | bytes 1419272 | tf_op jit(solution)/shard_map/t1/ppermute | solution.py:29
  95.2 10.1 %collective-permute-start.24 = (bf16[32,3696]{1,0:T(8,128)(2,1)S(1)}, bf16[32,3696]{1,0:T(8,128)(2,1)S(1)}, u32[]{:S(2)}, u32[]{:S(2)}) collective-permute-start(bf16[32,3696]{1,0:T(8,128)(2,1)S(1)} %get-tuple-element.81), channel_id=1, source_target_pairs={{0,12},{1,13},{2,14},{3,15},{4,0},{5,1},{6,2},{7,3},{8,4},{9,5},{1... | collective-permute-start | bytes 709640 | tf_op jit(solution)/shard_map/from_up/ppermute | solution.py:29
  95.6 19.2 %collective-permute-start.22 = (bf16[64,3696]{1,0:T(8,128)(2,1)S(1)}, bf16[64,3696]{1,0:T(8,128)(2,1)S(1)}, u32[]{:S(2)}, u32[]{:S(2)}) collective-permute-start(bf16[64,3696]{1,0:T(8,128)(2,1)S(1)} %get-tuple-element.78), channel_id=1, source_target_pairs={{0,1},{1,0},{2,3},{3,2},{4,5},{5,4},{6,7},{7,6},{8,9},{9,8},{10,11... | collective-permute-start | bytes 1419272 | tf_op jit(solution)/shard_map/t2/ppermute | solution.py:29
  96.5 11.9 %copy-start.1 = (bf16[128,512]{1,0:T(8,128)(2,1)S(1)}, bf16[128,512]{1,0:T(8,128)(2,1)}, u32[]{:S(2)}) copy-start(bf16[128,512]{1,0:T(8,128)(2,1)} %stream.2) | copy-start | bytes 393220
  96.5 18.3 %collective-permute-start.23 = (bf16[32,3696]{1,0:T(8,128)(2,1)S(1)}, bf16[32,3696]{1,0:T(8,128)(2,1)S(1)}, u32[]{:S(2)}, u32[]{:S(2)}) collective-permute-start(bf16[32,3696]{1,0:T(8,128)(2,1)S(1)} %get-tuple-element.75), channel_id=1, source_target_pairs={{0,4},{1,5},{2,6},{3,7},{4,8},{5,9},{6,10},{7,11},{8,12},{9,13},{1... | collective-permute-start | bytes 709640 | tf_op jit(solution)/shard_map/from_down/ppermute | solution.py:29
  105.4 10.8 %collective-permute-start.26 = (bf16[32,3696]{1,0:T(8,128)(2,1)S(1)}, bf16[32,3696]{1,0:T(8,128)(2,1)S(1)}, u32[]{:S(2)}, u32[]{:S(2)}) collective-permute-start(bf16[32,3696]{1,0:T(8,128)(2,1)S(1)} %get-tuple-element.87), channel_id=1, source_target_pairs={{0,12},{1,13},{2,14},{3,15},{4,0},{5,1},{6,2},{7,3},{8,4},{9,5},{1... | collective-permute-start | bytes 709640 | tf_op jit(solution)/shard_map/pure_a/ppermute | solution.py:29
  107.3 12.5 %collective-permute-start.27 = (bf16[32,3696]{1,0:T(8,128)(2,1)S(1)}, bf16[32,3696]{1,0:T(8,128)(2,1)S(1)}, u32[]{:S(2)}, u32[]{:S(2)}) collective-permute-start(bf16[32,3696]{1,0:T(8,128)(2,1)S(1)} %get-tuple-element.88), channel_id=1, source_target_pairs={{0,4},{1,5},{2,6},{3,7},{4,8},{5,9},{6,10},{7,11},{8,12},{9,13},{1... | collective-permute-start | bytes 709640 | tf_op jit(solution)/shard_map/pure_b/ppermute | solution.py:29
  125.9 6.7 %collective-permute-start.29 = (bf16[3696,512]{1,0:T(8,128)(2,1)S(1)}, bf16[3696,512]{1,0:T(8,128)(2,1)S(1)}, u32[]{:S(2)}, u32[]{:S(2)}) collective-permute-start(bf16[3696,512]{1,0:T(8,128)(2,1)S(1)} %merge_body.1), channel_id=1, source_target_pairs={{0,128},{128,0},{1,129},{129,1},{2,130},{130,2},{3,131},{131,3},{4... | collective-permute-start | bytes 11354120 | tf_op jit(solution)/shard_map/part/ppermute | solution.py:29
  126.0 13.3 %collective-permute-start.30 = (bf16[64,3696]{1,0:T(8,128)(2,1)S(1)}, bf16[64,3696]{1,0:T(8,128)(2,1)S(1)}, u32[]{:S(2)}, u32[]{:S(2)}) collective-permute-start(bf16[64,3696]{1,0:T(8,128)(2,1)S(1)} %get-tuple-element.93), channel_id=1, source_target_pairs={{0,1},{1,0},{2,3},{3,2},{4,5},{5,4},{6,7},{7,6},{8,9},{9,8},{10,11... | collective-permute-start | bytes 1419272 | tf_op jit(solution)/shard_map/t3/ppermute | solution.py:29
  126.6 12.7 %collective-permute-start.31 = (bf16[32,3696]{1,0:T(8,128)(2,1)S(1)}, bf16[32,3696]{1,0:T(8,128)(2,1)S(1)}, u32[]{:S(2)}, u32[]{:S(2)}) collective-permute-start(bf16[32,3696]{1,0:T(8,128)(2,1)S(1)} %get-tuple-element.89), channel_id=1, source_target_pairs={{0,4},{1,5},{2,6},{3,7},{4,8},{5,9},{6,10},{7,11},{8,12},{9,13},{1... | collective-permute-start | bytes 709640 | tf_op jit(solution)/shard_map/mixed_a/ppermute | solution.py:29
  126.7 12.6 %collective-permute-start.32 = (bf16[32,3696]{1,0:T(8,128)(2,1)S(1)}, bf16[32,3696]{1,0:T(8,128)(2,1)S(1)}, u32[]{:S(2)}, u32[]{:S(2)}) collective-permute-start(bf16[32,3696]{1,0:T(8,128)(2,1)S(1)} %get-tuple-element.96), channel_id=1, source_target_pairs={{0,12},{1,13},{2,14},{3,15},{4,0},{5,1},{6,2},{7,3},{8,4},{9,5},{1... | collective-permute-start | bytes 709640 | tf_op jit(solution)/shard_map/mixed_b/ppermute | solution.py:29

commit v8 on v7

--- a/solution.py
+++ b/solution.py
@@ -391,8 +391,8 @@
     payload_mate = col(payload, MATE, "payload_mate")
     ready = after(hidden, payload)
     y3 = col(ready, PAIR, "y3")
-    down = col(ready, ZUP, "down")
-    up = col(ready, ZDOWN, "up")
+    down = col(hidden, ZUP, "down")
+    up = col(hidden, ZDOWN, "up")
 
     w_half = lax.dynamic_slice_in_dim(w_down, p * HIGH, LO, 0)
     got = col(after(w_half, payload_mate), MATE, "got")

time: 141 us -> 141 us (level)
  starting transfers between devices: 45.2 us -> 38.5 us
  waiting for transfers between devices: 68.3 us -> 75 us
    ppermute x33, starting transfers between devices: 45.2 us -> 38.5 us  [send(): return lax.ppermute(a, axis, perm)]
    ppermute x33, waiting for transfers between devices: 68.3 us -> 75 us  [send(): return lax.ppermute(a, axis, perm)]
where the time goes in v8:
time: 141 us; the launch traced here: 140 us
  waiting for transfers between devices  75 us (53%)
  starting transfers between devices  38.5 us (27%)
  Pallas kernels  18.9 us (13%)
  other arithmetic  4.65 us (3%)
  local copies, waits for them, and re-layouts  1.74 us (1%)
  between operations  1.51 us (1%)
    ppermute x33, waiting for transfers between devices, send(): return lax.ppermute(a, axis, perm)  75 us
    ppermute x33, starting transfers between devices, send(): return lax.ppermute(a, axis, perm)  38.5 us
    pallas_call x14, Pallas kernels, call(): pl.pallas_call(body, out_shape=out_shape, scratch_shapes=list(scratch), c...  18.9 us
    convert_element_type x1, other arithmetic, per_device(): weight_grad = (part.astype(f32) + part_other.astype(f32)).astype(bf16)  2.96 us
  transfers between devices with their start and end apart: 33, of which 18 were waited for; matrix products, arithmetic and copies ran while one was open for 4% of the time, Pallas kernels for 11%

profile of v8, /device:TPU:6, one launch (start us, length us, event | category | flops | bytes accessed | tf_op | source)
XLA Modules:
  0.0 140.3 jit_solution(9751421385790056905)
XLA Ops:
  0.6 1.6 %prep_body.1 = bf16[144,512]{1,0:T(8,128)(2,1)} custom-call(bf16[128,512]{1,0:T(8,128)(2,1)} %stream.2, f32[1,512]{1,0:T(1,128)} %bitcast.6, f32[1,512]{1,0:T(1,128)} %bitcast.7, f32[1,128]{1,0:T(1,128)} %reward.1, s32[1,128]{1,0:T(1,128)} %segment.1), custom_call_target="tpu_custom_call" | custom-call | tf_op jit(solution)/shard_map/prep_body/pallas_call | solution.py:55
  2.3 3.1 %collective-permute-start.2 = (bf16[144,512]{1,0:T(8,128)(2,1)}, bf16[144,512]{1,0:T(8,128)(2,1)S(1)}, u32[]{:S(2)}, u32[]{:S(2)}) collective-permute-start(bf16[144,512]{1,0:T(8,128)(2,1)} %prep_body.1), channel_id=1, source_target_pairs={{0,3},{1,2},{2,1},{3,0},{4,7},{5,6},{6,5},{7,4},{8,11},{9,10},{10,... | collective-permute-start | bytes 442376 | tf_op jit(solution)/shard_map/payload_mate/ppermute | solution.py:29
  5.4 3.3 %collective-permute-start = (bf16[64,3696]{1,0:T(8,128)(2,1)}, bf16[64,3696]{1,0:T(8,128)(2,1)S(1)}, u32[]{:S(2)}, u32[]{:S(2)}) collective-permute-start(bf16[64,3696]{1,0:T(8,128)(2,1)} %refs_4_.3), channel_id=1, source_target_pairs={{0,4},{1,5},{2,6},{3,7},{4,8},{5,9},{6,10},{7,11},{8,12},{9,13},{1... | collective-permute-start | bytes 1419272 | tf_op jit(solution)/shard_map/down/ppermute | solution.py:29
  8.7 3.0 %collective-permute-start.1 = (bf16[64,3696]{1,0:T(8,128)(2,1)}, bf16[64,3696]{1,0:T(8,128)(2,1)S(1)}, u32[]{:S(2)}, u32[]{:S(2)}) collective-permute-start(bf16[64,3696]{1,0:T(8,128)(2,1)} %refs_4_.3), channel_id=1, source_target_pairs={{0,12},{1,13},{2,14},{3,15},{4,0},{5,1},{6,2},{7,3},{8,4},{9,5},{1... | collective-permute-start | bytes 1419272 | tf_op jit(solution)/shard_map/up/ppermute | solution.py:29
  11.7 0.1 collective-permute-start.4
  11.8 0.9 pad_maximum_fusion.2.own
  12.8 0.9 collective-permute-start.3
  13.7 1.6 %constant_dynamic-slice_fusion = bf16[1856,512]{1,0:T(8,128)(2,1)S(1)} fusion(bf16[3696,512]{1,0:T(8,128)(2,1)} %w.3, s32[]{:T(128)S(6)} %select_n.3), kind=kLoop, calls=%fused_computation.10 | loop fusion | bytes 3801092 | tf_op jit(solution)/shard_map/dynamic_slice | solution.py:397
  15.4 1.1 collective-permute-start.15
  16.5 4.4 %collective-permute-done.3.other = bf16[144,1024]{1,0:T(8,128)(2,1)S(1)} collective-permute-done((bf16[144,1024]{1,0:T(8,128)(2,1)S(1)}, bf16[144,1024]{1,0:T(8,128)(2,1)S(1)}, u32[]{:S(2)}, u32[]{:S(2)}) %collective-permute-start.3) | collective-permute-done | bytes 294944 | tf_op jit(solution)/shard_map/block_x1/ppermute | solution.py:29
  20.9 0.2 pick_body.1
  21.1 0.6 collective-permute-start.9
  21.7 2.3 %collective-permute-done.4.refs_7_ = bf16[64,3696]{1,0:T(8,128)(2,1)S(1)} collective-permute-done((bf16[64,3696]{1,0:T(8,128)(2,1)}, bf16[64,3696]{1,0:T(8,128)(2,1)S(1)}, u32[]{:S(2)}, u32[]{:S(2)}) %collective-permute-start.4) | collective-permute-done | bytes 473120 | tf_op jit(solution)/shard_map/y3/ppermute | solution.py:29
  24.0 0.3 collective-permute-start.5
  24.3 3.3 %collective-permute-done.5 = f32[8,128]{1,0:T(8,128)S(1)} collective-permute-done((f32[8,128]{1,0:T(8,128)S(1)}, f32[8,128]{1,0:T(8,128)S(1)}, u32[]{:S(2)}, u32[]{:S(2)}) %collective-permute-start.5) | collective-permute-done | bytes 4128 | tf_op jit(solution)/shard_map/sums0/ppermute | solution.py:29
  27.6 6.3 %collective-permute-done.1.refs_2_ = bf16[64,3696]{1,0:T(8,128)(2,1)S(1)} collective-permute-done((bf16[64,3696]{1,0:T(8,128)(2,1)}, bf16[64,3696]{1,0:T(8,128)(2,1)S(1)}, u32[]{:S(2)}, u32[]{:S(2)}) %collective-permute-start.1) | collective-permute-done | bytes 473120 | tf_op jit(solution)/shard_map/up/ppermute | solution.py:29
  33.9 3.8 %collective-permute-start.8 = (f32[8,128]{1,0:T(8,128)S(1)}, f32[8,128]{1,0:T(8,128)S(1)}, u32[]{:S(2)}, u32[]{:S(2)}) collective-permute-start(f32[8,128]{1,0:T(8,128)S(1)} %add.18), channel_id=1, source_target_pairs={{0,4},{1,5},{2,6},{3,7},{4,0},{5,1},{6,2},{7,3},{8,12},{9,13},{10,... | collective-permute-start | bytes 12296 | tf_op jit(solution)/shard_map/sums1/ppermute | solution.py:29
  37.7 0.1 collective-permute-start.6
  37.8 4.2 %collective-permute-start.7 = (bf16[32,3696]{1,0:T(8,128)(2,1)S(1)}, bf16[32,3696]{1,0:T(8,128)(2,1)S(1)}, u32[]{:S(2)}, u32[]{:S(2)}) collective-permute-start(bf16[32,3696]{1,0:T(8,128)(2,1)S(1)} %slice.7), channel_id=1, source_target_pairs={{0,12},{1,13},{2,14},{3,15},{4,0},{5,1},{6,2},{7,3},{8,4},{9,5},{1... | collective-permute-start | bytes 709640 | tf_op jit(solution)/shard_map/far_b/ppermute | solution.py:29
  42.0 0.1 pad_maximum_fusion
  42.1 0.2 collective-permute-start.12
  42.4 6.0 %collective-permute-done.6.refs_0_ = bf16[32,3696]{1,0:T(8,128)(2,1)S(1)} collective-permute-done((bf16[32,3696]{1,0:T(8,128)(2,1)S(1)}, bf16[32,3696]{1,0:T(8,128)(2,1)S(1)}, u32[]{:S(2)}, u32[]{:S(2)}) %collective-permute-start.6) | collective-permute-done | bytes 236576 | tf_op jit(solution)/shard_map/far_a/ppermute | solution.py:29
  48.4 3.3 %collective-permute-start.17 = (bf16[288,1024]{1,0:T(8,128)(2,1)S(1)}, bf16[288,1024]{1,0:T(8,128)(2,1)S(1)}, u32[]{:S(2)}, u32[]{:S(2)}) collective-permute-start(bf16[288,1024]{1,0:T(8,128)(2,1)S(1)} %constant_dynamic-update-slice_fusion.2.here), channel_id=1, source_target_pairs={{0,64},{16,80},{32,96},{48,112},{64,0},{80,16},{96,32},{112,48},{1... | collective-permute-start | bytes 1769480 | tf_op jit(solution)/shard_map/block_zlo/ppermute | solution.py:29
  51.8 0.2 collective-permute-start.11
  52.0 1.2 collective-permute-done.13
  53.2 0.5 collective-permute-start.14
  53.6 4.4 %collective-permute-done.14 = f32[24,128]{1,0:T(8,128)S(1)} collective-permute-done((f32[24,128]{1,0:T(8,128)S(1)}, f32[24,128]{1,0:T(8,128)S(1)}, u32[]{:S(2)}, u32[]{:S(2)}) %collective-permute-start.14) | collective-permute-done | bytes 12320 | tf_op jit(solution)/shard_map/tiny_x3/ppermute | solution.py:29
  58.1 5.9 %collective-permute-done.16.there = f32[48,128]{1,0:T(8,128)S(1)} collective-permute-done((f32[48,128]{1,0:T(8,128)S(1)}, f32[48,128]{1,0:T(8,128)S(1)}, u32[]{:S(2)}, u32[]{:S(2)}) %collective-permute-start.16) | collective-permute-done | bytes 24608 | tf_op jit(solution)/shard_map/tiny_zlo/ppermute | solution.py:29
  64.6 0.8 coefs_body.1.coefs
  65.4 0.5 collective-permute-start.18
  65.9 1.2 grad_body.1
  67.1 3.2 %collective-permute-done.18.coefs_mate = f32[8,128]{1,0:T(8,128)S(1)} collective-permute-done((f32[8,128]{1,0:T(8,128)S(1)}, f32[8,128]{1,0:T(8,128)S(1)}, u32[]{:S(2)}, u32[]{:S(2)}) %collective-permute-start.18) | collective-permute-done | bytes 4128 | tf_op jit(solution)/shard_map/coefs_mate/ppermute | solution.py:29
  70.3 3.1 %collective-permute-done.11.refs_5_ = bf16[64,3696]{1,0:T(8,128)(2,1)S(1)} collective-permute-done((bf16[64,3696]{1,0:T(8,128)(2,1)S(1)}, bf16[64,3696]{1,0:T(8,128)(2,1)S(1)}, u32[]{:S(2)}, u32[]{:S(2)}) %collective-permute-start.11) | collective-permute-done | bytes 473120 | tf_op jit(solution)/shard_map/y0/ppermute | solution.py:29
  73.5 2.2 %outer_mate.1 = (bf16[3696,256]{1,0:T(8,128)(2,1)S(1)}, f32[3696,256]{1,0:T(8,128)S(1)}) custom-call(bf16[32,3696]{1,0:T(8,128)(2,1)S(1)} %collective-permute-done.6.refs_0_, bf16[32,3696]{1,0:T(8,128)(2,1)S(1)} %collective-permute-done.7.refs_1_, bf16[64,3696]{1,0:T(8,128)(2,1)S(1)} %collective-permute-done.1.refs_2_, ...), custom_call_target="tpu_custom_call" | custom-call | flops 1937768448 | bytes 8388608 | tf_op jit(solution)/shard_map/outer_mate/pallas_call | solution.py:55
  75.7 0.1 collective-permute-start.21
  75.8 4.0 %inner_sent.1 = (bf16[64,3696]{1,0:T(8,128)(2,1)S(1)}, bf16[64,3696]{1,0:T(8,128)(2,1)S(1)}, bf16[64,3696]{1,0:T(8,128)(2,1)S(1)}, bf16[64,3696]{1,0:T(8,128)(2,1)S(1)}) custom-call(bf16[256,1024]{1,0:T(8,128)(2,1)S(1)} %get-tuple-element.67.refs_9_.g, bf16[3696,512]{1,0:T(8,128)(2,1)S(1)} %copy-done, bf16[1856,512]{1,0:T(8,128)(2,1)S(1)} %collective-permute-done.15.got, ...), custom_call_target="tpu_custom_call" | custom-call | flops 1937768448 | bytes 10485760 | tf_op jit(solution)/shard_map/inner_sent/pallas_call | solution.py:55
  79.8 0.6 add_convert_fusion.1
  80.4 0.5 collective-permute-start.28
  80.9 0.2 collective-permute-start.20
  81.1 1.8 %collective-permute-start.25 = (bf16[64,3696]{1,0:T(8,128)(2,1)S(1)}, bf16[64,3696]{1,0:T(8,128)(2,1)S(1)}, u32[]{:S(2)}, u32[]{:S(2)}) collective-permute-start(bf16[64,3696]{1,0:T(8,128)(2,1)S(1)} %get-tuple-element.85), channel_id=1, source_target_pairs={{0,1},{1,0},{2,3},{3,2},{4,5},{5,4},{6,7},{7,6},{8,9},{9,8},{10,11... | collective-permute-start | bytes 1419272 | tf_op jit(solution)/shard_map/t1/ppermute | solution.py:29
  82.9 4.0 %inner_own.1 = (f32[64,3696]{1,0:T(8,128)S(1)}, f32[64,3696]{1,0:T(8,128)S(1)}, f32[64,3696]{1,0:T(8,128)S(1)}, f32[64,3696]{1,0:T(8,128)S(1)}) custom-call(bf16[256,1024]{1,0:T(8,128)(2,1)S(1)} %get-tuple-element.76.refs_8_.g, bf16[3696,512]{1,0:T(8,128)(2,1)S(1)} %copy-done, bf16[1856,512]{1,0:T(8,128)(2,1)S(1)} %collective-permute-done.15.got, ...), custom_call_target="tpu_custom_call" | custom-call | flops 1937768448 | bytes 10485760 | tf_op jit(solution)/shard_map/inner_own/pallas_call | solution.py:55
  86.9 7.7 %collective-permute-done.20.other = bf16[64,3696]{1,0:T(8,128)(2,1)S(1)} collective-permute-done((bf16[64,3696]{1,0:T(8,128)(2,1)S(1)}, bf16[64,3696]{1,0:T(8,128)(2,1)S(1)}, u32[]{:S(2)}, u32[]{:S(2)}) %collective-permute-start.20) | collective-permute-done | bytes 473120 | tf_op jit(solution)/shard_map/t0/ppermute | solution.py:29
  94.7 0.4 collective-permute-start.24
  95.1 0.2 collective-permute-start.22
  95.2 2.6 %collective-permute-start.23 = (bf16[32,3696]{1,0:T(8,128)(2,1)S(1)}, bf16[32,3696]{1,0:T(8,128)(2,1)S(1)}, u32[]{:S(2)}, u32[]{:S(2)}) collective-permute-start(bf16[32,3696]{1,0:T(8,128)(2,1)S(1)} %get-tuple-element.75), channel_id=1, source_target_pairs={{0,4},{1,5},{2,6},{3,7},{4,8},{5,9},{6,10},{7,11},{8,12},{9,13},{1... | collective-permute-start | bytes 709640 | tf_op jit(solution)/shard_map/from_down/ppermute | solution.py:29
  97.9 2.2 %outer_own.1.partial = f32[3696,512]{1,0:T(8,128)S(1)} custom-call(bf16[32,3696]{1,0:T(8,128)(2,1)S(1)} %collective-permute-done.6.refs_0_, bf16[32,3696]{1,0:T(8,128)(2,1)S(1)} %collective-permute-done.7.refs_1_, bf16[64,3696]{1,0:T(8,128)(2,1)S(1)} %collective-permute-done.1.refs_2_, bf16[64,3696]{1,0:T(8,128)(2,1)S(1)} %collective-permute-done.refs_3_, ...), custom_call_target="tpu_custom_call" | custom-call | flops 1937768448 | bytes 8388608 | tf_op jit(solution)/shard_map/outer_own/pallas_call | solution.py:55
  100.1 4.7 %collective-permute-done.25.other = bf16[64,3696]{1,0:T(8,128)(2,1)S(1)} collective-permute-done((bf16[64,3696]{1,0:T(8,128)(2,1)S(1)}, bf16[64,3696]{1,0:T(8,128)(2,1)S(1)}, u32[]{:S(2)}, u32[]{:S(2)}) %collective-permute-start.25) | collective-permute-done | bytes 473120 | tf_op jit(solution)/shard_map/t1/ppermute | solution.py:29
  104.9 2.1 %collective-permute-start.26 = (bf16[32,3696]{1,0:T(8,128)(2,1)S(1)}, bf16[32,3696]{1,0:T(8,128)(2,1)S(1)}, u32[]{:S(2)}, u32[]{:S(2)}) collective-permute-start(bf16[32,3696]{1,0:T(8,128)(2,1)S(1)} %get-tuple-element.87), channel_id=1, source_target_pairs={{0,12},{1,13},{2,14},{3,15},{4,0},{5,1},{6,2},{7,3},{8,4},{9,5},{1... | collective-permute-start | bytes 709640 | tf_op jit(solution)/shard_map/pure_a/ppermute | solution.py:29
  107.0 0.9 collective-permute-start.27
  107.9 0.9 own_grad_body.1
  108.7 5.5 %collective-permute-done.22.other = bf16[64,3696]{1,0:T(8,128)(2,1)S(1)} collective-permute-done((bf16[64,3696]{1,0:T(8,128)(2,1)S(1)}, bf16[64,3696]{1,0:T(8,128)(2,1)S(1)}, u32[]{:S(2)}, u32[]{:S(2)}) %collective-permute-start.22) | collective-permute-done | bytes 473120 | tf_op jit(solution)/shard_map/t2/ppermute | solution.py:29
  114.2 0.2 fold_body.4
  114.4 1.2 collective-permute-done.26.pure_a
  115.6 2.5 %collective-permute-done.27.pure_b = bf16[32,3696]{1,0:T(8,128)(2,1)S(1)} collective-permute-done((bf16[32,3696]{1,0:T(8,128)(2,1)S(1)}, bf16[32,3696]{1,0:T(8,128)(2,1)S(1)}, u32[]{:S(2)}, u32[]{:S(2)}) %collective-permute-start.27) | collective-permute-done | bytes 236576 | tf_op jit(solution)/shard_map/pure_b/ppermute | solution.py:29
  118.1 7.2 %collective-permute-done.28.recv = bf16[3696,256]{1,0:T(8,128)(2,1)S(1)} collective-permute-done((bf16[3696,256]{1,0:T(8,128)(2,1)S(1)}, bf16[3696,256]{1,0:T(8,128)(2,1)S(1)}, u32[]{:S(2)}, u32[]{:S(2)}) %collective-permute-start.28) | collective-permute-done | bytes 1892384 | tf_op jit(solution)/shard_map/w_recv/ppermute | solution.py:29
  125.3 0.6 merge_body.1
  125.9 0.1 collective-permute-start.29
  126.0 0.1 collective-permute-start.30
  126.1 0.4 collective-permute-start.31
  126.6 3.8 %collective-permute-start.32 = (bf16[32,3696]{1,0:T(8,128)(2,1)S(1)}, bf16[32,3696]{1,0:T(8,128)(2,1)S(1)}, u32[]{:S(2)}, u32[]{:S(2)}) collective-permute-start(bf16[32,3696]{1,0:T(8,128)(2,1)S(1)} %get-tuple-element.96), channel_id=1, source_target_pairs={{0,12},{1,13},{2,14},{3,15},{4,0},{5,1},{6,2},{7,3},{8,4},{9,5},{1... | collective-permute-start | bytes 709640 | tf_op jit(solution)/shard_map/mixed_b/ppermute | solution.py:29
  130.3 2.2 %collective-permute-done.29 = bf16[3696,512]{1,0:T(8,128)(2,1)S(1)} collective-permute-done((bf16[3696,512]{1,0:T(8,128)(2,1)S(1)}, bf16[3696,512]{1,0:T(8,128)(2,1)S(1)}, u32[]{:S(2)}, u32[]{:S(2)}) %collective-permute-start.29) | collective-permute-done | bytes 3784736 | tf_op jit(solution)/shard_map/part/ppermute | solution.py:29
  132.6 3.0 %add_convert_fusion = bf16[3696,512]{1,0:T(8,128)(2,1)} fusion(bf16[3696,512]{1,0:T(8,128)(2,1)S(1)} %collective-permute-done.29, bf16[3696,512]{1,0:T(8,128)(2,1)S(1)} %merge_body.1), kind=kLoop, calls=%fused_computation | loop fusion | flops 7569408 | bytes 11354112 | tf_op jit(solution)/shard_map/convert_element_type | solution.py:468
  135.5 3.8 %collective-permute-done.30.other = bf16[64,3696]{1,0:T(8,128)(2,1)S(1)} collective-permute-done((bf16[64,3696]{1,0:T(8,128)(2,1)S(1)}, bf16[64,3696]{1,0:T(8,128)(2,1)S(1)}, u32[]{:S(2)}, u32[]{:S(2)}) %collective-permute-start.30) | collective-permute-done | bytes 473120 | tf_op jit(solution)/shard_map/t3/ppermute | solution.py:29
  139.3 1.0 here_body.1
  (38 shorter events, 0.4 us)
Async XLA Ops:
  2.3 9.5 %collective-permute-start.2 = (bf16[144,512]{1,0:T(8,128)(2,1)}, bf16[144,512]{1,0:T(8,128)(2,1)S(1)}, u32[]{:S(2)}, u32[]{:S(2)}) collective-permute-start(bf16[144,512]{1,0:T(8,128)(2,1)} %prep_body.1), channel_id=1, source_target_pairs={{0,3},{1,2},{2,1},{3,0},{4,7},{5,6},{6,5},{7,4},{8,11},{9,10},{10,... | collective-permute-start | bytes 442376 | tf_op jit(solution)/shard_map/payload_mate/ppermute | solution.py:29
  5.4 22.2 %collective-permute-start = (bf16[64,3696]{1,0:T(8,128)(2,1)}, bf16[64,3696]{1,0:T(8,128)(2,1)S(1)}, u32[]{:S(2)}, u32[]{:S(2)}) collective-permute-start(bf16[64,3696]{1,0:T(8,128)(2,1)} %refs_4_.3), channel_id=1, source_target_pairs={{0,4},{1,5},{2,6},{3,7},{4,8},{5,9},{6,10},{7,11},{8,12},{9,13},{1... | collective-permute-start | bytes 1419272 | tf_op jit(solution)/shard_map/down/ppermute | solution.py:29
  8.7 25.2 %collective-permute-start.1 = (bf16[64,3696]{1,0:T(8,128)(2,1)}, bf16[64,3696]{1,0:T(8,128)(2,1)S(1)}, u32[]{:S(2)}, u32[]{:S(2)}) collective-permute-start(bf16[64,3696]{1,0:T(8,128)(2,1)} %refs_4_.3), channel_id=1, source_target_pairs={{0,12},{1,13},{2,14},{3,15},{4,0},{5,1},{6,2},{7,3},{8,4},{9,5},{1... | collective-permute-start | bytes 1419272 | tf_op jit(solution)/shard_map/up/ppermute | solution.py:29
  11.7 12.3 %collective-permute-start.4 = (bf16[64,3696]{1,0:T(8,128)(2,1)}, bf16[64,3696]{1,0:T(8,128)(2,1)S(1)}, u32[]{:S(2)}, u32[]{:S(2)}) collective-permute-start(bf16[64,3696]{1,0:T(8,128)(2,1)} %refs_4_.3), channel_id=1, source_target_pairs={{0,1},{1,0},{2,3},{3,2},{4,5},{5,4},{6,7},{7,6},{8,9},{9,8},{10,11... | collective-permute-start | bytes 1419272 | tf_op jit(solution)/shard_map/y3/ppermute | solution.py:29
  12.8 8.1 %collective-permute-start.3 = (bf16[144,1024]{1,0:T(8,128)(2,1)S(1)}, bf16[144,1024]{1,0:T(8,128)(2,1)S(1)}, u32[]{:S(2)}, u32[]{:S(2)}) collective-permute-start(bf16[144,1024]{1,0:T(8,128)(2,1)S(1)} %pad_maximum_fusion.2.own), channel_id=1, source_target_pairs={{0,16},{16,0},{32,48},{48,32},{64,80},{80,64},{96,112},{112,96},{1... | collective-permute-start | bytes 884744 | tf_op jit(solution)/shard_map/block_x1/ppermute | solution.py:29
  15.3 58.1 %copy-start.2 = (bf16[64,3696]{1,0:T(8,128)(2,1)S(1)}, bf16[64,3696]{1,0:T(8,128)(2,1)}, u32[]{:S(2)}) copy-start(bf16[64,3696]{1,0:T(8,128)(2,1)} %refs_4_.3) | copy-start | bytes 1419268
  15.4 48.6 %collective-permute-start.15 = (bf16[1856,512]{1,0:T(8,128)(2,1)S(1)}, bf16[1856,512]{1,0:T(8,128)(2,1)S(1)}, u32[]{:S(2)}, u32[]{:S(2)}) collective-permute-start(bf16[1856,512]{1,0:T(8,128)(2,1)S(1)} %constant_dynamic-slice_fusion), channel_id=1, source_target_pairs={{0,3},{1,2},{2,1},{3,0},{4,7},{5,6},{6,5},{7,4},{8,11},{9,10},{10,... | collective-permute-start | bytes 5701640 | tf_op jit(solution)/shard_map/got/ppermute | solution.py:29
  21.1 21.2 %collective-permute-start.9 = (bf16[144,1024]{1,0:T(8,128)(2,1)S(1)}, bf16[144,1024]{1,0:T(8,128)(2,1)S(1)}, u32[]{:S(2)}, u32[]{:S(2)}) collective-permute-start(bf16[144,1024]{1,0:T(8,128)(2,1)S(1)} %get-tuple-element.56.block), channel_id=1, source_target_pairs={{0,48},{16,32},{32,16},{48,0},{64,112},{80,96},{96,80},{112,64},{1... | collective-permute-start | bytes 884744 | tf_op jit(solution)/shard_map/block_x3/ppermute | solution.py:29
  24.0 3.6 %collective-permute-start.5 = (f32[8,128]{1,0:T(8,128)S(1)}, f32[8,128]{1,0:T(8,128)S(1)}, u32[]{:S(2)}, u32[]{:S(2)}) collective-permute-start(f32[8,128]{1,0:T(8,128)S(1)} %get-tuple-element.52), channel_id=1, source_target_pairs={{0,1},{1,0},{2,3},{3,2},{4,5},{5,4},{6,7},{7,6},{8,9},{9,8},{10,11... | collective-permute-start | bytes 12296 | tf_op jit(solution)/shard_map/sums0/ppermute | solution.py:29
  33.9 8.2 %collective-permute-start.8 = (f32[8,128]{1,0:T(8,128)S(1)}, f32[8,128]{1,0:T(8,128)S(1)}, u32[]{:S(2)}, u32[]{:S(2)}) collective-permute-start(f32[8,128]{1,0:T(8,128)S(1)} %add.18), channel_id=1, source_target_pairs={{0,4},{1,5},{2,6},{3,7},{4,0},{5,1},{6,2},{7,3},{8,12},{9,13},{10,... | collective-permute-start | bytes 12296 | tf_op jit(solution)/shard_map/sums1/ppermute | solution.py:29
  37.7 10.7 %collective-permute-start.6 = (bf16[32,3696]{1,0:T(8,128)(2,1)S(1)}, bf16[32,3696]{1,0:T(8,128)(2,1)S(1)}, u32[]{:S(2)}, u32[]{:S(2)}) collective-permute-start(bf16[32,3696]{1,0:T(8,128)(2,1)S(1)} %slice.6), channel_id=1, source_target_pairs={{0,4},{1,5},{2,6},{3,7},{4,8},{5,9},{6,10},{7,11},{8,12},{9,13},{1... | collective-permute-start | bytes 709640 | tf_op jit(solution)/shard_map/far_a/ppermute | solution.py:29
  37.8 13.9 %collective-permute-start.7 = (bf16[32,3696]{1,0:T(8,128)(2,1)S(1)}, bf16[32,3696]{1,0:T(8,128)(2,1)S(1)}, u32[]{:S(2)}, u32[]{:S(2)}) collective-permute-start(bf16[32,3696]{1,0:T(8,128)(2,1)S(1)} %slice.7), channel_id=1, source_target_pairs={{0,12},{1,13},{2,14},{3,15},{4,0},{5,1},{6,2},{7,3},{8,4},{9,5},{1... | collective-permute-start | bytes 709640 | tf_op jit(solution)/shard_map/far_b/ppermute | solution.py:29
  42.1 31.4 %collective-permute-start.12 = (bf16[2,64,3696]{2,1,0:T(8,128)(2,1)S(1)}, bf16[2,64,3696]{2,1,0:T(8,128)(2,1)S(1)}, u32[]{:S(2)}, u32[]{:S(2)}) collective-permute-start(bf16[2,64,3696]{2,1,0:T(8,128)(2,1)S(1)} %pad_maximum_fusion), channel_id=1, source_target_pairs={{0,1},{1,0},{2,3},{3,2},{4,5},{5,4},{6,7},{7,6},{8,9},{9,8},{10,11... | collective-permute-start | bytes 2838536 | tf_op jit(solution)/shard_map/y12/ppermute | solution.py:29
  42.3 9.4 %collective-permute-start.10 = (f32[8,128]{1,0:T(8,128)S(1)}, f32[8,128]{1,0:T(8,128)S(1)}, u32[]{:S(2)}, u32[]{:S(2)}) collective-permute-start(f32[8,128]{1,0:T(8,128)S(1)} %add.19), channel_id=1, source_target_pairs={{0,12},{1,13},{2,14},{3,15},{4,8},{5,9},{6,10},{7,11},{8,4},{9,5},... | collective-permute-start | bytes 12296 | tf_op jit(solution)/shard_map/sums2/ppermute | solution.py:29
  48.4 17.5 %collective-permute-start.17 = (bf16[288,1024]{1,0:T(8,128)(2,1)S(1)}, bf16[288,1024]{1,0:T(8,128)(2,1)S(1)}, u32[]{:S(2)}, u32[]{:S(2)}) collective-permute-start(bf16[288,1024]{1,0:T(8,128)(2,1)S(1)} %constant_dynamic-update-slice_fusion.2.here), channel_id=1, source_target_pairs={{0,64},{16,80},{32,96},{48,112},{64,0},{80,16},{96,32},{112,48},{1... | collective-permute-start | bytes 1769480 | tf_op jit(solution)/shard_map/block_zlo/ppermute | solution.py:29
  51.8 21.7 %collective-permute-start.11 = (bf16[64,3696]{1,0:T(8,128)(2,1)S(1)}, bf16[64,3696]{1,0:T(8,128)(2,1)S(1)}, u32[]{:S(2)}, u32[]{:S(2)}) collective-permute-start(bf16[64,3696]{1,0:T(8,128)(2,1)S(1)} %pad_maximum_fusion.1), channel_id=1, source_target_pairs={{0,1},{1,0},{2,3},{3,2},{4,5},{5,4},{6,7},{7,6},{8,9},{9,8},{10,11... | collective-permute-start | bytes 1419272 | tf_op jit(solution)/shard_map/y0/ppermute | solution.py:29
  52.0 1.2 collective-permute-start.13
  53.2 4.9 %collective-permute-start.14 = (f32[24,128]{1,0:T(8,128)S(1)}, f32[24,128]{1,0:T(8,128)S(1)}, u32[]{:S(2)}, u32[]{:S(2)}) collective-permute-start(f32[24,128]{1,0:T(8,128)S(1)} %pad_maximum_fusion.3), channel_id=1, source_target_pairs={{0,48},{16,32},{32,16},{48,0},{64,112},{80,96},{96,80},{112,64},{1... | collective-permute-start | bytes 36872 | tf_op jit(solution)/shard_map/tiny_x3/ppermute | solution.py:29
  58.1 5.9 %collective-permute-start.16 = (f32[48,128]{1,0:T(8,128)S(1)}, f32[48,128]{1,0:T(8,128)S(1)}, u32[]{:S(2)}, u32[]{:S(2)}) collective-permute-start(f32[48,128]{1,0:T(8,128)S(1)} %constant_dynamic-update-slice_fusion.here), channel_id=1, source_target_pairs={{0,64},{16,80},{32,96},{48,112},{64,0},{80,16},{96,32},{112,48},{1... | collective-permute-start | bytes 73736 | tf_op jit(solution)/shard_map/tiny_zlo/ppermute | solution.py:29
  64.0 11.8 %collective-permute-start.19 = (bf16[1856,512]{1,0:T(8,128)(2,1)S(1)}, bf16[1856,512]{1,0:T(8,128)(2,1)S(1)}, u32[]{:S(2)}, u32[]{:S(2)}) collective-permute-start(bf16[1856,512]{1,0:T(8,128)(2,1)S(1)} %collective-permute-done.15.got), channel_id=1, source_target_pairs={{0,128},{128,0},{1,129},{129,1},{2,130},{130,2},{3,131},{131,3},{4... | collective-permute-start | bytes 5701640 | tf_op jit(solution)/shard_map/got_other/ppermute | solution.py:29
  65.4 4.9 %collective-permute-start.18 = (f32[8,128]{1,0:T(8,128)S(1)}, f32[8,128]{1,0:T(8,128)S(1)}, u32[]{:S(2)}, u32[]{:S(2)}) collective-permute-start(f32[8,128]{1,0:T(8,128)S(1)} %coefs_body.1.coefs), channel_id=1, source_target_pairs={{0,3},{1,2},{2,1},{3,0},{4,7},{5,6},{6,5},{7,4},{8,11},{9,10},{10,... | collective-permute-start | bytes 12296 | tf_op jit(solution)/shard_map/coefs_mate/ppermute | solution.py:29
  67.1 8.7 %copy-start = (bf16[3696,512]{1,0:T(8,128)(2,1)S(1)}, bf16[3696,512]{1,0:T(8,128)(2,1)}, u32[]{:S(2)}) copy-start(bf16[3696,512]{1,0:T(8,128)(2,1)} %w.3) | copy-start | bytes 11354116
  75.7 4.1 %collective-permute-start.21 = (bf16[3696,256]{1,0:T(8,128)(2,1)S(1)}, bf16[3696,256]{1,0:T(8,128)(2,1)S(1)}, u32[]{:S(2)}, u32[]{:S(2)}) collective-permute-start(bf16[3696,256]{1,0:T(8,128)(2,1)S(1)} %get-tuple-element.73), channel_id=1, source_target_pairs={{0,128},{128,0},{1,129},{129,1},{2,130},{130,2},{3,131},{131,3},{4... | collective-permute-start | bytes 5677064 | tf_op jit(solution)/shard_map/mate_got/ppermute | solution.py:29
  80.4 44.9 %collective-permute-start.28 = (bf16[3696,256]{1,0:T(8,128)(2,1)S(1)}, bf16[3696,256]{1,0:T(8,128)(2,1)S(1)}, u32[]{:S(2)}, u32[]{:S(2)}) collective-permute-start(bf16[3696,256]{1,0:T(8,128)(2,1)S(1)} %add_convert_fusion.1), channel_id=1, source_target_pairs={{0,3},{1,2},{2,1},{3,0},{4,7},{5,6},{6,5},{7,4},{8,11},{9,10},{10,... | collective-permute-start | bytes 5677064 | tf_op jit(solution)/shard_map/w_recv/ppermute | solution.py:29
  80.9 13.7 %collective-permute-start.20 = (bf16[64,3696]{1,0:T(8,128)(2,1)S(1)}, bf16[64,3696]{1,0:T(8,128)(2,1)S(1)}, u32[]{:S(2)}, u32[]{:S(2)}) collective-permute-start(bf16[64,3696]{1,0:T(8,128)(2,1)S(1)} %get-tuple-element.69), channel_id=1, source_target_pairs={{0,1},{1,0},{2,3},{3,2},{4,5},{5,4},{6,7},{7,6},{8,9},{9,8},{10,11... | collective-permute-start | bytes 1419272 | tf_op jit(solution)/shard_map/t0/ppermute | solution.py:29
  81.1 23.7 %collective-permute-start.25 = (bf16[64,3696]{1,0:T(8,128)(2,1)S(1)}, bf16[64,3696]{1,0:T(8,128)(2,1)S(1)}, u32[]{:S(2)}, u32[]{:S(2)}) collective-permute-start(bf16[64,3696]{1,0:T(8,128)(2,1)S(1)} %get-tuple-element.85), channel_id=1, source_target_pairs={{0,1},{1,0},{2,3},{3,2},{4,5},{5,4},{6,7},{7,6},{8,9},{9,8},{10,11... | collective-permute-start | bytes 1419272 | tf_op jit(solution)/shard_map/t1/ppermute | solution.py:29
  94.7 10.1 %collective-permute-start.24 = (bf16[32,3696]{1,0:T(8,128)(2,1)S(1)}, bf16[32,3696]{1,0:T(8,128)(2,1)S(1)}, u32[]{:S(2)}, u32[]{:S(2)}) collective-permute-start(bf16[32,3696]{1,0:T(8,128)(2,1)S(1)} %get-tuple-element.81), channel_id=1, source_target_pairs={{0,12},{1,13},{2,14},{3,15},{4,0},{5,1},{6,2},{7,3},{8,4},{9,5},{1... | collective-permute-start | bytes 709640 | tf_op jit(solution)/shard_map/from_up/ppermute | solution.py:29
  95.1 19.2 %collective-permute-start.22 = (bf16[64,3696]{1,0:T(8,128)(2,1)S(1)}, bf16[64,3696]{1,0:T(8,128)(2,1)S(1)}, u32[]{:S(2)}, u32[]{:S(2)}) collective-permute-start(bf16[64,3696]{1,0:T(8,128)(2,1)S(1)} %get-tuple-element.78), channel_id=1, source_target_pairs={{0,1},{1,0},{2,3},{3,2},{4,5},{5,4},{6,7},{7,6},{8,9},{9,8},{10,11... | collective-permute-start | bytes 1419272 | tf_op jit(solution)/shard_map/t2/ppermute | solution.py:29
  95.2 12.6 %copy-start.1 = (bf16[128,512]{1,0:T(8,128)(2,1)S(1)}, bf16[128,512]{1,0:T(8,128)(2,1)}, u32[]{:S(2)}) copy-start(bf16[128,512]{1,0:T(8,128)(2,1)} %stream.2) | copy-start | bytes 393220
  95.2 19.0 %collective-permute-start.23 = (bf16[32,3696]{1,0:T(8,128)(2,1)S(1)}, bf16[32,3696]{1,0:T(8,128)(2,1)S(1)}, u32[]{:S(2)}, u32[]{:S(2)}) collective-permute-start(bf16[32,3696]{1,0:T(8,128)(2,1)S(1)} %get-tuple-element.75), channel_id=1, source_target_pairs={{0,4},{1,5},{2,6},{3,7},{4,8},{5,9},{6,10},{7,11},{8,12},{9,13},{1... | collective-permute-start | bytes 709640 | tf_op jit(solution)/shard_map/from_down/ppermute | solution.py:29
  104.9 10.8 %collective-permute-start.26 = (bf16[32,3696]{1,0:T(8,128)(2,1)S(1)}, bf16[32,3696]{1,0:T(8,128)(2,1)S(1)}, u32[]{:S(2)}, u32[]{:S(2)}) collective-permute-start(bf16[32,3696]{1,0:T(8,128)(2,1)S(1)} %get-tuple-element.87), channel_id=1, source_target_pairs={{0,12},{1,13},{2,14},{3,15},{4,0},{5,1},{6,2},{7,3},{8,4},{9,5},{1... | collective-permute-start | bytes 709640 | tf_op jit(solution)/shard_map/pure_a/ppermute | solution.py:29
  107.0 11.2 %collective-permute-start.27 = (bf16[32,3696]{1,0:T(8,128)(2,1)S(1)}, bf16[32,3696]{1,0:T(8,128)(2,1)S(1)}, u32[]{:S(2)}, u32[]{:S(2)}) collective-permute-start(bf16[32,3696]{1,0:T(8,128)(2,1)S(1)} %get-tuple-element.88), channel_id=1, source_target_pairs={{0,4},{1,5},{2,6},{3,7},{4,8},{5,9},{6,10},{7,11},{8,12},{9,13},{1... | collective-permute-start | bytes 709640 | tf_op jit(solution)/shard_map/pure_b/ppermute | solution.py:29
  125.9 6.7 %collective-permute-start.29 = (bf16[3696,512]{1,0:T(8,128)(2,1)S(1)}, bf16[3696,512]{1,0:T(8,128)(2,1)S(1)}, u32[]{:S(2)}, u32[]{:S(2)}) collective-permute-start(bf16[3696,512]{1,0:T(8,128)(2,1)S(1)} %merge_body.1), channel_id=1, source_target_pairs={{0,128},{128,0},{1,129},{129,1},{2,130},{130,2},{3,131},{131,3},{4... | collective-permute-start | bytes 11354120 | tf_op jit(solution)/shard_map/part/ppermute | solution.py:29
  126.0 13.3 %collective-permute-start.30 = (bf16[64,3696]{1,0:T(8,128)(2,1)S(1)}, bf16[64,3696]{1,0:T(8,128)(2,1)S(1)}, u32[]{:S(2)}, u32[]{:S(2)}) collective-permute-start(bf16[64,3696]{1,0:T(8,128)(2,1)S(1)} %get-tuple-element.93), channel_id=1, source_target_pairs={{0,1},{1,0},{2,3},{3,2},{4,5},{5,4},{6,7},{7,6},{8,9},{9,8},{10,11... | collective-permute-start | bytes 1419272 | tf_op jit(solution)/shard_map/t3/ppermute | solution.py:29
  126.1 13.2 %collective-permute-start.31 = (bf16[32,3696]{1,0:T(8,128)(2,1)S(1)}, bf16[32,3696]{1,0:T(8,128)(2,1)S(1)}, u32[]{:S(2)}, u32[]{:S(2)}) collective-permute-start(bf16[32,3696]{1,0:T(8,128)(2,1)S(1)} %get-tuple-element.89), channel_id=1, source_target_pairs={{0,4},{1,5},{2,6},{3,7},{4,8},{5,9},{6,10},{7,11},{8,12},{9,13},{1... | collective-permute-start | bytes 709640 | tf_op jit(solution)/shard_map/mixed_a/ppermute | solution.py:29
  126.6 12.8 %collective-permute-start.32 = (bf16[32,3696]{1,0:T(8,128)(2,1)S(1)}, bf16[32,3696]{1,0:T(8,128)(2,1)S(1)}, u32[]{:S(2)}, u32[]{:S(2)}) collective-permute-start(bf16[32,3696]{1,0:T(8,128)(2,1)S(1)} %get-tuple-element.96), channel_id=1, source_target_pairs={{0,12},{1,13},{2,14},{3,15},{4,0},{5,1},{6,2},{7,3},{8,4},{9,5},{1... | collective-permute-start | bytes 709640 | tf_op jit(solution)/shard_map/mixed_b/ppermute | solution.py:29

commit v9 on v8

--- a/solution.py
+++ b/solution.py
@@ -389,8 +389,7 @@
         grant=56,
     )
     payload_mate = col(payload, MATE, "payload_mate")
-    ready = after(hidden, payload)
-    y3 = col(ready, PAIR, "y3")
+    y3 = col(after(hidden, payload_mate), PAIR, "y3")
     down = col(hidden, ZUP, "down")
     up = col(hidden, ZDOWN, "up")
 

time: 141 us -> 142 us (level)
  no operation moved by 1% of the time
where the time goes in v9:
time: 142 us; the launch traced here: 141 us
  waiting for transfers between devices  75 us (53%)
  starting transfers between devices  38.9 us (27%)
  Pallas kernels  18.9 us (13%)
  other arithmetic  4.65 us (3%)
  local copies, waits for them, and re-layouts  1.74 us (1%)
  between operations  1.5 us (1%)
    ppermute x33, waiting for transfers between devices, send(): return lax.ppermute(a, axis, perm)  75 us
    ppermute x33, starting transfers between devices, send(): return lax.ppermute(a, axis, perm)  38.9 us
    pallas_call x14, Pallas kernels, call(): pl.pallas_call(body, out_shape=out_shape, scratch_shapes=list(scratch), c...  18.9 us
    convert_element_type x1, other arithmetic, per_device(): weight_grad = (part.astype(f32) + part_other.astype(f32)).astype(bf16)  2.96 us
  transfers between devices with their start and end apart: 33, of which 18 were waited for; matrix products, arithmetic and copies ran while one was open for 4% of the time, Pallas kernels for 11%

profile of v9, /device:TPU:6, one launch (start us, length us, event | category | flops | bytes accessed | tf_op | source)
XLA Modules:
  0.0 140.7 jit_solution(11659266825039219510)
XLA Ops:
  0.6 1.6 %prep_body.1 = bf16[144,512]{1,0:T(8,128)(2,1)} custom-call(bf16[128,512]{1,0:T(8,128)(2,1)} %stream.2, f32[1,512]{1,0:T(1,128)} %bitcast.6, f32[1,512]{1,0:T(1,128)} %bitcast.7, f32[1,128]{1,0:T(1,128)} %reward.1, s32[1,128]{1,0:T(1,128)} %segment.1), custom_call_target="tpu_custom_call" | custom-call | tf_op jit(solution)/shard_map/prep_body/pallas_call | solution.py:55
  2.3 3.1 %collective-permute-start.2 = (bf16[144,512]{1,0:T(8,128)(2,1)}, bf16[144,512]{1,0:T(8,128)(2,1)S(1)}, u32[]{:S(2)}, u32[]{:S(2)}) collective-permute-start(bf16[144,512]{1,0:T(8,128)(2,1)} %prep_body.1), channel_id=1, source_target_pairs={{0,3},{1,2},{2,1},{3,0},{4,7},{5,6},{6,5},{7,4},{8,11},{9,10},{10,... | collective-permute-start | bytes 442376 | tf_op jit(solution)/shard_map/payload_mate/ppermute | solution.py:29
  5.4 3.3 %collective-permute-start = (bf16[64,3696]{1,0:T(8,128)(2,1)}, bf16[64,3696]{1,0:T(8,128)(2,1)S(1)}, u32[]{:S(2)}, u32[]{:S(2)}) collective-permute-start(bf16[64,3696]{1,0:T(8,128)(2,1)} %refs_4_.3), channel_id=1, source_target_pairs={{0,4},{1,5},{2,6},{3,7},{4,8},{5,9},{6,10},{7,11},{8,12},{9,13},{1... | collective-permute-start | bytes 1419272 | tf_op jit(solution)/shard_map/down/ppermute | solution.py:29
  8.7 3.0 %collective-permute-start.1 = (bf16[64,3696]{1,0:T(8,128)(2,1)}, bf16[64,3696]{1,0:T(8,128)(2,1)S(1)}, u32[]{:S(2)}, u32[]{:S(2)}) collective-permute-start(bf16[64,3696]{1,0:T(8,128)(2,1)} %refs_4_.3), channel_id=1, source_target_pairs={{0,12},{1,13},{2,14},{3,15},{4,0},{5,1},{6,2},{7,3},{8,4},{9,5},{1... | collective-permute-start | bytes 1419272 | tf_op jit(solution)/shard_map/up/ppermute | solution.py:29
  11.7 0.9 pad_maximum_fusion.2.own
  12.6 0.9 collective-permute-start.3
  13.6 0.1 collective-permute-start.4
  13.7 1.6 %constant_dynamic-slice_fusion = bf16[1856,512]{1,0:T(8,128)(2,1)S(1)} fusion(bf16[3696,512]{1,0:T(8,128)(2,1)} %w.3, s32[]{:T(128)S(6)} %select_n.3), kind=kLoop, calls=%fused_computation.10 | loop fusion | bytes 3801092 | tf_op jit(solution)/shard_map/dynamic_slice | solution.py:396
  15.4 1.1 collective-permute-start.15
  16.5 4.4 %collective-permute-done.3.other = bf16[144,1024]{1,0:T(8,128)(2,1)S(1)} collective-permute-done((bf16[144,1024]{1,0:T(8,128)(2,1)S(1)}, bf16[144,1024]{1,0:T(8,128)(2,1)S(1)}, u32[]{:S(2)}, u32[]{:S(2)}) %collective-permute-start.3) | collective-permute-done | bytes 294944 | tf_op jit(solution)/shard_map/block_x1/ppermute | solution.py:29
  20.9 0.2 pick_body.1
  21.1 0.6 collective-permute-start.9
  21.7 3.9 %collective-permute-done.4.refs_7_ = bf16[64,3696]{1,0:T(8,128)(2,1)S(1)} collective-permute-done((bf16[64,3696]{1,0:T(8,128)(2,1)}, bf16[64,3696]{1,0:T(8,128)(2,1)S(1)}, u32[]{:S(2)}, u32[]{:S(2)}) %collective-permute-start.4) | collective-permute-done | bytes 473120 | tf_op jit(solution)/shard_map/y3/ppermute | solution.py:29
  25.5 0.3 collective-permute-start.5
  25.8 3.3 %collective-permute-done.5 = f32[8,128]{1,0:T(8,128)S(1)} collective-permute-done((f32[8,128]{1,0:T(8,128)S(1)}, f32[8,128]{1,0:T(8,128)S(1)}, u32[]{:S(2)}, u32[]{:S(2)}) %collective-permute-start.5) | collective-permute-done | bytes 4128 | tf_op jit(solution)/shard_map/sums0/ppermute | solution.py:29
  29.1 4.7 %collective-permute-done.1.refs_2_ = bf16[64,3696]{1,0:T(8,128)(2,1)S(1)} collective-permute-done((bf16[64,3696]{1,0:T(8,128)(2,1)}, bf16[64,3696]{1,0:T(8,128)(2,1)S(1)}, u32[]{:S(2)}, u32[]{:S(2)}) %collective-permute-start.1) | collective-permute-done | bytes 473120 | tf_op jit(solution)/shard_map/up/ppermute | solution.py:29
  33.9 3.8 %collective-permute-start.8 = (f32[8,128]{1,0:T(8,128)S(1)}, f32[8,128]{1,0:T(8,128)S(1)}, u32[]{:S(2)}, u32[]{:S(2)}) collective-permute-start(f32[8,128]{1,0:T(8,128)S(1)} %add.18), channel_id=1, source_target_pairs={{0,4},{1,5},{2,6},{3,7},{4,0},{5,1},{6,2},{7,3},{8,12},{9,13},{10,... | collective-permute-start | bytes 12296 | tf_op jit(solution)/shard_map/sums1/ppermute | solution.py:29
  37.8 4.2 %collective-permute-start.7 = (bf16[32,3696]{1,0:T(8,128)(2,1)S(1)}, bf16[32,3696]{1,0:T(8,128)(2,1)S(1)}, u32[]{:S(2)}, u32[]{:S(2)}) collective-permute-start(bf16[32,3696]{1,0:T(8,128)(2,1)S(1)} %slice.7), channel_id=1, source_target_pairs={{0,12},{1,13},{2,14},{3,15},{4,0},{5,1},{6,2},{7,3},{8,4},{9,5},{1... | collective-permute-start | bytes 709640 | tf_op jit(solution)/shard_map/far_b/ppermute | solution.py:29
  42.0 0.1 pad_maximum_fusion
  42.1 0.2 collective-permute-start.12
  42.4 6.1 %collective-permute-done.10 = f32[8,128]{1,0:T(8,128)S(1)} collective-permute-done((f32[8,128]{1,0:T(8,128)S(1)}, f32[8,128]{1,0:T(8,128)S(1)}, u32[]{:S(2)}, u32[]{:S(2)}) %collective-permute-start.10) | collective-permute-done | bytes 4128 | tf_op jit(solution)/shard_map/sums2/ppermute | solution.py:29
  48.4 3.3 %collective-permute-start.17 = (bf16[288,1024]{1,0:T(8,128)(2,1)S(1)}, bf16[288,1024]{1,0:T(8,128)(2,1)S(1)}, u32[]{:S(2)}, u32[]{:S(2)}) collective-permute-start(bf16[288,1024]{1,0:T(8,128)(2,1)S(1)} %constant_dynamic-update-slice_fusion.2.here), channel_id=1, source_target_pairs={{0,64},{16,80},{32,96},{48,112},{64,0},{80,16},{96,32},{112,48},{1... | collective-permute-start | bytes 1769480 | tf_op jit(solution)/shard_map/block_zlo/ppermute | solution.py:29
  51.8 0.2 collective-permute-start.11
  52.0 1.2 collective-permute-done.13
  53.2 0.5 collective-permute-start.14
  53.7 4.4 %collective-permute-done.14 = f32[24,128]{1,0:T(8,128)S(1)} collective-permute-done((f32[24,128]{1,0:T(8,128)S(1)}, f32[24,128]{1,0:T(8,128)S(1)}, u32[]{:S(2)}, u32[]{:S(2)}) %collective-permute-start.14) | collective-permute-done | bytes 12320 | tf_op jit(solution)/shard_map/tiny_x3/ppermute | solution.py:29
  58.1 0.1 collective-permute-start.16
  58.2 5.8 %collective-permute-done.16.there = f32[48,128]{1,0:T(8,128)S(1)} collective-permute-done((f32[48,128]{1,0:T(8,128)S(1)}, f32[48,128]{1,0:T(8,128)S(1)}, u32[]{:S(2)}, u32[]{:S(2)}) %collective-permute-start.16) | collective-permute-done | bytes 24608 | tf_op jit(solution)/shard_map/tiny_zlo/ppermute | solution.py:29
  64.7 0.8 coefs_body.1.coefs
  65.5 0.5 collective-permute-start.18
  66.0 1.2 grad_body.1
  67.2 3.2 %collective-permute-done.18.coefs_mate = f32[8,128]{1,0:T(8,128)S(1)} collective-permute-done((f32[8,128]{1,0:T(8,128)S(1)}, f32[8,128]{1,0:T(8,128)S(1)}, u32[]{:S(2)}, u32[]{:S(2)}) %collective-permute-start.18) | collective-permute-done | bytes 4128 | tf_op jit(solution)/shard_map/coefs_mate/ppermute | solution.py:29
  70.4 3.1 %collective-permute-done.11.refs_5_ = bf16[64,3696]{1,0:T(8,128)(2,1)S(1)} collective-permute-done((bf16[64,3696]{1,0:T(8,128)(2,1)S(1)}, bf16[64,3696]{1,0:T(8,128)(2,1)S(1)}, u32[]{:S(2)}, u32[]{:S(2)}) %collective-permute-start.11) | collective-permute-done | bytes 473120 | tf_op jit(solution)/shard_map/y0/ppermute | solution.py:29
  73.5 2.2 %outer_mate.1 = (bf16[3696,256]{1,0:T(8,128)(2,1)S(1)}, f32[3696,256]{1,0:T(8,128)S(1)}) custom-call(bf16[32,3696]{1,0:T(8,128)(2,1)S(1)} %collective-permute-done.6.refs_0_, bf16[32,3696]{1,0:T(8,128)(2,1)S(1)} %collective-permute-done.7.refs_1_, bf16[64,3696]{1,0:T(8,128)(2,1)S(1)} %collective-permute-done.1.refs_2_, ...), custom_call_target="tpu_custom_call" | custom-call | flops 1937768448 | bytes 8388608 | tf_op jit(solution)/shard_map/outer_mate/pallas_call | solution.py:55
  75.7 0.1 collective-permute-start.21
  75.8 4.0 %inner_sent.1 = (bf16[64,3696]{1,0:T(8,128)(2,1)S(1)}, bf16[64,3696]{1,0:T(8,128)(2,1)S(1)}, bf16[64,3696]{1,0:T(8,128)(2,1)S(1)}, bf16[64,3696]{1,0:T(8,128)(2,1)S(1)}) custom-call(bf16[256,1024]{1,0:T(8,128)(2,1)S(1)} %get-tuple-element.67.refs_9_.g, bf16[3696,512]{1,0:T(8,128)(2,1)S(1)} %copy-done, bf16[1856,512]{1,0:T(8,128)(2,1)S(1)} %collective-permute-done.15.got, ...), custom_call_target="tpu_custom_call" | custom-call | flops 1937768448 | bytes 10485760 | tf_op jit(solution)/shard_map/inner_sent/pallas_call | solution.py:55
  79.8 0.6 add_convert_fusion.1
  80.4 0.5 collective-permute-start.28
  80.9 0.2 collective-permute-start.20
  81.1 1.8 %collective-permute-start.25 = (bf16[64,3696]{1,0:T(8,128)(2,1)S(1)}, bf16[64,3696]{1,0:T(8,128)(2,1)S(1)}, u32[]{:S(2)}, u32[]{:S(2)}) collective-permute-start(bf16[64,3696]{1,0:T(8,128)(2,1)S(1)} %get-tuple-element.85), channel_id=1, source_target_pairs={{0,1},{1,0},{2,3},{3,2},{4,5},{5,4},{6,7},{7,6},{8,9},{9,8},{10,11... | collective-permute-start | bytes 1419272 | tf_op jit(solution)/shard_map/t1/ppermute | solution.py:29
  82.9 4.0 %inner_own.1 = (f32[64,3696]{1,0:T(8,128)S(1)}, f32[64,3696]{1,0:T(8,128)S(1)}, f32[64,3696]{1,0:T(8,128)S(1)}, f32[64,3696]{1,0:T(8,128)S(1)}) custom-call(bf16[256,1024]{1,0:T(8,128)(2,1)S(1)} %get-tuple-element.76.refs_8_.g, bf16[3696,512]{1,0:T(8,128)(2,1)S(1)} %copy-done, bf16[1856,512]{1,0:T(8,128)(2,1)S(1)} %collective-permute-done.15.got, ...), custom_call_target="tpu_custom_call" | custom-call | flops 1937768448 | bytes 10485760 | tf_op jit(solution)/shard_map/inner_own/pallas_call | solution.py:55
  86.9 7.7 %collective-permute-done.20.other = bf16[64,3696]{1,0:T(8,128)(2,1)S(1)} collective-permute-done((bf16[64,3696]{1,0:T(8,128)(2,1)S(1)}, bf16[64,3696]{1,0:T(8,128)(2,1)S(1)}, u32[]{:S(2)}, u32[]{:S(2)}) %collective-permute-start.20) | collective-permute-done | bytes 473120 | tf_op jit(solution)/shard_map/t0/ppermute | solution.py:29
  94.7 0.4 collective-permute-start.24
  95.1 0.2 collective-permute-start.22
  95.2 2.6 %collective-permute-start.23 = (bf16[32,3696]{1,0:T(8,128)(2,1)S(1)}, bf16[32,3696]{1,0:T(8,128)(2,1)S(1)}, u32[]{:S(2)}, u32[]{:S(2)}) collective-permute-start(bf16[32,3696]{1,0:T(8,128)(2,1)S(1)} %get-tuple-element.75), channel_id=1, source_target_pairs={{0,4},{1,5},{2,6},{3,7},{4,8},{5,9},{6,10},{7,11},{8,12},{9,13},{1... | collective-permute-start | bytes 709640 | tf_op jit(solution)/shard_map/from_down/ppermute | solution.py:29
  97.9 2.2 %outer_own.1.partial = f32[3696,512]{1,0:T(8,128)S(1)} custom-call(bf16[32,3696]{1,0:T(8,128)(2,1)S(1)} %collective-permute-done.6.refs_0_, bf16[32,3696]{1,0:T(8,128)(2,1)S(1)} %collective-permute-done.7.refs_1_, bf16[64,3696]{1,0:T(8,128)(2,1)S(1)} %collective-permute-done.1.refs_2_, bf16[64,3696]{1,0:T(8,128)(2,1)S(1)} %collective-permute-done.refs_3_, ...), custom_call_target="tpu_custom_call" | custom-call | flops 1937768448 | bytes 8388608 | tf_op jit(solution)/shard_map/outer_own/pallas_call | solution.py:55
  100.1 4.7 %collective-permute-done.25.other = bf16[64,3696]{1,0:T(8,128)(2,1)S(1)} collective-permute-done((bf16[64,3696]{1,0:T(8,128)(2,1)S(1)}, bf16[64,3696]{1,0:T(8,128)(2,1)S(1)}, u32[]{:S(2)}, u32[]{:S(2)}) %collective-permute-start.25) | collective-permute-done | bytes 473120 | tf_op jit(solution)/shard_map/t1/ppermute | solution.py:29
  104.9 2.1 %collective-permute-start.26 = (bf16[32,3696]{1,0:T(8,128)(2,1)S(1)}, bf16[32,3696]{1,0:T(8,128)(2,1)S(1)}, u32[]{:S(2)}, u32[]{:S(2)}) collective-permute-start(bf16[32,3696]{1,0:T(8,128)(2,1)S(1)} %get-tuple-element.87), channel_id=1, source_target_pairs={{0,12},{1,13},{2,14},{3,15},{4,0},{5,1},{6,2},{7,3},{8,4},{9,5},{1... | collective-permute-start | bytes 709640 | tf_op jit(solution)/shard_map/pure_a/ppermute | solution.py:29
  107.0 1.2 collective-permute-start.27
  108.2 0.9 own_grad_body.1
  109.1 5.2 %collective-permute-done.22.other = bf16[64,3696]{1,0:T(8,128)(2,1)S(1)} collective-permute-done((bf16[64,3696]{1,0:T(8,128)(2,1)S(1)}, bf16[64,3696]{1,0:T(8,128)(2,1)S(1)}, u32[]{:S(2)}, u32[]{:S(2)}) %collective-permute-start.22) | collective-permute-done | bytes 473120 | tf_op jit(solution)/shard_map/t2/ppermute | solution.py:29
  114.2 0.2 fold_body.4
  114.4 3.1 %collective-permute-done.26.pure_a = bf16[32,3696]{1,0:T(8,128)(2,1)S(1)} collective-permute-done((bf16[32,3696]{1,0:T(8,128)(2,1)S(1)}, bf16[32,3696]{1,0:T(8,128)(2,1)S(1)}, u32[]{:S(2)}, u32[]{:S(2)}) %collective-permute-start.26) | collective-permute-done | bytes 236576 | tf_op jit(solution)/shard_map/pure_a/ppermute | solution.py:29
  117.5 7.9 %collective-permute-done.28.recv = bf16[3696,256]{1,0:T(8,128)(2,1)S(1)} collective-permute-done((bf16[3696,256]{1,0:T(8,128)(2,1)S(1)}, bf16[3696,256]{1,0:T(8,128)(2,1)S(1)}, u32[]{:S(2)}, u32[]{:S(2)}) %collective-permute-start.28) | collective-permute-done | bytes 1892384 | tf_op jit(solution)/shard_map/w_recv/ppermute | solution.py:29
  125.3 0.6 merge_body.1
  125.9 0.1 collective-permute-start.29
  126.0 0.1 collective-permute-start.30
  126.1 0.4 collective-permute-start.31
  126.6 3.8 %collective-permute-start.32 = (bf16[32,3696]{1,0:T(8,128)(2,1)S(1)}, bf16[32,3696]{1,0:T(8,128)(2,1)S(1)}, u32[]{:S(2)}, u32[]{:S(2)}) collective-permute-start(bf16[32,3696]{1,0:T(8,128)(2,1)S(1)} %get-tuple-element.96), channel_id=1, source_target_pairs={{0,12},{1,13},{2,14},{3,15},{4,0},{5,1},{6,2},{7,3},{8,4},{9,5},{1... | collective-permute-start | bytes 709640 | tf_op jit(solution)/shard_map/mixed_b/ppermute | solution.py:29
  130.3 2.2 %collective-permute-done.29 = bf16[3696,512]{1,0:T(8,128)(2,1)S(1)} collective-permute-done((bf16[3696,512]{1,0:T(8,128)(2,1)S(1)}, bf16[3696,512]{1,0:T(8,128)(2,1)S(1)}, u32[]{:S(2)}, u32[]{:S(2)}) %collective-permute-start.29) | collective-permute-done | bytes 3784736 | tf_op jit(solution)/shard_map/part/ppermute | solution.py:29
  132.6 3.0 %add_convert_fusion = bf16[3696,512]{1,0:T(8,128)(2,1)} fusion(bf16[3696,512]{1,0:T(8,128)(2,1)S(1)} %collective-permute-done.29, bf16[3696,512]{1,0:T(8,128)(2,1)S(1)} %merge_body.1), kind=kLoop, calls=%fused_computation | loop fusion | flops 7569408 | bytes 11354112 | tf_op jit(solution)/shard_map/convert_element_type | solution.py:467
  135.5 3.8 %collective-permute-done.30.other = bf16[64,3696]{1,0:T(8,128)(2,1)S(1)} collective-permute-done((bf16[64,3696]{1,0:T(8,128)(2,1)S(1)}, bf16[64,3696]{1,0:T(8,128)(2,1)S(1)}, u32[]{:S(2)}, u32[]{:S(2)}) %collective-permute-start.30) | collective-permute-done | bytes 473120 | tf_op jit(solution)/shard_map/t3/ppermute | solution.py:29
  139.3 0.4 collective-permute-done.32.mixed_b
  139.7 1.0 here_body.1
  (38 shorter events, 0.5 us)
Async XLA Ops:
  2.3 9.4 %collective-permute-start.2 = (bf16[144,512]{1,0:T(8,128)(2,1)}, bf16[144,512]{1,0:T(8,128)(2,1)S(1)}, u32[]{:S(2)}, u32[]{:S(2)}) collective-permute-start(bf16[144,512]{1,0:T(8,128)(2,1)} %prep_body.1), channel_id=1, source_target_pairs={{0,3},{1,2},{2,1},{3,0},{4,7},{5,6},{6,5},{7,4},{8,11},{9,10},{10,... | collective-permute-start | bytes 442376 | tf_op jit(solution)/shard_map/payload_mate/ppermute | solution.py:29
  5.4 23.8 %collective-permute-start = (bf16[64,3696]{1,0:T(8,128)(2,1)}, bf16[64,3696]{1,0:T(8,128)(2,1)S(1)}, u32[]{:S(2)}, u32[]{:S(2)}) collective-permute-start(bf16[64,3696]{1,0:T(8,128)(2,1)} %refs_4_.3), channel_id=1, source_target_pairs={{0,4},{1,5},{2,6},{3,7},{4,8},{5,9},{6,10},{7,11},{8,12},{9,13},{1... | collective-permute-start | bytes 1419272 | tf_op jit(solution)/shard_map/down/ppermute | solution.py:29
  8.7 25.2 %collective-permute-start.1 = (bf16[64,3696]{1,0:T(8,128)(2,1)}, bf16[64,3696]{1,0:T(8,128)(2,1)S(1)}, u32[]{:S(2)}, u32[]{:S(2)}) collective-permute-start(bf16[64,3696]{1,0:T(8,128)(2,1)} %refs_4_.3), channel_id=1, source_target_pairs={{0,12},{1,13},{2,14},{3,15},{4,0},{5,1},{6,2},{7,3},{8,4},{9,5},{1... | collective-permute-start | bytes 1419272 | tf_op jit(solution)/shard_map/up/ppermute | solution.py:29
  12.6 8.3 %collective-permute-start.3 = (bf16[144,1024]{1,0:T(8,128)(2,1)S(1)}, bf16[144,1024]{1,0:T(8,128)(2,1)S(1)}, u32[]{:S(2)}, u32[]{:S(2)}) collective-permute-start(bf16[144,1024]{1,0:T(8,128)(2,1)S(1)} %pad_maximum_fusion.2.own), channel_id=1, source_target_pairs={{0,16},{16,0},{32,48},{48,32},{64,80},{80,64},{96,112},{112,96},{1... | collective-permute-start | bytes 884744 | tf_op jit(solution)/shard_map/block_x1/ppermute | solution.py:29
  13.6 12.0 %collective-permute-start.4 = (bf16[64,3696]{1,0:T(8,128)(2,1)}, bf16[64,3696]{1,0:T(8,128)(2,1)S(1)}, u32[]{:S(2)}, u32[]{:S(2)}) collective-permute-start(bf16[64,3696]{1,0:T(8,128)(2,1)} %refs_4_.3), channel_id=1, source_target_pairs={{0,1},{1,0},{2,3},{3,2},{4,5},{5,4},{6,7},{7,6},{8,9},{9,8},{10,11... | collective-permute-start | bytes 1419272 | tf_op jit(solution)/shard_map/y3/ppermute | solution.py:29
  15.3 58.1 %copy-start.2 = (bf16[64,3696]{1,0:T(8,128)(2,1)S(1)}, bf16[64,3696]{1,0:T(8,128)(2,1)}, u32[]{:S(2)}) copy-start(bf16[64,3696]{1,0:T(8,128)(2,1)} %refs_4_.3) | copy-start | bytes 1419268
  15.4 48.7 %collective-permute-start.15 = (bf16[1856,512]{1,0:T(8,128)(2,1)S(1)}, bf16[1856,512]{1,0:T(8,128)(2,1)S(1)}, u32[]{:S(2)}, u32[]{:S(2)}) collective-permute-start(bf16[1856,512]{1,0:T(8,128)(2,1)S(1)} %constant_dynamic-slice_fusion), channel_id=1, source_target_pairs={{0,3},{1,2},{2,1},{3,0},{4,7},{5,6},{6,5},{7,4},{8,11},{9,10},{10,... | collective-permute-start | bytes 5701640 | tf_op jit(solution)/shard_map/got/ppermute | solution.py:29
  21.1 21.2 %collective-permute-start.9 = (bf16[144,1024]{1,0:T(8,128)(2,1)S(1)}, bf16[144,1024]{1,0:T(8,128)(2,1)S(1)}, u32[]{:S(2)}, u32[]{:S(2)}) collective-permute-start(bf16[144,1024]{1,0:T(8,128)(2,1)S(1)} %get-tuple-element.56.block), channel_id=1, source_target_pairs={{0,48},{16,32},{32,16},{48,0},{64,112},{80,96},{96,80},{112,64},{1... | collective-permute-start | bytes 884744 | tf_op jit(solution)/shard_map/block_x3/ppermute | solution.py:29
  25.5 3.6 %collective-permute-start.5 = (f32[8,128]{1,0:T(8,128)S(1)}, f32[8,128]{1,0:T(8,128)S(1)}, u32[]{:S(2)}, u32[]{:S(2)}) collective-permute-start(f32[8,128]{1,0:T(8,128)S(1)} %get-tuple-element.52), channel_id=1, source_target_pairs={{0,1},{1,0},{2,3},{3,2},{4,5},{5,4},{6,7},{7,6},{8,9},{9,8},{10,11... | collective-permute-start | bytes 12296 | tf_op jit(solution)/shard_map/sums0/ppermute | solution.py:29
  33.9 8.2 %collective-permute-start.8 = (f32[8,128]{1,0:T(8,128)S(1)}, f32[8,128]{1,0:T(8,128)S(1)}, u32[]{:S(2)}, u32[]{:S(2)}) collective-permute-start(f32[8,128]{1,0:T(8,128)S(1)} %add.18), channel_id=1, source_target_pairs={{0,4},{1,5},{2,6},{3,7},{4,0},{5,1},{6,2},{7,3},{8,12},{9,13},{10,... | collective-permute-start | bytes 12296 | tf_op jit(solution)/shard_map/sums1/ppermute | solution.py:29
  37.7 14.1 %collective-permute-start.6 = (bf16[32,3696]{1,0:T(8,128)(2,1)S(1)}, bf16[32,3696]{1,0:T(8,128)(2,1)S(1)}, u32[]{:S(2)}, u32[]{:S(2)}) collective-permute-start(bf16[32,3696]{1,0:T(8,128)(2,1)S(1)} %slice.6), channel_id=1, source_target_pairs={{0,4},{1,5},{2,6},{3,7},{4,8},{5,9},{6,10},{7,11},{8,12},{9,13},{1... | collective-permute-start | bytes 709640 | tf_op jit(solution)/shard_map/far_a/ppermute | solution.py:29
  37.8 14.0 %collective-permute-start.7 = (bf16[32,3696]{1,0:T(8,128)(2,1)S(1)}, bf16[32,3696]{1,0:T(8,128)(2,1)S(1)}, u32[]{:S(2)}, u32[]{:S(2)}) collective-permute-start(bf16[32,3696]{1,0:T(8,128)(2,1)S(1)} %slice.7), channel_id=1, source_target_pairs={{0,12},{1,13},{2,14},{3,15},{4,0},{5,1},{6,2},{7,3},{8,4},{9,5},{1... | collective-permute-start | bytes 709640 | tf_op jit(solution)/shard_map/far_b/ppermute | solution.py:29
  42.1 31.4 %collective-permute-start.12 = (bf16[2,64,3696]{2,1,0:T(8,128)(2,1)S(1)}, bf16[2,64,3696]{2,1,0:T(8,128)(2,1)S(1)}, u32[]{:S(2)}, u32[]{:S(2)}) collective-permute-start(bf16[2,64,3696]{2,1,0:T(8,128)(2,1)S(1)} %pad_maximum_fusion), channel_id=1, source_target_pairs={{0,1},{1,0},{2,3},{3,2},{4,5},{5,4},{6,7},{7,6},{8,9},{9,8},{10,11... | collective-permute-start | bytes 2838536 | tf_op jit(solution)/shard_map/y12/ppermute | solution.py:29
  42.3 6.1 %collective-permute-start.10 = (f32[8,128]{1,0:T(8,128)S(1)}, f32[8,128]{1,0:T(8,128)S(1)}, u32[]{:S(2)}, u32[]{:S(2)}) collective-permute-start(f32[8,128]{1,0:T(8,128)S(1)} %add.19), channel_id=1, source_target_pairs={{0,12},{1,13},{2,14},{3,15},{4,8},{5,9},{6,10},{7,11},{8,4},{9,5},... | collective-permute-start | bytes 12296 | tf_op jit(solution)/shard_map/sums2/ppermute | solution.py:29
  48.4 17.6 %collective-permute-start.17 = (bf16[288,1024]{1,0:T(8,128)(2,1)S(1)}, bf16[288,1024]{1,0:T(8,128)(2,1)S(1)}, u32[]{:S(2)}, u32[]{:S(2)}) collective-permute-start(bf16[288,1024]{1,0:T(8,128)(2,1)S(1)} %constant_dynamic-update-slice_fusion.2.here), channel_id=1, source_target_pairs={{0,64},{16,80},{32,96},{48,112},{64,0},{80,16},{96,32},{112,48},{1... | collective-permute-start | bytes 1769480 | tf_op jit(solution)/shard_map/block_zlo/ppermute | solution.py:29
  51.8 21.7 %collective-permute-start.11 = (bf16[64,3696]{1,0:T(8,128)(2,1)S(1)}, bf16[64,3696]{1,0:T(8,128)(2,1)S(1)}, u32[]{:S(2)}, u32[]{:S(2)}) collective-permute-start(bf16[64,3696]{1,0:T(8,128)(2,1)S(1)} %pad_maximum_fusion.1), channel_id=1, source_target_pairs={{0,1},{1,0},{2,3},{3,2},{4,5},{5,4},{6,7},{7,6},{8,9},{9,8},{10,11... | collective-permute-start | bytes 1419272 | tf_op jit(solution)/shard_map/y0/ppermute | solution.py:29
  52.0 1.2 collective-permute-start.13
  53.2 4.9 %collective-permute-start.14 = (f32[24,128]{1,0:T(8,128)S(1)}, f32[24,128]{1,0:T(8,128)S(1)}, u32[]{:S(2)}, u32[]{:S(2)}) collective-permute-start(f32[24,128]{1,0:T(8,128)S(1)} %pad_maximum_fusion.3), channel_id=1, source_target_pairs={{0,48},{16,32},{32,16},{48,0},{64,112},{80,96},{96,80},{112,64},{1... | collective-permute-start | bytes 36872 | tf_op jit(solution)/shard_map/tiny_x3/ppermute | solution.py:29
  58.1 5.9 %collective-permute-start.16 = (f32[48,128]{1,0:T(8,128)S(1)}, f32[48,128]{1,0:T(8,128)S(1)}, u32[]{:S(2)}, u32[]{:S(2)}) collective-permute-start(f32[48,128]{1,0:T(8,128)S(1)} %constant_dynamic-update-slice_fusion.here), channel_id=1, source_target_pairs={{0,64},{16,80},{32,96},{48,112},{64,0},{80,16},{96,32},{112,48},{1... | collective-permute-start | bytes 73736 | tf_op jit(solution)/shard_map/tiny_zlo/ppermute | solution.py:29
  64.1 11.7 %collective-permute-start.19 = (bf16[1856,512]{1,0:T(8,128)(2,1)S(1)}, bf16[1856,512]{1,0:T(8,128)(2,1)S(1)}, u32[]{:S(2)}, u32[]{:S(2)}) collective-permute-start(bf16[1856,512]{1,0:T(8,128)(2,1)S(1)} %collective-permute-done.15.got), channel_id=1, source_target_pairs={{0,128},{128,0},{1,129},{129,1},{2,130},{130,2},{3,131},{131,3},{4... | collective-permute-start | bytes 5701640 | tf_op jit(solution)/shard_map/got_other/ppermute | solution.py:29
  65.5 4.9 %collective-permute-start.18 = (f32[8,128]{1,0:T(8,128)S(1)}, f32[8,128]{1,0:T(8,128)S(1)}, u32[]{:S(2)}, u32[]{:S(2)}) collective-permute-start(f32[8,128]{1,0:T(8,128)S(1)} %coefs_body.1.coefs), channel_id=1, source_target_pairs={{0,3},{1,2},{2,1},{3,0},{4,7},{5,6},{6,5},{7,4},{8,11},{9,10},{10,... | collective-permute-start | bytes 12296 | tf_op jit(solution)/shard_map/coefs_mate/ppermute | solution.py:29
  67.2 8.6 %copy-start = (bf16[3696,512]{1,0:T(8,128)(2,1)S(1)}, bf16[3696,512]{1,0:T(8,128)(2,1)}, u32[]{:S(2)}) copy-start(bf16[3696,512]{1,0:T(8,128)(2,1)} %w.3) | copy-start | bytes 11354116
  75.7 4.1 %collective-permute-start.21 = (bf16[3696,256]{1,0:T(8,128)(2,1)S(1)}, bf16[3696,256]{1,0:T(8,128)(2,1)S(1)}, u32[]{:S(2)}, u32[]{:S(2)}) collective-permute-start(bf16[3696,256]{1,0:T(8,128)(2,1)S(1)} %get-tuple-element.73), channel_id=1, source_target_pairs={{0,128},{128,0},{1,129},{129,1},{2,130},{130,2},{3,131},{131,3},{4... | collective-permute-start | bytes 5677064 | tf_op jit(solution)/shard_map/mate_got/ppermute | solution.py:29
  80.4 44.9 %collective-permute-start.28 = (bf16[3696,256]{1,0:T(8,128)(2,1)S(1)}, bf16[3696,256]{1,0:T(8,128)(2,1)S(1)}, u32[]{:S(2)}, u32[]{:S(2)}) collective-permute-start(bf16[3696,256]{1,0:T(8,128)(2,1)S(1)} %add_convert_fusion.1), channel_id=1, source_target_pairs={{0,3},{1,2},{2,1},{3,0},{4,7},{5,6},{6,5},{7,4},{8,11},{9,10},{10,... | collective-permute-start | bytes 5677064 | tf_op jit(solution)/shard_map/w_recv/ppermute | solution.py:29
  80.9 13.7 %collective-permute-start.20 = (bf16[64,3696]{1,0:T(8,128)(2,1)S(1)}, bf16[64,3696]{1,0:T(8,128)(2,1)S(1)}, u32[]{:S(2)}, u32[]{:S(2)}) collective-permute-start(bf16[64,3696]{1,0:T(8,128)(2,1)S(1)} %get-tuple-element.69), channel_id=1, source_target_pairs={{0,1},{1,0},{2,3},{3,2},{4,5},{5,4},{6,7},{7,6},{8,9},{9,8},{10,11... | collective-permute-start | bytes 1419272 | tf_op jit(solution)/shard_map/t0/ppermute | solution.py:29
  81.1 23.7 %collective-permute-start.25 = (bf16[64,3696]{1,0:T(8,128)(2,1)S(1)}, bf16[64,3696]{1,0:T(8,128)(2,1)S(1)}, u32[]{:S(2)}, u32[]{:S(2)}) collective-permute-start(bf16[64,3696]{1,0:T(8,128)(2,1)S(1)} %get-tuple-element.85), channel_id=1, source_target_pairs={{0,1},{1,0},{2,3},{3,2},{4,5},{5,4},{6,7},{7,6},{8,9},{9,8},{10,11... | collective-permute-start | bytes 1419272 | tf_op jit(solution)/shard_map/t1/ppermute | solution.py:29
  94.7 10.1 %collective-permute-start.24 = (bf16[32,3696]{1,0:T(8,128)(2,1)S(1)}, bf16[32,3696]{1,0:T(8,128)(2,1)S(1)}, u32[]{:S(2)}, u32[]{:S(2)}) collective-permute-start(bf16[32,3696]{1,0:T(8,128)(2,1)S(1)} %get-tuple-element.81), channel_id=1, source_target_pairs={{0,12},{1,13},{2,14},{3,15},{4,0},{5,1},{6,2},{7,3},{8,4},{9,5},{1... | collective-permute-start | bytes 709640 | tf_op jit(solution)/shard_map/from_up/ppermute | solution.py:29
  95.1 19.2 %collective-permute-start.22 = (bf16[64,3696]{1,0:T(8,128)(2,1)S(1)}, bf16[64,3696]{1,0:T(8,128)(2,1)S(1)}, u32[]{:S(2)}, u32[]{:S(2)}) collective-permute-start(bf16[64,3696]{1,0:T(8,128)(2,1)S(1)} %get-tuple-element.78), channel_id=1, source_target_pairs={{0,1},{1,0},{2,3},{3,2},{4,5},{5,4},{6,7},{7,6},{8,9},{9,8},{10,11... | collective-permute-start | bytes 1419272 | tf_op jit(solution)/shard_map/t2/ppermute | solution.py:29
  95.2 12.9 %copy-start.1 = (bf16[128,512]{1,0:T(8,128)(2,1)S(1)}, bf16[128,512]{1,0:T(8,128)(2,1)}, u32[]{:S(2)}) copy-start(bf16[128,512]{1,0:T(8,128)(2,1)} %stream.2) | copy-start | bytes 393220
  95.2 19.0 %collective-permute-start.23 = (bf16[32,3696]{1,0:T(8,128)(2,1)S(1)}, bf16[32,3696]{1,0:T(8,128)(2,1)S(1)}, u32[]{:S(2)}, u32[]{:S(2)}) collective-permute-start(bf16[32,3696]{1,0:T(8,128)(2,1)S(1)} %get-tuple-element.75), channel_id=1, source_target_pairs={{0,4},{1,5},{2,6},{3,7},{4,8},{5,9},{6,10},{7,11},{8,12},{9,13},{1... | collective-permute-start | bytes 709640 | tf_op jit(solution)/shard_map/from_down/ppermute | solution.py:29
  104.9 12.6 %collective-permute-start.26 = (bf16[32,3696]{1,0:T(8,128)(2,1)S(1)}, bf16[32,3696]{1,0:T(8,128)(2,1)S(1)}, u32[]{:S(2)}, u32[]{:S(2)}) collective-permute-start(bf16[32,3696]{1,0:T(8,128)(2,1)S(1)} %get-tuple-element.87), channel_id=1, source_target_pairs={{0,12},{1,13},{2,14},{3,15},{4,0},{5,1},{6,2},{7,3},{8,4},{9,5},{1... | collective-permute-start | bytes 709640 | tf_op jit(solution)/shard_map/pure_a/ppermute | solution.py:29
  107.0 10.5 %collective-permute-start.27 = (bf16[32,3696]{1,0:T(8,128)(2,1)S(1)}, bf16[32,3696]{1,0:T(8,128)(2,1)S(1)}, u32[]{:S(2)}, u32[]{:S(2)}) collective-permute-start(bf16[32,3696]{1,0:T(8,128)(2,1)S(1)} %get-tuple-element.88), channel_id=1, source_target_pairs={{0,4},{1,5},{2,6},{3,7},{4,8},{5,9},{6,10},{7,11},{8,12},{9,13},{1... | collective-permute-start | bytes 709640 | tf_op jit(solution)/shard_map/pure_b/ppermute | solution.py:29
  125.9 6.7 %collective-permute-start.29 = (bf16[3696,512]{1,0:T(8,128)(2,1)S(1)}, bf16[3696,512]{1,0:T(8,128)(2,1)S(1)}, u32[]{:S(2)}, u32[]{:S(2)}) collective-permute-start(bf16[3696,512]{1,0:T(8,128)(2,1)S(1)} %merge_body.1), channel_id=1, source_target_pairs={{0,128},{128,0},{1,129},{129,1},{2,130},{130,2},{3,131},{131,3},{4... | collective-permute-start | bytes 11354120 | tf_op jit(solution)/shard_map/part/ppermute | solution.py:29
  126.0 13.3 %collective-permute-start.30 = (bf16[64,3696]{1,0:T(8,128)(2,1)S(1)}, bf16[64,3696]{1,0:T(8,128)(2,1)S(1)}, u32[]{:S(2)}, u32[]{:S(2)}) collective-permute-start(bf16[64,3696]{1,0:T(8,128)(2,1)S(1)} %get-tuple-element.93), channel_id=1, source_target_pairs={{0,1},{1,0},{2,3},{3,2},{4,5},{5,4},{6,7},{7,6},{8,9},{9,8},{10,11... | collective-permute-start | bytes 1419272 | tf_op jit(solution)/shard_map/t3/ppermute | solution.py:29
  126.1 13.2 %collective-permute-start.31 = (bf16[32,3696]{1,0:T(8,128)(2,1)S(1)}, bf16[32,3696]{1,0:T(8,128)(2,1)S(1)}, u32[]{:S(2)}, u32[]{:S(2)}) collective-permute-start(bf16[32,3696]{1,0:T(8,128)(2,1)S(1)} %get-tuple-element.89), channel_id=1, source_target_pairs={{0,4},{1,5},{2,6},{3,7},{4,8},{5,9},{6,10},{7,11},{8,12},{9,13},{1... | collective-permute-start | bytes 709640 | tf_op jit(solution)/shard_map/mixed_a/ppermute | solution.py:29
  126.6 13.2 %collective-permute-start.32 = (bf16[32,3696]{1,0:T(8,128)(2,1)S(1)}, bf16[32,3696]{1,0:T(8,128)(2,1)S(1)}, u32[]{:S(2)}, u32[]{:S(2)}) collective-permute-start(bf16[32,3696]{1,0:T(8,128)(2,1)S(1)} %get-tuple-element.96), channel_id=1, source_target_pairs={{0,12},{1,13},{2,14},{3,15},{4,0},{5,1},{6,2},{7,3},{8,4},{9,5},{1... | collective-permute-start | bytes 709640 | tf_op jit(solution)/shard_map/mixed_b/ppermute | solution.py:29

commit v10 on v7

--- a/solution.py
+++ b/solution.py
@@ -230,9 +230,9 @@
 
 
 LO = 1856
-CHUNKS = ((0, 1024), (1024, 2048), (2048, 3072), (3072, 3696))
+CHUNKS = ((0, 512), (512, 1536), (1536, 2560), (2560, 3696))
 HIGH = 3696 - LO
-SPANS = ((0, LO), (LO, 3696))
+SPANS = ((0, 512), (512, LO), (LO, 2560), (2560, 3696))
 def inner_body(g, w, got, other, *refs):
     out, (w_v, m_v, sems) = refs[:4], refs[4:]
     p = lax.axis_index("dp")
@@ -241,22 +241,22 @@
 
     def mate_copy(j, low, high):
         a, b = SPANS[j]
-        src, off = (low, high)[j], (0, HIGH)[j]
+        src, off = (low, low, high, high)[j], (0, 0, HIGH, HIGH)[j]
         return pltpu.make_async_copy(src.at[a - off : b - off], m_v.at[a:b], sems.at[4 + j])
 
     @pl.when(p == 0)
     def _():
-        for j in range(2):
+        for j in range(4):
             mate_copy(j, got, other).start()
 
     @pl.when(p == 1)
     def _():
-        for j in range(2):
+        for j in range(4):
             mate_copy(j, other, got).start()
 
     left, right = g[:, :512], g[:, 512:]
     nt = (((1,), (1,)), ((), ()))
-    waits = ((0,), (1,), (), ())
+    waits = ((0,), (1,), (2,), (3,))
     for i, (a, b) in enumerate(CHUNKS):
         pltpu.make_async_copy(w.at[a:b], w_v.at[a:b], sems.at[i]).wait()
         for j in waits[i]:
@@ -279,7 +279,7 @@
         scratch=[
             pltpu.VMEM((3696, 512), bf16),
             pltpu.VMEM((3696, 512), bf16),
-            pltpu.SemaphoreType.DMA((6,)),
+            pltpu.SemaphoreType.DMA((8,)),
         ],
         flops=2 * 256 * 1024 * 3696,
         moved=10 << 20,

time: 141 us -> 141 us (level)
  transfers between devices with their start and end apart: 33 -> 33, of which waited for: 18 -> 18; matrix products, arithmetic and copies ran while one was open for 4% -> 4% of each run, Pallas kernels for 11% -> 12%
where the time goes in v10:
time: 141 us
  waiting for transfers between devices  67.9 us (48%)
  starting transfers between devices  45.2 us (32%)
  Pallas kernels  19.6 us (14%)
  other arithmetic  4.66 us (3%)
  local copies, waits for them, and re-layouts  1.74 us (1%)
  between operations  1.5 us (1%)
    ppermute x33, waiting for transfers between devices, send(): return lax.ppermute(a, axis, perm)  67.9 us
    ppermute x33, starting transfers between devices, send(): return lax.ppermute(a, axis, perm)  45.2 us
    pallas_call x14, Pallas kernels, call(): pl.pallas_call(body, out_shape=out_shape, scratch_shapes=list(scratch), c...  19.6 us
    convert_element_type x1, other arithmetic, per_device(): weight_grad = (part.astype(f32) + part_other.astype(f32)).astype(bf16)  2.97 us
  transfers between devices with their start and end apart: 33, of which 18 were waited for; matrix products, arithmetic and copies ran while one was open for 4% of the time, Pallas kernels for 12%

profile of v10, /device:TPU:6, one launch (start us, length us, event | category | flops | bytes accessed | tf_op | source)
XLA Modules:
  0.0 140.7 jit_solution(15191291196419213753)
XLA Ops:
  0.6 1.6 %prep_body.1 = bf16[144,512]{1,0:T(8,128)(2,1)} custom-call(bf16[128,512]{1,0:T(8,128)(2,1)} %stream.2, f32[1,512]{1,0:T(1,128)} %bitcast.6, f32[1,512]{1,0:T(1,128)} %bitcast.7, f32[1,128]{1,0:T(1,128)} %reward.1, s32[1,128]{1,0:T(1,128)} %segment.1), custom_call_target="tpu_custom_call" | custom-call | tf_op jit(solution)/shard_map/prep_body/pallas_call | solution.py:55
  2.3 3.1 %collective-permute-start.2 = (bf16[144,512]{1,0:T(8,128)(2,1)}, bf16[144,512]{1,0:T(8,128)(2,1)S(1)}, u32[]{:S(2)}, u32[]{:S(2)}) collective-permute-start(bf16[144,512]{1,0:T(8,128)(2,1)} %prep_body.1), channel_id=1, source_target_pairs={{0,3},{1,2},{2,1},{3,0},{4,7},{5,6},{6,5},{7,4},{8,11},{9,10},{10,... | collective-permute-start | bytes 442376 | tf_op jit(solution)/shard_map/payload_mate/ppermute | solution.py:29
  5.4 0.1 collective-permute-start.4
  5.5 3.3 %collective-permute-start = (bf16[64,3696]{1,0:T(8,128)(2,1)}, bf16[64,3696]{1,0:T(8,128)(2,1)S(1)}, u32[]{:S(2)}, u32[]{:S(2)}) collective-permute-start(bf16[64,3696]{1,0:T(8,128)(2,1)} %refs_4_.3), channel_id=1, source_target_pairs={{0,4},{1,5},{2,6},{3,7},{4,8},{5,9},{6,10},{7,11},{8,12},{9,13},{1... | collective-permute-start | bytes 1419272 | tf_op jit(solution)/shard_map/down/ppermute | solution.py:29
  8.8 3.0 %collective-permute-start.1 = (bf16[64,3696]{1,0:T(8,128)(2,1)}, bf16[64,3696]{1,0:T(8,128)(2,1)S(1)}, u32[]{:S(2)}, u32[]{:S(2)}) collective-permute-start(bf16[64,3696]{1,0:T(8,128)(2,1)} %refs_4_.3), channel_id=1, source_target_pairs={{0,12},{1,13},{2,14},{3,15},{4,0},{5,1},{6,2},{7,3},{8,4},{9,5},{1... | collective-permute-start | bytes 1419272 | tf_op jit(solution)/shard_map/up/ppermute | solution.py:29
  11.8 0.9 pad_maximum_fusion.2.own
  12.8 0.9 collective-permute-start.3
  13.7 1.6 %constant_dynamic-slice_fusion = bf16[1856,512]{1,0:T(8,128)(2,1)S(1)} fusion(bf16[3696,512]{1,0:T(8,128)(2,1)} %w.3, s32[]{:T(128)S(6)} %select_n.3), kind=kLoop, calls=%fused_computation.10 | loop fusion | bytes 3801092 | tf_op jit(solution)/shard_map/dynamic_slice | solution.py:397
  15.4 1.1 collective-permute-start.15
  16.5 4.4 %collective-permute-done.3.other = bf16[144,1024]{1,0:T(8,128)(2,1)S(1)} collective-permute-done((bf16[144,1024]{1,0:T(8,128)(2,1)S(1)}, bf16[144,1024]{1,0:T(8,128)(2,1)S(1)}, u32[]{:S(2)}, u32[]{:S(2)}) %collective-permute-start.3) | collective-permute-done | bytes 294944 | tf_op jit(solution)/shard_map/block_x1/ppermute | solution.py:29
  20.9 0.2 pick_body.1
  21.1 0.6 collective-permute-start.9
  21.7 1.7 %collective-permute-start.5 = (f32[8,128]{1,0:T(8,128)S(1)}, f32[8,128]{1,0:T(8,128)S(1)}, u32[]{:S(2)}, u32[]{:S(2)}) collective-permute-start(f32[8,128]{1,0:T(8,128)S(1)} %get-tuple-element.52), channel_id=1, source_target_pairs={{0,1},{1,0},{2,3},{3,2},{4,5},{5,4},{6,7},{7,6},{8,9},{9,8},{10,11... | collective-permute-start | bytes 12296 | tf_op jit(solution)/shard_map/sums0/ppermute | solution.py:29
  23.4 1.8 %collective-permute-done.5 = f32[8,128]{1,0:T(8,128)S(1)} collective-permute-done((f32[8,128]{1,0:T(8,128)S(1)}, f32[8,128]{1,0:T(8,128)S(1)}, u32[]{:S(2)}, u32[]{:S(2)}) %collective-permute-start.5) | collective-permute-done | bytes 4128 | tf_op jit(solution)/shard_map/sums0/ppermute | solution.py:29
  25.3 1.3 collective-permute-done.refs_3_
  26.6 7.3 %collective-permute-done.1.refs_2_ = bf16[64,3696]{1,0:T(8,128)(2,1)S(1)} collective-permute-done((bf16[64,3696]{1,0:T(8,128)(2,1)}, bf16[64,3696]{1,0:T(8,128)(2,1)S(1)}, u32[]{:S(2)}, u32[]{:S(2)}) %collective-permute-start.1) | collective-permute-done | bytes 473120 | tf_op jit(solution)/shard_map/up/ppermute | solution.py:29
  33.9 3.8 %collective-permute-start.8 = (f32[8,128]{1,0:T(8,128)S(1)}, f32[8,128]{1,0:T(8,128)S(1)}, u32[]{:S(2)}, u32[]{:S(2)}) collective-permute-start(f32[8,128]{1,0:T(8,128)S(1)} %add.18), channel_id=1, source_target_pairs={{0,4},{1,5},{2,6},{3,7},{4,0},{5,1},{6,2},{7,3},{8,12},{9,13},{10,... | collective-permute-start | bytes 12296 | tf_op jit(solution)/shard_map/sums1/ppermute | solution.py:29
  37.7 0.1 collective-permute-start.6
  37.8 4.2 %collective-permute-start.7 = (bf16[32,3696]{1,0:T(8,128)(2,1)S(1)}, bf16[32,3696]{1,0:T(8,128)(2,1)S(1)}, u32[]{:S(2)}, u32[]{:S(2)}) collective-permute-start(bf16[32,3696]{1,0:T(8,128)(2,1)S(1)} %slice.7), channel_id=1, source_target_pairs={{0,12},{1,13},{2,14},{3,15},{4,0},{5,1},{6,2},{7,3},{8,4},{9,5},{1... | collective-permute-start | bytes 709640 | tf_op jit(solution)/shard_map/far_b/ppermute | solution.py:29
  42.0 0.1 pad_maximum_fusion
  42.1 1.8 %collective-permute-start.12 = (bf16[2,64,3696]{2,1,0:T(8,128)(2,1)S(1)}, bf16[2,64,3696]{2,1,0:T(8,128)(2,1)S(1)}, u32[]{:S(2)}, u32[]{:S(2)}) collective-permute-start(bf16[2,64,3696]{2,1,0:T(8,128)(2,1)S(1)} %pad_maximum_fusion), channel_id=1, source_target_pairs={{0,1},{1,0},{2,3},{3,2},{4,5},{5,4},{6,7},{7,6},{8,9},{9,8},{10,11... | collective-permute-start | bytes 2838536 | tf_op jit(solution)/shard_map/y12/ppermute | solution.py:29
  44.0 4.5 %collective-permute-done.6.refs_0_ = bf16[32,3696]{1,0:T(8,128)(2,1)S(1)} collective-permute-done((bf16[32,3696]{1,0:T(8,128)(2,1)S(1)}, bf16[32,3696]{1,0:T(8,128)(2,1)S(1)}, u32[]{:S(2)}, u32[]{:S(2)}) %collective-permute-start.6) | collective-permute-done | bytes 236576 | tf_op jit(solution)/shard_map/far_a/ppermute | solution.py:29
  48.5 3.3 %collective-permute-start.17 = (bf16[288,1024]{1,0:T(8,128)(2,1)S(1)}, bf16[288,1024]{1,0:T(8,128)(2,1)S(1)}, u32[]{:S(2)}, u32[]{:S(2)}) collective-permute-start(bf16[288,1024]{1,0:T(8,128)(2,1)S(1)} %constant_dynamic-update-slice_fusion.2.here), channel_id=1, source_target_pairs={{0,64},{16,80},{32,96},{48,112},{64,0},{80,16},{96,32},{112,48},{1... | collective-permute-start | bytes 1769480 | tf_op jit(solution)/shard_map/block_zlo/ppermute | solution.py:29
  51.8 1.8 %collective-permute-start.11 = (bf16[64,3696]{1,0:T(8,128)(2,1)S(1)}, bf16[64,3696]{1,0:T(8,128)(2,1)S(1)}, u32[]{:S(2)}, u32[]{:S(2)}) collective-permute-start(bf16[64,3696]{1,0:T(8,128)(2,1)S(1)} %pad_maximum_fusion.1), channel_id=1, source_target_pairs={{0,1},{1,0},{2,3},{3,2},{4,5},{5,4},{6,7},{7,6},{8,9},{9,8},{10,11... | collective-permute-start | bytes 1419272 | tf_op jit(solution)/shard_map/y0/ppermute | solution.py:29
  53.6 1.2 collective-permute-done.13
  54.8 0.5 collective-permute-start.14
  55.3 4.4 %collective-permute-done.14 = f32[24,128]{1,0:T(8,128)S(1)} collective-permute-done((f32[24,128]{1,0:T(8,128)S(1)}, f32[24,128]{1,0:T(8,128)S(1)}, u32[]{:S(2)}, u32[]{:S(2)}) %collective-permute-start.14) | collective-permute-done | bytes 12320 | tf_op jit(solution)/shard_map/tiny_x3/ppermute | solution.py:29
  59.7 4.4 %collective-permute-done.16.there = f32[48,128]{1,0:T(8,128)S(1)} collective-permute-done((f32[48,128]{1,0:T(8,128)S(1)}, f32[48,128]{1,0:T(8,128)S(1)}, u32[]{:S(2)}, u32[]{:S(2)}) %collective-permute-start.16) | collective-permute-done | bytes 24608 | tf_op jit(solution)/shard_map/tiny_zlo/ppermute | solution.py:29
  64.7 0.8 coefs_body.1.coefs
  65.5 1.0 collective-permute-start.18
  66.5 1.2 grad_body.1
  67.7 2.7 %collective-permute-done.18.coefs_mate = f32[8,128]{1,0:T(8,128)S(1)} collective-permute-done((f32[8,128]{1,0:T(8,128)S(1)}, f32[8,128]{1,0:T(8,128)S(1)}, u32[]{:S(2)}, u32[]{:S(2)}) %collective-permute-start.18) | collective-permute-done | bytes 4128 | tf_op jit(solution)/shard_map/coefs_mate/ppermute | solution.py:29
  70.4 3.1 %collective-permute-done.11.refs_5_ = bf16[64,3696]{1,0:T(8,128)(2,1)S(1)} collective-permute-done((bf16[64,3696]{1,0:T(8,128)(2,1)S(1)}, bf16[64,3696]{1,0:T(8,128)(2,1)S(1)}, u32[]{:S(2)}, u32[]{:S(2)}) %collective-permute-start.11) | collective-permute-done | bytes 473120 | tf_op jit(solution)/shard_map/y0/ppermute | solution.py:29
  73.5 2.2 %outer_mate.1 = (bf16[3696,256]{1,0:T(8,128)(2,1)S(1)}, f32[3696,256]{1,0:T(8,128)S(1)}) custom-call(bf16[32,3696]{1,0:T(8,128)(2,1)S(1)} %collective-permute-done.6.refs_0_, bf16[32,3696]{1,0:T(8,128)(2,1)S(1)} %collective-permute-done.7.refs_1_, bf16[64,3696]{1,0:T(8,128)(2,1)S(1)} %collective-permute-done.1.refs_2_, ...), custom_call_target="tpu_custom_call" | custom-call | flops 1937768448 | bytes 8388608 | tf_op jit(solution)/shard_map/outer_mate/pallas_call | solution.py:55
  75.7 0.1 collective-permute-start.21
  75.8 4.3 %inner_sent.1 = (bf16[64,3696]{1,0:T(8,128)(2,1)S(1)}, bf16[64,3696]{1,0:T(8,128)(2,1)S(1)}, bf16[64,3696]{1,0:T(8,128)(2,1)S(1)}, bf16[64,3696]{1,0:T(8,128)(2,1)S(1)}) custom-call(bf16[256,1024]{1,0:T(8,128)(2,1)S(1)} %get-tuple-element.67.refs_9_.g, bf16[3696,512]{1,0:T(8,128)(2,1)S(1)} %copy-done, bf16[1856,512]{1,0:T(8,128)(2,1)S(1)} %collective-permute-done.15.got, ...), custom_call_target="tpu_custom_call" | custom-call | flops 1937768448 | bytes 10485760 | tf_op jit(solution)/shard_map/inner_sent/pallas_call | solution.py:55
  80.1 0.6 add_convert_fusion.1
  80.8 1.0 collective-permute-start.28
  81.7 0.9 collective-permute-start.20
  82.7 1.1 collective-permute-start.25
  83.8 4.3 %inner_own.1 = (f32[64,3696]{1,0:T(8,128)S(1)}, f32[64,3696]{1,0:T(8,128)S(1)}, f32[64,3696]{1,0:T(8,128)S(1)}, f32[64,3696]{1,0:T(8,128)S(1)}) custom-call(bf16[256,1024]{1,0:T(8,128)(2,1)S(1)} %get-tuple-element.76.refs_8_.g, bf16[3696,512]{1,0:T(8,128)(2,1)S(1)} %copy-done, bf16[1856,512]{1,0:T(8,128)(2,1)S(1)} %collective-permute-done.15.got, ...), custom_call_target="tpu_custom_call" | custom-call | flops 1937768448 | bytes 10485760 | tf_op jit(solution)/shard_map/inner_own/pallas_call | solution.py:55
  88.1 7.4 %collective-permute-done.20.other = bf16[64,3696]{1,0:T(8,128)(2,1)S(1)} collective-permute-done((bf16[64,3696]{1,0:T(8,128)(2,1)S(1)}, bf16[64,3696]{1,0:T(8,128)(2,1)S(1)}, u32[]{:S(2)}, u32[]{:S(2)}) %collective-permute-start.20) | collective-permute-done | bytes 473120 | tf_op jit(solution)/shard_map/t0/ppermute | solution.py:29
  95.4 0.1 fold_body.3
  95.5 0.4 collective-permute-start.24
  95.9 0.9 collective-permute-start.22
  96.8 2.6 %collective-permute-start.23 = (bf16[32,3696]{1,0:T(8,128)(2,1)S(1)}, bf16[32,3696]{1,0:T(8,128)(2,1)S(1)}, u32[]{:S(2)}, u32[]{:S(2)}) collective-permute-start(bf16[32,3696]{1,0:T(8,128)(2,1)S(1)} %get-tuple-element.75), channel_id=1, source_target_pairs={{0,4},{1,5},{2,6},{3,7},{4,8},{5,9},{6,10},{7,11},{8,12},{9,13},{1... | collective-permute-start | bytes 709640 | tf_op jit(solution)/shard_map/from_down/ppermute | solution.py:29
  99.4 2.2 %outer_own.1.partial = f32[3696,512]{1,0:T(8,128)S(1)} custom-call(bf16[32,3696]{1,0:T(8,128)(2,1)S(1)} %collective-permute-done.6.refs_0_, bf16[32,3696]{1,0:T(8,128)(2,1)S(1)} %collective-permute-done.7.refs_1_, bf16[64,3696]{1,0:T(8,128)(2,1)S(1)} %collective-permute-done.1.refs_2_, bf16[64,3696]{1,0:T(8,128)(2,1)S(1)} %collective-permute-done.refs_3_, ...), custom_call_target="tpu_custom_call" | custom-call | flops 1937768448 | bytes 8388608 | tf_op jit(solution)/shard_map/outer_own/pallas_call | solution.py:55
  101.6 4.0 %collective-permute-done.25.other = bf16[64,3696]{1,0:T(8,128)(2,1)S(1)} collective-permute-done((bf16[64,3696]{1,0:T(8,128)(2,1)S(1)}, bf16[64,3696]{1,0:T(8,128)(2,1)S(1)}, u32[]{:S(2)}, u32[]{:S(2)}) %collective-permute-start.25) | collective-permute-done | bytes 473120 | tf_op jit(solution)/shard_map/t1/ppermute | solution.py:29
  105.7 1.9 %collective-permute-start.26 = (bf16[32,3696]{1,0:T(8,128)(2,1)S(1)}, bf16[32,3696]{1,0:T(8,128)(2,1)S(1)}, u32[]{:S(2)}, u32[]{:S(2)}) collective-permute-start(bf16[32,3696]{1,0:T(8,128)(2,1)S(1)} %get-tuple-element.87), channel_id=1, source_target_pairs={{0,12},{1,13},{2,14},{3,15},{4,0},{5,1},{6,2},{7,3},{8,4},{9,5},{1... | collective-permute-start | bytes 709640 | tf_op jit(solution)/shard_map/pure_a/ppermute | solution.py:29
  107.6 1.1 collective-permute-start.27
  108.7 0.9 own_grad_body.1
  109.6 5.5 %collective-permute-done.22.other = bf16[64,3696]{1,0:T(8,128)(2,1)S(1)} collective-permute-done((bf16[64,3696]{1,0:T(8,128)(2,1)S(1)}, bf16[64,3696]{1,0:T(8,128)(2,1)S(1)}, u32[]{:S(2)}, u32[]{:S(2)}) %collective-permute-start.22) | collective-permute-done | bytes 473120 | tf_op jit(solution)/shard_map/t2/ppermute | solution.py:29
  115.1 0.2 fold_body.4
  115.2 1.3 collective-permute-done.26.pure_a
  116.5 3.6 %collective-permute-done.27.pure_b = bf16[32,3696]{1,0:T(8,128)(2,1)S(1)} collective-permute-done((bf16[32,3696]{1,0:T(8,128)(2,1)S(1)}, bf16[32,3696]{1,0:T(8,128)(2,1)S(1)}, u32[]{:S(2)}, u32[]{:S(2)}) %collective-permute-start.27) | collective-permute-done | bytes 236576 | tf_op jit(solution)/shard_map/pure_b/ppermute | solution.py:29
  120.1 5.5 %collective-permute-done.28.recv = bf16[3696,256]{1,0:T(8,128)(2,1)S(1)} collective-permute-done((bf16[3696,256]{1,0:T(8,128)(2,1)S(1)}, bf16[3696,256]{1,0:T(8,128)(2,1)S(1)}, u32[]{:S(2)}, u32[]{:S(2)}) %collective-permute-start.28) | collective-permute-done | bytes 1892384 | tf_op jit(solution)/shard_map/w_recv/ppermute | solution.py:29
  125.7 0.6 merge_body.1
  126.3 0.1 collective-permute-start.29
  126.4 0.6 collective-permute-start.30
  127.0 4.1 %collective-permute-start.32 = (bf16[32,3696]{1,0:T(8,128)(2,1)S(1)}, bf16[32,3696]{1,0:T(8,128)(2,1)S(1)}, u32[]{:S(2)}, u32[]{:S(2)}) collective-permute-start(bf16[32,3696]{1,0:T(8,128)(2,1)S(1)} %get-tuple-element.96), channel_id=1, source_target_pairs={{0,12},{1,13},{2,14},{3,15},{4,0},{5,1},{6,2},{7,3},{8,4},{9,5},{1... | collective-permute-start | bytes 709640 | tf_op jit(solution)/shard_map/mixed_b/ppermute | solution.py:29
  131.1 1.8 %collective-permute-done.29 = bf16[3696,512]{1,0:T(8,128)(2,1)S(1)} collective-permute-done((bf16[3696,512]{1,0:T(8,128)(2,1)S(1)}, bf16[3696,512]{1,0:T(8,128)(2,1)S(1)}, u32[]{:S(2)}, u32[]{:S(2)}) %collective-permute-start.29) | collective-permute-done | bytes 3784736 | tf_op jit(solution)/shard_map/part/ppermute | solution.py:29
  132.9 3.0 %add_convert_fusion = bf16[3696,512]{1,0:T(8,128)(2,1)} fusion(bf16[3696,512]{1,0:T(8,128)(2,1)S(1)} %collective-permute-done.29, bf16[3696,512]{1,0:T(8,128)(2,1)S(1)} %merge_body.1), kind=kLoop, calls=%fused_computation | loop fusion | flops 7569408 | bytes 11354112 | tf_op jit(solution)/shard_map/convert_element_type | solution.py:468
  135.9 3.8 %collective-permute-done.30.other = bf16[64,3696]{1,0:T(8,128)(2,1)S(1)} collective-permute-done((bf16[64,3696]{1,0:T(8,128)(2,1)S(1)}, bf16[64,3696]{1,0:T(8,128)(2,1)S(1)}, u32[]{:S(2)}, u32[]{:S(2)}) %collective-permute-start.30) | collective-permute-done | bytes 473120 | tf_op jit(solution)/shard_map/t3/ppermute | solution.py:29
  139.7 1.0 here_body.1
  (38 shorter events, 0.4 us)
Async XLA Ops:
  2.3 9.5 %collective-permute-start.2 = (bf16[144,512]{1,0:T(8,128)(2,1)}, bf16[144,512]{1,0:T(8,128)(2,1)S(1)}, u32[]{:S(2)}, u32[]{:S(2)}) collective-permute-start(bf16[144,512]{1,0:T(8,128)(2,1)} %prep_body.1), channel_id=1, source_target_pairs={{0,3},{1,2},{2,1},{3,0},{4,7},{5,6},{6,5},{7,4},{8,11},{9,10},{10,... | collective-permute-start | bytes 442376 | tf_op jit(solution)/shard_map/payload_mate/ppermute | solution.py:29
  5.4 16.3 %collective-permute-start.4 = (bf16[64,3696]{1,0:T(8,128)(2,1)}, bf16[64,3696]{1,0:T(8,128)(2,1)S(1)}, u32[]{:S(2)}, u32[]{:S(2)}) collective-permute-start(bf16[64,3696]{1,0:T(8,128)(2,1)} %refs_4_.3), channel_id=1, source_target_pairs={{0,1},{1,0},{2,3},{3,2},{4,5},{5,4},{6,7},{7,6},{8,9},{9,8},{10,11... | collective-permute-start | bytes 1419272 | tf_op jit(solution)/shard_map/y3/ppermute | solution.py:29
  5.5 21.0 %collective-permute-start = (bf16[64,3696]{1,0:T(8,128)(2,1)}, bf16[64,3696]{1,0:T(8,128)(2,1)S(1)}, u32[]{:S(2)}, u32[]{:S(2)}) collective-permute-start(bf16[64,3696]{1,0:T(8,128)(2,1)} %refs_4_.3), channel_id=1, source_target_pairs={{0,4},{1,5},{2,6},{3,7},{4,8},{5,9},{6,10},{7,11},{8,12},{9,13},{1... | collective-permute-start | bytes 1419272 | tf_op jit(solution)/shard_map/down/ppermute | solution.py:29
  8.8 25.1 %collective-permute-start.1 = (bf16[64,3696]{1,0:T(8,128)(2,1)}, bf16[64,3696]{1,0:T(8,128)(2,1)S(1)}, u32[]{:S(2)}, u32[]{:S(2)}) collective-permute-start(bf16[64,3696]{1,0:T(8,128)(2,1)} %refs_4_.3), channel_id=1, source_target_pairs={{0,12},{1,13},{2,14},{3,15},{4,0},{5,1},{6,2},{7,3},{8,4},{9,5},{1... | collective-permute-start | bytes 1419272 | tf_op jit(solution)/shard_map/up/ppermute | solution.py:29
  12.8 8.1 %collective-permute-start.3 = (bf16[144,1024]{1,0:T(8,128)(2,1)S(1)}, bf16[144,1024]{1,0:T(8,128)(2,1)S(1)}, u32[]{:S(2)}, u32[]{:S(2)}) collective-permute-start(bf16[144,1024]{1,0:T(8,128)(2,1)S(1)} %pad_maximum_fusion.2.own), channel_id=1, source_target_pairs={{0,16},{16,0},{32,48},{48,32},{64,80},{80,64},{96,112},{112,96},{1... | collective-permute-start | bytes 884744 | tf_op jit(solution)/shard_map/block_x1/ppermute | solution.py:29
  15.3 58.1 %copy-start.2 = (bf16[64,3696]{1,0:T(8,128)(2,1)S(1)}, bf16[64,3696]{1,0:T(8,128)(2,1)}, u32[]{:S(2)}) copy-start(bf16[64,3696]{1,0:T(8,128)(2,1)} %refs_4_.3) | copy-start | bytes 1419268
  15.4 48.7 %collective-permute-start.15 = (bf16[1856,512]{1,0:T(8,128)(2,1)S(1)}, bf16[1856,512]{1,0:T(8,128)(2,1)S(1)}, u32[]{:S(2)}, u32[]{:S(2)}) collective-permute-start(bf16[1856,512]{1,0:T(8,128)(2,1)S(1)} %constant_dynamic-slice_fusion), channel_id=1, source_target_pairs={{0,3},{1,2},{2,1},{3,0},{4,7},{5,6},{6,5},{7,4},{8,11},{9,10},{10,... | collective-permute-start | bytes 5701640 | tf_op jit(solution)/shard_map/got/ppermute | solution.py:29
  21.1 22.8 %collective-permute-start.9 = (bf16[144,1024]{1,0:T(8,128)(2,1)S(1)}, bf16[144,1024]{1,0:T(8,128)(2,1)S(1)}, u32[]{:S(2)}, u32[]{:S(2)}) collective-permute-start(bf16[144,1024]{1,0:T(8,128)(2,1)S(1)} %get-tuple-element.56.block), channel_id=1, source_target_pairs={{0,48},{16,32},{32,16},{48,0},{64,112},{80,96},{96,80},{112,64},{1... | collective-permute-start | bytes 884744 | tf_op jit(solution)/shard_map/block_x3/ppermute | solution.py:29
  21.7 3.6 %collective-permute-start.5 = (f32[8,128]{1,0:T(8,128)S(1)}, f32[8,128]{1,0:T(8,128)S(1)}, u32[]{:S(2)}, u32[]{:S(2)}) collective-permute-start(f32[8,128]{1,0:T(8,128)S(1)} %get-tuple-element.52), channel_id=1, source_target_pairs={{0,1},{1,0},{2,3},{3,2},{4,5},{5,4},{6,7},{7,6},{8,9},{9,8},{10,11... | collective-permute-start | bytes 12296 | tf_op jit(solution)/shard_map/sums0/ppermute | solution.py:29
  33.9 8.2 %collective-permute-start.8 = (f32[8,128]{1,0:T(8,128)S(1)}, f32[8,128]{1,0:T(8,128)S(1)}, u32[]{:S(2)}, u32[]{:S(2)}) collective-permute-start(f32[8,128]{1,0:T(8,128)S(1)} %add.18), channel_id=1, source_target_pairs={{0,4},{1,5},{2,6},{3,7},{4,0},{5,1},{6,2},{7,3},{8,12},{9,13},{10,... | collective-permute-start | bytes 12296 | tf_op jit(solution)/shard_map/sums1/ppermute | solution.py:29
  37.7 10.8 %collective-permute-start.6 = (bf16[32,3696]{1,0:T(8,128)(2,1)S(1)}, bf16[32,3696]{1,0:T(8,128)(2,1)S(1)}, u32[]{:S(2)}, u32[]{:S(2)}) collective-permute-start(bf16[32,3696]{1,0:T(8,128)(2,1)S(1)} %slice.6), channel_id=1, source_target_pairs={{0,4},{1,5},{2,6},{3,7},{4,8},{5,9},{6,10},{7,11},{8,12},{9,13},{1... | collective-permute-start | bytes 709640 | tf_op jit(solution)/shard_map/far_a/ppermute | solution.py:29
  37.8 14.0 %collective-permute-start.7 = (bf16[32,3696]{1,0:T(8,128)(2,1)S(1)}, bf16[32,3696]{1,0:T(8,128)(2,1)S(1)}, u32[]{:S(2)}, u32[]{:S(2)}) collective-permute-start(bf16[32,3696]{1,0:T(8,128)(2,1)S(1)} %slice.7), channel_id=1, source_target_pairs={{0,12},{1,13},{2,14},{3,15},{4,0},{5,1},{6,2},{7,3},{8,4},{9,5},{1... | collective-permute-start | bytes 709640 | tf_op jit(solution)/shard_map/far_b/ppermute | solution.py:29
  42.1 31.4 %collective-permute-start.12 = (bf16[2,64,3696]{2,1,0:T(8,128)(2,1)S(1)}, bf16[2,64,3696]{2,1,0:T(8,128)(2,1)S(1)}, u32[]{:S(2)}, u32[]{:S(2)}) collective-permute-start(bf16[2,64,3696]{2,1,0:T(8,128)(2,1)S(1)} %pad_maximum_fusion), channel_id=1, source_target_pairs={{0,1},{1,0},{2,3},{3,2},{4,5},{5,4},{6,7},{7,6},{8,9},{9,8},{10,11... | collective-permute-start | bytes 2838536 | tf_op jit(solution)/shard_map/y12/ppermute | solution.py:29
  43.9 7.9 %collective-permute-start.10 = (f32[8,128]{1,0:T(8,128)S(1)}, f32[8,128]{1,0:T(8,128)S(1)}, u32[]{:S(2)}, u32[]{:S(2)}) collective-permute-start(f32[8,128]{1,0:T(8,128)S(1)} %add.19), channel_id=1, source_target_pairs={{0,12},{1,13},{2,14},{3,15},{4,8},{5,9},{6,10},{7,11},{8,4},{9,5},... | collective-permute-start | bytes 12296 | tf_op jit(solution)/shard_map/sums2/ppermute | solution.py:29
  48.5 18.1 %collective-permute-start.17 = (bf16[288,1024]{1,0:T(8,128)(2,1)S(1)}, bf16[288,1024]{1,0:T(8,128)(2,1)S(1)}, u32[]{:S(2)}, u32[]{:S(2)}) collective-permute-start(bf16[288,1024]{1,0:T(8,128)(2,1)S(1)} %constant_dynamic-update-slice_fusion.2.here), channel_id=1, source_target_pairs={{0,64},{16,80},{32,96},{48,112},{64,0},{80,16},{96,32},{112,48},{1... | collective-permute-start | bytes 1769480 | tf_op jit(solution)/shard_map/block_zlo/ppermute | solution.py:29
  51.8 21.6 %collective-permute-start.11 = (bf16[64,3696]{1,0:T(8,128)(2,1)S(1)}, bf16[64,3696]{1,0:T(8,128)(2,1)S(1)}, u32[]{:S(2)}, u32[]{:S(2)}) collective-permute-start(bf16[64,3696]{1,0:T(8,128)(2,1)S(1)} %pad_maximum_fusion.1), channel_id=1, source_target_pairs={{0,1},{1,0},{2,3},{3,2},{4,5},{5,4},{6,7},{7,6},{8,9},{9,8},{10,11... | collective-permute-start | bytes 1419272 | tf_op jit(solution)/shard_map/y0/ppermute | solution.py:29
  53.6 1.2 collective-permute-start.13
  54.8 4.9 %collective-permute-start.14 = (f32[24,128]{1,0:T(8,128)S(1)}, f32[24,128]{1,0:T(8,128)S(1)}, u32[]{:S(2)}, u32[]{:S(2)}) collective-permute-start(f32[24,128]{1,0:T(8,128)S(1)} %pad_maximum_fusion.3), channel_id=1, source_target_pairs={{0,48},{16,32},{32,16},{48,0},{64,112},{80,96},{96,80},{112,64},{1... | collective-permute-start | bytes 36872 | tf_op jit(solution)/shard_map/tiny_x3/ppermute | solution.py:29
  59.7 4.4 %collective-permute-start.16 = (f32[48,128]{1,0:T(8,128)S(1)}, f32[48,128]{1,0:T(8,128)S(1)}, u32[]{:S(2)}, u32[]{:S(2)}) collective-permute-start(f32[48,128]{1,0:T(8,128)S(1)} %constant_dynamic-update-slice_fusion.here), channel_id=1, source_target_pairs={{0,64},{16,80},{32,96},{48,112},{64,0},{80,16},{96,32},{112,48},{1... | collective-permute-start | bytes 73736 | tf_op jit(solution)/shard_map/tiny_zlo/ppermute | solution.py:29
  64.1 11.7 %collective-permute-start.19 = (bf16[1856,512]{1,0:T(8,128)(2,1)S(1)}, bf16[1856,512]{1,0:T(8,128)(2,1)S(1)}, u32[]{:S(2)}, u32[]{:S(2)}) collective-permute-start(bf16[1856,512]{1,0:T(8,128)(2,1)S(1)} %collective-permute-done.15.got), channel_id=1, source_target_pairs={{0,128},{128,0},{1,129},{129,1},{2,130},{130,2},{3,131},{131,3},{4... | collective-permute-start | bytes 5701640 | tf_op jit(solution)/shard_map/got_other/ppermute | solution.py:29
  65.5 4.9 %collective-permute-start.18 = (f32[8,128]{1,0:T(8,128)S(1)}, f32[8,128]{1,0:T(8,128)S(1)}, u32[]{:S(2)}, u32[]{:S(2)}) collective-permute-start(f32[8,128]{1,0:T(8,128)S(1)} %coefs_body.1.coefs), channel_id=1, source_target_pairs={{0,3},{1,2},{2,1},{3,0},{4,7},{5,6},{6,5},{7,4},{8,11},{9,10},{10,... | collective-permute-start | bytes 12296 | tf_op jit(solution)/shard_map/coefs_mate/ppermute | solution.py:29
  67.7 8.1 %copy-start = (bf16[3696,512]{1,0:T(8,128)(2,1)S(1)}, bf16[3696,512]{1,0:T(8,128)(2,1)}, u32[]{:S(2)}) copy-start(bf16[3696,512]{1,0:T(8,128)(2,1)} %w.3) | copy-start | bytes 11354116
  75.7 4.5 %collective-permute-start.21 = (bf16[3696,256]{1,0:T(8,128)(2,1)S(1)}, bf16[3696,256]{1,0:T(8,128)(2,1)S(1)}, u32[]{:S(2)}, u32[]{:S(2)}) collective-permute-start(bf16[3696,256]{1,0:T(8,128)(2,1)S(1)} %get-tuple-element.73), channel_id=1, source_target_pairs={{0,128},{128,0},{1,129},{129,1},{2,130},{130,2},{3,131},{131,3},{4... | collective-permute-start | bytes 5677064 | tf_op jit(solution)/shard_map/mate_got/ppermute | solution.py:29
  80.8 44.9 %collective-permute-start.28 = (bf16[3696,256]{1,0:T(8,128)(2,1)S(1)}, bf16[3696,256]{1,0:T(8,128)(2,1)S(1)}, u32[]{:S(2)}, u32[]{:S(2)}) collective-permute-start(bf16[3696,256]{1,0:T(8,128)(2,1)S(1)} %add_convert_fusion.1), channel_id=1, source_target_pairs={{0,3},{1,2},{2,1},{3,0},{4,7},{5,6},{6,5},{7,4},{8,11},{9,10},{10,... | collective-permute-start | bytes 5677064 | tf_op jit(solution)/shard_map/w_recv/ppermute | solution.py:29
  81.7 13.7 %collective-permute-start.20 = (bf16[64,3696]{1,0:T(8,128)(2,1)S(1)}, bf16[64,3696]{1,0:T(8,128)(2,1)S(1)}, u32[]{:S(2)}, u32[]{:S(2)}) collective-permute-start(bf16[64,3696]{1,0:T(8,128)(2,1)S(1)} %get-tuple-element.69), channel_id=1, source_target_pairs={{0,1},{1,0},{2,3},{3,2},{4,5},{5,4},{6,7},{7,6},{8,9},{9,8},{10,11... | collective-permute-start | bytes 1419272 | tf_op jit(solution)/shard_map/t0/ppermute | solution.py:29
  82.7 23.0 %collective-permute-start.25 = (bf16[64,3696]{1,0:T(8,128)(2,1)S(1)}, bf16[64,3696]{1,0:T(8,128)(2,1)S(1)}, u32[]{:S(2)}, u32[]{:S(2)}) collective-permute-start(bf16[64,3696]{1,0:T(8,128)(2,1)S(1)} %get-tuple-element.85), channel_id=1, source_target_pairs={{0,1},{1,0},{2,3},{3,2},{4,5},{5,4},{6,7},{7,6},{8,9},{9,8},{10,11... | collective-permute-start | bytes 1419272 | tf_op jit(solution)/shard_map/t1/ppermute | solution.py:29
  95.5 10.1 %collective-permute-start.24 = (bf16[32,3696]{1,0:T(8,128)(2,1)S(1)}, bf16[32,3696]{1,0:T(8,128)(2,1)S(1)}, u32[]{:S(2)}, u32[]{:S(2)}) collective-permute-start(bf16[32,3696]{1,0:T(8,128)(2,1)S(1)} %get-tuple-element.81), channel_id=1, source_target_pairs={{0,12},{1,13},{2,14},{3,15},{4,0},{5,1},{6,2},{7,3},{8,4},{9,5},{1... | collective-permute-start | bytes 709640 | tf_op jit(solution)/shard_map/from_up/ppermute | solution.py:29
  95.9 19.2 %collective-permute-start.22 = (bf16[64,3696]{1,0:T(8,128)(2,1)S(1)}, bf16[64,3696]{1,0:T(8,128)(2,1)S(1)}, u32[]{:S(2)}, u32[]{:S(2)}) collective-permute-start(bf16[64,3696]{1,0:T(8,128)(2,1)S(1)} %get-tuple-element.78), channel_id=1, source_target_pairs={{0,1},{1,0},{2,3},{3,2},{4,5},{5,4},{6,7},{7,6},{8,9},{9,8},{10,11... | collective-permute-start | bytes 1419272 | tf_op jit(solution)/shard_map/t2/ppermute | solution.py:29
  96.8 11.9 %copy-start.1 = (bf16[128,512]{1,0:T(8,128)(2,1)S(1)}, bf16[128,512]{1,0:T(8,128)(2,1)}, u32[]{:S(2)}) copy-start(bf16[128,512]{1,0:T(8,128)(2,1)} %stream.2) | copy-start | bytes 393220
  96.8 18.2 %collective-permute-start.23 = (bf16[32,3696]{1,0:T(8,128)(2,1)S(1)}, bf16[32,3696]{1,0:T(8,128)(2,1)S(1)}, u32[]{:S(2)}, u32[]{:S(2)}) collective-permute-start(bf16[32,3696]{1,0:T(8,128)(2,1)S(1)} %get-tuple-element.75), channel_id=1, source_target_pairs={{0,4},{1,5},{2,6},{3,7},{4,8},{5,9},{6,10},{7,11},{8,12},{9,13},{1... | collective-permute-start | bytes 709640 | tf_op jit(solution)/shard_map/from_down/ppermute | solution.py:29
  105.7 10.8 %collective-permute-start.26 = (bf16[32,3696]{1,0:T(8,128)(2,1)S(1)}, bf16[32,3696]{1,0:T(8,128)(2,1)S(1)}, u32[]{:S(2)}, u32[]{:S(2)}) collective-permute-start(bf16[32,3696]{1,0:T(8,128)(2,1)S(1)} %get-tuple-element.87), channel_id=1, source_target_pairs={{0,12},{1,13},{2,14},{3,15},{4,0},{5,1},{6,2},{7,3},{8,4},{9,5},{1... | collective-permute-start | bytes 709640 | tf_op jit(solution)/shard_map/pure_a/ppermute | solution.py:29
  107.6 12.5 %collective-permute-start.27 = (bf16[32,3696]{1,0:T(8,128)(2,1)S(1)}, bf16[32,3696]{1,0:T(8,128)(2,1)S(1)}, u32[]{:S(2)}, u32[]{:S(2)}) collective-permute-start(bf16[32,3696]{1,0:T(8,128)(2,1)S(1)} %get-tuple-element.88), channel_id=1, source_target_pairs={{0,4},{1,5},{2,6},{3,7},{4,8},{5,9},{6,10},{7,11},{8,12},{9,13},{1... | collective-permute-start | bytes 709640 | tf_op jit(solution)/shard_map/pure_b/ppermute | solution.py:29
  126.3 6.7 %collective-permute-start.29 = (bf16[3696,512]{1,0:T(8,128)(2,1)S(1)}, bf16[3696,512]{1,0:T(8,128)(2,1)S(1)}, u32[]{:S(2)}, u32[]{:S(2)}) collective-permute-start(bf16[3696,512]{1,0:T(8,128)(2,1)S(1)} %merge_body.1), channel_id=1, source_target_pairs={{0,128},{128,0},{1,129},{129,1},{2,130},{130,2},{3,131},{131,3},{4... | collective-permute-start | bytes 11354120 | tf_op jit(solution)/shard_map/part/ppermute | solution.py:29
  126.4 13.3 %collective-permute-start.30 = (bf16[64,3696]{1,0:T(8,128)(2,1)S(1)}, bf16[64,3696]{1,0:T(8,128)(2,1)S(1)}, u32[]{:S(2)}, u32[]{:S(2)}) collective-permute-start(bf16[64,3696]{1,0:T(8,128)(2,1)S(1)} %get-tuple-element.93), channel_id=1, source_target_pairs={{0,1},{1,0},{2,3},{3,2},{4,5},{5,4},{6,7},{7,6},{8,9},{9,8},{10,11... | collective-permute-start | bytes 1419272 | tf_op jit(solution)/shard_map/t3/ppermute | solution.py:29
  127.0 12.7 %collective-permute-start.31 = (bf16[32,3696]{1,0:T(8,128)(2,1)S(1)}, bf16[32,3696]{1,0:T(8,128)(2,1)S(1)}, u32[]{:S(2)}, u32[]{:S(2)}) collective-permute-start(bf16[32,3696]{1,0:T(8,128)(2,1)S(1)} %get-tuple-element.89), channel_id=1, source_target_pairs={{0,4},{1,5},{2,6},{3,7},{4,8},{5,9},{6,10},{7,11},{8,12},{9,13},{1... | collective-permute-start | bytes 709640 | tf_op jit(solution)/shard_map/mixed_a/ppermute | solution.py:29
  127.0 12.6 %collective-permute-start.32 = (bf16[32,3696]{1,0:T(8,128)(2,1)S(1)}, bf16[32,3696]{1,0:T(8,128)(2,1)S(1)}, u32[]{:S(2)}, u32[]{:S(2)}) collective-permute-start(bf16[32,3696]{1,0:T(8,128)(2,1)S(1)} %get-tuple-element.96), channel_id=1, source_target_pairs={{0,12},{1,13},{2,14},{3,15},{4,0},{5,1},{6,2},{7,3},{8,4},{9,5},{1... | collective-permute-start | bytes 709640 | tf_op jit(solution)/shard_map/mixed_b/ppermute | solution.py:29
